TPU v7x, 256 devices: a whole 4x4x8 slice. The times are simulated.
256 devices in a mesh: loop: 32 (over y_lo, z, core), rep: 8 (over x, y_hi).
Axes of the slice: x: 4, y: 4 (y_hi: 2, y_lo: 2; y = y_hi * 2 + y_lo), z: 8, core: 2. Of those that a mesh axis runs over, the one named last changes fastest.
Arguments:
- ham_blocks: bfloat16 [256, 24, 128, 128], P('loop', 'rep'), may hold values from -0.109375 to 0.109375
- margin_blocks: bfloat16 [256, 24, 128, 128], P('loop', 'rep'), may hold values from -0.109375 to 0.109375
- block_cols: int32 [256, 24], P('loop'), may hold values from 0 to 255, as said below
- block_counts: int32 [256], P('loop'), may hold values from 12 to 24
- pert_real: bfloat16 [32768, 1024], P('loop', 'rep'), may hold values from -6 to 6
- pert_imag: bfloat16 [32768, 1024], P('loop', 'rep'), may hold values from -6 to 6
- drive_real: bfloat16 [32768, 1024], P('loop', 'rep'), may hold values from -6 to 6
- drive_imag: bfloat16 [32768, 1024], P('loop', 'rep'), may hold values from -6 to 6
Outputs:
- new_real: float32 [32768, 1024], P('loop', 'rep')
- new_imag: float32 [32768, 1024], P('loop', 'rep')
Inputs may be any that keep to these rules, and one draw needn't show every extreme that they name: `block_cols`: the 24 entries of a row are distinct block columns.
All inputs are finite; a program needn't handle non-finite values.
Results may differ from a plain program's by a relative error of at most 0.0003.
Values may be sent and summed in bfloat16 or wider, within the bound.
No kernel may reach another device: no remote copies, remote signals or barrier semaphores. Data moves between devices by JAX's collectives and lax.ppermute only.
A program may use at most 128 MiB of HBM per device.

v0:
```python
import jax
import jax.numpy as jnp
from jax import lax
from jax.sharding import PartitionSpec as P

frequency = 0.7
damping = 0.5
step_length = 0.5


def per_device(
    ham_blocks,
    margin_blocks,
    block_cols,
    block_counts,
    pert_real,
    pert_imag,
    drive_real,
    drive_imag,
):
    ham_rows, margin_rows = (
        lax.all_gather(ham_blocks, "rep", axis=1, tiled=True),
        lax.all_gather(margin_blocks, "rep", axis=1, tiled=True),
    )
    rows_here = ham_rows.shape[0]
    slots = ham_rows.shape[1]
    block = ham_rows.shape[2]
    width = pert_real.shape[1]
    total_blocks = rows_here * lax.axis_size("loop")
    live = jnp.arange(slots, dtype=jnp.int32)[None, :] < block_counts[:, None]
    whole_real, whole_imag = (
        lax.all_gather(pert_real, "loop", axis=0, tiled=True),
        lax.all_gather(pert_imag, "loop", axis=0, tiled=True),
    )
    joined = jnp.concatenate([whole_real, whole_imag], axis=1).reshape(
        total_blocks, block, 2 * width
    )
    picked = joined[block_cols]
    picked = jnp.where(live[:, :, None, None], picked, jnp.zeros((), jnp.bfloat16))
    ham_prod = jnp.einsum("ikab,ikbn->ian", ham_rows, picked, preferred_element_type=jnp.float32)
    margin_prod = jnp.einsum(
        "ikab,ikbn->ian", margin_rows, picked, preferred_element_type=jnp.float32
    )
    ham_prod = ham_prod.reshape(rows_here * block, 2 * width)
    margin_prod = margin_prod.reshape(rows_here * block, 2 * width)
    ham_real, ham_imag = (ham_prod[:, :width], ham_prod[:, width:])
    ovl_real, ovl_imag = (margin_prod[:, :width], margin_prod[:, width:])
    res_real = drive_real.astype(jnp.float32) - (
        ham_real - frequency * ovl_real + damping * ovl_imag
    )
    res_imag = drive_imag.astype(jnp.float32) - (
        ham_imag - frequency * ovl_imag - damping * ovl_real
    )
    new_real = pert_real.astype(jnp.float32) + step_length * res_real
    new_imag = pert_imag.astype(jnp.float32) + step_length * res_imag
    return (new_real, new_imag)


def solution(mesh):
    return jax.shard_map(
        per_device,
        mesh=mesh,
        in_specs=(
            P("loop", "rep", None, None),
            P("loop", "rep", None, None),
            P("loop", None),
            P("loop"),
            P("loop", "rep"),
            P("loop", "rep"),
            P("loop", "rep"),
            P("loop", "rep"),
        ),
        out_specs=(P("loop", "rep"), P("loop", "rep")),
        check_vma=False,
    )
```

profile of v0, /device:TPU:1, one launch (start us, length us, event | category | flops | bytes accessed | tf_op | source)
XLA Modules:
  0.0 368.3 jit_solution(14518250644076242140)
XLA Ops:
  7.2 0.0 all-gather.5.cloned.1.call-start
  7.2 0.7 all-gather.5.cloned.1.call-update
  7.9 0.0 all-gather.7.cloned.1.call-start
  7.9 0.7 all-gather.7.cloned.1.call-update
  8.6 0.0 all-gather.9.cloned.1.call-start
  8.7 0.7 all-gather.9.cloned.1.call-update
  9.4 0.0 all-gather.11.cloned.1.call-start
  9.4 0.5 all-gather.11.cloned.1.call-update
  10.0 0.7 compare_select_fusion
  10.6 0.1 reshape.39
  10.7 0.7 iota_compare_fusion
  11.5 74.9 %all-gather.5.cloned.1.call-done = bf16[32768,128]{1,0:T(8,128)(2,1)} async-done(((bf16[1024,128]{1,0:T(8,128)(2,1)}), bf16[32768,128]{1,0:T(8,128)(2,1)}) %all-gather.5.cloned.1.call-update) | async-done | bytes 8388624 | tf_op jit(solution)/shard_map/all_gather | solution.py:32
  86.4 74.1 %all-gather.7.cloned.1.call-done = bf16[32768,128]{1,0:T(8,128)(2,1)} async-done(((bf16[1024,128]{1,0:T(8,128)(2,1)}), bf16[32768,128]{1,0:T(8,128)(2,1)}) %all-gather.7.cloned.1.call-update) | async-done | bytes 8388624 | tf_op jit(solution)/shard_map/all_gather | solution.py:33
  160.5 13.9 %pad_maximum_fusion = bf16[32768,256]{1,0:T(8,128)(2,1)} fusion(bf16[32768,128]{1,0:T(8,128)(2,1)} %all-gather.7.cloned.1.call-done, bf16[32768,128]{1,0:T(8,128)(2,1)} %all-gather.5.cloned.1.call-done), kind=kLoop, calls=%fused_computation.1 | loop fusion | flops 33554432 | bytes 33554432 | tf_op jit(solution)/shard_map/concatenate | solution.py:35
  174.3 14.6 %gather_fusion = bf16[192,128,256]{2,1,0:T(8,128)(2,1)} fusion(bf16[256,128,256]{2,1,0:T(8,128)(2,1)} %bitcast.16, s32[1024]{0:T(1024)S(1)} %pad_clamp_fusion), kind=kCustom, calls=%fused_computation | custom fusion | bytes 25166592 | tf_op jit(solution)/shard_map/gather | solution.py:38
  189.0 67.9 %all-gather.9.cloned.1.call-done = bf16[8,24,128,128]{3,2,1,0:T(8,128)(2,1)} async-done(((bf16[8,3,128,128]{3,2,1,0:T(8,128)(2,1)}), bf16[8,24,128,128]{3,2,1,0:T(8,128)(2,1)}) %all-gather.9.cloned.1.call-update) | async-done | bytes 6291472 | tf_op jit(solution)/shard_map/all_gather | solution.py:22
  256.9 8.4 %fusion = f32[8,256,128,1]{1,2,3,0:T(8,128)S(1)} fusion(bf16[8,24,128,128]{3,2,1,0:T(8,128)(2,1)} %all-gather.9.cloned.1.call-done, bf16[8,24,128,256]{3,2,1,0:T(8,128)(2,1)} %bitcast.17, pred[8,24]{1,0:T(8,128)(4,1)S(1)} %iota_compare_fusion), kind=kOutput, calls=%fused_computation.3 | convolution fusion | flops 1616904192 | bytes 19923136 | tf_op jit(solution)/shard_map/ikab,ikbn->ian/dot_general | solution.py:40
  265.3 0.0 copy-start
  265.3 0.0 copy-start.1
  265.3 0.0 copy-start.2
  265.3 0.0 copy-start.3
  265.3 86.7 %all-gather.11.cloned.1.call-done = bf16[8,24,128,128]{3,2,1,0:T(8,128)(2,1)} async-done(((bf16[8,3,128,128]{3,2,1,0:T(8,128)(2,1)}), bf16[8,24,128,128]{3,2,1,0:T(8,128)(2,1)}) %all-gather.11.cloned.1.call-update) | async-done | bytes 6291472 | tf_op jit(solution)/shard_map/all_gather | solution.py:23
  352.0 8.4 %fusion.1 = f32[8,256,128,1]{1,2,3,0:T(8,128)S(1)} fusion(bf16[8,24,128,128]{3,2,1,0:T(8,128)(2,1)} %all-gather.11.cloned.1.call-done, bf16[8,24,128,256]{3,2,1,0:T(8,128)(2,1)} %bitcast.18, pred[8,24]{1,0:T(8,128)(4,1)S(1)} %iota_compare_fusion), kind=kOutput, calls=%fused_computation.4 | convolution fusion | flops 1616904192 | bytes 19923136 | tf_op jit(solution)/shard_map/ikab,ikbn->ian/dot_general | solution.py:41
  360.5 0.0 copy-done
  360.5 0.0 copy-done.1
  360.5 0.0 copy-done.2
  360.5 0.0 copy-done.3
  360.5 1.3 fusion.7
  (1 shorter events, 0.0 us)
Async XLA Ops:
  7.2 79.2 %all-gather.5.cloned.1.call-start = ((), (), s32[]{:S(2)}) async-start(), calls=%async_computation | async-start | bytes 8650752 | tf_op jit(solution)/shard_map/all_gather | solution.py:32
  7.9 152.6 %all-gather.7.cloned.1.call-start = ((), (), s32[]{:S(2)}) async-start(), calls=%async_computation.1 | async-start | bytes 8650752 | tf_op jit(solution)/shard_map/all_gather | solution.py:33
  8.6 248.2 %all-gather.9.cloned.1.call-start = ((), (), s32[]{:S(2)}) async-start(), calls=%async_computation.2 | async-start | bytes 7077888 | tf_op jit(solution)/shard_map/all_gather | solution.py:22
  9.4 342.7 %all-gather.11.cloned.1.call-start = ((), (), s32[]{:S(2)}) async-start(), calls=%async_computation.3 | async-start | bytes 7077888 | tf_op jit(solution)/shard_map/all_gather | solution.py:23
  265.3 95.2 %copy-start = (bf16[1024,128]{1,0:T(8,128)(2,1)S(1)}, bf16[1024,128]{1,0:T(8,128)(2,1)}, u32[]{:S(2)}) copy-start(bf16[1024,128]{1,0:T(8,128)(2,1)} %param.12) | copy-start | bytes 786436
  265.3 95.2 %copy-start.1 = (bf16[1024,128]{1,0:T(8,128)(2,1)S(1)}, bf16[1024,128]{1,0:T(8,128)(2,1)}, u32[]{:S(2)}) copy-start(bf16[1024,128]{1,0:T(8,128)(2,1)} %param.13) | copy-start | bytes 786436
  265.3 95.2 %copy-start.2 = (bf16[1024,128]{1,0:T(8,128)(2,1)S(1)}, bf16[1024,128]{1,0:T(8,128)(2,1)}, u32[]{:S(2)}) copy-start(bf16[1024,128]{1,0:T(8,128)(2,1)} %param.15) | copy-start | bytes 786436
  265.3 95.2 %copy-start.3 = (bf16[1024,128]{1,0:T(8,128)(2,1)S(1)}, bf16[1024,128]{1,0:T(8,128)(2,1)}, u32[]{:S(2)}) copy-start(bf16[1024,128]{1,0:T(8,128)(2,1)} %param.14) | copy-start | bytes 786436
Sparse Core Ops, SparseCore 0:
  9.9 76.4 all-gather.4
  88.2 72.1 all-gather.6
  163.1 93.7 all-gather.8
  259.3 92.6 all-gather.10
where the time goes:
time: 369 us; the launch traced here: 368 us
  waiting for transfers between devices  306 us (83%)
  matrix products  16.8 us (5%)
  other arithmetic  16.6 us (4%)
  local copies, waits for them, and re-layouts  14.7 us (4%)
  between operations  13.8 us (4%)
    all_gather x1, waiting for transfers between devices, per_device(): lax.all_gather(margin_blocks, 'rep', axis=1, tiled=True)  86.7 us
    all_gather x1, waiting for transfers between devices, per_device(): lax.all_gather(pert_real, 'loop', axis=0, tiled=True)  74.9 us
    all_gather x1, waiting for transfers between devices, per_device(): lax.all_gather(pert_imag, 'loop', axis=0, tiled=True)  74.1 us
    all_gather x1, waiting for transfers between devices, per_device(): lax.all_gather(ham_blocks, 'rep', axis=1, tiled=True)  67.9 us
    gather x1, local copies, waits for them, and re-layouts, per_device(): picked = joined[block_cols]  14.6 us
    concatenate x1, other arithmetic, per_device(): jnp.concatenate([whole_real, whole_imag], axis=1)  13.9 us
    dot_general x1, matrix products, per_device(): jnp.einsum('ikab,ikbn->ian', margin_rows, picked, preferred_element_type=...  8.4 us
    dot_general x1, matrix products, per_device(): jnp.einsum('ikab,ikbn->ian', ham_rows, picked, preferred_element_type=jnp...  8.4 us
  transfers between devices with their start and end apart: 4, of which 4 were waited for; matrix products, arithmetic and copies ran while one was open for 10% of the time, Pallas kernels for 0%

commit v1 on v0

v1 whole, which is shorter than its diff:
```python
import functools

import jax
import jax.numpy as jnp
from jax import lax
from jax.experimental import pallas as pl
from jax.experimental.pallas import tpu as pltpu
from jax.sharding import PartitionSpec as P

frequency = 0.7
damping = 0.5
step_length = 0.5

AXES = ("ylo", "z", "core", "x", "yhi")
SIZES = (2, 8, 2, 4, 2)
BLOCK = 128


def moves(axis, by):
    place = AXES.index(axis)
    stride = 1
    for size in SIZES[place + 1 :]:
        stride *= size
    total = 1
    for size in SIZES:
        total *= size
    pairs = []
    for source in range(total):
        at = source // stride % SIZES[place]
        pairs.append((source, source + ((at + by) % SIZES[place] - at) * stride))
    return pairs


def shift(array, axis, by=1):
    return lax.ppermute(array, AXES, moves(axis, by))


def slot_list():
    out = []
    for j in range(3):
        out.append(("own", j, 0, 0, j))
    for j in range(3):
        out.append(("from_left", j, 3, 0, j))
    for j in range(3):
        out.append(("from_right", j, 1, 0, j))
    for j in range(3):
        out.append(("far", j, 2, 0, j))
    for j in range(3):
        out.append(("part", j, 0, 1, j))
    for j in range(2):
        out.append(("part_left", j, 3, 1, j))
    for j in range(2):
        out.append(("part_right", j, 1, 1, j))
    for j in range(2):
        out.append(("part_far", j, 2, 1, j))
    out.append(("late", 0, 3, 1, 2))
    out.append(("late", 1, 1, 1, 2))
    out.append(("late_far", 0, 2, 1, 2))
    return out


def product_kernel(
    half,
    last,
    place_ref,
    cols_ref,
    counts_ref,
    *refs,
):
    refs = list(refs)
    panel_own, panel_other = refs[:2]
    pieces = {
        "own": refs[2],
        "from_left": refs[3],
        "from_right": refs[4],
        "far": (refs[5], refs[6]),
        "part": refs[7],
        "part_left": refs[8],
        "part_right": refs[9],
        "part_far": (refs[10], refs[11]),
        "late": refs[12],
        "late_far": refs[13],
    }
    if last:
        before, pert_real, pert_imag, drive_real, drive_imag = refs[14:19]
        new_real, new_imag, panel, sems = refs[19:]
    else:
        acc_out, panel, sems = refs[14:]
    row = pl.program_id(0)
    count = panel_own.shape[0]
    my_ylo, my_core, my_x, my_yhi = (place_ref[n] for n in range(4))

    @pl.when(row == 0)
    def _():
        copies = [
            pltpu.make_async_copy(panel_own, panel.at[pl.ds(my_core * count, count)], sems.at[0]),
            pltpu.make_async_copy(panel_other, panel.at[pl.ds((1 - my_core) * count, count)], sems.at[1]),
        ]
        for copy in copies:
            copy.start()
        for copy in copies:
            copy.wait()

    slots = slot_list()
    total = None
    for first in range(0, 24, 8):
        left, right = [], []
        for name, position, dx, dy, j in slots[first : first + 8]:
            ref = pieces[name]
            if isinstance(ref, tuple):
                top, bottom = ref[0][0, position], ref[1][0, position]
            else:
                top, bottom = ref[0, 0, position], ref[1, 0, position]
            left.append(jnp.concatenate([top, bottom], axis=0))
            slot = 3 * (2 * ((my_x + dx) & 3) + (my_yhi ^ dy)) + j
            column = cols_ref[row, slot]
            owner = column >> 3
            use = (slot < counts_ref[row]) & (((owner >> 4) ^ my_ylo) == half)
            block = panel[(owner & 1) * count + ((owner >> 1) & 7) * 8 + (column & 7)]
            right.append(jnp.where(use, block, jnp.zeros_like(block)))
        term = jnp.dot(
            jnp.concatenate(left, axis=1),
            jnp.concatenate(right, axis=0),
            preferred_element_type=jnp.float32,
        )
        total = term if total is None else total + term
    if not last:
        acc_out[0] = total
        return
    total = total + before[0]
    ham_real, ham_imag = total[:BLOCK, :BLOCK], total[:BLOCK, BLOCK:]
    ovl_real, ovl_imag = total[BLOCK:, :BLOCK], total[BLOCK:, BLOCK:]
    res_real = drive_real[...].astype(jnp.float32) - (
        ham_real - frequency * ovl_real + damping * ovl_imag
    )
    res_imag = drive_imag[...].astype(jnp.float32) - (
        ham_imag - frequency * ovl_imag - damping * ovl_real
    )
    new_real[...] = pert_real[...].astype(jnp.float32) + step_length * res_real
    new_imag[...] = pert_imag[...].astype(jnp.float32) + step_length * res_imag


def products(half, place, cols, counts, panel_own, panel_other, pieces, tail=None):
    last = tail is not None
    rows = cols.shape[0]
    whole = pl.BlockSpec(memory_space=pl.ANY)

    def by_row(array):
        if array.ndim == 5:
            n = array.shape[2]
            return pl.BlockSpec((2, 1, n, BLOCK, BLOCK), lambda i, *_: (0, i, 0, 0, 0))
        n = array.shape[1]
        return pl.BlockSpec((1, n, BLOCK, BLOCK), lambda i, *_: (i, 0, 0, 0))

    acc_spec = pl.BlockSpec((1, 2 * BLOCK, 2 * BLOCK), lambda i, *_: (i, 0, 0))
    flat_spec = pl.BlockSpec((BLOCK, BLOCK), lambda i, *_: (i, 0))
    in_specs = [whole, whole] + [by_row(a) for a in pieces]
    args = [panel_own, panel_other] + list(pieces)
    if last:
        in_specs += [acc_spec] + [flat_spec] * 4
        args += list(tail)
        out_specs = [flat_spec] * 2
        out_shape = [jax.ShapeDtypeStruct((rows * BLOCK, BLOCK), jnp.float32)] * 2
    else:
        out_specs = acc_spec
        out_shape = jax.ShapeDtypeStruct((rows, 2 * BLOCK, 2 * BLOCK), jnp.float32)
    return pl.pallas_call(
        functools.partial(product_kernel, half, last),
        grid_spec=pltpu.PrefetchScalarGridSpec(
            num_scalar_prefetch=3,
            grid=(rows,),
            in_specs=in_specs,
            out_specs=out_specs,
            scratch_shapes=[
                pltpu.VMEM((2 * panel_own.shape[0], BLOCK, 2 * BLOCK), jnp.bfloat16),
                pltpu.SemaphoreType.DMA((2,)),
            ],
        ),
        out_shape=out_shape,
        compiler_params=pltpu.CompilerParams(vmem_limit_bytes=40 * 2**20),
        cost_estimate=pl.CostEstimate(
            flops=2 * rows * 24 * 2 * BLOCK * BLOCK * 2 * BLOCK,
            bytes_accessed=22 * 2**20,
            transcendentals=0,
        ),
        name="products_last" if last else "products_first",
    )(place, cols, counts, *args)


def per_device(
    ham_blocks,
    margin_blocks,
    block_cols,
    block_counts,
    pert_real,
    pert_imag,
    drive_real,
    drive_imag,
):
    rows = block_cols.shape[0]
    place = jnp.stack([lax.axis_index(a) for a in ("ylo", "core", "x", "yhi")]).astype(jnp.int32)

    panel = jnp.concatenate([pert_real, pert_imag], axis=1).reshape(rows, BLOCK, 2 * BLOCK)
    both = jnp.stack([ham_blocks, margin_blocks], axis=0)

    near = lax.all_gather(panel, "z", axis=0, tiled=True)
    neighbour = shift(panel, "ylo")
    from_left = shift(both, "x", 1)
    from_right = shift(both, "x", -1)
    part = shift(both, "yhi")
    far = lax.all_gather(neighbour, "z", axis=0, tiled=True)
    near_other = shift(near, "core")

    far_ham = shift(from_left[0], "x", 1)
    far_margin = shift(from_right[1], "x", -1)
    late = shift(jnp.concatenate([from_left[:, :, 2:], from_right[:, :, 2:]], axis=2), "yhi")
    part_two = part[:, :, :2]
    part_left = shift(part_two, "x", 1)
    part_right = shift(part_two, "x", -1)
    late_far = shift(jnp.stack([far_ham[:, 2:], far_margin[:, 2:]], axis=0), "yhi")
    part_far_ham = shift(part_left[0], "x", 1)
    part_far_margin = shift(part_right[1], "x", -1)
    far_other = shift(far, "core")

    pieces = (
        both,
        from_left,
        from_right,
        far_ham,
        far_margin,
        part,
        part_left,
        part_right,
        part_far_ham,
        part_far_margin,
        late,
        late_far,
    )
    before = products(0, place, block_cols, block_counts, near, near_other, pieces)
    new_real, new_imag = products(
        1,
        place,
        block_cols,
        block_counts,
        far,
        far_other,
        pieces,
        (before, pert_real, pert_imag, drive_real, drive_imag),
    )
    return new_real, new_imag


def solution(mesh):
    fine = jax.sharding.Mesh(mesh.devices.reshape(SIZES), AXES)
    loop, rep = ("ylo", "z", "core"), ("x", "yhi")
    return jax.shard_map(
        per_device,
        mesh=fine,
        in_specs=(
            P(loop, rep, None, None),
            P(loop, rep, None, None),
            P(loop, None),
            P(loop),
            P(loop, rep),
            P(loop, rep),
            P(loop, rep),
            P(loop, rep),
        ),
        out_specs=(P(loop, rep), P(loop, rep)),
        check_vma=False,
    )
```

time: 369 us -> 239 us (0.65)
  waiting for transfers between devices: 306 us -> 156 us
  starting transfers between devices: 0.15 us -> 23.5 us
  Pallas kernels: 0 us -> 23.3 us
  matrix products: 16.8 us -> 0 us
  other arithmetic: 16.6 us -> 3.17 us
    all_gather x4 -> x2, waiting for transfers between devices: 304 us -> 97.2 us  [the longest x1 55.1 us: per_device(): far = lax.all_gather(neighbour, 'z', axis=0, tiled=True)]
    ppermute x0 -> x14, waiting for transfers between devices: none -> 59.1 us  [shift(): return lax.ppermute(array, AXES, moves(axis, by))]
    ppermute x0 -> x14, starting transfers between devices: none -> 23.4 us  [shift(): return lax.ppermute(array, AXES, moves(axis, by))]
    pallas_call x0 -> x2, Pallas kernels: none -> 23.3 us  [products(): pl.pallas_call(functools.partial(product_kernel, half, last), grid_spec=p...]
    dot_general x2 -> x0, matrix products: 16.8 us -> none  [the longest x1 8.4 us: per_device(): jnp.einsum('ikab,ikbn->ian', margin_rows, picked, preferred_element_type=...]
    gather x1 -> x0, local copies, waits for them, and re-layouts: 14.6 us -> none  [per_device(): picked = joined[block_cols]]
    concatenate x1 -> x2, other arithmetic: 13.9 us -> 2.09 us  [the longest x1 1.99 us: per_device(): jnp.concatenate([pert_real, pert_imag], axis=1)]
    unnamed x8 -> x44, local copies, waits for them, and re-layouts: 0.03 us -> 7.58 us
  transfers between devices with their start and end apart: 4 -> 16, of which waited for: 4 -> 5; matrix products, arithmetic and copies ran while one was open for 10% -> 5% of each run, Pallas kernels for 0% -> 5%
where the time goes in v1:
time: 239 us
  waiting for transfers between devices  156 us (65%)
  starting transfers between devices  23.5 us (10%)
  Pallas kernels  23.3 us (10%)
  local copies, waits for them, and re-layouts  18 us (8%)
  between operations  14.5 us (6%)
  other arithmetic  3.17 us (1%)
    ppermute x14, waiting for transfers between devices, shift(): return lax.ppermute(array, AXES, moves(axis, by))  59.1 us
    all_gather x1, waiting for transfers between devices, per_device(): far = lax.all_gather(neighbour, 'z', axis=0, tiled=True)  55.1 us
    all_gather x1, waiting for transfers between devices, per_device(): near = lax.all_gather(panel, 'z', axis=0, tiled=True)  42.1 us
    ppermute x14, starting transfers between devices, shift(): return lax.ppermute(array, AXES, moves(axis, by))  23.4 us
    pallas_call x2, Pallas kernels, products(): pl.pallas_call(functools.partial(product_kernel, half, last), grid_spec=p...  23.3 us
    unnamed x44, local copies, waits for them, and re-layouts  7.58 us
  transfers between devices with their start and end apart: 16, of which 5 were waited for; matrix products, arithmetic and copies ran while one was open for 5% of the time, Pallas kernels for 5%

profile of v1, /device:TPU:1, one launch (start us, length us, event | category | flops | bytes accessed | tf_op | source)
XLA Modules:
  0.0 238.8 jit_solution(9997601814650876482)
XLA Ops:
  7.2 0.0 all-gather.5.cloned.1.call-start
  7.2 2.0 pad_maximum_fusion.2
  9.2 0.0 all-gather.5.cloned.1.call-update
  9.2 0.0 all-gather.3.cloned.1.call-start
  9.3 2.2 collective-permute-start
  11.5 10.7 %collective-permute-done = bf16[8,128,256]{2,1,0:T(8,128)(2,1)S(1)} collective-permute-done((bf16[8,128,256]{2,1,0:T(8,128)(2,1)}, bf16[8,128,256]{2,1,0:T(8,128)(2,1)S(1)}, u32[]{:S(2)}, u32[]{:S(2)}) %collective-permute-start) | collective-permute-done | bytes 524320 | tf_op jit(solution)/shard_map/ppermute | solution.py:35
  22.2 0.8 copy-done.21
  23.0 0.0 all-gather.3.cloned.1.call-update
  23.1 0.2 copy_bitcast_fusion
  23.2 0.1 pad_maximum_fusion
  23.4 3.5 %collective-permute-start.3 = (bf16[2,8,3,128,128]{4,3,1,2,0:T(8,128)(2,1)S(1)}, bf16[2,8,3,128,128]{4,3,1,2,0:T(8,128)(2,1)S(1)}, u32[]{:S(2)}, u32[]{:S(2)}) collective-permute-start(bf16[2,8,3,128,128]{4,3,1,2,0:T(8,128)(2,1)S(1)} %pad_maximum_fusion), channel_id=1, source_target_pairs={{0,6},{1,7},{2,0},{3,1},{4,2},{5,3},{6,4},{7,5},{8,14},{9,15},{10,... | collective-permute-start | bytes 4718600 | tf_op jit(solution)/shard_map/ppermute | solution.py:35
  26.9 0.0 collective-permute-start.2
  26.9 42.1 %all-gather.5.cloned.1.call-done.refs_0_ = bf16[64,128,256]{2,1,0:T(8,128)(2,1)} async-done(((bf16[8,128,256]{2,1,0:T(8,128)(2,1)}), bf16[64,128,256]{2,1,0:T(8,128)(2,1)}) %all-gather.5.cloned.1.call-update) | async-done | bytes 4194320 | tf_op jit(solution)/shard_map/all_gather | solution.py:206
  69.0 0.7 collective-permute-start.13
  69.7 55.1 %all-gather.3.cloned.1.call-done.refs_0_ = bf16[64,128,256]{2,1,0:T(8,128)(2,1)} async-done(((bf16[8,128,256]{2,1,0:T(8,128)(2,1)}), bf16[64,128,256]{2,1,0:T(8,128)(2,1)}) %all-gather.3.cloned.1.call-update) | async-done | bytes 4194320 | tf_op jit(solution)/shard_map/all_gather | solution.py:211
  124.8 0.7 collective-permute-start.1
  125.5 2.7 %collective-permute-start.6 = (bf16[2,8,3,128,128]{4,3,1,2,0:T(8,128)(2,1)S(1)}, bf16[2,8,3,128,128]{4,3,1,2,0:T(8,128)(2,1)S(1)}, u32[]{:S(2)}, u32[]{:S(2)}) collective-permute-start(bf16[2,8,3,128,128]{4,3,1,2,0:T(8,128)(2,1)S(1)} %pad_maximum_fusion), channel_id=1, source_target_pairs={{0,1},{1,0},{2,3},{3,2},{4,5},{5,4},{6,7},{7,6},{8,9},{9,8},{10,11... | collective-permute-start | bytes 4718600 | tf_op jit(solution)/shard_map/ppermute | solution.py:35
  128.3 0.1 slice_bitcast_fusion
  128.3 2.5 %collective-permute-start.5 = (bf16[8,3,128,128]{3,2,0,1:T(8,128)(2,1)S(1)}, bf16[8,3,128,128]{3,2,0,1:T(8,128)(2,1)S(1)}, u32[]{:S(2)}, u32[]{:S(2)}) collective-permute-start(bf16[8,3,128,128]{3,2,0,1:T(8,128)(2,1)S(1)} %slice_bitcast_fusion), channel_id=1, source_target_pairs={{0,6},{1,7},{2,0},{3,1},{4,2},{5,3},{6,4},{7,5},{8,14},{9,15},{10,... | collective-permute-start | bytes 2359304 | tf_op jit(solution)/shard_map/ppermute | solution.py:35
  130.8 0.0 collective-permute-done.2
  130.8 1.2 slice_bitcast_fusion.1
  132.0 0.1 collective-permute-start.4
  132.1 30.9 %collective-permute-done.6 = bf16[2,8,3,128,128]{4,3,1,2,0:T(8,128)(2,1)S(1)} collective-permute-done((bf16[2,8,3,128,128]{4,3,1,2,0:T(8,128)(2,1)S(1)}, bf16[2,8,3,128,128]{4,3,1,2,0:T(8,128)(2,1)S(1)}, u32[]{:S(2)}, u32[]{:S(2)}) %collective-permute-start.6) | collective-permute-done | bytes 1572896 | tf_op jit(solution)/shard_map/ppermute | solution.py:35
  163.1 0.1 slice.38
  163.2 1.3 collective-permute-start.7
  164.4 1.5 collective-permute-start.8
  165.9 1.1 slice.41
  167.1 0.1 pad_maximum_fusion.1
  167.2 2.8 %collective-permute-start.11 = (bf16[2,8,2,128,128]{4,3,1,2,0:T(8,128)(2,1)S(1)}, bf16[2,8,2,128,128]{4,3,1,2,0:T(8,128)(2,1)S(1)}, u32[]{:S(2)}, u32[]{:S(2)}) collective-permute-start(bf16[2,8,2,128,128]{4,3,1,2,0:T(8,128)(2,1)S(1)} %pad_maximum_fusion.1), channel_id=1, source_target_pairs={{0,1},{1,0},{2,3},{3,2},{4,5},{5,4},{6,7},{7,6},{8,9},{9,8},{10,11... | collective-permute-start | bytes 3145736 | tf_op jit(solution)/shard_map/ppermute | solution.py:35
  170.1 0.9 pad_maximum_fusion.3
  170.9 17.4 %collective-permute-done.7 = bf16[2,8,2,128,128]{4,3,1,2,0:T(8,128)(2,1)S(1)} collective-permute-done((bf16[2,8,2,128,128]{4,3,1,2,0:T(8,128)(2,1)S(1)}, bf16[2,8,2,128,128]{4,3,1,2,0:T(8,128)(2,1)S(1)}, u32[]{:S(2)}, u32[]{:S(2)}) %collective-permute-start.7) | collective-permute-done | bytes 1048608 | tf_op jit(solution)/shard_map/ppermute | solution.py:35
  188.4 0.8 slice_bitcast_fusion.3
  189.2 0.9 slice_bitcast_fusion.2
  190.1 2.7 %collective-permute-start.10 = (bf16[8,2,128,128]{3,2,0,1:T(8,128)(2,1)}, bf16[8,2,128,128]{3,2,0,1:T(8,128)(2,1)}, u32[]{:S(2)}, u32[]{:S(2)}) collective-permute-start(bf16[8,2,128,128]{3,2,0,1:T(8,128)(2,1)} %slice_bitcast_fusion.2), channel_id=1, source_target_pairs={{0,6},{1,7},{2,0},{3,1},{4,2},{5,3},{6,4},{7,5},{8,14},{9,15},{10,... | collective-permute-start | bytes 1572872 | tf_op jit(solution)/shard_map/ppermute | solution.py:35
  192.7 0.0 collective-permute-done.11
  192.7 1.1 copy-done.17
  193.8 2.7 %collective-permute-start.12 = (bf16[2,8,1,128,128]{4,3,2,1,0:T(8,128)(2,1)}, bf16[2,8,1,128,128]{4,3,2,1,0:T(8,128)(2,1)S(1)}, u32[]{:S(2)}, u32[]{:S(2)}) collective-permute-start(bf16[2,8,1,128,128]{4,3,2,1,0:T(8,128)(2,1)} %pad_maximum_fusion.3), channel_id=1, source_target_pairs={{0,1},{1,0},{2,3},{3,2},{4,5},{5,4},{6,7},{7,6},{8,9},{9,8},{10,11... | collective-permute-start | bytes 1572872 | tf_op jit(solution)/shard_map/ppermute | solution.py:35
  196.6 1.5 copy.49.refs_2_
  198.1 0.1 pad_add_fusion.place_ref
  198.2 1.7 copy.50.refs_3_
  199.9 0.2 copy-done.8
  200.1 0.2 copy.51.refs_4_
  200.2 1.2 copy-done.10
  201.5 0.2 copy.54.refs_7_
  201.6 1.0 copy-done.16
  202.6 0.1 copy.52.refs_5_
  202.7 1.1 copy-done.14
  203.7 0.1 copy.53.refs_6_
  203.8 0.1 copy.55.refs_8_
  203.9 1.1 copy-done.12
  205.0 0.1 copy.56.refs_9_
  205.1 1.1 copy-done.18
  206.2 0.1 copy.59.refs_12_
  206.3 0.0 copy-start.4
  206.3 0.0 copy-start.5
  206.3 1.1 copy.57.refs_10_
  207.4 0.0 collective-permute-done.10
  207.4 1.1 copy.58.refs_11_
  208.5 0.0 copy-start
  208.5 0.0 copy-start.1
  208.5 0.0 copy-start.2
  208.5 0.0 copy-start.3
  208.6 10.9 %products_first.1.refs_14_ = f32[8,256,256]{2,1,0:T(8,128)} custom-call(s32[4]{0:T(128)S(1)} %pad_add_fusion.place_ref, s32[8,24]{1,0:T(8,128)S(1)} %copy-done.4, s32[8]{0:T(128)S(1)} %copy-done.5, bf16[64,128,256]{2,1,0:T(8,128)(2,1)} %all-gather.5.cloned.1.call-done.refs_0_, bf16[64,128,256]{2,1,0:T(8,128)(2,1)} %collective-permute-done.13.refs_1_, ...), custom_call_target="tpu_custom_call" | custom-call | flops 3221225472 | bytes 23068672 | tf_op jit(solution)/shard_map/products_first/pallas_call | solution.py:167
  219.6 12.4 %products_last.1 = (f32[1024,128]{1,0:T(8,128)}, f32[1024,128]{1,0:T(8,128)}) custom-call(s32[4]{0:T(128)S(1)} %pad_add_fusion.place_ref, s32[8,24]{1,0:T(8,128)S(1)} %copy-done.4, s32[8]{0:T(128)S(1)} %copy-done.5, bf16[64,128,256]{2,1,0:T(8,128)(2,1)} %all-gather.3.cloned.1.call-done.refs_0_, bf16[64,128,256]{2,1,0:T(8,128)(2,1)} %collective-permute-done.1.refs_1_, ...), custom_call_target="tpu_custom_call" | custom-call | flops 3221225472 | bytes 23068672 | tf_op jit(solution)/shard_map/products_last/pallas_call | solution.py:167
  (42 shorter events, 0.2 us)
Async XLA Ops:
  7.2 15.9 %copy-start.20 = (bf16[8,3,128,128]{3,2,1,0:T(8,128)(2,1)S(1)}, bf16[8,3,128,128]{3,2,1,0:T(8,128)(2,1)}, u32[]{:S(2)}) copy-start(bf16[8,3,128,128]{3,2,1,0:T(8,128)(2,1)} %param.8) | copy-start | bytes 2359300
  7.2 15.9 %copy-start.19 = (bf16[8,3,128,128]{3,2,1,0:T(8,128)(2,1)S(1)}, bf16[8,3,128,128]{3,2,1,0:T(8,128)(2,1)}, u32[]{:S(2)}) copy-start(bf16[8,3,128,128]{3,2,1,0:T(8,128)(2,1)} %param.9) | copy-start | bytes 2359300
  7.2 61.9 %all-gather.5.cloned.1.call-start = ((), (), s32[]{:S(2)}) async-start(), calls=%async_computation.1 | async-start | bytes 4718592 | tf_op jit(solution)/shard_map/all_gather | solution.py:206
  9.2 115.6 %all-gather.3.cloned.1.call-start = ((), (), s32[]{:S(2)}) async-start(), calls=%async_computation | async-start | bytes 4718592 | tf_op jit(solution)/shard_map/all_gather | solution.py:211
  9.3 12.9 %collective-permute-start = (bf16[8,128,256]{2,1,0:T(8,128)(2,1)}, bf16[8,128,256]{2,1,0:T(8,128)(2,1)S(1)}, u32[]{:S(2)}, u32[]{:S(2)}) collective-permute-start(bf16[8,128,256]{2,1,0:T(8,128)(2,1)} %bitcast.24), channel_id=1, source_target_pairs={{0,128},{1,129},{2,130},{3,131},{4,132},{5,133},{6,134},{7,135},{8... | collective-permute-start | bytes 1572872 | tf_op jit(solution)/shard_map/ppermute | solution.py:35
  22.2 0.8 copy-start.21
  23.4 108.6 %copy-start.6 = (bf16[2,8,3,128,128]{4,3,1,2,0:T(8,128)(2,1)}, bf16[2,8,3,128,128]{4,3,1,2,0:T(8,128)(2,1)S(1)}, u32[]{:S(2)}) copy-start(bf16[2,8,3,128,128]{4,3,1,2,0:T(8,128)(2,1)S(1)} %pad_maximum_fusion) | copy-start | bytes 4718596
  23.4 104.9 %collective-permute-start.3 = (bf16[2,8,3,128,128]{4,3,1,2,0:T(8,128)(2,1)S(1)}, bf16[2,8,3,128,128]{4,3,1,2,0:T(8,128)(2,1)S(1)}, u32[]{:S(2)}, u32[]{:S(2)}) collective-permute-start(bf16[2,8,3,128,128]{4,3,1,2,0:T(8,128)(2,1)S(1)} %pad_maximum_fusion), channel_id=1, source_target_pairs={{0,6},{1,7},{2,0},{3,1},{4,2},{5,3},{6,4},{7,5},{8,14},{9,15},{10,... | collective-permute-start | bytes 4718600 | tf_op jit(solution)/shard_map/ppermute | solution.py:35
  26.9 103.9 %collective-permute-start.2 = (bf16[2,8,3,128,128]{4,3,1,2,0:T(8,128)(2,1)S(1)}, bf16[2,8,3,128,128]{4,3,1,2,0:T(8,128)(2,1)}, u32[]{:S(2)}, u32[]{:S(2)}) collective-permute-start(bf16[2,8,3,128,128]{4,3,1,2,0:T(8,128)(2,1)S(1)} %pad_maximum_fusion), channel_id=1, source_target_pairs={{0,2},{1,3},{2,4},{3,5},{4,6},{5,7},{6,0},{7,1},{8,10},{9,11},{10,... | collective-permute-start | bytes 4718600 | tf_op jit(solution)/shard_map/ppermute | solution.py:35
  69.0 139.5 %collective-permute-start.13 = (bf16[64,128,256]{2,1,0:T(8,128)(2,1)}, bf16[64,128,256]{2,1,0:T(8,128)(2,1)}, u32[]{:S(2)}, u32[]{:S(2)}) collective-permute-start(bf16[64,128,256]{2,1,0:T(8,128)(2,1)} %all-gather.5.cloned.1.call-done.refs_0_), channel_id=1, source_target_pairs={{0,8},{1,9},{2,10},{3,11},{4,12},{5,13},{6,14},{7,15},{8,0},{9,1},... | collective-permute-start | bytes 12582920 | tf_op jit(solution)/shard_map/ppermute | solution.py:35
  124.8 94.7 %collective-permute-start.1 = (bf16[64,128,256]{2,1,0:T(8,128)(2,1)}, bf16[64,128,256]{2,1,0:T(8,128)(2,1)}, u32[]{:S(2)}, u32[]{:S(2)}) collective-permute-start(bf16[64,128,256]{2,1,0:T(8,128)(2,1)} %all-gather.3.cloned.1.call-done.refs_0_), channel_id=1, source_target_pairs={{0,8},{1,9},{2,10},{3,11},{4,12},{5,13},{6,14},{7,15},{8,0},{9,1},... | collective-permute-start | bytes 12582920 | tf_op jit(solution)/shard_map/ppermute | solution.py:35
  125.5 37.5 %collective-permute-start.6 = (bf16[2,8,3,128,128]{4,3,1,2,0:T(8,128)(2,1)S(1)}, bf16[2,8,3,128,128]{4,3,1,2,0:T(8,128)(2,1)S(1)}, u32[]{:S(2)}, u32[]{:S(2)}) collective-permute-start(bf16[2,8,3,128,128]{4,3,1,2,0:T(8,128)(2,1)S(1)} %pad_maximum_fusion), channel_id=1, source_target_pairs={{0,1},{1,0},{2,3},{3,2},{4,5},{5,4},{6,7},{7,6},{8,9},{9,8},{10,11... | collective-permute-start | bytes 4718600 | tf_op jit(solution)/shard_map/ppermute | solution.py:35
  128.3 38.7 %copy-start.7 = (bf16[2,8,3,128,128]{4,3,1,2,0:T(8,128)(2,1)}, bf16[2,8,3,128,128]{4,3,1,2,0:T(8,128)(2,1)S(1)}, u32[]{:S(2)}) copy-start(bf16[2,8,3,128,128]{4,3,1,2,0:T(8,128)(2,1)S(1)} %collective-permute-done.3) | copy-start | bytes 4718596
  128.3 36.1 %collective-permute-start.5 = (bf16[8,3,128,128]{3,2,0,1:T(8,128)(2,1)S(1)}, bf16[8,3,128,128]{3,2,0,1:T(8,128)(2,1)S(1)}, u32[]{:S(2)}, u32[]{:S(2)}) collective-permute-start(bf16[8,3,128,128]{3,2,0,1:T(8,128)(2,1)S(1)} %slice_bitcast_fusion), channel_id=1, source_target_pairs={{0,6},{1,7},{2,0},{3,1},{4,2},{5,3},{6,4},{7,5},{8,14},{9,15},{10,... | collective-permute-start | bytes 2359304 | tf_op jit(solution)/shard_map/ppermute | solution.py:35
  132.0 35.2 %collective-permute-start.4 = (bf16[8,3,128,128]{3,2,0,1:T(8,128)(2,1)S(1)}, bf16[8,3,128,128]{3,2,0,1:T(8,128)(2,1)S(1)}, u32[]{:S(2)}, u32[]{:S(2)}) collective-permute-start(bf16[8,3,128,128]{3,2,0,1:T(8,128)(2,1)S(1)} %slice_bitcast_fusion.1), channel_id=1, source_target_pairs={{0,2},{1,3},{2,4},{3,5},{4,6},{5,7},{6,0},{7,1},{8,10},{9,11},{10,... | collective-permute-start | bytes 2359304 | tf_op jit(solution)/shard_map/ppermute | solution.py:35
  163.1 4.0 %copy-start.9 = (bf16[2,8,3,128,128]{4,3,1,2,0:T(8,128)(2,1)}, bf16[2,8,3,128,128]{4,3,1,2,0:T(8,128)(2,1)S(1)}, u32[]{:S(2)}) copy-start(bf16[2,8,3,128,128]{4,3,1,2,0:T(8,128)(2,1)S(1)} %collective-permute-done.6) | copy-start | bytes 4718596
  163.2 25.2 %collective-permute-start.7 = (bf16[2,8,2,128,128]{4,3,1,2,0:T(8,128)(2,1)S(1)}, bf16[2,8,2,128,128]{4,3,1,2,0:T(8,128)(2,1)S(1)}, u32[]{:S(2)}, u32[]{:S(2)}) collective-permute-start(bf16[2,8,2,128,128]{4,3,1,2,0:T(8,128)(2,1)S(1)} %slice.38), channel_id=1, source_target_pairs={{0,2},{1,3},{2,4},{3,5},{4,6},{5,7},{6,0},{7,1},{8,10},{9,11},{10,... | collective-permute-start | bytes 3145736 | tf_op jit(solution)/shard_map/ppermute | solution.py:35
  164.4 5.6 %copy-start.13 = (bf16[8,3,128,128]{3,2,0,1:T(8,128)(2,1)}, bf16[8,3,128,128]{3,2,0,1:T(8,128)(2,1)S(1)}, u32[]{:S(2)}) copy-start(bf16[8,3,128,128]{3,2,0,1:T(8,128)(2,1)S(1)} %collective-permute-done.5) | copy-start | bytes 2359300
  164.4 24.8 %collective-permute-start.8 = (bf16[2,8,2,128,128]{4,3,1,2,0:T(8,128)(2,1)S(1)}, bf16[2,8,2,128,128]{4,3,1,2,0:T(8,128)(2,1)S(1)}, u32[]{:S(2)}, u32[]{:S(2)}) collective-permute-start(bf16[2,8,2,128,128]{4,3,1,2,0:T(8,128)(2,1)S(1)} %slice.38), channel_id=1, source_target_pairs={{0,6},{1,7},{2,0},{3,1},{4,2},{5,3},{6,4},{7,5},{8,14},{9,15},{10,... | collective-permute-start | bytes 3145736 | tf_op jit(solution)/shard_map/ppermute | solution.py:35
  167.2 22.0 %copy-start.15 = (bf16[8,3,128,128]{3,2,0,1:T(8,128)(2,1)}, bf16[8,3,128,128]{3,2,0,1:T(8,128)(2,1)S(1)}, u32[]{:S(2)}) copy-start(bf16[8,3,128,128]{3,2,0,1:T(8,128)(2,1)S(1)} %collective-permute-done.4) | copy-start | bytes 2359300
  167.2 25.5 %collective-permute-start.11 = (bf16[2,8,2,128,128]{4,3,1,2,0:T(8,128)(2,1)S(1)}, bf16[2,8,2,128,128]{4,3,1,2,0:T(8,128)(2,1)S(1)}, u32[]{:S(2)}, u32[]{:S(2)}) collective-permute-start(bf16[2,8,2,128,128]{4,3,1,2,0:T(8,128)(2,1)S(1)} %pad_maximum_fusion.1), channel_id=1, source_target_pairs={{0,1},{1,0},{2,3},{3,2},{4,5},{5,4},{6,7},{7,6},{8,9},{9,8},{10,11... | collective-permute-start | bytes 3145736 | tf_op jit(solution)/shard_map/ppermute | solution.py:35
  189.2 17.1 %collective-permute-start.9 = (bf16[8,2,128,128]{3,2,0,1:T(8,128)(2,1)}, bf16[8,2,128,128]{3,2,0,1:T(8,128)(2,1)}, u32[]{:S(2)}, u32[]{:S(2)}) collective-permute-start(bf16[8,2,128,128]{3,2,0,1:T(8,128)(2,1)} %slice_bitcast_fusion.3), channel_id=1, source_target_pairs={{0,2},{1,3},{2,4},{3,5},{4,6},{5,7},{6,0},{7,1},{8,10},{9,11},{10,... | collective-permute-start | bytes 1572872 | tf_op jit(solution)/shard_map/ppermute | solution.py:35
  189.2 3.5 %copy-start.11 = (bf16[2,8,2,128,128]{4,3,1,2,0:T(8,128)(2,1)}, bf16[2,8,2,128,128]{4,3,1,2,0:T(8,128)(2,1)S(1)}, u32[]{:S(2)}) copy-start(bf16[2,8,2,128,128]{4,3,1,2,0:T(8,128)(2,1)S(1)} %collective-permute-done.8) | copy-start | bytes 3145732
  190.1 17.3 %collective-permute-start.10 = (bf16[8,2,128,128]{3,2,0,1:T(8,128)(2,1)}, bf16[8,2,128,128]{3,2,0,1:T(8,128)(2,1)}, u32[]{:S(2)}, u32[]{:S(2)}) collective-permute-start(bf16[8,2,128,128]{3,2,0,1:T(8,128)(2,1)} %slice_bitcast_fusion.2), channel_id=1, source_target_pairs={{0,6},{1,7},{2,0},{3,1},{4,2},{5,3},{6,4},{7,5},{8,14},{9,15},{10,... | collective-permute-start | bytes 1572872 | tf_op jit(solution)/shard_map/ppermute | solution.py:35
  192.7 1.1 copy-start.17
  193.8 14.7 %collective-permute-start.12 = (bf16[2,8,1,128,128]{4,3,2,1,0:T(8,128)(2,1)}, bf16[2,8,1,128,128]{4,3,2,1,0:T(8,128)(2,1)S(1)}, u32[]{:S(2)}, u32[]{:S(2)}) collective-permute-start(bf16[2,8,1,128,128]{4,3,2,1,0:T(8,128)(2,1)} %pad_maximum_fusion.3), channel_id=1, source_target_pairs={{0,1},{1,0},{2,3},{3,2},{4,5},{5,4},{6,7},{7,6},{8,9},{9,8},{10,11... | collective-permute-start | bytes 1572872 | tf_op jit(solution)/shard_map/ppermute | solution.py:35
  198.2 1.9 copy-start.8
  200.0 1.4 copy-start.10
  201.5 1.1 copy-start.16
  202.6 1.1 copy-start.14
  203.7 1.2 copy-start.12
  204.9 1.2 copy-start.18
  206.3 2.3 copy-start.4
  206.3 2.3 copy-start.5
  208.5 11.0 %copy-start = (bf16[1024,128]{1,0:T(8,128)(2,1)S(1)}, bf16[1024,128]{1,0:T(8,128)(2,1)}, u32[]{:S(2)}) copy-start(bf16[1024,128]{1,0:T(8,128)(2,1)} %refs_16_.1) | copy-start | bytes 786436
  208.5 11.0 %copy-start.1 = (bf16[1024,128]{1,0:T(8,128)(2,1)S(1)}, bf16[1024,128]{1,0:T(8,128)(2,1)}, u32[]{:S(2)}) copy-start(bf16[1024,128]{1,0:T(8,128)(2,1)} %refs_15_.1) | copy-start | bytes 786436
  208.5 11.0 %copy-start.2 = (bf16[1024,128]{1,0:T(8,128)(2,1)S(1)}, bf16[1024,128]{1,0:T(8,128)(2,1)}, u32[]{:S(2)}) copy-start(bf16[1024,128]{1,0:T(8,128)(2,1)} %refs_17_.1) | copy-start | bytes 786436
  208.5 11.0 %copy-start.3 = (bf16[1024,128]{1,0:T(8,128)(2,1)S(1)}, bf16[1024,128]{1,0:T(8,128)(2,1)}, u32[]{:S(2)}) copy-start(bf16[1024,128]{1,0:T(8,128)(2,1)} %refs_18_.1) | copy-start | bytes 786436
Sparse Core Ops, SparseCore 0:
  10.4 58.6 all-gather.4
  71.4 53.4 all-gather.2

commit v2 on v0

v2 whole, which is shorter than its diff:
```python
import jax
import jax.numpy as jnp
from jax import lax
from jax.experimental import pallas as pl
from jax.experimental.pallas import tpu as pltpu
from jax.sharding import PartitionSpec as P

frequency = 0.7
damping = 0.5
step_length = 0.5

AXES = ("ylo", "z", "core", "x", "yhi")
SIZES = (2, 8, 2, 4, 2)
BLOCK = 128


def moves(axis, by):
    place = AXES.index(axis)
    stride = 1
    for size in SIZES[place + 1 :]:
        stride *= size
    total = 1
    for size in SIZES:
        total *= size
    pairs = []
    for source in range(total):
        at = source // stride % SIZES[place]
        pairs.append((source, source + ((at + by) % SIZES[place] - at) * stride))
    return pairs


def shift(array, axis, by=1):
    return lax.ppermute(array, AXES, moves(axis, by))


PIECES = (
    (0, 0, (0, 1, 2)),
    (3, 0, (0, 1, 2)),
    (1, 0, (0, 1, 2)),
    (2, 0, (0, 1, 2)),
    (0, 1, (0, 1, 2)),
    (3, 1, (0, 1)),
    (1, 1, (0, 1)),
    (2, 1, (0, 1)),
    (3, 1, (2,)),
    (1, 1, (2,)),
    (2, 1, (2,)),
)
GROUP = 4


def list_kernel(place_ref, cols_ref, counts_ref, order_ref, used_ref):
    rows, slots = cols_ref.shape
    my_ylo, my_core, my_x, my_yhi = (place_ref[n] for n in range(4))

    def one_row(row, carry):
        for which in range(2):
            used_ref[which, row] = 0
            for n in range(order_ref.shape[2]):
                order_ref[which, row, n] = 0
        place = 0
        for dx, dy, local in PIECES:
            for j in local:
                slot = 3 * (2 * ((my_x + dx) & 3) + (my_yhi ^ dy)) + j
                column = cols_ref[row, slot]
                owner = column >> 3
                far = (owner >> 4) ^ my_ylo
                other = (owner & 1) ^ my_core
                which = far * other
                at = ((owner >> 1) & 7) * 8 + (column & 7) + (1 - which) * (2 * far + other) * 64

                @pl.when(slot < counts_ref[row])
                def _(which=which, at=at, place=place):
                    n = used_ref[which, row]
                    order_ref[which, row, n] = place * 256 + at
                    used_ref[which, row] = n + 1

                place += 1
        return carry

    lax.fori_loop(0, rows, one_row, 0)


def make_lists(place, cols, counts):
    rows = cols.shape[0]
    smem = pl.BlockSpec(memory_space=pltpu.SMEM)
    return pl.pallas_call(
        list_kernel,
        in_specs=[smem] * 3,
        out_specs=[smem] * 2,
        out_shape=[
            jax.ShapeDtypeStruct((2, rows, 24 + GROUP), jnp.int32),
            jax.ShapeDtypeStruct((2, rows), jnp.int32),
        ],
        name="make_lists",
    )(place, cols, counts)


def add_products(which, order_ref, used_ref, blocks, panel, acc, fresh):
    def one_row(row, carry):
        used = used_ref[which, row]
        if fresh:
            acc[row] = jnp.zeros(acc.shape[1:], acc.dtype)

        def one_group(group, carry):
            left, right = [], []
            for n in range(GROUP):
                code = order_ref[which, row, group * GROUP + n]
                place, at = code >> 8, code & 255
                left.append(jnp.concatenate([blocks[0, place, row], blocks[1, place, row]], axis=0))
                block = panel[at]
                right.append(jnp.where(group * GROUP + n < used, block, jnp.zeros_like(block)))
            acc[row] += jnp.dot(
                jnp.concatenate(left, axis=1),
                jnp.concatenate(right, axis=0),
                preferred_element_type=jnp.float32,
            )
            return carry

        return lax.fori_loop(0, (used + GROUP - 1) // GROUP, one_group, carry)

    lax.fori_loop(0, used_ref.shape[1], one_row, 0)


def fetch(pairs, sems):
    copies = [pltpu.make_async_copy(a, b, sems.at[n]) for n, (a, b) in enumerate(pairs)]
    for copy in copies:
        copy.start()
    for copy in copies:
        copy.wait()


def first_kernel(order_ref, used_ref, near, near_other, far, *refs):
    pieces, (blocks, acc, panel, sems) = refs[:12], refs[12:]
    count = near.shape[0]
    pairs = [(ref, panel.at[pl.ds(n * count, count)]) for n, ref in enumerate((near, near_other, far))]
    at = 0
    for n, piece in enumerate(pieces):
        if n in (4, 9):
            continue
        if n in (3, 8):
            size = piece.shape[0]
            pairs.append((piece, blocks.at[0, pl.ds(at, size)]))
            pairs.append((pieces[n + 1], blocks.at[1, pl.ds(at, size)]))
        else:
            size = piece.shape[1]
            pairs.append((piece, blocks.at[:, pl.ds(at, size)]))
        at += size
    fetch(pairs, sems)
    add_products(0, order_ref, used_ref, blocks, panel, acc, True)


def last_kernel(
    order_ref,
    used_ref,
    far_other,
    blocks,
    before,
    pert_real,
    pert_imag,
    drive_real,
    drive_imag,
    new_real,
    new_imag,
    acc,
    panel,
    sems,
):
    fetch([(far_other, panel)], sems)
    acc[...] = before[...]
    add_products(1, order_ref, used_ref, blocks, panel, acc, False)

    def one_row(row, carry):
        total = acc[row]
        lines = pl.ds(row * BLOCK, BLOCK)
        ham_real, ham_imag = total[:BLOCK, :BLOCK], total[:BLOCK, BLOCK:]
        ovl_real, ovl_imag = total[BLOCK:, :BLOCK], total[BLOCK:, BLOCK:]
        res_real = drive_real[lines].astype(jnp.float32) - (
            ham_real - frequency * ovl_real + damping * ovl_imag
        )
        res_imag = drive_imag[lines].astype(jnp.float32) - (
            ham_imag - frequency * ovl_imag - damping * ovl_real
        )
        new_real[lines] = pert_real[lines].astype(jnp.float32) + step_length * res_real
        new_imag[lines] = pert_imag[lines].astype(jnp.float32) + step_length * res_imag
        return carry

    lax.fori_loop(0, acc.shape[0], one_row, 0)


SMEM = pl.BlockSpec(memory_space=pltpu.SMEM)
VMEM = pl.BlockSpec(memory_space=pltpu.VMEM)
ANY = pl.BlockSpec(memory_space=pl.ANY)


def nothing(*refs):
    pass


def after(array, *others):
    return pl.pallas_call(
        nothing,
        in_specs=[ANY] * (1 + len(others)),
        out_specs=ANY,
        out_shape=jax.ShapeDtypeStruct(array.shape, array.dtype),
        input_output_aliases={0: 0},
        compiler_params=pltpu.CompilerParams(vmem_limit_bytes=2**16),
        name="gate",
    )(in_hbm(array), *map(in_hbm, others))


def in_hbm(array):
    return pltpu.with_memory_space_constraint(array, pltpu.HBM)


def held(array):
    return pltpu.with_memory_space_constraint(array, pltpu.VMEM)


def cost(micros):
    return pl.CostEstimate(flops=0, bytes_accessed=int(micros * 3.0e6), transcendentals=0)


def first_products(order, used, near, near_other, far, pieces):
    rows, count = used.shape[1], near.shape[0]
    return pl.pallas_call(
        first_kernel,
        in_specs=[SMEM, SMEM] + [ANY] * (3 + len(pieces)),
        out_specs=[VMEM, VMEM],
        out_shape=[
            pltpu.VMEM((2, 24, rows, BLOCK, BLOCK), jnp.bfloat16),
            pltpu.VMEM((rows, 2 * BLOCK, 2 * BLOCK), jnp.float32),
        ],
        scratch_shapes=[
            pltpu.VMEM((3 * count, BLOCK, 2 * BLOCK), jnp.bfloat16),
            pltpu.SemaphoreType.DMA((3 + len(pieces),)),
        ],
        compiler_params=pltpu.CompilerParams(vmem_limit_bytes=FIRST_LIMIT),
        cost_estimate=cost(10),
        name="products_first",
    )(order, used, in_hbm(near), in_hbm(near_other), in_hbm(far), *map(in_hbm, pieces))


def last_products(order, used, far_other, blocks, before, *flat):
    rows = used.shape[1]
    return pl.pallas_call(
        last_kernel,
        in_specs=[SMEM, SMEM, ANY, VMEM, VMEM] + [VMEM] * 4,
        out_specs=[VMEM] * 2,
        out_shape=[jax.ShapeDtypeStruct((rows * BLOCK, BLOCK), jnp.float32)] * 2,
        scratch_shapes=[
            pltpu.VMEM(before.shape, jnp.float32),
            pltpu.VMEM(far_other.shape, far_other.dtype),
            pltpu.SemaphoreType.DMA((1,)),
        ],
        compiler_params=pltpu.CompilerParams(vmem_limit_bytes=LATER_LIMIT),
        cost_estimate=cost(4),
        name="products_last",
    )(order, used, far_other, held(blocks), held(before), *flat)


FIRST_LIMIT = 15 * 2**20
LATER_LIMIT = 9 * 2**20


def per_device(
    ham_blocks,
    margin_blocks,
    block_cols,
    block_counts,
    pert_real,
    pert_imag,
    drive_real,
    drive_imag,
):
    rows = block_cols.shape[0]
    place = jnp.stack([lax.axis_index(a) for a in ("ylo", "core", "x", "yhi")]).astype(jnp.int32)

    both = jnp.stack([ham_blocks.swapaxes(0, 1), margin_blocks.swapaxes(0, 1)], axis=0)
    panel = jnp.concatenate([pert_real, pert_imag], axis=1).reshape(rows, BLOCK, 2 * BLOCK)

    from_left = shift(both, "x", 1)
    from_right = shift(both, "x", -1)
    part = shift(both, "yhi")
    near = lax.all_gather(panel, "z", axis=0, tiled=True)
    order, used = make_lists(place, block_cols, block_counts)

    neighbour = shift(panel, "ylo")
    far = lax.all_gather(after(neighbour, from_left, from_right, part, order), "z", axis=0, tiled=True)
    far_ham = shift(from_left[0], "x", 1)
    far_margin = shift(from_right[1], "x", -1)
    late = shift(jnp.concatenate([from_left[:, 2:], from_right[:, 2:]], axis=1), "yhi")

    part_two = after(part[:, :2], far_ham, far_margin)
    part_left = shift(part_two, "x", 1)
    part_right = shift(part_two, "x", -1)
    near = after(near, far_ham, far_margin, late)
    near_other = shift(near, "core")
    late_far = shift(jnp.stack([far_ham[2:], far_margin[2:]], axis=0), "yhi")
    part_far_ham = shift(part_left[0], "x", 1)
    part_far_margin = shift(part_right[1], "x", -1)

    pieces = (
        both,
        from_left,
        from_right,
        far_ham,
        far_margin,
        part,
        part_left,
        part_right,
        part_far_ham,
        part_far_margin,
        late,
        late_far,
    )
    far = after(far, part_far_ham, part_far_margin, late_far)
    far_other = shift(far, "core")
    blocks, acc = first_products(order, used, near, near_other, far, pieces)
    new_real, new_imag = last_products(
        order, used, far_other, blocks, acc, pert_real, pert_imag, drive_real, drive_imag
    )
    return new_real, new_imag


def solution(mesh):
    fine = jax.sharding.Mesh(mesh.devices.reshape(SIZES), AXES)
    loop, rep = ("ylo", "z", "core"), ("x", "yhi")
    return jax.shard_map(
        per_device,
        mesh=fine,
        in_specs=(
            P(loop, rep, None, None),
            P(loop, rep, None, None),
            P(loop, None),
            P(loop),
            P(loop, rep),
            P(loop, rep),
            P(loop, rep),
            P(loop, rep),
        ),
        out_specs=(P(loop, rep), P(loop, rep)),
        check_vma=False,
    )
```

time: 369 us -> 158 us (0.43)
  waiting for transfers between devices: 306 us -> 74.9 us
  Pallas kernels: 0 us -> 27.6 us
  starting transfers between devices: 0.15 us -> 26.3 us
  matrix products: 16.8 us -> 0 us
  other arithmetic: 16.6 us -> 4.06 us
    all_gather x4 -> x2, waiting for transfers between devices: 304 us -> 0.92 us  [the longest x1 0.92 us: per_device(): lax.all_gather(after(neighbour, from_left, from_right, part, order), 'z',...]
    ppermute x0 -> x14, waiting for transfers between devices: none -> 74 us  [shift(): return lax.ppermute(array, AXES, moves(axis, by))]
    pallas_call x0 -> x7, Pallas kernels: none -> 27.6 us  [the longest x1 17.8 us: first_products(): pl.pallas_call(first_kernel, in_specs=[SMEM, SMEM] + [ANY] * (3 + len(pie...]
    ppermute x0 -> x14, starting transfers between devices: none -> 26.3 us  [shift(): return lax.ppermute(array, AXES, moves(axis, by))]
    dot_general x2 -> x0, matrix products: 16.8 us -> none  [the longest x1 8.4 us: per_device(): jnp.einsum('ikab,ikbn->ian', margin_rows, picked, preferred_element_type=...]
    gather x1 -> x0, local copies, waits for them, and re-layouts: 14.6 us -> none  [per_device(): picked = joined[block_cols]]
    concatenate x1 -> x2, other arithmetic: 13.9 us -> 2.09 us  [the longest x1 1.99 us: per_device(): jnp.concatenate([pert_real, pert_imag], axis=1)]
    unnamed x8 -> x38, local copies, waits for them, and re-layouts: 0.03 us -> 3.87 us
  transfers between devices with their start and end apart: 4 -> 16, of which waited for: 4 -> 7; matrix products, arithmetic and copies ran while one was open for 10% -> 6% of each run, Pallas kernels for 0% -> 14%
where the time goes in v2:
time: 158 us; the launch traced here: 159 us
  waiting for transfers between devices  74.9 us (47%)
  Pallas kernels  27.6 us (17%)
  starting transfers between devices  26.3 us (17%)
  between operations  14.3 us (9%)
  local copies, waits for them, and re-layouts  11.5 us (7%)
  other arithmetic  4.06 us (3%)
    ppermute x14, waiting for transfers between devices, shift(): return lax.ppermute(array, AXES, moves(axis, by))  74 us
    ppermute x14, starting transfers between devices, shift(): return lax.ppermute(array, AXES, moves(axis, by))  26.3 us
    pallas_call x1, Pallas kernels, first_products(): pl.pallas_call(first_kernel, in_specs=[SMEM, SMEM] + [ANY] * (3 + len(pie...  17.8 us
    pallas_call x1, Pallas kernels, last_products(): pl.pallas_call(last_kernel, in_specs=[SMEM, SMEM, ANY, VMEM, VMEM] + [VME...  5.43 us
    pallas_call x1, Pallas kernels, make_lists(): pl.pallas_call(list_kernel, in_specs=[smem] * 3, out_specs=[smem] * 2, ou...  4.35 us
    unnamed x38, local copies, waits for them, and re-layouts  3.87 us
  transfers between devices with their start and end apart: 16, of which 7 were waited for; matrix products, arithmetic and copies ran while one was open for 6% of the time, Pallas kernels for 14%

profile of v2, /device:TPU:1, one launch (start us, length us, event | category | flops | bytes accessed | tf_op | source)
XLA Modules:
  0.0 158.7 jit_solution(8914651452527612074)
XLA Ops:
  7.2 0.0 all-gather.5.cloned.1.call-start
  7.2 2.0 %pad_maximum_fusion.2 = bf16[1024,256]{1,0:T(8,128)(2,1)} fusion(bf16[1024,128]{1,0:T(8,128)(2,1)} %pert_imag.1, bf16[1024,128]{1,0:T(8,128)(2,1)} %pert_real.1), kind=kLoop, calls=%fused_computation.8 | loop fusion | flops 1048576 | bytes 1048576 | tf_op jit(solution)/shard_map/concatenate | solution.py:280
  9.2 0.0 all-gather.5.cloned.1.call-update
  9.2 0.0 all-gather.3.cloned.1.call-start
  9.3 0.2 copy_bitcast_fusion
  9.5 1.3 pad_maximum_fusion.refs_0_
  10.8 3.7 %collective-permute-start.3 = (bf16[2,3,8,128,128]{4,3,2,1,0:T(8,128)(2,1)}, bf16[2,3,8,128,128]{4,3,2,1,0:T(8,128)(2,1)}, u32[]{:S(2)}, u32[]{:S(2)}) collective-permute-start(bf16[2,3,8,128,128]{4,3,2,1,0:T(8,128)(2,1)} %pad_maximum_fusion.refs_0_), channel_id=1, source_target_pairs={{0,1},{1,0},{2,3},{3,2},{4,5},{5,4},{6,7},{7,6},{8,9},{9,8},{10,11... | collective-permute-start | bytes 4718600 | tf_op jit(solution)/shard_map/ppermute | solution.py:33
  14.5 2.5 %collective-permute-start.2 = (bf16[2,3,8,128,128]{4,3,2,1,0:T(8,128)(2,1)}, bf16[2,3,8,128,128]{4,3,2,1,0:T(8,128)(2,1)S(1)}, u32[]{:S(2)}, u32[]{:S(2)}) collective-permute-start(bf16[2,3,8,128,128]{4,3,2,1,0:T(8,128)(2,1)} %pad_maximum_fusion.refs_0_), channel_id=1, source_target_pairs={{0,6},{1,7},{2,0},{3,1},{4,2},{5,3},{6,4},{7,5},{8,14},{9,15},{10,... | collective-permute-start | bytes 4718600 | tf_op jit(solution)/shard_map/ppermute | solution.py:33
  17.0 0.0 collective-permute-start.1
  17.0 0.4 collective-permute-start
  17.4 0.6 pad_add_fusion.place_ref
  18.0 4.3 %make_lists.1 = (s32[2,8,28]{2,1,0:T(8,128)}, s32[2,8]{1,0:T(2,128)}) custom-call(s32[4]{0:T(128)} %pad_add_fusion.place_ref, s32[8,24]{1,0:T(8,128)} %cols_ref.1, s32[8]{0:T(128)} %counts_ref.1), custom_call_target="tpu_custom_call" | custom-call | tf_op jit(solution)/shard_map/make_lists/pallas_call | solution.py:87
  22.4 37.9 %collective-permute-done.refs_0_ = bf16[8,128,256]{2,1,0:T(8,128)(2,1)} collective-permute-done((bf16[8,128,256]{2,1,0:T(8,128)(2,1)}, bf16[8,128,256]{2,1,0:T(8,128)(2,1)}, u32[]{:S(2)}, u32[]{:S(2)}) %collective-permute-start) | collective-permute-done | bytes 524320 | tf_op jit(solution)/shard_map/ppermute | solution.py:33
  60.3 0.0 collective-permute-done.3.refs_3_.refs_5_
  60.3 0.0 collective-permute-done.2.refs_2_
  60.3 0.0 collective-permute-done.1.refs_1_
  60.3 1.1 copy-done.6
  61.5 0.5 copy-done.7
  62.0 0.0 all-gather.3.cloned.1.call-update
  62.0 1.3 slice_bitcast_fusion
  63.3 2.6 %collective-permute-start.5 = (bf16[3,8,128,128]{3,2,1,0:T(8,128)(2,1)S(1)}, bf16[3,8,128,128]{3,2,1,0:T(8,128)(2,1)S(1)}, u32[]{:S(2)}, u32[]{:S(2)}) collective-permute-start(bf16[3,8,128,128]{3,2,1,0:T(8,128)(2,1)S(1)} %slice_bitcast_fusion), channel_id=1, source_target_pairs={{0,6},{1,7},{2,0},{3,1},{4,2},{5,3},{6,4},{7,5},{8,14},{9,15},{10,... | collective-permute-start | bytes 2359304 | tf_op jit(solution)/shard_map/ppermute | solution.py:33
  65.9 0.0 copy-done.8
  65.9 0.1 slice_bitcast_fusion.1
  65.9 0.1 collective-permute-start.4
  66.0 2.3 %slice.36.refs_0_ = bf16[2,2,8,128,128]{4,3,2,1,0:T(8,128)(2,1)} slice(bf16[2,3,8,128,128]{4,3,2,1,0:T(8,128)(2,1)} %collective-permute-done.3.refs_3_.refs_5_), slice={[0:2], [0:2], [0:8], [0:128], [0:128]} | slice | bytes 2097152 | tf_op jit(solution)/shard_map/slice | solution.py:294
  68.3 12.8 %collective-permute-done.5.refs_2_.refs_4_ = bf16[3,8,128,128]{3,2,1,0:T(8,128)(2,1)S(1)} collective-permute-done((bf16[3,8,128,128]{3,2,1,0:T(8,128)(2,1)S(1)}, bf16[3,8,128,128]{3,2,1,0:T(8,128)(2,1)S(1)}, u32[]{:S(2)}, u32[]{:S(2)}) %collective-permute-start.5) | collective-permute-done | bytes 786464 | tf_op jit(solution)/shard_map/ppermute | solution.py:33
  81.2 3.3 %collective-permute-done.4.refs_1_.refs_3_ = bf16[3,8,128,128]{3,2,1,0:T(8,128)(2,1)S(1)} collective-permute-done((bf16[3,8,128,128]{3,2,1,0:T(8,128)(2,1)S(1)}, bf16[3,8,128,128]{3,2,1,0:T(8,128)(2,1)S(1)}, u32[]{:S(2)}, u32[]{:S(2)}) %collective-permute-start.4) | collective-permute-done | bytes 786464 | tf_op jit(solution)/shard_map/ppermute | solution.py:33
  84.4 0.9 copy-done.10
  85.3 1.0 collective-permute-start.8
  86.4 0.4 collective-permute-start.6
  86.8 0.0 slice-done.1
  86.8 0.1 pad_maximum_fusion.1
  86.9 1.6 %collective-permute-start.12 = (bf16[2,2,8,128,128]{4,3,2,1,0:T(8,128)(2,1)S(1)}, bf16[2,2,8,128,128]{4,3,2,1,0:T(8,128)(2,1)S(1)}, u32[]{:S(2)}, u32[]{:S(2)}) collective-permute-start(bf16[2,2,8,128,128]{4,3,2,1,0:T(8,128)(2,1)S(1)} %pad_maximum_fusion.1), channel_id=1, source_target_pairs={{0,1},{1,0},{2,3},{3,2},{4,5},{5,4},{6,7},{7,6},{8,9},{9,8},{10,11... | collective-permute-start | bytes 3145736 | tf_op jit(solution)/shard_map/ppermute | solution.py:33
  88.5 1.0 slice_bitcast_fusion.4
  89.5 1.0 slice_bitcast_fusion.5
  90.5 0.1 pad_maximum_fusion.3
  90.5 1.5 collective-permute-start.10
  92.1 15.5 %collective-permute-done.8.refs_7_ = bf16[2,2,8,128,128]{4,3,2,1,0:T(8,128)(2,1)S(1)} collective-permute-done((bf16[2,2,8,128,128]{4,3,2,1,0:T(8,128)(2,1)}, bf16[2,2,8,128,128]{4,3,2,1,0:T(8,128)(2,1)S(1)}, u32[]{:S(2)}, u32[]{:S(2)}) %collective-permute-start.8) | collective-permute-done | bytes 1048608 | tf_op jit(solution)/shard_map/ppermute | solution.py:33
  107.6 1.0 slice_bitcast_fusion.2
  108.5 2.5 %collective-permute-start.9 = (bf16[2,8,128,128]{3,2,1,0:T(8,128)(2,1)}, bf16[2,8,128,128]{3,2,1,0:T(8,128)(2,1)S(1)}, u32[]{:S(2)}, u32[]{:S(2)}) collective-permute-start(bf16[2,8,128,128]{3,2,1,0:T(8,128)(2,1)} %slice_bitcast_fusion.2), channel_id=1, source_target_pairs={{0,6},{1,7},{2,0},{3,1},{4,2},{5,3},{6,4},{7,5},{8,14},{9,15},{10,... | collective-permute-start | bytes 1572872 | tf_op jit(solution)/shard_map/ppermute | solution.py:33
  111.1 0.0 collective-permute-done.6.refs_6_
  111.1 0.9 slice_bitcast_fusion.3
  112.0 0.0 copy-done.12
  112.0 0.0 collective-permute-start.7
  112.0 0.3 copy-done.13
  112.3 0.0 collective-permute-done.12.refs_3_.refs_10_
  112.3 1.0 copy-done.11
  113.2 5.6 %collective-permute-start.13 = (bf16[64,128,256]{2,1,0:T(8,128)(2,1)}, bf16[64,128,256]{2,1,0:T(8,128)(2,1)}, u32[]{:S(2)}, u32[]{:S(2)}) collective-permute-start(bf16[64,128,256]{2,1,0:T(8,128)(2,1)} %gate.7.near), channel_id=1, source_target_pairs={{0,8},{1,9},{2,10},{3,11},{4,12},{5,13},{6,14},{7,15},{8,0},{9,1},... | collective-permute-start | bytes 12582920 | tf_op jit(solution)/shard_map/ppermute | solution.py:33
  118.9 2.2 %collective-permute-done.10.refs_3_.refs_11_ = bf16[2,1,8,128,128]{4,3,2,1,0:T(8,128)(2,1)S(1)} collective-permute-done((bf16[2,1,8,128,128]{4,3,2,1,0:T(8,128)(2,1)S(1)}, bf16[2,1,8,128,128]{4,3,2,1,0:T(8,128)(2,1)S(1)}, u32[]{:S(2)}, u32[]{:S(2)}) %collective-permute-start.10) | collective-permute-done | bytes 524320 | tf_op jit(solution)/shard_map/ppermute | solution.py:33
  121.1 0.0 collective-permute-done.9.refs_2_.refs_9_
  121.1 2.3 %collective-permute-done.7.refs_1_.refs_8_ = bf16[2,8,128,128]{3,2,1,0:T(8,128)(2,1)S(1)} collective-permute-done((bf16[2,8,128,128]{3,2,1,0:T(8,128)(2,1)}, bf16[2,8,128,128]{3,2,1,0:T(8,128)(2,1)S(1)}, u32[]{:S(2)}, u32[]{:S(2)}) %collective-permute-start.7) | collective-permute-done | bytes 524320 | tf_op jit(solution)/shard_map/ppermute | solution.py:33
  123.4 0.9 all-gather.3.cloned.1.call-done.refs_0_
  124.3 0.0 copy-done.14
  124.3 4.2 %collective-permute-start.11 = (bf16[64,128,256]{2,1,0:T(8,128)(2,1)}, bf16[64,128,256]{2,1,0:T(8,128)(2,1)S(1)}, u32[]{:S(2)}, u32[]{:S(2)}) collective-permute-start(bf16[64,128,256]{2,1,0:T(8,128)(2,1)} %gate.6.far), channel_id=1, source_target_pairs={{0,8},{1,9},{2,10},{3,11},{4,12},{5,13},{6,14},{7,15},{8,0},{9,1},... | collective-permute-start | bytes 12582920 | tf_op jit(solution)/shard_map/ppermute | solution.py:33
  128.5 0.0 collective-permute-done.13.near_other
  128.5 0.0 copy-done.4
  128.5 0.0 copy-start
  128.5 0.0 copy-start.1
  128.6 0.0 copy-start.2
  128.6 0.0 copy-start.3
  128.6 17.8 %products_first.1 = (bf16[2,24,8,128,128]{4,3,2,1,0:T(8,128)(2,1)S(1)}, f32[8,256,256]{2,1,0:T(8,128)S(1)}) custom-call(s32[2,8,28]{2,1,0:T(8,128)S(1)} %copy-done.4, s32[2,8]{1,0:T(2,128)S(1)} %copy-done.5, bf16[64,128,256]{2,1,0:T(8,128)(2,1)} %gate.7.near, bf16[64,128,256]{2,1,0:T(8,128)(2,1)} %collective-permute-done.13.near_other, ...), custom_call_target="tpu_custom_call" | custom-call | bytes 30000000 | tf_op jit(solution)/shard_map/products_first/pallas_call | solution.py:226
  146.4 0.0 collective-permute-done.11.far_other
  146.4 0.0 copy-done
  146.4 5.4 %products_last.1 = (f32[1024,128]{1,0:T(8,128)}, f32[1024,128]{1,0:T(8,128)}) custom-call(s32[2,8,28]{2,1,0:T(8,128)S(1)} %copy-done.4, s32[2,8]{1,0:T(2,128)S(1)} %copy-done.5, bf16[64,128,256]{2,1,0:T(8,128)(2,1)S(1)} %collective-permute-done.11.far_other, bf16[2,24,8,128,128]{4,3,2,1,0:T(8,128)(2,1)S(1)} %get-tuple-element.8.blocks, ...), custom_call_target="tpu_custom_call" | custom-call | bytes 12000000 | tf_op jit(solution)/shard_map/products_last/pallas_call | solution.py:246
  (32 shorter events, 0.1 us)
Async XLA Ops:
  7.2 2.1 %copy-start.17 = (bf16[8,3,128,128]{3,2,1,0:T(8,128)(2,1)S(1)}, bf16[8,3,128,128]{3,2,1,0:T(8,128)(2,1)}, u32[]{:S(2)}) copy-start(bf16[8,3,128,128]{3,2,1,0:T(8,128)(2,1)} %param.9) | copy-start | bytes 2359300
  7.2 2.1 %copy-start.18 = (bf16[8,3,128,128]{3,2,1,0:T(8,128)(2,1)S(1)}, bf16[8,3,128,128]{3,2,1,0:T(8,128)(2,1)}, u32[]{:S(2)}) copy-start(bf16[8,3,128,128]{3,2,1,0:T(8,128)(2,1)} %param.8) | copy-start | bytes 2359300
  7.2 105.1 %all-gather.5.cloned.1.call-start = ((), (), s32[]{:S(2)}) async-start(), calls=%async_computation.1 | async-start | bytes 4718592 | tf_op jit(solution)/shard_map/all_gather | solution.py:285
  9.2 115.0 %all-gather.3.cloned.1.call-start = ((), (), s32[]{:S(2)}) async-start(), calls=%async_computation | async-start | bytes 4718592 | tf_op jit(solution)/shard_map/all_gather | solution.py:289
  10.8 49.5 %collective-permute-start.3 = (bf16[2,3,8,128,128]{4,3,2,1,0:T(8,128)(2,1)}, bf16[2,3,8,128,128]{4,3,2,1,0:T(8,128)(2,1)}, u32[]{:S(2)}, u32[]{:S(2)}) collective-permute-start(bf16[2,3,8,128,128]{4,3,2,1,0:T(8,128)(2,1)} %pad_maximum_fusion.refs_0_), channel_id=1, source_target_pairs={{0,1},{1,0},{2,3},{3,2},{4,5},{5,4},{6,7},{7,6},{8,9},{9,8},{10,11... | collective-permute-start | bytes 4718600 | tf_op jit(solution)/shard_map/ppermute | solution.py:33
  14.5 45.8 %collective-permute-start.2 = (bf16[2,3,8,128,128]{4,3,2,1,0:T(8,128)(2,1)}, bf16[2,3,8,128,128]{4,3,2,1,0:T(8,128)(2,1)S(1)}, u32[]{:S(2)}, u32[]{:S(2)}) collective-permute-start(bf16[2,3,8,128,128]{4,3,2,1,0:T(8,128)(2,1)} %pad_maximum_fusion.refs_0_), channel_id=1, source_target_pairs={{0,6},{1,7},{2,0},{3,1},{4,2},{5,3},{6,4},{7,5},{8,14},{9,15},{10,... | collective-permute-start | bytes 4718600 | tf_op jit(solution)/shard_map/ppermute | solution.py:33
  17.0 43.3 %collective-permute-start.1 = (bf16[2,3,8,128,128]{4,3,2,1,0:T(8,128)(2,1)}, bf16[2,3,8,128,128]{4,3,2,1,0:T(8,128)(2,1)S(1)}, u32[]{:S(2)}, u32[]{:S(2)}) collective-permute-start(bf16[2,3,8,128,128]{4,3,2,1,0:T(8,128)(2,1)} %pad_maximum_fusion.refs_0_), channel_id=1, source_target_pairs={{0,2},{1,3},{2,4},{3,5},{4,6},{5,7},{6,0},{7,1},{8,10},{9,11},{10,... | collective-permute-start | bytes 4718600 | tf_op jit(solution)/shard_map/ppermute | solution.py:33
  17.0 43.3 %collective-permute-start = (bf16[8,128,256]{2,1,0:T(8,128)(2,1)}, bf16[8,128,256]{2,1,0:T(8,128)(2,1)}, u32[]{:S(2)}, u32[]{:S(2)}) collective-permute-start(bf16[8,128,256]{2,1,0:T(8,128)(2,1)} %bitcast.4), channel_id=1, source_target_pairs={{0,128},{1,129},{2,130},{3,131},{4,132},{5,133},{6,134},{7,135},{8... | collective-permute-start | bytes 1572872 | tf_op jit(solution)/shard_map/ppermute | solution.py:33
  60.3 1.2 copy-start.6
  60.3 1.6 %copy-start.7 = (bf16[2,3,8,128,128]{4,3,2,1,0:T(8,128)(2,1)}, bf16[2,3,8,128,128]{4,3,2,1,0:T(8,128)(2,1)S(1)}, u32[]{:S(2)}) copy-start(bf16[2,3,8,128,128]{4,3,2,1,0:T(8,128)(2,1)S(1)} %collective-permute-done.1.refs_1_) | copy-start | bytes 4718596
  62.0 3.9 %copy-start.8 = (bf16[2,3,8,128,128]{4,3,2,1,0:T(8,128)(2,1)S(1)}, bf16[2,3,8,128,128]{4,3,2,1,0:T(8,128)(2,1)}, u32[]{:S(2)}) copy-start(bf16[2,3,8,128,128]{4,3,2,1,0:T(8,128)(2,1)} %copy-done.7) | copy-start | bytes 4718596
  63.3 17.9 %collective-permute-start.5 = (bf16[3,8,128,128]{3,2,1,0:T(8,128)(2,1)S(1)}, bf16[3,8,128,128]{3,2,1,0:T(8,128)(2,1)S(1)}, u32[]{:S(2)}, u32[]{:S(2)}) collective-permute-start(bf16[3,8,128,128]{3,2,1,0:T(8,128)(2,1)S(1)} %slice_bitcast_fusion), channel_id=1, source_target_pairs={{0,6},{1,7},{2,0},{3,1},{4,2},{5,3},{6,4},{7,5},{8,14},{9,15},{10,... | collective-permute-start | bytes 2359304 | tf_op jit(solution)/shard_map/ppermute | solution.py:33
  65.9 18.5 %collective-permute-start.4 = (bf16[3,8,128,128]{3,2,1,0:T(8,128)(2,1)S(1)}, bf16[3,8,128,128]{3,2,1,0:T(8,128)(2,1)S(1)}, u32[]{:S(2)}, u32[]{:S(2)}) collective-permute-start(bf16[3,8,128,128]{3,2,1,0:T(8,128)(2,1)S(1)} %slice_bitcast_fusion.1), channel_id=1, source_target_pairs={{0,2},{1,3},{2,4},{3,5},{4,6},{5,7},{6,0},{7,1},{8,10},{9,11},{10,... | collective-permute-start | bytes 2359304 | tf_op jit(solution)/shard_map/ppermute | solution.py:33
  81.2 3.3 %copy-start.9 = (bf16[3,8,128,128]{3,2,1,0:T(8,128)(2,1)}, bf16[3,8,128,128]{3,2,1,0:T(8,128)(2,1)S(1)}, u32[]{:S(2)}) copy-start(bf16[3,8,128,128]{3,2,1,0:T(8,128)(2,1)S(1)} %collective-permute-done.5.refs_2_.refs_4_) | copy-start | bytes 2359300
  84.4 0.9 copy-start.10
  85.3 1.5 slice-start
  85.3 1.5 slice-start.1
  85.3 22.2 %collective-permute-start.8 = (bf16[2,2,8,128,128]{4,3,2,1,0:T(8,128)(2,1)}, bf16[2,2,8,128,128]{4,3,2,1,0:T(8,128)(2,1)S(1)}, u32[]{:S(2)}, u32[]{:S(2)}) collective-permute-start(bf16[2,2,8,128,128]{4,3,2,1,0:T(8,128)(2,1)} %gate.5), channel_id=1, source_target_pairs={{0,6},{1,7},{2,0},{3,1},{4,2},{5,3},{6,4},{7,5},{8,14},{9,15},{10,... | collective-permute-start | bytes 3145736 | tf_op jit(solution)/shard_map/ppermute | solution.py:33
  86.4 24.7 %collective-permute-start.6 = (bf16[2,2,8,128,128]{4,3,2,1,0:T(8,128)(2,1)}, bf16[2,2,8,128,128]{4,3,2,1,0:T(8,128)(2,1)S(1)}, u32[]{:S(2)}, u32[]{:S(2)}) collective-permute-start(bf16[2,2,8,128,128]{4,3,2,1,0:T(8,128)(2,1)} %gate.5), channel_id=1, source_target_pairs={{0,2},{1,3},{2,4},{3,5},{4,6},{5,7},{6,0},{7,1},{8,10},{9,11},{10,... | collective-permute-start | bytes 3145736 | tf_op jit(solution)/shard_map/ppermute | solution.py:33
  86.9 25.3 %collective-permute-start.12 = (bf16[2,2,8,128,128]{4,3,2,1,0:T(8,128)(2,1)S(1)}, bf16[2,2,8,128,128]{4,3,2,1,0:T(8,128)(2,1)S(1)}, u32[]{:S(2)}, u32[]{:S(2)}) collective-permute-start(bf16[2,2,8,128,128]{4,3,2,1,0:T(8,128)(2,1)S(1)} %pad_maximum_fusion.1), channel_id=1, source_target_pairs={{0,1},{1,0},{2,3},{3,2},{4,5},{5,4},{6,7},{7,6},{8,9},{9,8},{10,11... | collective-permute-start | bytes 3145736 | tf_op jit(solution)/shard_map/ppermute | solution.py:33
  90.5 30.6 %collective-permute-start.10 = (bf16[2,1,8,128,128]{4,3,2,1,0:T(8,128)(2,1)S(1)}, bf16[2,1,8,128,128]{4,3,2,1,0:T(8,128)(2,1)S(1)}, u32[]{:S(2)}, u32[]{:S(2)}) collective-permute-start(bf16[2,1,8,128,128]{4,3,2,1,0:T(8,128)(2,1)S(1)} %pad_maximum_fusion.3), channel_id=1, source_target_pairs={{0,1},{1,0},{2,3},{3,2},{4,5},{5,4},{6,7},{7,6},{8,9},{9,8},{10,11... | collective-permute-start | bytes 1572872 | tf_op jit(solution)/shard_map/ppermute | solution.py:33
  107.6 4.4 %copy-start.12 = (bf16[2,2,8,128,128]{4,3,2,1,0:T(8,128)(2,1)}, bf16[2,2,8,128,128]{4,3,2,1,0:T(8,128)(2,1)S(1)}, u32[]{:S(2)}) copy-start(bf16[2,2,8,128,128]{4,3,2,1,0:T(8,128)(2,1)S(1)} %collective-permute-done.8.refs_7_) | copy-start | bytes 3145732
  108.5 12.6 %collective-permute-start.9 = (bf16[2,8,128,128]{3,2,1,0:T(8,128)(2,1)}, bf16[2,8,128,128]{3,2,1,0:T(8,128)(2,1)S(1)}, u32[]{:S(2)}, u32[]{:S(2)}) collective-permute-start(bf16[2,8,128,128]{3,2,1,0:T(8,128)(2,1)} %slice_bitcast_fusion.2), channel_id=1, source_target_pairs={{0,6},{1,7},{2,0},{3,1},{4,2},{5,3},{6,4},{7,5},{8,14},{9,15},{10,... | collective-permute-start | bytes 1572872 | tf_op jit(solution)/shard_map/ppermute | solution.py:33
  111.1 1.2 copy-start.13
  112.0 11.4 %collective-permute-start.7 = (bf16[2,8,128,128]{3,2,1,0:T(8,128)(2,1)}, bf16[2,8,128,128]{3,2,1,0:T(8,128)(2,1)S(1)}, u32[]{:S(2)}, u32[]{:S(2)}) collective-permute-start(bf16[2,8,128,128]{3,2,1,0:T(8,128)(2,1)} %slice_bitcast_fusion.3), channel_id=1, source_target_pairs={{0,2},{1,3},{2,4},{3,5},{4,6},{5,7},{6,0},{7,1},{8,10},{9,11},{10,... | collective-permute-start | bytes 1572872 | tf_op jit(solution)/shard_map/ppermute | solution.py:33
  112.3 1.0 copy-start.11
  113.2 15.3 %copy-start.4 = (s32[2,8,28]{2,1,0:T(8,128)S(1)}, s32[2,8,28]{2,1,0:T(8,128)}, u32[]{:S(2)}) copy-start(s32[2,8,28]{2,1,0:T(8,128)} %get-tuple-element.6.refs_4_.order_ref) | copy-start | bytes 5380
  113.2 15.3 %copy-start.5 = (s32[2,8]{1,0:T(2,128)S(1)}, s32[2,8]{1,0:T(2,128)}, u32[]{:S(2)}) copy-start(s32[2,8]{1,0:T(2,128)} %get-tuple-element.7.used_ref) | copy-start | bytes 196
  113.2 15.3 %collective-permute-start.13 = (bf16[64,128,256]{2,1,0:T(8,128)(2,1)}, bf16[64,128,256]{2,1,0:T(8,128)(2,1)}, u32[]{:S(2)}, u32[]{:S(2)}) collective-permute-start(bf16[64,128,256]{2,1,0:T(8,128)(2,1)} %gate.7.near), channel_id=1, source_target_pairs={{0,8},{1,9},{2,10},{3,11},{4,12},{5,13},{6,14},{7,15},{8,0},{9,1},... | collective-permute-start | bytes 12582920 | tf_op jit(solution)/shard_map/ppermute | solution.py:33
  121.1 3.2 %copy-start.14 = (bf16[2,1,8,128,128]{4,3,2,1,0:T(8,128)(2,1)}, bf16[2,1,8,128,128]{4,3,2,1,0:T(8,128)(2,1)S(1)}, u32[]{:S(2)}) copy-start(bf16[2,1,8,128,128]{4,3,2,1,0:T(8,128)(2,1)S(1)} %collective-permute-done.10.refs_3_.refs_11_) | copy-start | bytes 1572868
  121.1 3.2 %copy-start.15 = (bf16[2,8,128,128]{3,2,1,0:T(8,128)(2,1)}, bf16[2,8,128,128]{3,2,1,0:T(8,128)(2,1)S(1)}, u32[]{:S(2)}) copy-start(bf16[2,8,128,128]{3,2,1,0:T(8,128)(2,1)S(1)} %collective-permute-done.9.refs_2_.refs_9_) | copy-start | bytes 1572868
  123.4 0.9 copy-start.16
  124.3 22.1 %collective-permute-start.11 = (bf16[64,128,256]{2,1,0:T(8,128)(2,1)}, bf16[64,128,256]{2,1,0:T(8,128)(2,1)S(1)}, u32[]{:S(2)}, u32[]{:S(2)}) collective-permute-start(bf16[64,128,256]{2,1,0:T(8,128)(2,1)} %gate.6.far), channel_id=1, source_target_pairs={{0,8},{1,9},{2,10},{3,11},{4,12},{5,13},{6,14},{7,15},{8,0},{9,1},... | collective-permute-start | bytes 12582920 | tf_op jit(solution)/shard_map/ppermute | solution.py:33
  128.5 17.9 %copy-start = (bf16[1024,128]{1,0:T(8,128)(2,1)S(1)}, bf16[1024,128]{1,0:T(8,128)(2,1)}, u32[]{:S(2)}) copy-start(bf16[1024,128]{1,0:T(8,128)(2,1)} %pert_imag.1) | copy-start | bytes 786436
  128.5 17.9 %copy-start.1 = (bf16[1024,128]{1,0:T(8,128)(2,1)S(1)}, bf16[1024,128]{1,0:T(8,128)(2,1)}, u32[]{:S(2)}) copy-start(bf16[1024,128]{1,0:T(8,128)(2,1)} %pert_real.1) | copy-start | bytes 786436
  128.6 17.9 %copy-start.2 = (bf16[1024,128]{1,0:T(8,128)(2,1)S(1)}, bf16[1024,128]{1,0:T(8,128)(2,1)}, u32[]{:S(2)}) copy-start(bf16[1024,128]{1,0:T(8,128)(2,1)} %drive_real.1) | copy-start | bytes 786436
  128.6 17.8 %copy-start.3 = (bf16[1024,128]{1,0:T(8,128)(2,1)S(1)}, bf16[1024,128]{1,0:T(8,128)(2,1)}, u32[]{:S(2)}) copy-start(bf16[1024,128]{1,0:T(8,128)(2,1)} %drive_imag.1) | copy-start | bytes 786436
Sparse Core Ops, SparseCore 0:
  10.4 58.6 all-gather.4
  70.8 53.4 all-gather.2

commit v3 on v2

v3 whole, which is shorter than its diff:
```python
import jax
import jax.numpy as jnp
from jax import lax
from jax.experimental import pallas as pl
from jax.experimental.pallas import tpu as pltpu
from jax.sharding import PartitionSpec as P

frequency = 0.7
damping = 0.5
step_length = 0.5

AXES = ("ylo", "z", "core", "x", "yhi")
SIZES = (2, 8, 2, 4, 2)
BLOCK = 128


def moves(axis, by):
    place = AXES.index(axis)
    stride = 1
    for size in SIZES[place + 1 :]:
        stride *= size
    total = 1
    for size in SIZES:
        total *= size
    pairs = []
    for source in range(total):
        at = source // stride % SIZES[place]
        pairs.append((source, source + ((at + by) % SIZES[place] - at) * stride))
    return pairs


def shift(array, axis, by=1):
    return lax.ppermute(array, AXES, moves(axis, by))


PIECES = (
    (0, 0, (0, 1, 2)),
    (3, 0, (0, 1, 2)),
    (1, 0, (0, 1, 2)),
    (2, 0, (0, 1, 2)),
    (0, 1, (0, 1)),
    (3, 1, (0, 1)),
    (1, 1, (0, 1)),
    (2, 1, (0, 1)),
    (0, 1, (2,)),
    (3, 1, (2,)),
    (1, 1, (2,)),
    (2, 1, (2,)),
)
STEP = 4
SKIP = 2**16


def list_kernel(place_ref, cols_ref, counts_ref, order_ref, row_ref, pairs_ref):
    rows, slots = cols_ref.shape
    my_ylo, my_core, my_x, my_yhi = (place_ref[n] for n in range(4))

    def one_row(row, ends):
        for which in range(3):
            pairs_ref[which] = ends[which]
        place = 0
        for dx, dy, local in PIECES:
            for j in local:
                slot = 3 * (2 * ((my_x + dx) & 3) + (my_yhi ^ dy)) + j
                column = cols_ref[row, slot]
                owner = column >> 3
                far = (owner >> 4) ^ my_ylo
                other = (owner & 1) ^ my_core
                which = far * (1 + other)
                at = ((owner >> 1) & 7) * 8 + (column & 7) + (1 - far) * other * 64

                @pl.when(slot < counts_ref[row])
                def _(which=which, at=at, place=place):
                    n = pairs_ref[which]
                    order_ref[which, n] = place * 256 + at
                    row_ref[which, n >> 1] = row
                    pairs_ref[which] = n + 1

                place += 1
        out = []
        for which in range(3):
            n = pairs_ref[which]
            order_ref[which, n] = SKIP
            out.append((n + 1) & ~1)
        return tuple(out)

    ends = lax.fori_loop(0, rows, one_row, (0, 0, 0))
    for which in range(3):
        for n in range(2 * STEP):
            order_ref[which, ends[which] + n] = SKIP
        for n in range(STEP):
            row_ref[which, (ends[which] >> 1) + n] = rows - 1
        pairs_ref[which] = ends[which] >> 1


def make_lists(place, cols, counts):
    most = cols.shape[0] * 24
    return pl.pallas_call(
        list_kernel,
        in_specs=[SMEM] * 3,
        out_specs=[SMEM] * 3,
        out_shape=[
            jax.ShapeDtypeStruct((3, most + 2 * STEP), jnp.int32),
            jax.ShapeDtypeStruct((3, most // 2 + STEP), jnp.int32),
            jax.ShapeDtypeStruct((3,), jnp.int32),
        ],
        name="make_lists",
    )(place, cols, counts)


def add_products(which, lists, blocks, panel, acc):
    order_ref, row_ref, pairs_ref = lists

    def one_step(step, carry):
        terms = []
        for pair in range(STEP):
            left, right = [], []
            for n in range(2):
                code = order_ref[which, (step * STEP + pair) * 2 + n]
                place, at = (code >> 8) & 31, code & 255
                row = row_ref[which, step * STEP + pair]
                left.append(jnp.concatenate([blocks[0, place, row], blocks[1, place, row]], axis=0))
                block = panel[at]
                right.append(jnp.where(code < SKIP, block, jnp.zeros_like(block)))
            terms.append(
                jnp.dot(
                    jnp.concatenate(left, axis=1),
                    jnp.concatenate(right, axis=0),
                    preferred_element_type=jnp.float32,
                )
            )
        for pair, term in enumerate(terms):
            acc[row_ref[which, step * STEP + pair]] += term
        return carry

    lax.fori_loop(0, (pairs_ref[which] + STEP - 1) // STEP, one_step, 0)


def fetch(pairs, sems):
    copies = [pltpu.make_async_copy(a, b, sems.at[n]) for n, (a, b) in enumerate(pairs)]
    for copy in copies:
        copy.start()
    for copy in copies:
        copy.wait()


def split_pieces(pieces, blocks):
    pairs, at = [], 0
    for piece in pieces:
        if isinstance(piece, tuple):
            size = piece[0].shape[0]
            pairs += [(piece[n], blocks.at[n, pl.ds(at, size)]) for n in range(2)]
        else:
            size = piece.shape[1]
            pairs.append((piece, blocks.at[:, pl.ds(at, size)]))
        at += size
    return pairs


def group_pieces(refs):
    return [*refs[:3], (refs[3], refs[4]), *refs[5:8], (refs[8], refs[9]), *refs[10:12]]


def near_kernel(order_ref, row_ref, pairs_ref, near, near_other, *refs):
    pieces, (acc, blocks, panel, sems) = refs[:12], refs[12:]
    count = near.shape[0]
    pairs = [(ref, panel.at[pl.ds(n * count, count)]) for n, ref in enumerate((near, near_other))]
    fetch(pairs + split_pieces(group_pieces(pieces), blocks), sems)
    acc[...] = jnp.zeros_like(acc)
    add_products(0, (order_ref, row_ref, pairs_ref), blocks, panel, acc)


def far_kernel(order_ref, row_ref, pairs_ref, far, before, *refs):
    pieces, (blocks, acc, panel, sems) = refs[:12], refs[12:]
    fetch([(far, panel), (before, acc)] + split_pieces(group_pieces(pieces), blocks), sems)
    add_products(1, (order_ref, row_ref, pairs_ref), blocks, panel, acc)


def last_kernel(
    order_ref,
    row_ref,
    pairs_ref,
    panel,
    blocks,
    before,
    pert_real,
    pert_imag,
    drive_real,
    drive_imag,
    new_real,
    new_imag,
    acc,
):
    acc[...] = before[...]
    add_products(2, (order_ref, row_ref, pairs_ref), blocks, panel, acc)

    def one_row(row, carry):
        total = acc[row]
        lines = pl.ds(row * BLOCK, BLOCK)
        ham_real, ham_imag = total[:BLOCK, :BLOCK], total[:BLOCK, BLOCK:]
        ovl_real, ovl_imag = total[BLOCK:, :BLOCK], total[BLOCK:, BLOCK:]
        res_real = drive_real[lines].astype(jnp.float32) - (
            ham_real - frequency * ovl_real + damping * ovl_imag
        )
        res_imag = drive_imag[lines].astype(jnp.float32) - (
            ham_imag - frequency * ovl_imag - damping * ovl_real
        )
        new_real[lines] = pert_real[lines].astype(jnp.float32) + step_length * res_real
        new_imag[lines] = pert_imag[lines].astype(jnp.float32) + step_length * res_imag
        return carry

    lax.fori_loop(0, acc.shape[0], one_row, 0)


SMEM = pl.BlockSpec(memory_space=pltpu.SMEM)
VMEM = pl.BlockSpec(memory_space=pltpu.VMEM)
ANY = pl.BlockSpec(memory_space=pl.ANY)


def nothing(*refs):
    pass


def after(array, *others):
    return pl.pallas_call(
        nothing,
        in_specs=[ANY] * (1 + len(others)),
        out_specs=ANY,
        out_shape=jax.ShapeDtypeStruct(array.shape, array.dtype),
        input_output_aliases={0: 0},
        compiler_params=pltpu.CompilerParams(vmem_limit_bytes=2**16),
        name="gate",
    )(in_hbm(array), *map(in_hbm, others))


def in_hbm(array):
    return pltpu.with_memory_space_constraint(array, pltpu.HBM)


def held(array):
    return pltpu.with_memory_space_constraint(array, pltpu.VMEM)


def cost(micros):
    return pl.CostEstimate(flops=0, bytes_accessed=int(micros * 3.0e6), transcendentals=0)


def near_products(lists, rows, near, near_other, pieces):
    count = near.shape[0]
    return pl.pallas_call(
        near_kernel,
        in_specs=[SMEM] * 3 + [ANY] * (2 + len(pieces)),
        out_specs=VMEM,
        out_shape=jax.ShapeDtypeStruct((rows, 2 * BLOCK, 2 * BLOCK), jnp.float32),
        scratch_shapes=[
            pltpu.VMEM((2, 24, rows, BLOCK, BLOCK), jnp.bfloat16),
            pltpu.VMEM((2 * count, BLOCK, 2 * BLOCK), jnp.bfloat16),
            pltpu.SemaphoreType.DMA((2 + len(pieces),)),
        ],
        compiler_params=pltpu.CompilerParams(vmem_limit_bytes=30 * 2**20),
        cost_estimate=cost(10),
        name="products_near",
    )(*lists, in_hbm(near), in_hbm(near_other), *map(in_hbm, pieces))


def far_products(lists, far, before, pieces):
    rows = before.shape[0]
    return pl.pallas_call(
        far_kernel,
        in_specs=[SMEM] * 3 + [ANY] * (2 + len(pieces)),
        out_specs=[VMEM, VMEM],
        out_shape=[
            pltpu.VMEM((2, 24, rows, BLOCK, BLOCK), jnp.bfloat16),
            pltpu.VMEM(before.shape, jnp.float32),
        ],
        scratch_shapes=[
            pltpu.VMEM(far.shape, jnp.bfloat16),
            pltpu.SemaphoreType.DMA((2 + len(pieces),)),
        ],
        compiler_params=pltpu.CompilerParams(vmem_limit_bytes=7 * 2**20),
        cost_estimate=cost(8),
        name="products_far",
    )(*lists, in_hbm(far), in_hbm(before), *map(in_hbm, pieces))


def last_products(lists, far_other, blocks, before, *flat):
    rows = before.shape[0]
    return pl.pallas_call(
        last_kernel,
        in_specs=[SMEM] * 3 + [VMEM] * 7,
        out_specs=[VMEM] * 2,
        out_shape=[jax.ShapeDtypeStruct((rows * BLOCK, BLOCK), jnp.float32)] * 2,
        scratch_shapes=[pltpu.VMEM(before.shape, jnp.float32)],
        compiler_params=pltpu.CompilerParams(vmem_limit_bytes=7 * 2**20),
        cost_estimate=cost(4),
        name="products_last",
    )(*lists, held(far_other), held(blocks), held(before), *flat)


def per_device(
    ham_blocks,
    margin_blocks,
    block_cols,
    block_counts,
    pert_real,
    pert_imag,
    drive_real,
    drive_imag,
):
    rows = block_cols.shape[0]
    place = jnp.stack([lax.axis_index(a) for a in ("ylo", "core", "x", "yhi")]).astype(jnp.int32)

    both = jnp.stack([ham_blocks.swapaxes(0, 1), margin_blocks.swapaxes(0, 1)], axis=0)
    panel = jnp.concatenate([pert_real, pert_imag], axis=1).reshape(rows, BLOCK, 2 * BLOCK)

    from_left = shift(both, "x", 1)
    from_right = shift(both, "x", -1)
    part = shift(both[:, :2], "yhi")
    near = lax.all_gather(panel, "z", axis=0, tiled=True)
    lists = make_lists(place, block_cols, block_counts)
    neighbour = shift(panel, "ylo")

    far = lax.all_gather(after(neighbour, from_left, from_right, part, *lists), "z", axis=0, tiled=True)
    far_ham = shift(from_left[0], "x", 1)
    far_margin = shift(from_right[1], "x", -1)
    part_left = shift(part, "x", 1)
    part_right = shift(part, "x", -1)
    late = shift(
        jnp.concatenate([both[:, 2:], from_left[:, 2:], from_right[:, 2:]], axis=1), "yhi"
    )

    near = after(near, far_ham, far_margin, part_left, part_right, late)
    near_other = shift(near, "core")
    late_far = shift(jnp.stack([far_ham[2:], far_margin[2:]], axis=0), "yhi")
    part_far_ham = shift(part_left[0], "x", 1)
    part_far_margin = shift(part_right[1], "x", -1)

    pieces = (
        both,
        from_left,
        from_right,
        far_ham,
        far_margin,
        part,
        part_left,
        part_right,
        part_far_ham,
        part_far_margin,
        late,
        late_far,
    )
    acc = near_products(lists, rows, near, near_other, pieces)
    far = after(far, acc)
    far_other = shift(far, "core")
    blocks, acc = far_products(lists, far, acc, pieces)
    new_real, new_imag = last_products(
        lists, far_other, blocks, acc, pert_real, pert_imag, drive_real, drive_imag
    )
    return new_real, new_imag


def solution(mesh):
    fine = jax.sharding.Mesh(mesh.devices.reshape(SIZES), AXES)
    loop, rep = ("ylo", "z", "core"), ("x", "yhi")
    return jax.shard_map(
        per_device,
        mesh=fine,
        in_specs=(
            P(loop, rep, None, None),
            P(loop, rep, None, None),
            P(loop, None),
            P(loop),
            P(loop, rep),
            P(loop, rep),
            P(loop, rep),
            P(loop, rep),
        ),
        out_specs=(P(loop, rep), P(loop, rep)),
        check_vma=False,
    )
```

time: 158 us -> 165 us (1.044)
  waiting for transfers between devices: 74.9 us -> 79.1 us
  starting transfers between devices: 26.3 us -> 22.6 us
  other arithmetic: 4.06 us -> 6.39 us
  Pallas kernels: 27.6 us -> 29.8 us
    ppermute x14, waiting for transfers between devices: 74 us -> 79.1 us  [shift(): return lax.ppermute(array, AXES, moves(axis, by))]
    ppermute x14, starting transfers between devices: 26.3 us -> 22.5 us  [shift(): return lax.ppermute(array, AXES, moves(axis, by))]
    unnamed x38 -> x46, local copies, waits for them, and re-layouts: 3.87 us -> 6.74 us
    slice x1 -> x0, local copies, waits for them, and re-layouts: 2.32 us -> none  [per_device(): part_two = after(part[:, :2], far_ham, far_margin)]
    another operation x1 -> x3, other arithmetic: 1.31 us -> 3.62 us  [per_device(): jnp.stack([ham_blocks.swapaxes(0, 1), margin_blocks.swapaxes(0, 1)], axis=0)]
    pallas_call x3 -> x4, Pallas kernels: 27.6 us -> 29.8 us  [the longest x1 12 us: near_products(): pl.pallas_call(near_kernel, in_specs=[SMEM] * 3 + [ANY] * (2 + len(pieces...]
  transfers between devices with their start and end apart: 16 -> 16, of which waited for: 7 -> 8; matrix products, arithmetic and copies ran while one was open for 6% -> 5% of each run, Pallas kernels for 14% -> 16%
where the time goes in v3:
time: 165 us
  waiting for transfers between devices  79.1 us (48%)
  Pallas kernels  29.8 us (18%)
  starting transfers between devices  22.6 us (14%)
  between operations  14.3 us (9%)
  local copies, waits for them, and re-layouts  12.3 us (7%)
  other arithmetic  6.39 us (4%)
    ppermute x14, waiting for transfers between devices, shift(): return lax.ppermute(array, AXES, moves(axis, by))  79.1 us
    ppermute x14, starting transfers between devices, shift(): return lax.ppermute(array, AXES, moves(axis, by))  22.5 us
    pallas_call x1, Pallas kernels, near_products(): pl.pallas_call(near_kernel, in_specs=[SMEM] * 3 + [ANY] * (2 + len(pieces...  12 us
    pallas_call x1, Pallas kernels, far_products(): pl.pallas_call(far_kernel, in_specs=[SMEM] * 3 + [ANY] * (2 + len(pieces)...  9.6 us
    unnamed x46, local copies, waits for them, and re-layouts  6.74 us
    pallas_call x1, Pallas kernels, make_lists(): pl.pallas_call(list_kernel, in_specs=[SMEM] * 3, out_specs=[SMEM] * 3, ou...  4.42 us
    pallas_call x1, Pallas kernels, last_products(): pl.pallas_call(last_kernel, in_specs=[SMEM] * 3 + [VMEM] * 7, out_specs=[...  3.8 us
    another operation x3, other arithmetic, per_device(): jnp.stack([ham_blocks.swapaxes(0, 1), margin_blocks.swapaxes(0, 1)], axis=0)  3.62 us
  transfers between devices with their start and end apart: 16, of which 8 were waited for; matrix products, arithmetic and copies ran while one was open for 5% of the time, Pallas kernels for 16%

profile of v3, /device:TPU:1, one launch (start us, length us, event | category | flops | bytes accessed | tf_op | source)
XLA Modules:
  0.0 164.6 jit_solution(4180771567035128526)
XLA Ops:
  7.2 0.0 copy-start.21
  7.2 0.0 copy-start.22
  7.2 0.0 all-gather.5.cloned.1.call-start
  7.2 2.0 %pad_maximum_fusion.2 = bf16[1024,256]{1,0:T(8,128)(2,1)} fusion(bf16[1024,128]{1,0:T(8,128)(2,1)} %pert_imag.1, bf16[1024,128]{1,0:T(8,128)(2,1)} %pert_real.1), kind=kLoop, calls=%fused_computation.14 | loop fusion | flops 1048576 | bytes 1048576 | tf_op jit(solution)/shard_map/concatenate | solution.py:314
  9.2 0.0 all-gather.5.cloned.1.call-update
  9.2 0.0 all-gather.3.cloned.1.call-start
  9.3 0.0 copy-done.21
  9.3 0.2 copy_bitcast_fusion
  9.5 1.5 pad_maximum_fusion.refs_0_
  11.0 3.3 %collective-permute-start.2 = (bf16[2,3,8,128,128]{4,3,2,1,0:T(8,128)(2,1)}, bf16[2,3,8,128,128]{4,3,2,1,0:T(8,128)(2,1)S(1)}, u32[]{:S(2)}, u32[]{:S(2)}) collective-permute-start(bf16[2,3,8,128,128]{4,3,2,1,0:T(8,128)(2,1)} %pad_maximum_fusion.refs_0_), channel_id=1, source_target_pairs={{0,6},{1,7},{2,0},{3,1},{4,2},{5,3},{6,4},{7,5},{8,14},{9,15},{10,... | collective-permute-start | bytes 4718600 | tf_op jit(solution)/shard_map/ppermute | solution.py:33
  14.3 0.0 collective-permute-start.1
  14.3 1.1 fusion
  15.4 2.9 %collective-permute-start.3 = (bf16[2,2,8,128,128]{4,3,2,1,0:T(8,128)(2,1)}, bf16[2,2,8,128,128]{4,3,2,1,0:T(8,128)(2,1)}, u32[]{:S(2)}, u32[]{:S(2)}) collective-permute-start(bf16[2,2,8,128,128]{4,3,2,1,0:T(8,128)(2,1)} %fusion), channel_id=1, source_target_pairs={{0,1},{1,0},{2,3},{3,2},{4,5},{5,4},{6,7},{7,6},{8,9},{9,8},{10,11... | collective-permute-start | bytes 3145736 | tf_op jit(solution)/shard_map/ppermute | solution.py:33
  18.3 0.4 collective-permute-start
  18.7 0.6 pad_add_fusion.place_ref
  19.2 4.4 %make_lists.1 = (s32[3,200]{1,0:T(4,128)}, s32[3,100]{1,0:T(4,128)}, s32[3]{0:T(128)}) custom-call(s32[4]{0:T(128)} %pad_add_fusion.place_ref, s32[8,24]{1,0:T(8,128)} %cols_ref.1, s32[8]{0:T(128)} %counts_ref.1), custom_call_target="tpu_custom_call" | custom-call | tf_op jit(solution)/shard_map/make_lists/pallas_call | solution.py:98
  23.7 28.8 %collective-permute-done.refs_0_ = bf16[8,128,256]{2,1,0:T(8,128)(2,1)} collective-permute-done((bf16[8,128,256]{2,1,0:T(8,128)(2,1)}, bf16[8,128,256]{2,1,0:T(8,128)(2,1)}, u32[]{:S(2)}, u32[]{:S(2)}) %collective-permute-start) | collective-permute-done | bytes 524320 | tf_op jit(solution)/shard_map/ppermute | solution.py:33
  52.5 0.0 collective-permute-done.3.refs_3_.refs_5_
  52.5 0.0 collective-permute-done.2.refs_2_
  52.5 0.0 collective-permute-done.1.refs_1_
  52.5 1.1 copy-done.8
  53.6 0.5 copy-done.10
  54.1 0.0 all-gather.3.cloned.1.call-update
  54.2 1.1 fusion.1
  55.2 0.0 slice-start
  55.3 0.0 slice-start.1
  55.3 1.0 slice-done
  56.3 0.2 slice-done.1
  56.5 0.2 pad_maximum_fusion.1
  56.7 1.6 collective-permute-start.8
  58.3 2.4 %collective-permute-start.7 = (bf16[2,2,8,128,128]{4,3,2,1,0:T(8,128)(2,1)}, bf16[2,2,8,128,128]{4,3,2,1,0:T(8,128)(2,1)S(1)}, u32[]{:S(2)}, u32[]{:S(2)}) collective-permute-start(bf16[2,2,8,128,128]{4,3,2,1,0:T(8,128)(2,1)} %collective-permute-done.3.refs_3_.refs_5_), channel_id=1, source_target_pairs={{0,6},{1,7},{2,0},{3,1},{4,2},{5,3},{6,4},{7,5},{8,14},{9,15},{10,... | collective-permute-start | bytes 3145736 | tf_op jit(solution)/shard_map/ppermute | solution.py:33
  60.7 0.0 collective-permute-start.6
  60.7 0.1 slice_bitcast_fusion
  60.7 2.8 %collective-permute-start.5 = (bf16[3,8,128,128]{3,2,1,0:T(8,128)(2,1)S(1)}, bf16[3,8,128,128]{3,2,1,0:T(8,128)(2,1)S(1)}, u32[]{:S(2)}, u32[]{:S(2)}) collective-permute-start(bf16[3,8,128,128]{3,2,1,0:T(8,128)(2,1)S(1)} %slice_bitcast_fusion), channel_id=1, source_target_pairs={{0,6},{1,7},{2,0},{3,1},{4,2},{5,3},{6,4},{7,5},{8,14},{9,15},{10,... | collective-permute-start | bytes 2359304 | tf_op jit(solution)/shard_map/ppermute | solution.py:33
  63.5 0.1 slice_bitcast_fusion.1
  63.6 0.1 collective-permute-start.4
  63.7 17.4 %collective-permute-done.7.refs_4_.refs_7_ = bf16[2,2,8,128,128]{4,3,2,1,0:T(8,128)(2,1)S(1)} collective-permute-done((bf16[2,2,8,128,128]{4,3,2,1,0:T(8,128)(2,1)}, bf16[2,2,8,128,128]{4,3,2,1,0:T(8,128)(2,1)S(1)}, u32[]{:S(2)}, u32[]{:S(2)}) %collective-permute-start.7) | collective-permute-done | bytes 1048608 | tf_op jit(solution)/shard_map/ppermute | solution.py:33
  81.1 3.0 %collective-permute-done.6.refs_3_.refs_6_ = bf16[2,2,8,128,128]{4,3,2,1,0:T(8,128)(2,1)} collective-permute-done((bf16[2,2,8,128,128]{4,3,2,1,0:T(8,128)(2,1)}, bf16[2,2,8,128,128]{4,3,2,1,0:T(8,128)(2,1)}, u32[]{:S(2)}, u32[]{:S(2)}) %collective-permute-start.6) | collective-permute-done | bytes 1048608 | tf_op jit(solution)/shard_map/ppermute | solution.py:33
  84.1 13.8 %collective-permute-done.5.refs_2_.refs_4_ = bf16[3,8,128,128]{3,2,1,0:T(8,128)(2,1)S(1)} collective-permute-done((bf16[3,8,128,128]{3,2,1,0:T(8,128)(2,1)S(1)}, bf16[3,8,128,128]{3,2,1,0:T(8,128)(2,1)S(1)}, u32[]{:S(2)}, u32[]{:S(2)}) %collective-permute-start.5) | collective-permute-done | bytes 786464 | tf_op jit(solution)/shard_map/ppermute | solution.py:33
  97.9 3.0 %collective-permute-done.4.refs_1_.refs_3_ = bf16[3,8,128,128]{3,2,1,0:T(8,128)(2,1)S(1)} collective-permute-done((bf16[3,8,128,128]{3,2,1,0:T(8,128)(2,1)S(1)}, bf16[3,8,128,128]{3,2,1,0:T(8,128)(2,1)S(1)}, u32[]{:S(2)}, u32[]{:S(2)}) %collective-permute-start.4) | collective-permute-done | bytes 786464 | tf_op jit(solution)/shard_map/ppermute | solution.py:33
  101.0 0.0 collective-permute-done.8.refs_5_.refs_10_
  101.0 0.9 copy-done.16
  101.9 3.5 %collective-permute-start.9 = (bf16[64,128,256]{2,1,0:T(8,128)(2,1)}, bf16[64,128,256]{2,1,0:T(8,128)(2,1)S(1)}, u32[]{:S(2)}, u32[]{:S(2)}) collective-permute-start(bf16[64,128,256]{2,1,0:T(8,128)(2,1)} %gate.4.near), channel_id=1, source_target_pairs={{0,8},{1,9},{2,10},{3,11},{4,12},{5,13},{6,14},{7,15},{8,0},{9,1},... | collective-permute-start | bytes 12582920 | tf_op jit(solution)/shard_map/ppermute | solution.py:33
  105.4 1.1 slice_bitcast_fusion.2
  106.5 0.3 collective-permute-start.11
  106.9 1.1 slice_bitcast_fusion.3
  108.0 1.3 collective-permute-start.10
  109.2 1.0 slice_bitcast_fusion.4
  110.2 1.0 slice_bitcast_fusion.5
  111.2 0.1 pad_maximum_fusion.3
  111.2 1.5 collective-permute-start.12
  112.8 7.5 %collective-permute-done.11.refs_9_ = bf16[2,8,128,128]{3,2,1,0:T(8,128)(2,1)S(1)} collective-permute-done((bf16[2,8,128,128]{3,2,1,0:T(8,128)(2,1)S(1)}, bf16[2,8,128,128]{3,2,1,0:T(8,128)(2,1)S(1)}, u32[]{:S(2)}, u32[]{:S(2)}) %collective-permute-start.11) | collective-permute-done | bytes 524320 | tf_op jit(solution)/shard_map/ppermute | solution.py:33
  120.3 2.3 %collective-permute-done.10.refs_8_ = bf16[2,8,128,128]{3,2,1,0:T(8,128)(2,1)S(1)} collective-permute-done((bf16[2,8,128,128]{3,2,1,0:T(8,128)(2,1)S(1)}, bf16[2,8,128,128]{3,2,1,0:T(8,128)(2,1)S(1)}, u32[]{:S(2)}, u32[]{:S(2)}) %collective-permute-start.10) | collective-permute-done | bytes 524320 | tf_op jit(solution)/shard_map/ppermute | solution.py:33
  122.6 3.1 %collective-permute-done.12.refs_11_ = bf16[2,1,8,128,128]{4,3,2,1,0:T(8,128)(2,1)S(1)} collective-permute-done((bf16[2,1,8,128,128]{4,3,2,1,0:T(8,128)(2,1)S(1)}, bf16[2,1,8,128,128]{4,3,2,1,0:T(8,128)(2,1)S(1)}, u32[]{:S(2)}, u32[]{:S(2)}) %collective-permute-start.12) | collective-permute-done | bytes 524320 | tf_op jit(solution)/shard_map/ppermute | solution.py:33
  125.7 0.0 collective-permute-done.9.near_other
  125.8 0.8 copy-done.20
  126.5 2.0 %copy-done.17 = bf16[64,128,256]{2,1,0:T(8,128)(2,1)} copy-done((bf16[64,128,256]{2,1,0:T(8,128)(2,1)}, bf16[64,128,256]{2,1,0:T(8,128)(2,1)S(1)}, u32[]{:S(2)}) %copy-start.17) | copy-done | bytes 4194328
  128.6 12.0 %products_near.1.refs_1_.before = f32[8,256,256]{2,1,0:T(8,128)S(1)} custom-call(s32[3,200]{1,0:T(4,128)S(1)} %copy-done.5, s32[3,100]{1,0:T(4,128)S(1)} %copy-done.6, s32[3]{0:T(128)S(1)} %copy-done.7, bf16[64,128,256]{2,1,0:T(8,128)(2,1)} %gate.4.near, bf16[64,128,256]{2,1,0:T(8,128)(2,1)} %copy-done.17, ...), custom_call_target="tpu_custom_call" | custom-call | bytes 30000000 | tf_op jit(solution)/shard_map/products_near/pallas_call | solution.py:250
  140.6 1.3 copy-done
  142.0 0.0 copy-start.4
  142.0 2.4 %collective-permute-start.13 = (bf16[64,128,256]{2,1,0:T(8,128)(2,1)}, bf16[64,128,256]{2,1,0:T(8,128)(2,1)S(1)}, u32[]{:S(2)}, u32[]{:S(2)}) collective-permute-start(bf16[64,128,256]{2,1,0:T(8,128)(2,1)} %gate.5.far), channel_id=1, source_target_pairs={{0,8},{1,9},{2,10},{3,11},{4,12},{5,13},{6,14},{7,15},{8,0},{9,1},... | collective-permute-start | bytes 12582920 | tf_op jit(solution)/shard_map/ppermute | solution.py:33
  144.3 9.6 %products_far.1 = (bf16[2,24,8,128,128]{4,3,2,1,0:T(8,128)(2,1)S(1)}, f32[8,256,256]{2,1,0:T(8,128)S(1)}) custom-call(s32[3,200]{1,0:T(4,128)S(1)} %copy-done.5, s32[3,100]{1,0:T(4,128)S(1)} %copy-done.6, s32[3]{0:T(128)S(1)} %copy-done.7, bf16[64,128,256]{2,1,0:T(8,128)(2,1)} %gate.5.far, f32[8,256,256]{2,1,0:T(8,128)} %copy-done, ...), custom_call_target="tpu_custom_call" | custom-call | bytes 24000000 | tf_op jit(solution)/shard_map/products_far/pallas_call | solution.py:268
  153.9 0.0 collective-permute-done.13.panel
  154.0 3.8 %products_last.1 = (f32[1024,128]{1,0:T(8,128)}, f32[1024,128]{1,0:T(8,128)}) custom-call(s32[3,200]{1,0:T(4,128)S(1)} %copy-done.5, s32[3,100]{1,0:T(4,128)S(1)} %copy-done.6, s32[3]{0:T(128)S(1)} %copy-done.7, bf16[64,128,256]{2,1,0:T(8,128)(2,1)S(1)} %collective-permute-done.13.panel, bf16[2,24,8,128,128]{4,3,2,1,0:T(8,128)(2,1)S(1)} %get-tuple-element.10.blocks, ...), custom_call_target="tpu_custom_call" | custom-call | bytes 12000000 | tf_op jit(solution)/shard_map/products_last/pallas_call | solution.py:288
  (41 shorter events, 0.1 us)
Async XLA Ops:
  7.2 2.1 %copy-start.21 = (bf16[8,3,128,128]{3,2,1,0:T(8,128)(2,1)S(1)}, bf16[8,3,128,128]{3,2,1,0:T(8,128)(2,1)}, u32[]{:S(2)}) copy-start(bf16[8,3,128,128]{3,2,1,0:T(8,128)(2,1)} %param.9) | copy-start | bytes 2359300
  7.2 2.1 %copy-start.22 = (bf16[8,3,128,128]{3,2,1,0:T(8,128)(2,1)S(1)}, bf16[8,3,128,128]{3,2,1,0:T(8,128)(2,1)}, u32[]{:S(2)}) copy-start(bf16[8,3,128,128]{3,2,1,0:T(8,128)(2,1)} %param.8) | copy-start | bytes 2359300
  7.2 93.8 %all-gather.5.cloned.1.call-start = ((), (), s32[]{:S(2)}) async-start(), calls=%async_computation.1 | async-start | bytes 4718592 | tf_op jit(solution)/shard_map/all_gather | solution.py:319
  9.2 132.7 %all-gather.3.cloned.1.call-start = ((), (), s32[]{:S(2)}) async-start(), calls=%async_computation | async-start | bytes 4718592 | tf_op jit(solution)/shard_map/all_gather | solution.py:323
  9.5 4.8 %copy-start.13 = (bf16[1,3,8,128,128]{4,3,2,1,0:T(8,128)(2,1)}, bf16[1,3,8,128,128]{4,3,2,1,0:T(8,128)(2,1)S(1)}, u32[]{:S(2)}) copy-start(bf16[1,3,8,128,128]{4,3,2,1,0:T(8,128)(2,1)S(1)} %get-tuple-element.12) | copy-start | bytes 2359300
  9.5 4.8 %copy-start.14 = (bf16[1,3,8,128,128]{4,3,2,1,0:T(8,128)(2,1)}, bf16[1,3,8,128,128]{4,3,2,1,0:T(8,128)(2,1)S(1)}, u32[]{:S(2)}) copy-start(bf16[1,3,8,128,128]{4,3,2,1,0:T(8,128)(2,1)S(1)} %get-tuple-element.13) | copy-start | bytes 2359300
  11.0 41.5 %collective-permute-start.2 = (bf16[2,3,8,128,128]{4,3,2,1,0:T(8,128)(2,1)}, bf16[2,3,8,128,128]{4,3,2,1,0:T(8,128)(2,1)S(1)}, u32[]{:S(2)}, u32[]{:S(2)}) collective-permute-start(bf16[2,3,8,128,128]{4,3,2,1,0:T(8,128)(2,1)} %pad_maximum_fusion.refs_0_), channel_id=1, source_target_pairs={{0,6},{1,7},{2,0},{3,1},{4,2},{5,3},{6,4},{7,5},{8,14},{9,15},{10,... | collective-permute-start | bytes 4718600 | tf_op jit(solution)/shard_map/ppermute | solution.py:33
  14.3 38.2 %collective-permute-start.1 = (bf16[2,3,8,128,128]{4,3,2,1,0:T(8,128)(2,1)}, bf16[2,3,8,128,128]{4,3,2,1,0:T(8,128)(2,1)S(1)}, u32[]{:S(2)}, u32[]{:S(2)}) collective-permute-start(bf16[2,3,8,128,128]{4,3,2,1,0:T(8,128)(2,1)} %pad_maximum_fusion.refs_0_), channel_id=1, source_target_pairs={{0,2},{1,3},{2,4},{3,5},{4,6},{5,7},{6,0},{7,1},{8,10},{9,11},{10,... | collective-permute-start | bytes 4718600 | tf_op jit(solution)/shard_map/ppermute | solution.py:33
  15.4 37.1 %collective-permute-start.3 = (bf16[2,2,8,128,128]{4,3,2,1,0:T(8,128)(2,1)}, bf16[2,2,8,128,128]{4,3,2,1,0:T(8,128)(2,1)}, u32[]{:S(2)}, u32[]{:S(2)}) collective-permute-start(bf16[2,2,8,128,128]{4,3,2,1,0:T(8,128)(2,1)} %fusion), channel_id=1, source_target_pairs={{0,1},{1,0},{2,3},{3,2},{4,5},{5,4},{6,7},{7,6},{8,9},{9,8},{10,11... | collective-permute-start | bytes 3145736 | tf_op jit(solution)/shard_map/ppermute | solution.py:33
  18.3 34.2 %collective-permute-start = (bf16[8,128,256]{2,1,0:T(8,128)(2,1)}, bf16[8,128,256]{2,1,0:T(8,128)(2,1)}, u32[]{:S(2)}, u32[]{:S(2)}) collective-permute-start(bf16[8,128,256]{2,1,0:T(8,128)(2,1)} %bitcast.4), channel_id=1, source_target_pairs={{0,128},{1,129},{2,130},{3,131},{4,132},{5,133},{6,134},{7,135},{8... | collective-permute-start | bytes 1572872 | tf_op jit(solution)/shard_map/ppermute | solution.py:33
  52.5 1.2 copy-start.8
  52.5 1.6 %copy-start.10 = (bf16[2,3,8,128,128]{4,3,2,1,0:T(8,128)(2,1)}, bf16[2,3,8,128,128]{4,3,2,1,0:T(8,128)(2,1)S(1)}, u32[]{:S(2)}) copy-start(bf16[2,3,8,128,128]{4,3,2,1,0:T(8,128)(2,1)S(1)} %collective-permute-done.1.refs_1_) | copy-start | bytes 4718596
  55.2 1.1 slice-start
  55.3 1.2 slice-start.1
  56.5 4.2 %copy-start.9 = (bf16[2,3,8,128,128]{4,3,2,1,0:T(8,128)(2,1)S(1)}, bf16[2,3,8,128,128]{4,3,2,1,0:T(8,128)(2,1)}, u32[]{:S(2)}) copy-start(bf16[2,3,8,128,128]{4,3,2,1,0:T(8,128)(2,1)} %copy-done.8) | copy-start | bytes 4718596
  56.6 6.9 %copy-start.11 = (bf16[2,3,8,128,128]{4,3,2,1,0:T(8,128)(2,1)S(1)}, bf16[2,3,8,128,128]{4,3,2,1,0:T(8,128)(2,1)}, u32[]{:S(2)}) copy-start(bf16[2,3,8,128,128]{4,3,2,1,0:T(8,128)(2,1)} %copy-done.10) | copy-start | bytes 4718596
  56.7 44.3 %collective-permute-start.8 = (bf16[2,3,8,128,128]{4,3,2,1,0:T(8,128)(2,1)S(1)}, bf16[2,3,8,128,128]{4,3,2,1,0:T(8,128)(2,1)}, u32[]{:S(2)}, u32[]{:S(2)}) collective-permute-start(bf16[2,3,8,128,128]{4,3,2,1,0:T(8,128)(2,1)S(1)} %pad_maximum_fusion.1), channel_id=1, source_target_pairs={{0,1},{1,0},{2,3},{3,2},{4,5},{5,4},{6,7},{7,6},{8,9},{9,8},{10,11... | collective-permute-start | bytes 4718600 | tf_op jit(solution)/shard_map/ppermute | solution.py:33
  58.3 22.8 %collective-permute-start.7 = (bf16[2,2,8,128,128]{4,3,2,1,0:T(8,128)(2,1)}, bf16[2,2,8,128,128]{4,3,2,1,0:T(8,128)(2,1)S(1)}, u32[]{:S(2)}, u32[]{:S(2)}) collective-permute-start(bf16[2,2,8,128,128]{4,3,2,1,0:T(8,128)(2,1)} %collective-permute-done.3.refs_3_.refs_5_), channel_id=1, source_target_pairs={{0,6},{1,7},{2,0},{3,1},{4,2},{5,3},{6,4},{7,5},{8,14},{9,15},{10,... | collective-permute-start | bytes 3145736 | tf_op jit(solution)/shard_map/ppermute | solution.py:33
  60.7 23.4 %collective-permute-start.6 = (bf16[2,2,8,128,128]{4,3,2,1,0:T(8,128)(2,1)}, bf16[2,2,8,128,128]{4,3,2,1,0:T(8,128)(2,1)}, u32[]{:S(2)}, u32[]{:S(2)}) collective-permute-start(bf16[2,2,8,128,128]{4,3,2,1,0:T(8,128)(2,1)} %collective-permute-done.3.refs_3_.refs_5_), channel_id=1, source_target_pairs={{0,2},{1,3},{2,4},{3,5},{4,6},{5,7},{6,0},{7,1},{8,10},{9,11},{10,... | collective-permute-start | bytes 3145736 | tf_op jit(solution)/shard_map/ppermute | solution.py:33
  60.7 37.2 %collective-permute-start.5 = (bf16[3,8,128,128]{3,2,1,0:T(8,128)(2,1)S(1)}, bf16[3,8,128,128]{3,2,1,0:T(8,128)(2,1)S(1)}, u32[]{:S(2)}, u32[]{:S(2)}) collective-permute-start(bf16[3,8,128,128]{3,2,1,0:T(8,128)(2,1)S(1)} %slice_bitcast_fusion), channel_id=1, source_target_pairs={{0,6},{1,7},{2,0},{3,1},{4,2},{5,3},{6,4},{7,5},{8,14},{9,15},{10,... | collective-permute-start | bytes 2359304 | tf_op jit(solution)/shard_map/ppermute | solution.py:33
  63.6 37.4 %collective-permute-start.4 = (bf16[3,8,128,128]{3,2,1,0:T(8,128)(2,1)S(1)}, bf16[3,8,128,128]{3,2,1,0:T(8,128)(2,1)S(1)}, u32[]{:S(2)}, u32[]{:S(2)}) collective-permute-start(bf16[3,8,128,128]{3,2,1,0:T(8,128)(2,1)S(1)} %slice_bitcast_fusion.1), channel_id=1, source_target_pairs={{0,2},{1,3},{2,4},{3,5},{4,6},{5,7},{6,0},{7,1},{8,10},{9,11},{10,... | collective-permute-start | bytes 2359304 | tf_op jit(solution)/shard_map/ppermute | solution.py:33
  81.1 19.9 %copy-start.12 = (bf16[2,2,8,128,128]{4,3,2,1,0:T(8,128)(2,1)}, bf16[2,2,8,128,128]{4,3,2,1,0:T(8,128)(2,1)S(1)}, u32[]{:S(2)}) copy-start(bf16[2,2,8,128,128]{4,3,2,1,0:T(8,128)(2,1)S(1)} %collective-permute-done.7.refs_4_.refs_7_) | copy-start | bytes 3145732
  97.9 3.0 %copy-start.15 = (bf16[3,8,128,128]{3,2,1,0:T(8,128)(2,1)}, bf16[3,8,128,128]{3,2,1,0:T(8,128)(2,1)S(1)}, u32[]{:S(2)}) copy-start(bf16[3,8,128,128]{3,2,1,0:T(8,128)(2,1)S(1)} %collective-permute-done.5.refs_2_.refs_4_) | copy-start | bytes 2359300
  101.0 0.9 copy-start.16
  101.9 23.9 %collective-permute-start.9 = (bf16[64,128,256]{2,1,0:T(8,128)(2,1)}, bf16[64,128,256]{2,1,0:T(8,128)(2,1)S(1)}, u32[]{:S(2)}, u32[]{:S(2)}) collective-permute-start(bf16[64,128,256]{2,1,0:T(8,128)(2,1)} %gate.4.near), channel_id=1, source_target_pairs={{0,8},{1,9},{2,10},{3,11},{4,12},{5,13},{6,14},{7,15},{8,0},{9,1},... | collective-permute-start | bytes 12582920 | tf_op jit(solution)/shard_map/ppermute | solution.py:33
  106.5 22.1 %copy-start.5 = (s32[3,200]{1,0:T(4,128)S(1)}, s32[3,200]{1,0:T(4,128)}, u32[]{:S(2)}) copy-start(s32[3,200]{1,0:T(4,128)} %get-tuple-element.7.refs_4_.order_ref) | copy-start | bytes 7204
  106.5 22.1 %copy-start.6 = (s32[3,100]{1,0:T(4,128)S(1)}, s32[3,100]{1,0:T(4,128)}, u32[]{:S(2)}) copy-start(s32[3,100]{1,0:T(4,128)} %get-tuple-element.8.refs_5_.row_ref) | copy-start | bytes 3604
  106.5 22.1 %copy-start.7 = (s32[3]{0:T(128)S(1)}, s32[3]{0:T(128)}, u32[]{:S(2)}) copy-start(s32[3]{0:T(128)} %get-tuple-element.9.refs_6_.pairs_ref) | copy-start | bytes 40
  106.5 13.7 %collective-permute-start.11 = (bf16[2,8,128,128]{3,2,1,0:T(8,128)(2,1)S(1)}, bf16[2,8,128,128]{3,2,1,0:T(8,128)(2,1)S(1)}, u32[]{:S(2)}, u32[]{:S(2)}) collective-permute-start(bf16[2,8,128,128]{3,2,1,0:T(8,128)(2,1)S(1)} %slice_bitcast_fusion.2), channel_id=1, source_target_pairs={{0,6},{1,7},{2,0},{3,1},{4,2},{5,3},{6,4},{7,5},{8,14},{9,15},{10,... | collective-permute-start | bytes 1572872 | tf_op jit(solution)/shard_map/ppermute | solution.py:33
  108.0 14.6 %collective-permute-start.10 = (bf16[2,8,128,128]{3,2,1,0:T(8,128)(2,1)S(1)}, bf16[2,8,128,128]{3,2,1,0:T(8,128)(2,1)S(1)}, u32[]{:S(2)}, u32[]{:S(2)}) collective-permute-start(bf16[2,8,128,128]{3,2,1,0:T(8,128)(2,1)S(1)} %slice_bitcast_fusion.3), channel_id=1, source_target_pairs={{0,2},{1,3},{2,4},{3,5},{4,6},{5,7},{6,0},{7,1},{8,10},{9,11},{10,... | collective-permute-start | bytes 1572872 | tf_op jit(solution)/shard_map/ppermute | solution.py:33
  111.2 14.5 %collective-permute-start.12 = (bf16[2,1,8,128,128]{4,3,2,1,0:T(8,128)(2,1)S(1)}, bf16[2,1,8,128,128]{4,3,2,1,0:T(8,128)(2,1)S(1)}, u32[]{:S(2)}, u32[]{:S(2)}) collective-permute-start(bf16[2,1,8,128,128]{4,3,2,1,0:T(8,128)(2,1)S(1)} %pad_maximum_fusion.3), channel_id=1, source_target_pairs={{0,1},{1,0},{2,3},{3,2},{4,5},{5,4},{6,7},{7,6},{8,9},{9,8},{10,11... | collective-permute-start | bytes 1572872 | tf_op jit(solution)/shard_map/ppermute | solution.py:33
  120.3 5.5 %copy-start.18 = (bf16[2,8,128,128]{3,2,1,0:T(8,128)(2,1)}, bf16[2,8,128,128]{3,2,1,0:T(8,128)(2,1)S(1)}, u32[]{:S(2)}) copy-start(bf16[2,8,128,128]{3,2,1,0:T(8,128)(2,1)S(1)} %collective-permute-done.11.refs_9_) | copy-start | bytes 1572868
  122.6 3.2 %copy-start.19 = (bf16[2,8,128,128]{3,2,1,0:T(8,128)(2,1)}, bf16[2,8,128,128]{3,2,1,0:T(8,128)(2,1)S(1)}, u32[]{:S(2)}) copy-start(bf16[2,8,128,128]{3,2,1,0:T(8,128)(2,1)S(1)} %collective-permute-done.10.refs_8_) | copy-start | bytes 1572868
  125.7 0.8 copy-start.20
  126.5 2.0 %copy-start.17 = (bf16[64,128,256]{2,1,0:T(8,128)(2,1)}, bf16[64,128,256]{2,1,0:T(8,128)(2,1)S(1)}, u32[]{:S(2)}) copy-start(bf16[64,128,256]{2,1,0:T(8,128)(2,1)S(1)} %collective-permute-done.9.near_other) | copy-start | bytes 12582916
  140.6 1.3 copy-start
  141.9 12.0 %copy-start.1 = (bf16[1024,128]{1,0:T(8,128)(2,1)S(1)}, bf16[1024,128]{1,0:T(8,128)(2,1)}, u32[]{:S(2)}) copy-start(bf16[1024,128]{1,0:T(8,128)(2,1)} %pert_imag.1) | copy-start | bytes 786436
  141.9 12.0 %copy-start.2 = (bf16[1024,128]{1,0:T(8,128)(2,1)S(1)}, bf16[1024,128]{1,0:T(8,128)(2,1)}, u32[]{:S(2)}) copy-start(bf16[1024,128]{1,0:T(8,128)(2,1)} %pert_real.1) | copy-start | bytes 786436
  142.0 12.0 %copy-start.3 = (bf16[1024,128]{1,0:T(8,128)(2,1)S(1)}, bf16[1024,128]{1,0:T(8,128)(2,1)}, u32[]{:S(2)}) copy-start(bf16[1024,128]{1,0:T(8,128)(2,1)} %drive_real.1) | copy-start | bytes 786436
  142.0 12.0 %copy-start.4 = (bf16[1024,128]{1,0:T(8,128)(2,1)S(1)}, bf16[1024,128]{1,0:T(8,128)(2,1)}, u32[]{:S(2)}) copy-start(bf16[1024,128]{1,0:T(8,128)(2,1)} %drive_imag.1) | copy-start | bytes 786436
  142.0 12.0 %collective-permute-start.13 = (bf16[64,128,256]{2,1,0:T(8,128)(2,1)}, bf16[64,128,256]{2,1,0:T(8,128)(2,1)S(1)}, u32[]{:S(2)}, u32[]{:S(2)}) collective-permute-start(bf16[64,128,256]{2,1,0:T(8,128)(2,1)} %gate.5.far), channel_id=1, source_target_pairs={{0,8},{1,9},{2,10},{3,11},{4,12},{5,13},{6,14},{7,15},{8,0},{9,1},... | collective-permute-start | bytes 12582920 | tf_op jit(solution)/shard_map/ppermute | solution.py:33
Sparse Core Ops, SparseCore 0:
  10.4 58.6 all-gather.4
  70.8 53.4 all-gather.2

commit v4 on v3

--- a/solution.py
+++ b/solution.py
@@ -48,12 +48,13 @@
     (2, 1, (2,)),
 )
 STEP = 4
+EARLY = 18
 SKIP = 2**16
 
 
 def list_kernel(place_ref, cols_ref, counts_ref, order_ref, row_ref, pairs_ref):
     rows, slots = cols_ref.shape
-    my_ylo, my_core, my_x, my_yhi = (place_ref[n] for n in range(4))
+    my_ylo, my_z, my_core, my_x, my_yhi = (place_ref[n] for n in range(5))
 
     def one_row(row, ends):
         for which in range(3):
@@ -66,8 +67,17 @@
                 owner = column >> 3
                 far = (owner >> 4) ^ my_ylo
                 other = (owner & 1) ^ my_core
-                which = far * (1 + other)
-                at = ((owner >> 1) & 7) * 8 + (column & 7) + (1 - far) * other * 64
+                ahead = ((owner >> 1) - my_z) & 7
+                turn = jnp.where(ahead < 4, 2 * ahead, 15 - 2 * ahead)
+                last = far & (turn + 2 * other >= 7).astype(jnp.int32)
+                which = 2 * last + (1 - last) * (far | int(place >= EARLY))
+                at = jnp.where(
+                    far == 0,
+                    (owner & 15) * 8,
+                    jnp.where(
+                        last == 1, other * (turn - 4) * 8, 128 + 56 * other + turn * 8
+                    ),
+                ) + (column & 7)
 
                 @pl.when(slot < counts_ref[row])
                 def _(which=which, at=at, place=place):
@@ -84,7 +94,10 @@
             out.append((n + 1) & ~1)
         return tuple(out)
 
-    ends = lax.fori_loop(0, rows, one_row, (0, 0, 0))
+    ends = lax.fori_loop(0, rows // 2, one_row, (0, 0, 0))
+    for which in range(3):
+        pairs_ref[3 + which] = ends[which] >> 1
+    ends = lax.fori_loop(rows // 2, rows, one_row, ends)
     for which in range(3):
         for n in range(2 * STEP):
             order_ref[which, ends[which] + n] = SKIP
@@ -102,13 +115,13 @@
         out_shape=[
             jax.ShapeDtypeStruct((3, most + 2 * STEP), jnp.int32),
             jax.ShapeDtypeStruct((3, most // 2 + STEP), jnp.int32),
-            jax.ShapeDtypeStruct((3,), jnp.int32),
+            jax.ShapeDtypeStruct((6,), jnp.int32),
         ],
         name="make_lists",
     )(place, cols, counts)
 
 
-def add_products(which, lists, blocks, panel, acc):
+def add_products(which, lists, blocks, panel, acc, first, end):
     order_ref, row_ref, pairs_ref = lists
 
     def one_step(step, carry):
@@ -133,54 +146,81 @@
             acc[row_ref[which, step * STEP + pair]] += term
         return carry
 
-    lax.fori_loop(0, (pairs_ref[which] + STEP - 1) // STEP, one_step, 0)
-
-
-def fetch(pairs, sems):
-    copies = [pltpu.make_async_copy(a, b, sems.at[n]) for n, (a, b) in enumerate(pairs)]
-    for copy in copies:
+    lax.fori_loop(first, end, one_step, 0)
+
+
+def all_steps(which, lists):
+    return (lists[2][which] + STEP - 1) // STEP
+
+
+def run(which, lists, panel_parts, pieces, panel, blocks, acc, before, sems):
+    half = blocks.shape[2] // 2
+    early, at = [], 0
+    for part in panel_parts:
+        early.append((part, panel.at[pl.ds(at, part.shape[0])]))
+        at += part.shape[0]
+    if before is not None:
+        early.append((before, acc))
+    rounds = [early + split_pieces(pieces, blocks, 0, half), split_pieces(pieces, blocks, half, half)]
+    copies, used = [], 0
+    for pairs in rounds:
+        copies.append([pltpu.make_async_copy(a, b, sems.at[used + n]) for n, (a, b) in enumerate(pairs)])
+        used += len(pairs)
+    for copy in copies[0] + copies[1]:
         copy.start()
-    for copy in copies:
+    if before is None:
+        acc[...] = jnp.zeros_like(acc)
+    for copy in copies[0]:
         copy.wait()
-
-
-def split_pieces(pieces, blocks):
+    middle = lists[2][3 + which] // STEP
+    add_products(which, lists, blocks, panel, acc, 0, middle)
+    for copy in copies[1]:
+        copy.wait()
+    add_products(which, lists, blocks, panel, acc, middle, all_steps(which, lists))
+
+
+def split_pieces(pieces, blocks, first, rows):
     pairs, at = [], 0
+    lines = pl.ds(first, rows)
     for piece in pieces:
         if isinstance(piece, tuple):
             size = piece[0].shape[0]
-            pairs += [(piece[n], blocks.at[n, pl.ds(at, size)]) for n in range(2)]
+            pairs += [(piece[n].at[:, lines], blocks.at[n, pl.ds(at, size), lines]) for n in range(2)]
         else:
             size = piece.shape[1]
-            pairs.append((piece, blocks.at[:, pl.ds(at, size)]))
+            pairs.append((piece.at[:, :, lines], blocks.at[:, pl.ds(at, size), lines]))
         at += size
     return pairs
 
 
 def group_pieces(refs):
-    return [*refs[:3], (refs[3], refs[4]), *refs[5:8], (refs[8], refs[9]), *refs[10:12]]
-
-
-def near_kernel(order_ref, row_ref, pairs_ref, near, near_other, *refs):
-    pieces, (acc, blocks, panel, sems) = refs[:12], refs[12:]
-    count = near.shape[0]
-    pairs = [(ref, panel.at[pl.ds(n * count, count)]) for n, ref in enumerate((near, near_other))]
-    fetch(pairs + split_pieces(group_pieces(pieces), blocks), sems)
-    acc[...] = jnp.zeros_like(acc)
-    add_products(0, (order_ref, row_ref, pairs_ref), blocks, panel, acc)
-
-
-def far_kernel(order_ref, row_ref, pairs_ref, far, before, *refs):
-    pieces, (blocks, acc, panel, sems) = refs[:12], refs[12:]
-    fetch([(far, panel), (before, acc)] + split_pieces(group_pieces(pieces), blocks), sems)
-    add_products(1, (order_ref, row_ref, pairs_ref), blocks, panel, acc)
+    out = [*refs[:3], (refs[3], refs[4]), *refs[5:8]]
+    if len(refs) > 8:
+        out += [(refs[8], refs[9]), *refs[10:12]]
+    return out
+
+
+def early_kernel(order_ref, row_ref, pairs_ref, near, *refs):
+    pieces, (acc, blocks, panel, sems) = refs[:8], refs[8:]
+    lists = (order_ref, row_ref, pairs_ref)
+    run(0, lists, [near], group_pieces(pieces), panel, blocks, acc, None, sems)
+
+
+def main_kernel(order_ref, row_ref, pairs_ref, *refs):
+    parts, before, pieces = refs[:9], refs[9], refs[10:22]
+    blocks, acc, panel, sems = refs[22:]
+    lists = (order_ref, row_ref, pairs_ref)
+    run(1, lists, parts, group_pieces(pieces), panel, blocks, acc, before, sems)
 
 
 def last_kernel(
     order_ref,
     row_ref,
     pairs_ref,
-    panel,
+    end_up,
+    end_down,
+    other_third,
+    other_end,
     blocks,
     before,
     pert_real,
@@ -190,9 +230,20 @@
     new_real,
     new_imag,
     acc,
+    panel,
+    sems,
 ):
+    copies, at = [], 0
+    for n, part in enumerate((end_up, end_down, other_third, other_end)):
+        copies.append(pltpu.make_async_copy(part, panel.at[pl.ds(at, part.shape[0])], sems.at[n]))
+        at += part.shape[0]
+    for copy in copies:
+        copy.start()
     acc[...] = before[...]
-    add_products(2, (order_ref, row_ref, pairs_ref), blocks, panel, acc)
+    for copy in copies:
+        copy.wait()
+    lists = (order_ref, row_ref, pairs_ref)
+    add_products(2, lists, blocks, panel, acc, 0, all_steps(2, lists))
 
     def one_row(row, carry):
         total = acc[row]
@@ -245,56 +296,59 @@
     return pl.CostEstimate(flops=0, bytes_accessed=int(micros * 3.0e6), transcendentals=0)
 
 
-def near_products(lists, rows, near, near_other, pieces):
-    count = near.shape[0]
+def early_products(lists, rows, near, pieces):
     return pl.pallas_call(
-        near_kernel,
-        in_specs=[SMEM] * 3 + [ANY] * (2 + len(pieces)),
+        early_kernel,
+        in_specs=[SMEM] * 3 + [ANY] * (1 + len(pieces)),
         out_specs=VMEM,
         out_shape=jax.ShapeDtypeStruct((rows, 2 * BLOCK, 2 * BLOCK), jnp.float32),
         scratch_shapes=[
-            pltpu.VMEM((2, 24, rows, BLOCK, BLOCK), jnp.bfloat16),
-            pltpu.VMEM((2 * count, BLOCK, 2 * BLOCK), jnp.bfloat16),
-            pltpu.SemaphoreType.DMA((2 + len(pieces),)),
+            pltpu.VMEM((2, EARLY, rows, BLOCK, BLOCK), jnp.bfloat16),
+            pltpu.VMEM(near.shape, jnp.bfloat16),
+            pltpu.SemaphoreType.DMA((1 + 2 * len(pieces),)),
         ],
-        compiler_params=pltpu.CompilerParams(vmem_limit_bytes=30 * 2**20),
+        compiler_params=pltpu.CompilerParams(vmem_limit_bytes=24 * 2**20),
         cost_estimate=cost(10),
-        name="products_near",
-    )(*lists, in_hbm(near), in_hbm(near_other), *map(in_hbm, pieces))
-
-
-def far_products(lists, far, before, pieces):
+        name="products_early",
+    )(*lists, in_hbm(near), *map(in_hbm, pieces))
+
+
+def main_products(lists, parts, before, pieces):
     rows = before.shape[0]
     return pl.pallas_call(
-        far_kernel,
-        in_specs=[SMEM] * 3 + [ANY] * (2 + len(pieces)),
+        main_kernel,
+        in_specs=[SMEM] * 3 + [ANY] * (len(parts) + 1 + len(pieces)),
         out_specs=[VMEM, VMEM],
         out_shape=[
             pltpu.VMEM((2, 24, rows, BLOCK, BLOCK), jnp.bfloat16),
             pltpu.VMEM(before.shape, jnp.float32),
         ],
         scratch_shapes=[
-            pltpu.VMEM(far.shape, jnp.bfloat16),
-            pltpu.SemaphoreType.DMA((2 + len(pieces),)),
+            pltpu.VMEM((sum(a.shape[0] for a in parts), BLOCK, 2 * BLOCK), jnp.bfloat16),
+            pltpu.SemaphoreType.DMA((len(parts) + 1 + 2 * len(pieces),)),
         ],
-        compiler_params=pltpu.CompilerParams(vmem_limit_bytes=7 * 2**20),
-        cost_estimate=cost(8),
-        name="products_far",
-    )(*lists, in_hbm(far), in_hbm(before), *map(in_hbm, pieces))
-
-
-def last_products(lists, far_other, blocks, before, *flat):
+        compiler_params=pltpu.CompilerParams(vmem_limit_bytes=17 * 2**20),
+        cost_estimate=cost(10),
+        name="products_main",
+    )(*lists, *map(in_hbm, parts), in_hbm(before), *map(in_hbm, pieces))
+
+
+def last_products(lists, parts, blocks, before, *flat):
     rows = before.shape[0]
     return pl.pallas_call(
         last_kernel,
-        in_specs=[SMEM] * 3 + [VMEM] * 7,
+        in_specs=[SMEM] * 3 + [ANY] * 4 + [VMEM] * 6,
         out_specs=[VMEM] * 2,
         out_shape=[jax.ShapeDtypeStruct((rows * BLOCK, BLOCK), jnp.float32)] * 2,
-        scratch_shapes=[pltpu.VMEM(before.shape, jnp.float32)],
-        compiler_params=pltpu.CompilerParams(vmem_limit_bytes=7 * 2**20),
+        scratch_shapes=[
+            pltpu.VMEM(before.shape, jnp.float32),
+            pltpu.VMEM((sum(a.shape[0] for a in parts), BLOCK, 2 * BLOCK), jnp.bfloat16),
+            pltpu.SemaphoreType.DMA((4,)),
+        ],
+        compiler_params=pltpu.CompilerParams(vmem_limit_bytes=9 * 2**20),
         cost_estimate=cost(4),
         name="products_last",
-    )(*lists, held(far_other), held(blocks), held(before), *flat)
+    )(*lists, *parts, held(blocks), held(before), *flat)
 
 
 def per_device(
@@ -308,53 +362,67 @@
     drive_imag,
 ):
     rows = block_cols.shape[0]
-    place = jnp.stack([lax.axis_index(a) for a in ("ylo", "core", "x", "yhi")]).astype(jnp.int32)
+    place = jnp.stack([lax.axis_index(a) for a in ("ylo", "z", "core", "x", "yhi")]).astype(jnp.int32)
 
     both = jnp.stack([ham_blocks.swapaxes(0, 1), margin_blocks.swapaxes(0, 1)], axis=0)
     panel = jnp.concatenate([pert_real, pert_imag], axis=1).reshape(rows, BLOCK, 2 * BLOCK)
 
+    near = lax.all_gather(panel, ("z", "core"), axis=0, tiled=True)
     from_left = shift(both, "x", 1)
     from_right = shift(both, "x", -1)
     part = shift(both[:, :2], "yhi")
-    near = lax.all_gather(panel, "z", axis=0, tiled=True)
+    neighbour = shift(panel, "ylo")
     lists = make_lists(place, block_cols, block_counts)
-    neighbour = shift(panel, "ylo")
-
-    far = lax.all_gather(after(neighbour, from_left, from_right, part, *lists), "z", axis=0, tiled=True)
+    up1, down1 = shift(neighbour, "z", 1), shift(neighbour, "z", -1)
+
     far_ham = shift(from_left[0], "x", 1)
     far_margin = shift(from_right[1], "x", -1)
+    late = shift(
+        after(jnp.concatenate([both[:, 2:], from_left[:, 2:], from_right[:, 2:]], axis=1), part),
+        "yhi",
+    )
+    up2, down2 = shift(up1, "z", 1), shift(down1, "z", -1)
+
+    part = after(part, far_ham, far_margin, lists[0])
     part_left = shift(part, "x", 1)
     part_right = shift(part, "x", -1)
-    late = shift(
-        jnp.concatenate([both[:, 2:], from_left[:, 2:], from_right[:, 2:]], axis=1), "yhi"
+    up3, down3 = shift(up2, "z", 1), shift(down2, "z", -1)
+    late_far = shift(
+        after(jnp.stack([far_ham[2:], far_margin[2:]], axis=0), late, part_left, part_right), "yhi"
     )
-
-    near = after(near, far_ham, far_margin, part_left, part_right, late)
-    near_other = shift(near, "core")
-    late_far = shift(jnp.stack([far_ham[2:], far_margin[2:]], axis=0), "yhi")
     part_far_ham = shift(part_left[0], "x", 1)
     part_far_margin = shift(part_right[1], "x", -1)
-
-    pieces = (
-        both,
-        from_left,
-        from_right,
-        far_ham,
-        far_margin,
-        part,
-        part_left,
-        part_right,
-        part_far_ham,
-        part_far_margin,
-        late,
-        late_far,
+    up4, down4 = shift(up3[: rows // 2], "z", 1), shift(down3[rows // 2 :], "z", -1)
+
+    early = (both, from_left, from_right, far_ham, far_margin, part, part_left, part_right)
+    acc = early_products(lists, rows, near, early)
+    other_first = shift(
+        after(
+            jnp.concatenate([neighbour, up1, down1, up2, down2], axis=0),
+            up3,
+            down3,
+            late_far,
+            part_far_ham,
+            part_far_margin,
+            acc,
+        ),
+        "core",
     )
-    acc = near_products(lists, rows, near, near_other, pieces)
-    far = after(far, acc)
-    far_other = shift(far, "core")
-    blocks, acc = far_products(lists, far, acc, pieces)
+    other_third = shift(jnp.concatenate([up3, down3], axis=0), "core")
+    other_end = shift(jnp.concatenate([up4, down4], axis=0), "core")
+
+    pieces = early + (part_far_ham, part_far_margin, late, late_far)
+    parts = (near, neighbour, up1, down1, up2, down2, up3, down3, other_first)
+    blocks, acc = main_products(lists, parts, acc, pieces)
     new_real, new_imag = last_products(
-        lists, far_other, blocks, acc, pert_real, pert_imag, drive_real, drive_imag
+        lists,
+        (up4, down4, other_third, other_end),
+        blocks,
+        acc,
+        pert_real,
+        pert_imag,
+        drive_real,
+        drive_imag,
     )
     return new_real, new_imag
 

time: 165 us -> 183 us (1.11)
  starting transfers between devices: 22.6 us -> 40.9 us
  waiting for transfers between devices: 79.1 us -> 67 us
  local copies, waits for them, and re-layouts: 12.3 us -> 24 us
    ppermute x14 -> x23, starting transfers between devices: 22.5 us -> 40.9 us  [shift(): return lax.ppermute(array, AXES, moves(axis, by))]
    ppermute x14 -> x23, waiting for transfers between devices: 79.1 us -> 67 us  [shift(): return lax.ppermute(array, AXES, moves(axis, by))]
    unnamed x46 -> x68, local copies, waits for them, and re-layouts: 6.74 us -> 13.5 us
    another operation x3, other arithmetic: 3.62 us -> 0.29 us  [per_device(): jnp.stack([ham_blocks.swapaxes(0, 1), margin_blocks.swapaxes(0, 1)], axis=0)]
    concatenate x0 -> x1, local copies, waits for them, and re-layouts: none -> 1.86 us  [per_device(): jnp.concatenate([neighbour, up1, down1, up2, down2], axis=0)]
  transfers between devices with their start and end apart: 16 -> 24, of which waited for: 8 -> 5; matrix products, arithmetic and copies ran while one was open for 5% -> 10% of each run, Pallas kernels for 16% -> 14%
where the time goes in v4:
time: 183 us; the launch traced here: 182 us
  waiting for transfers between devices  67 us (37%)
  starting transfers between devices  40.9 us (22%)
  Pallas kernels  29.9 us (16%)
  local copies, waits for them, and re-layouts  24 us (13%)
  between operations  14.5 us (8%)
  other arithmetic  5.81 us (3%)
    ppermute x23, waiting for transfers between devices, shift(): return lax.ppermute(array, AXES, moves(axis, by))  67 us
    ppermute x23, starting transfers between devices, shift(): return lax.ppermute(array, AXES, moves(axis, by))  40.9 us
    unnamed x68, local copies, waits for them, and re-layouts  13.5 us
    pallas_call x1, Pallas kernels, main_products(): pl.pallas_call(main_kernel, in_specs=[SMEM] * 3 + [ANY] * (len(parts) + 1...  11.9 us
    pallas_call x1, Pallas kernels, early_products(): pl.pallas_call(early_kernel, in_specs=[SMEM] * 3 + [ANY] * (1 + len(piece...  8.92 us
    pallas_call x1, Pallas kernels, make_lists(): pl.pallas_call(list_kernel, in_specs=[SMEM] * 3, out_specs=[SMEM] * 3, ou...  5.53 us
  transfers between devices with their start and end apart: 24, of which 5 were waited for; matrix products, arithmetic and copies ran while one was open for 10% of the time, Pallas kernels for 14%

profile of v4, /device:TPU:1, one launch (start us, length us, event | category | flops | bytes accessed | tf_op | source)
XLA Modules:
  0.0 182.1 jit_solution(17643537422336038291)
XLA Ops:
  7.2 0.0 all-gather.2.cloned.1.call-start
  7.2 2.0 %pad_maximum_fusion.3 = bf16[1024,256]{1,0:T(8,128)(2,1)} fusion(bf16[1024,128]{1,0:T(8,128)(2,1)} %pert_imag.1, bf16[1024,128]{1,0:T(8,128)(2,1)} %pert_real.1), kind=kLoop, calls=%fused_computation.15 | loop fusion | flops 1048576 | bytes 1048576 | tf_op jit(solution)/shard_map/concatenate | solution.py:368
  9.2 0.0 all-gather.2.cloned.1.call-update
  9.3 0.2 copy_bitcast_fusion
  9.4 0.1 pad_maximum_fusion.refs_0_.refs_10_
  9.6 2.1 %collective-permute-start.11 = (bf16[2,3,8,128,128]{4,3,2,1,0:T(8,128)(2,1)S(1)}, bf16[2,3,8,128,128]{4,3,2,1,0:T(8,128)(2,1)S(1)}, u32[]{:S(2)}, u32[]{:S(2)}) collective-permute-start(bf16[2,3,8,128,128]{4,3,2,1,0:T(8,128)(2,1)S(1)} %pad_maximum_fusion.refs_0_.refs_10_), channel_id=1, source_target_pairs={{0,2},{1,3},{2,4},{3,5},{4,6},{5,7},{6,0},{7,1},{8,10},{9,11},{10,... | collective-permute-start | bytes 4718600 | tf_op jit(solution)/shard_map/ppermute | solution.py:33
  11.7 1.4 collective-permute-start.13
  13.1 0.1 fusion
  13.2 3.1 %collective-permute-start.15 = (bf16[2,2,8,128,128]{4,3,2,1,0:T(8,128)(2,1)S(1)}, bf16[2,2,8,128,128]{4,3,2,1,0:T(8,128)(2,1)S(1)}, u32[]{:S(2)}, u32[]{:S(2)}) collective-permute-start(bf16[2,2,8,128,128]{4,3,2,1,0:T(8,128)(2,1)S(1)} %fusion), channel_id=1, source_target_pairs={{0,1},{1,0},{2,3},{3,2},{4,5},{5,4},{6,7},{7,6},{8,9},{9,8},{10,11... | collective-permute-start | bytes 3145736 | tf_op jit(solution)/shard_map/ppermute | solution.py:33
  16.3 0.4 collective-permute-start
  16.7 28.2 %collective-permute-done.11.refs_1_.refs_11_ = bf16[2,3,8,128,128]{4,3,2,1,0:T(8,128)(2,1)S(1)} collective-permute-done((bf16[2,3,8,128,128]{4,3,2,1,0:T(8,128)(2,1)S(1)}, bf16[2,3,8,128,128]{4,3,2,1,0:T(8,128)(2,1)S(1)}, u32[]{:S(2)}, u32[]{:S(2)}) %collective-permute-start.11) | collective-permute-done | bytes 1572896 | tf_op jit(solution)/shard_map/ppermute | solution.py:33
  44.9 1.0 slice_bitcast_fusion.1
  45.9 1.9 %collective-permute-start.12 = (bf16[3,8,128,128]{3,2,1,0:T(8,128)(2,1)}, bf16[3,8,128,128]{3,2,1,0:T(8,128)(2,1)S(1)}, u32[]{:S(2)}, u32[]{:S(2)}) collective-permute-start(bf16[3,8,128,128]{3,2,1,0:T(8,128)(2,1)} %slice_bitcast_fusion.1), channel_id=1, source_target_pairs={{0,2},{1,3},{2,4},{3,5},{4,6},{5,7},{6,0},{7,1},{8,10},{9,11},{10,... | collective-permute-start | bytes 2359304 | tf_op jit(solution)/shard_map/ppermute | solution.py:33
  47.8 1.0 slice_bitcast_fusion
  48.8 1.6 collective-permute-start.14
  50.4 0.1 fusion.1
  50.5 3.0 %collective-permute-start.1 = (bf16[8,128,256]{2,1,0:T(8,128)(2,1)S(1)}, bf16[8,128,256]{2,1,0:T(8,128)(2,1)S(1)}, u32[]{:S(2)}, u32[]{:S(2)}) collective-permute-start(bf16[8,128,256]{2,1,0:T(8,128)(2,1)S(1)} %collective-permute-done.refs_1_), channel_id=1, source_target_pairs={{0,16},{1,17},{2,18},{3,19},{4,20},{5,21},{6,22},{7,23},{8,24},{9,... | collective-permute-start | bytes 1572872 | tf_op jit(solution)/shard_map/ppermute | solution.py:33
  53.5 4.1 %collective-permute-start.5 = (bf16[8,128,256]{2,1,0:T(8,128)(2,1)S(1)}, bf16[8,128,256]{2,1,0:T(8,128)(2,1)S(1)}, u32[]{:S(2)}, u32[]{:S(2)}) collective-permute-start(bf16[8,128,256]{2,1,0:T(8,128)(2,1)S(1)} %collective-permute-done.refs_1_), channel_id=1, source_target_pairs={{0,112},{1,113},{2,114},{3,115},{4,116},{5,117},{6,118},{7,119},{8... | collective-permute-start | bytes 1572872 | tf_op jit(solution)/shard_map/ppermute | solution.py:33
  57.7 1.3 pad_maximum_fusion.1.refs_0_
  59.0 1.0 copy-done.8
  60.0 2.8 %collective-permute-start.16 = (bf16[2,3,8,128,128]{4,3,2,1,0:T(8,128)(2,1)}, bf16[2,3,8,128,128]{4,3,2,1,0:T(8,128)(2,1)}, u32[]{:S(2)}, u32[]{:S(2)}) collective-permute-start(bf16[2,3,8,128,128]{4,3,2,1,0:T(8,128)(2,1)} %gate.4), channel_id=1, source_target_pairs={{0,1},{1,0},{2,3},{3,2},{4,5},{5,4},{6,7},{7,6},{8,9},{9,8},{10,11... | collective-permute-start | bytes 4718600 | tf_op jit(solution)/shard_map/ppermute | solution.py:33
  62.8 16.5 %collective-permute-done.1.refs_2_ = bf16[8,128,256]{2,1,0:T(8,128)(2,1)S(1)} collective-permute-done((bf16[8,128,256]{2,1,0:T(8,128)(2,1)S(1)}, bf16[8,128,256]{2,1,0:T(8,128)(2,1)S(1)}, u32[]{:S(2)}, u32[]{:S(2)}) %collective-permute-start.1) | collective-permute-done | bytes 524320 | tf_op jit(solution)/shard_map/ppermute | solution.py:33
  79.4 2.7 %collective-permute-start.6 = (bf16[8,128,256]{2,1,0:T(8,128)(2,1)S(1)}, bf16[8,128,256]{2,1,0:T(8,128)(2,1)}, u32[]{:S(2)}, u32[]{:S(2)}) collective-permute-start(bf16[8,128,256]{2,1,0:T(8,128)(2,1)S(1)} %collective-permute-done.5.refs_3_), channel_id=1, source_target_pairs={{0,112},{1,113},{2,114},{3,115},{4,116},{5,117},{6,118},{7,119},{8... | collective-permute-start | bytes 1572872 | tf_op jit(solution)/shard_map/ppermute | solution.py:33
  82.0 0.6 stack.41.place_ref
  82.6 5.5 %make_lists.1 = (s32[3,200]{1,0:T(4,128)}, s32[3,100]{1,0:T(4,128)}, s32[6]{0:T(128)}) custom-call(s32[5]{0:T(128)} %stack.41.place_ref, s32[8,24]{1,0:T(8,128)} %cols_ref.1, s32[8]{0:T(128)} %counts_ref.1), custom_call_target="tpu_custom_call" | custom-call | tf_op jit(solution)/shard_map/make_lists/pallas_call | solution.py:111
  88.2 0.9 copy-done.14
  89.1 0.3 copy-done.15
  89.4 0.1 collective-permute-start.17
  89.4 2.6 %collective-permute-start.18 = (bf16[2,2,8,128,128]{4,3,2,1,0:T(8,128)(2,1)}, bf16[2,2,8,128,128]{4,3,2,1,0:T(8,128)(2,1)S(1)}, u32[]{:S(2)}, u32[]{:S(2)}) collective-permute-start(bf16[2,2,8,128,128]{4,3,2,1,0:T(8,128)(2,1)} %gate.5.refs_5_.refs_15_), channel_id=1, source_target_pairs={{0,6},{1,7},{2,0},{3,1},{4,2},{5,3},{6,4},{7,5},{8,14},{9,15},{10,... | collective-permute-start | bytes 3145736 | tf_op jit(solution)/shard_map/ppermute | solution.py:33
  92.0 1.0 collective-permute-done.2.refs_4_
  93.1 2.7 %collective-permute-start.7 = (bf16[8,128,256]{2,1,0:T(8,128)(2,1)}, bf16[8,128,256]{2,1,0:T(8,128)(2,1)S(1)}, u32[]{:S(2)}, u32[]{:S(2)}) collective-permute-start(bf16[8,128,256]{2,1,0:T(8,128)(2,1)} %collective-permute-done.6.refs_5_), channel_id=1, source_target_pairs={{0,112},{1,113},{2,114},{3,115},{4,116},{5,117},{6,118},{7,119},{8... | collective-permute-start | bytes 1572872 | tf_op jit(solution)/shard_map/ppermute | solution.py:33
  95.7 1.0 slice_bitcast_fusion.4
  96.7 1.0 slice_bitcast_fusion.5
  97.7 0.9 pad_maximum_fusion.5.refs_0_
  98.5 15.3 %collective-permute-done.17.refs_2_.refs_6_.refs_16_ = bf16[2,2,8,128,128]{4,3,2,1,0:T(8,128)(2,1)S(1)} collective-permute-done((bf16[2,2,8,128,128]{4,3,2,1,0:T(8,128)(2,1)}, bf16[2,2,8,128,128]{4,3,2,1,0:T(8,128)(2,1)S(1)}, u32[]{:S(2)}, u32[]{:S(2)}) %collective-permute-start.17) | collective-permute-done | bytes 1048608 | tf_op jit(solution)/shard_map/ppermute | solution.py:33
  113.9 1.0 copy-done.10
  114.8 1.0 copy-done.11
  115.9 2.4 %collective-permute-start.19 = (bf16[2,1,8,128,128]{4,3,2,1,0:T(8,128)(2,1)}, bf16[2,1,8,128,128]{4,3,2,1,0:T(8,128)(2,1)S(1)}, u32[]{:S(2)}, u32[]{:S(2)}) collective-permute-start(bf16[2,1,8,128,128]{4,3,2,1,0:T(8,128)(2,1)} %gate.6), channel_id=1, source_target_pairs={{0,1},{1,0},{2,3},{3,2},{4,5},{5,4},{6,7},{7,6},{8,9},{9,8},{10,11... | collective-permute-start | bytes 1572872 | tf_op jit(solution)/shard_map/ppermute | solution.py:33
  118.3 1.9 %slice_bitcast_fusion.3 = bf16[2,8,128,128]{3,2,1,0:T(8,128)(2,1)} fusion(bf16[2,2,8,128,128]{4,3,2,1,0:T(8,128)(2,1)} %copy-done.10), kind=kLoop, calls=%fused_computation.14 | loop fusion | bytes 1048576 | tf_op jit(solution)/shard_map/squeeze | solution.py:393
  120.2 1.9 %slice_bitcast_fusion.2 = bf16[2,8,128,128]{3,2,1,0:T(8,128)(2,1)} fusion(bf16[2,2,8,128,128]{4,3,2,1,0:T(8,128)(2,1)} %copy-done.11), kind=kLoop, calls=%fused_computation.13 | loop fusion | bytes 1048576 | tf_op jit(solution)/shard_map/squeeze | solution.py:394
  122.1 2.6 %collective-permute-start.21 = (bf16[2,8,128,128]{3,2,1,0:T(8,128)(2,1)}, bf16[2,8,128,128]{3,2,1,0:T(8,128)(2,1)S(1)}, u32[]{:S(2)}, u32[]{:S(2)}) collective-permute-start(bf16[2,8,128,128]{3,2,1,0:T(8,128)(2,1)} %slice_bitcast_fusion.2), channel_id=1, source_target_pairs={{0,6},{1,7},{2,0},{3,1},{4,2},{5,3},{6,4},{7,5},{8,14},{9,15},{10,... | collective-permute-start | bytes 1572872 | tf_op jit(solution)/shard_map/ppermute | solution.py:33
  124.8 0.8 constant_dynamic-update-slice_fusion.4
  125.6 0.8 constant_dynamic-update-slice_fusion.3
  126.4 0.9 constant_dynamic-update-slice_fusion.2
  127.3 1.9 %constant_dynamic-update-slice_fusion.1 = bf16[40,128,256]{2,1,0:T(8,128)(2,1)} fusion(bf16[40,128,256]{2,1,0:T(8,128)(2,1)} %constant_dynamic-update-slice_fusion.2, bf16[8,128,256]{2,1,0:T(8,128)(2,1)} %collective-permute-done.2.refs_4_), kind=kLoop, calls=%fused_computation.21 | loop fusion | bytes 1048576
  129.2 1.9 %constant_dynamic-update-slice_fusion.refs_0_ = bf16[40,128,256]{2,1,0:T(8,128)(2,1)} fusion(bf16[40,128,256]{2,1,0:T(8,128)(2,1)} %constant_dynamic-update-slice_fusion.1, bf16[8,128,256]{2,1,0:T(8,128)(2,1)} %collective-permute-done.6.refs_5_), kind=kLoop, calls=%fused_computation.20 | loop fusion | bytes 1048576 | tf_op jit(solution)/shard_map/concatenate | solution.py:401
  131.0 8.9 %products_early.1.refs_6_.refs_9_ = f32[8,256,256]{2,1,0:T(8,128)S(1)} custom-call(s32[3,200]{1,0:T(4,128)S(1)} %copy-done.5, s32[3,100]{1,0:T(4,128)S(1)} %copy-done.6, s32[6]{0:T(128)S(1)} %copy-done.7, bf16[128,128,256]{2,1,0:T(8,128)(2,1)} %all-gather.2.cloned.1.call-done.near.refs_0_, bf16[2,3,8,128,128]{4,3,2,1,0:T(8,128)(2,1)} %copy-done.9, ...), custom_call_target="tpu_custom_call" | custom-call | bytes 30000000 | tf_op jit(solution)/shard_map/products_early/pallas_call | solution.py:300
  140.0 1.4 copy-done
  141.5 0.7 copy-done.16
  142.2 0.2 copy-done.18
  142.4 0.2 copy-done.21
  142.5 0.2 copy-done.22
  142.7 0.8 copy-done.23
  143.5 3.1 %collective-permute-start.22 = (bf16[40,128,256]{2,1,0:T(8,128)(2,1)}, bf16[40,128,256]{2,1,0:T(8,128)(2,1)S(1)}, u32[]{:S(2)}, u32[]{:S(2)}) collective-permute-start(bf16[40,128,256]{2,1,0:T(8,128)(2,1)} %gate.7), channel_id=1, source_target_pairs={{0,8},{1,9},{2,10},{3,11},{4,12},{5,13},{6,14},{7,15},{8,0},{9,1},... | collective-permute-start | bytes 7864328 | tf_op jit(solution)/shard_map/ppermute | solution.py:33
  146.6 1.3 pad_maximum_fusion.2
  147.9 0.2 collective-permute-start.9
  148.1 0.1 collective-permute-start.4
  148.2 2.7 %collective-permute-start.8 = (bf16[4,128,256]{2,1,0:T(8,128)(2,1)S(1)}, bf16[4,128,256]{2,1,0:T(8,128)(2,1)S(1)}, u32[]{:S(2)}, u32[]{:S(2)}) collective-permute-start(bf16[4,128,256]{2,1,0:T(8,128)(2,1)S(1)} %slice.49), channel_id=1, source_target_pairs={{0,112},{1,113},{2,114},{3,115},{4,116},{5,117},{6,118},{7,119},{8... | collective-permute-start | bytes 786440 | tf_op jit(solution)/shard_map/ppermute | solution.py:33
  150.9 5.9 %collective-permute-done.4.end_up = bf16[4,128,256]{2,1,0:T(8,128)(2,1)S(1)} collective-permute-done((bf16[4,128,256]{2,1,0:T(8,128)(2,1)S(1)}, bf16[4,128,256]{2,1,0:T(8,128)(2,1)S(1)}, u32[]{:S(2)}, u32[]{:S(2)}) %collective-permute-start.4) | collective-permute-done | bytes 262176 | tf_op jit(solution)/shard_map/ppermute | solution.py:33
  156.9 0.0 copy-start.1
  156.9 1.3 collective-permute-start.10
  158.3 1.5 copy-done.20
  159.8 11.9 %products_main.1 = (bf16[2,24,8,128,128]{4,3,2,1,0:T(8,128)(2,1)S(1)}, f32[8,256,256]{2,1,0:T(8,128)S(1)}) custom-call(s32[3,200]{1,0:T(4,128)S(1)} %copy-done.5, s32[3,100]{1,0:T(4,128)S(1)} %copy-done.6, s32[6]{0:T(128)S(1)} %copy-done.7, bf16[128,128,256]{2,1,0:T(8,128)(2,1)} %all-gather.2.cloned.1.call-done.near.refs_0_, ...), custom_call_target="tpu_custom_call" | custom-call | bytes 30000000 | tf_op jit(solution)/shard_map/products_main/pallas_call | solution.py:318
  171.7 3.5 %products_last.1 = (f32[1024,128]{1,0:T(8,128)}, f32[1024,128]{1,0:T(8,128)}) custom-call(s32[3,200]{1,0:T(4,128)S(1)} %copy-done.5, s32[3,100]{1,0:T(4,128)S(1)} %copy-done.6, s32[6]{0:T(128)S(1)} %copy-done.7, bf16[4,128,256]{2,1,0:T(8,128)(2,1)S(1)} %collective-permute-done.4.end_up, bf16[4,128,256]{2,1,0:T(8,128)(2,1)S(1)} %collective-permute-done.8.end_down, ...), custom_call_target="tpu_custom_call" | custom-call | bytes 12000000 | tf_op jit(solution)/shard_map/products_last/pallas_call | solution.py:338
  (82 shorter events, 0.3 us)
Async XLA Ops:
  7.2 2.1 %copy-start.31 = (bf16[8,3,128,128]{3,2,1,0:T(8,128)(2,1)S(1)}, bf16[8,3,128,128]{3,2,1,0:T(8,128)(2,1)}, u32[]{:S(2)}) copy-start(bf16[8,3,128,128]{3,2,1,0:T(8,128)(2,1)} %param.8) | copy-start | bytes 2359300
  7.2 2.1 %copy-start.30 = (bf16[8,3,128,128]{3,2,1,0:T(8,128)(2,1)S(1)}, bf16[8,3,128,128]{3,2,1,0:T(8,128)(2,1)}, u32[]{:S(2)}) copy-start(bf16[8,3,128,128]{3,2,1,0:T(8,128)(2,1)} %param.9) | copy-start | bytes 2359300
  7.2 123.8 %all-gather.2.cloned.1.call-start = ((), (), s32[]{:S(2)}) async-start(), calls=%async_computation | async-start | bytes 8912896 | tf_op jit(solution)/shard_map/all_gather | solution.py:370
  9.4 6.9 %copy-start.29 = (bf16[1024,256]{1,0:T(8,128)(2,1)S(1)}, bf16[1024,256]{1,0:T(8,128)(2,1)}, u32[]{:S(2)}) copy-start(bf16[1024,256]{1,0:T(8,128)(2,1)} %pad_maximum_fusion.3) | copy-start | bytes 1572868
  9.6 36.3 %copy-start.9 = (bf16[2,3,8,128,128]{4,3,2,1,0:T(8,128)(2,1)}, bf16[2,3,8,128,128]{4,3,2,1,0:T(8,128)(2,1)S(1)}, u32[]{:S(2)}) copy-start(bf16[2,3,8,128,128]{4,3,2,1,0:T(8,128)(2,1)S(1)} %pad_maximum_fusion.refs_0_.refs_10_) | copy-start | bytes 4718596
  9.6 35.3 %collective-permute-start.11 = (bf16[2,3,8,128,128]{4,3,2,1,0:T(8,128)(2,1)S(1)}, bf16[2,3,8,128,128]{4,3,2,1,0:T(8,128)(2,1)S(1)}, u32[]{:S(2)}, u32[]{:S(2)}) collective-permute-start(bf16[2,3,8,128,128]{4,3,2,1,0:T(8,128)(2,1)S(1)} %pad_maximum_fusion.refs_0_.refs_10_), channel_id=1, source_target_pairs={{0,2},{1,3},{2,4},{3,5},{4,6},{5,7},{6,0},{7,1},{8,10},{9,11},{10,... | collective-permute-start | bytes 4718600 | tf_op jit(solution)/shard_map/ppermute | solution.py:33
  11.7 36.1 %collective-permute-start.13 = (bf16[2,3,8,128,128]{4,3,2,1,0:T(8,128)(2,1)S(1)}, bf16[2,3,8,128,128]{4,3,2,1,0:T(8,128)(2,1)S(1)}, u32[]{:S(2)}, u32[]{:S(2)}) collective-permute-start(bf16[2,3,8,128,128]{4,3,2,1,0:T(8,128)(2,1)S(1)} %pad_maximum_fusion.refs_0_.refs_10_), channel_id=1, source_target_pairs={{0,6},{1,7},{2,0},{3,1},{4,2},{5,3},{6,4},{7,5},{8,14},{9,15},{10,... | collective-permute-start | bytes 4718600 | tf_op jit(solution)/shard_map/ppermute | solution.py:33
  13.2 45.9 %collective-permute-start.15 = (bf16[2,2,8,128,128]{4,3,2,1,0:T(8,128)(2,1)S(1)}, bf16[2,2,8,128,128]{4,3,2,1,0:T(8,128)(2,1)S(1)}, u32[]{:S(2)}, u32[]{:S(2)}) collective-permute-start(bf16[2,2,8,128,128]{4,3,2,1,0:T(8,128)(2,1)S(1)} %fusion), channel_id=1, source_target_pairs={{0,1},{1,0},{2,3},{3,2},{4,5},{5,4},{6,7},{7,6},{8,9},{9,8},{10,11... | collective-permute-start | bytes 3145736 | tf_op jit(solution)/shard_map/ppermute | solution.py:33
  16.3 34.2 %collective-permute-start = (bf16[8,128,256]{2,1,0:T(8,128)(2,1)S(1)}, bf16[8,128,256]{2,1,0:T(8,128)(2,1)S(1)}, u32[]{:S(2)}, u32[]{:S(2)}) collective-permute-start(bf16[8,128,256]{2,1,0:T(8,128)(2,1)S(1)} %bitcast.27), channel_id=1, source_target_pairs={{0,128},{1,129},{2,130},{3,131},{4,132},{5,133},{6,134},{7,135},{8... | collective-permute-start | bytes 1572872 | tf_op jit(solution)/shard_map/ppermute | solution.py:33
  44.9 12.7 %copy-start.12 = (bf16[2,3,8,128,128]{4,3,2,1,0:T(8,128)(2,1)}, bf16[2,3,8,128,128]{4,3,2,1,0:T(8,128)(2,1)S(1)}, u32[]{:S(2)}) copy-start(bf16[2,3,8,128,128]{4,3,2,1,0:T(8,128)(2,1)S(1)} %collective-permute-done.11.refs_1_.refs_11_) | copy-start | bytes 4718596
  45.9 42.3 %collective-permute-start.12 = (bf16[3,8,128,128]{3,2,1,0:T(8,128)(2,1)}, bf16[3,8,128,128]{3,2,1,0:T(8,128)(2,1)S(1)}, u32[]{:S(2)}, u32[]{:S(2)}) collective-permute-start(bf16[3,8,128,128]{3,2,1,0:T(8,128)(2,1)} %slice_bitcast_fusion.1), channel_id=1, source_target_pairs={{0,2},{1,3},{2,4},{3,5},{4,6},{5,7},{6,0},{7,1},{8,10},{9,11},{10,... | collective-permute-start | bytes 2359304 | tf_op jit(solution)/shard_map/ppermute | solution.py:33
  47.8 9.8 %copy-start.13 = (bf16[2,3,8,128,128]{4,3,2,1,0:T(8,128)(2,1)}, bf16[2,3,8,128,128]{4,3,2,1,0:T(8,128)(2,1)S(1)}, u32[]{:S(2)}) copy-start(bf16[2,3,8,128,128]{4,3,2,1,0:T(8,128)(2,1)S(1)} %collective-permute-done.13.refs_2_.refs_12_) | copy-start | bytes 4718596
  48.8 39.4 %collective-permute-start.14 = (bf16[3,8,128,128]{3,2,1,0:T(8,128)(2,1)}, bf16[3,8,128,128]{3,2,1,0:T(8,128)(2,1)S(1)}, u32[]{:S(2)}, u32[]{:S(2)}) collective-permute-start(bf16[3,8,128,128]{3,2,1,0:T(8,128)(2,1)} %slice_bitcast_fusion), channel_id=1, source_target_pairs={{0,6},{1,7},{2,0},{3,1},{4,2},{5,3},{6,4},{7,5},{8,14},{9,15},{10,... | collective-permute-start | bytes 2359304 | tf_op jit(solution)/shard_map/ppermute | solution.py:33
  50.5 74.3 %copy-start.24 = (bf16[8,128,256]{2,1,0:T(8,128)(2,1)}, bf16[8,128,256]{2,1,0:T(8,128)(2,1)S(1)}, u32[]{:S(2)}) copy-start(bf16[8,128,256]{2,1,0:T(8,128)(2,1)S(1)} %collective-permute-done.refs_1_) | copy-start | bytes 1572868
  50.5 28.9 %collective-permute-start.1 = (bf16[8,128,256]{2,1,0:T(8,128)(2,1)S(1)}, bf16[8,128,256]{2,1,0:T(8,128)(2,1)S(1)}, u32[]{:S(2)}, u32[]{:S(2)}) collective-permute-start(bf16[8,128,256]{2,1,0:T(8,128)(2,1)S(1)} %collective-permute-done.refs_1_), channel_id=1, source_target_pairs={{0,16},{1,17},{2,18},{3,19},{4,20},{5,21},{6,22},{7,23},{8,24},{9,... | collective-permute-start | bytes 1572872 | tf_op jit(solution)/shard_map/ppermute | solution.py:33
  53.5 25.9 %collective-permute-start.5 = (bf16[8,128,256]{2,1,0:T(8,128)(2,1)S(1)}, bf16[8,128,256]{2,1,0:T(8,128)(2,1)S(1)}, u32[]{:S(2)}, u32[]{:S(2)}) collective-permute-start(bf16[8,128,256]{2,1,0:T(8,128)(2,1)S(1)} %collective-permute-done.refs_1_), channel_id=1, source_target_pairs={{0,112},{1,113},{2,114},{3,115},{4,116},{5,117},{6,118},{7,119},{8... | collective-permute-start | bytes 1572872 | tf_op jit(solution)/shard_map/ppermute | solution.py:33
  59.0 1.0 copy-start.8
  60.0 38.5 %collective-permute-start.16 = (bf16[2,3,8,128,128]{4,3,2,1,0:T(8,128)(2,1)}, bf16[2,3,8,128,128]{4,3,2,1,0:T(8,128)(2,1)}, u32[]{:S(2)}, u32[]{:S(2)}) collective-permute-start(bf16[2,3,8,128,128]{4,3,2,1,0:T(8,128)(2,1)} %gate.4), channel_id=1, source_target_pairs={{0,1},{1,0},{2,3},{3,2},{4,5},{5,4},{6,7},{7,6},{8,9},{9,8},{10,11... | collective-permute-start | bytes 4718600 | tf_op jit(solution)/shard_map/ppermute | solution.py:33
  79.3 34.5 %copy-start.25 = (bf16[8,128,256]{2,1,0:T(8,128)(2,1)}, bf16[8,128,256]{2,1,0:T(8,128)(2,1)S(1)}, u32[]{:S(2)}) copy-start(bf16[8,128,256]{2,1,0:T(8,128)(2,1)S(1)} %collective-permute-done.1.refs_2_) | copy-start | bytes 1572868
  79.3 13.7 %collective-permute-start.2 = (bf16[8,128,256]{2,1,0:T(8,128)(2,1)S(1)}, bf16[8,128,256]{2,1,0:T(8,128)(2,1)}, u32[]{:S(2)}, u32[]{:S(2)}) collective-permute-start(bf16[8,128,256]{2,1,0:T(8,128)(2,1)S(1)} %collective-permute-done.1.refs_2_), channel_id=1, source_target_pairs={{0,16},{1,17},{2,18},{3,19},{4,20},{5,21},{6,22},{7,23},{8,24},{9,... | collective-permute-start | bytes 1572872 | tf_op jit(solution)/shard_map/ppermute | solution.py:33
  79.4 39.0 %copy-start.27 = (bf16[8,128,256]{2,1,0:T(8,128)(2,1)}, bf16[8,128,256]{2,1,0:T(8,128)(2,1)S(1)}, u32[]{:S(2)}) copy-start(bf16[8,128,256]{2,1,0:T(8,128)(2,1)S(1)} %collective-permute-done.5.refs_3_) | copy-start | bytes 1572868
  79.4 13.7 %collective-permute-start.6 = (bf16[8,128,256]{2,1,0:T(8,128)(2,1)S(1)}, bf16[8,128,256]{2,1,0:T(8,128)(2,1)}, u32[]{:S(2)}, u32[]{:S(2)}) collective-permute-start(bf16[8,128,256]{2,1,0:T(8,128)(2,1)S(1)} %collective-permute-done.5.refs_3_), channel_id=1, source_target_pairs={{0,112},{1,113},{2,114},{3,115},{4,116},{5,117},{6,118},{7,119},{8... | collective-permute-start | bytes 1572872 | tf_op jit(solution)/shard_map/ppermute | solution.py:33
  88.2 0.9 copy-start.14
  88.2 1.1 copy-start.15
  89.4 24.5 %collective-permute-start.17 = (bf16[2,2,8,128,128]{4,3,2,1,0:T(8,128)(2,1)}, bf16[2,2,8,128,128]{4,3,2,1,0:T(8,128)(2,1)S(1)}, u32[]{:S(2)}, u32[]{:S(2)}) collective-permute-start(bf16[2,2,8,128,128]{4,3,2,1,0:T(8,128)(2,1)} %gate.5.refs_5_.refs_15_), channel_id=1, source_target_pairs={{0,2},{1,3},{2,4},{3,5},{4,6},{5,7},{6,0},{7,1},{8,10},{9,11},{10,... | collective-permute-start | bytes 3145736 | tf_op jit(solution)/shard_map/ppermute | solution.py:33
  89.4 24.5 %collective-permute-start.18 = (bf16[2,2,8,128,128]{4,3,2,1,0:T(8,128)(2,1)}, bf16[2,2,8,128,128]{4,3,2,1,0:T(8,128)(2,1)S(1)}, u32[]{:S(2)}, u32[]{:S(2)}) collective-permute-start(bf16[2,2,8,128,128]{4,3,2,1,0:T(8,128)(2,1)} %gate.5.refs_5_.refs_15_), channel_id=1, source_target_pairs={{0,6},{1,7},{2,0},{3,1},{4,2},{5,3},{6,4},{7,5},{8,14},{9,15},{10,... | collective-permute-start | bytes 3145736 | tf_op jit(solution)/shard_map/ppermute | solution.py:33
  93.1 48.3 %collective-permute-start.3 = (bf16[8,128,256]{2,1,0:T(8,128)(2,1)}, bf16[8,128,256]{2,1,0:T(8,128)(2,1)S(1)}, u32[]{:S(2)}, u32[]{:S(2)}) collective-permute-start(bf16[8,128,256]{2,1,0:T(8,128)(2,1)} %collective-permute-done.2.refs_4_), channel_id=1, source_target_pairs={{0,16},{1,17},{2,18},{3,19},{4,20},{5,21},{6,22},{7,23},{8,24},{9,... | collective-permute-start | bytes 1572872 | tf_op jit(solution)/shard_map/ppermute | solution.py:33
  93.1 48.3 %collective-permute-start.7 = (bf16[8,128,256]{2,1,0:T(8,128)(2,1)}, bf16[8,128,256]{2,1,0:T(8,128)(2,1)S(1)}, u32[]{:S(2)}, u32[]{:S(2)}) collective-permute-start(bf16[8,128,256]{2,1,0:T(8,128)(2,1)} %collective-permute-done.6.refs_5_), channel_id=1, source_target_pairs={{0,112},{1,113},{2,114},{3,115},{4,116},{5,117},{6,118},{7,119},{8... | collective-permute-start | bytes 1572872 | tf_op jit(solution)/shard_map/ppermute | solution.py:33
  113.9 1.0 copy-start.10
  114.8 1.0 copy-start.11
  115.9 9.7 %copy-start.26 = (bf16[8,128,256]{2,1,0:T(8,128)(2,1)S(1)}, bf16[8,128,256]{2,1,0:T(8,128)(2,1)}, u32[]{:S(2)}) copy-start(bf16[8,128,256]{2,1,0:T(8,128)(2,1)} %copy-done.25) | copy-start | bytes 1572868
  115.9 25.6 %collective-permute-start.19 = (bf16[2,1,8,128,128]{4,3,2,1,0:T(8,128)(2,1)}, bf16[2,1,8,128,128]{4,3,2,1,0:T(8,128)(2,1)S(1)}, u32[]{:S(2)}, u32[]{:S(2)}) collective-permute-start(bf16[2,1,8,128,128]{4,3,2,1,0:T(8,128)(2,1)} %gate.6), channel_id=1, source_target_pairs={{0,1},{1,0},{2,3},{3,2},{4,5},{5,4},{6,7},{7,6},{8,9},{9,8},{10,11... | collective-permute-start | bytes 1572872 | tf_op jit(solution)/shard_map/ppermute | solution.py:33
  120.2 6.2 %copy-start.28 = (bf16[8,128,256]{2,1,0:T(8,128)(2,1)S(1)}, bf16[8,128,256]{2,1,0:T(8,128)(2,1)}, u32[]{:S(2)}) copy-start(bf16[8,128,256]{2,1,0:T(8,128)(2,1)} %copy-done.27) | copy-start | bytes 1572868
  120.2 21.2 %collective-permute-start.20 = (bf16[2,8,128,128]{3,2,1,0:T(8,128)(2,1)}, bf16[2,8,128,128]{3,2,1,0:T(8,128)(2,1)S(1)}, u32[]{:S(2)}, u32[]{:S(2)}) collective-permute-start(bf16[2,8,128,128]{3,2,1,0:T(8,128)(2,1)} %slice_bitcast_fusion.3), channel_id=1, source_target_pairs={{0,2},{1,3},{2,4},{3,5},{4,6},{5,7},{6,0},{7,1},{8,10},{9,11},{10,... | collective-permute-start | bytes 1572872 | tf_op jit(solution)/shard_map/ppermute | solution.py:33
  122.1 19.3 %collective-permute-start.21 = (bf16[2,8,128,128]{3,2,1,0:T(8,128)(2,1)}, bf16[2,8,128,128]{3,2,1,0:T(8,128)(2,1)S(1)}, u32[]{:S(2)}, u32[]{:S(2)}) collective-permute-start(bf16[2,8,128,128]{3,2,1,0:T(8,128)(2,1)} %slice_bitcast_fusion.2), channel_id=1, source_target_pairs={{0,6},{1,7},{2,0},{3,1},{4,2},{5,3},{6,4},{7,5},{8,14},{9,15},{10,... | collective-permute-start | bytes 1572872 | tf_op jit(solution)/shard_map/ppermute | solution.py:33
  125.6 5.4 %copy-start.5 = (s32[3,200]{1,0:T(4,128)S(1)}, s32[3,200]{1,0:T(4,128)}, u32[]{:S(2)}) copy-start(s32[3,200]{1,0:T(4,128)} %get-tuple-element.7.refs_3_.order_ref) | copy-start | bytes 7204
  125.6 5.4 %copy-start.6 = (s32[3,100]{1,0:T(4,128)S(1)}, s32[3,100]{1,0:T(4,128)}, u32[]{:S(2)}) copy-start(s32[3,100]{1,0:T(4,128)} %get-tuple-element.8.row_ref) | copy-start | bytes 3604
  125.6 5.4 %copy-start.7 = (s32[6]{0:T(128)S(1)}, s32[6]{0:T(128)}, u32[]{:S(2)}) copy-start(s32[6]{0:T(128)} %get-tuple-element.9.pairs_ref) | copy-start | bytes 76
  140.0 1.4 copy-start
  141.4 0.8 copy-start.16
  141.4 1.0 copy-start.18
  141.4 1.1 copy-start.21
  141.4 1.3 copy-start.22
  142.7 0.8 copy-start.23
  143.5 4.6 %copy-start.17 = (bf16[8,128,256]{2,1,0:T(8,128)(2,1)S(1)}, bf16[8,128,256]{2,1,0:T(8,128)(2,1)}, u32[]{:S(2)}) copy-start(bf16[8,128,256]{2,1,0:T(8,128)(2,1)} %copy-done.16) | copy-start | bytes 1572868
  143.5 4.7 %copy-start.19 = (bf16[8,128,256]{2,1,0:T(8,128)(2,1)S(1)}, bf16[8,128,256]{2,1,0:T(8,128)(2,1)}, u32[]{:S(2)}) copy-start(bf16[8,128,256]{2,1,0:T(8,128)(2,1)} %copy-done.18) | copy-start | bytes 1572868
  143.5 14.8 %collective-permute-start.22 = (bf16[40,128,256]{2,1,0:T(8,128)(2,1)}, bf16[40,128,256]{2,1,0:T(8,128)(2,1)S(1)}, u32[]{:S(2)}, u32[]{:S(2)}) collective-permute-start(bf16[40,128,256]{2,1,0:T(8,128)(2,1)} %gate.7), channel_id=1, source_target_pairs={{0,8},{1,9},{2,10},{3,11},{4,12},{5,13},{6,14},{7,15},{8,0},{9,1},... | collective-permute-start | bytes 7864328 | tf_op jit(solution)/shard_map/ppermute | solution.py:33
  147.9 23.8 %collective-permute-start.9 = (bf16[16,128,256]{2,1,0:T(8,128)(2,1)S(1)}, bf16[16,128,256]{2,1,0:T(8,128)(2,1)S(1)}, u32[]{:S(2)}, u32[]{:S(2)}) collective-permute-start(bf16[16,128,256]{2,1,0:T(8,128)(2,1)S(1)} %pad_maximum_fusion.2), channel_id=1, source_target_pairs={{0,8},{1,9},{2,10},{3,11},{4,12},{5,13},{6,14},{7,15},{8,0},{9,1},... | collective-permute-start | bytes 3145736 | tf_op jit(solution)/shard_map/ppermute | solution.py:33
  148.1 8.8 %collective-permute-start.4 = (bf16[4,128,256]{2,1,0:T(8,128)(2,1)S(1)}, bf16[4,128,256]{2,1,0:T(8,128)(2,1)S(1)}, u32[]{:S(2)}, u32[]{:S(2)}) collective-permute-start(bf16[4,128,256]{2,1,0:T(8,128)(2,1)S(1)} %slice.48), channel_id=1, source_target_pairs={{0,16},{1,17},{2,18},{3,19},{4,20},{5,21},{6,22},{7,23},{8,24},{9,... | collective-permute-start | bytes 786440 | tf_op jit(solution)/shard_map/ppermute | solution.py:33
  148.2 8.6 %collective-permute-start.8 = (bf16[4,128,256]{2,1,0:T(8,128)(2,1)S(1)}, bf16[4,128,256]{2,1,0:T(8,128)(2,1)S(1)}, u32[]{:S(2)}, u32[]{:S(2)}) collective-permute-start(bf16[4,128,256]{2,1,0:T(8,128)(2,1)S(1)} %slice.49), channel_id=1, source_target_pairs={{0,112},{1,113},{2,114},{3,115},{4,116},{5,117},{6,118},{7,119},{8... | collective-permute-start | bytes 786440 | tf_op jit(solution)/shard_map/ppermute | solution.py:33
  156.9 14.8 %copy-start.1 = (bf16[1024,128]{1,0:T(8,128)(2,1)S(1)}, bf16[1024,128]{1,0:T(8,128)(2,1)}, u32[]{:S(2)}) copy-start(bf16[1024,128]{1,0:T(8,128)(2,1)} %pert_imag.1) | copy-start | bytes 786436
  156.9 14.8 %copy-start.2 = (bf16[1024,128]{1,0:T(8,128)(2,1)S(1)}, bf16[1024,128]{1,0:T(8,128)(2,1)}, u32[]{:S(2)}) copy-start(bf16[1024,128]{1,0:T(8,128)(2,1)} %pert_real.1) | copy-start | bytes 786436
  156.9 14.8 %copy-start.3 = (bf16[1024,128]{1,0:T(8,128)(2,1)S(1)}, bf16[1024,128]{1,0:T(8,128)(2,1)}, u32[]{:S(2)}) copy-start(bf16[1024,128]{1,0:T(8,128)(2,1)} %drive_real.1) | copy-start | bytes 786436
  156.9 14.8 %copy-start.4 = (bf16[1024,128]{1,0:T(8,128)(2,1)S(1)}, bf16[1024,128]{1,0:T(8,128)(2,1)}, u32[]{:S(2)}) copy-start(bf16[1024,128]{1,0:T(8,128)(2,1)} %drive_imag.1) | copy-start | bytes 786436
  156.9 14.7 %collective-permute-start.10 = (bf16[8,128,256]{2,1,0:T(8,128)(2,1)S(1)}, bf16[8,128,256]{2,1,0:T(8,128)(2,1)S(1)}, u32[]{:S(2)}, u32[]{:S(2)}) collective-permute-start(bf16[8,128,256]{2,1,0:T(8,128)(2,1)S(1)} %pad_maximum_fusion.4), channel_id=1, source_target_pairs={{0,8},{1,9},{2,10},{3,11},{4,12},{5,13},{6,14},{7,15},{8,0},{9,1},... | collective-permute-start | bytes 1572872 | tf_op jit(solution)/shard_map/ppermute | solution.py:33
  158.3 1.5 copy-start.20
Sparse Core Ops, SparseCore 0:
  10.4 69.6 all-gather.1

commit v5 on v3

--- a/solution.py
+++ b/solution.py
@@ -48,6 +48,8 @@
     (2, 1, (2,)),
 )
 STEP = 4
+EARLY = 18
+LISTS = 3
 SKIP = 2**16
 
 
@@ -56,7 +58,7 @@
     my_ylo, my_core, my_x, my_yhi = (place_ref[n] for n in range(4))
 
     def one_row(row, ends):
-        for which in range(3):
+        for which in range(LISTS):
             pairs_ref[which] = ends[which]
         place = 0
         for dx, dy, local in PIECES:
@@ -66,8 +68,8 @@
                 owner = column >> 3
                 far = (owner >> 4) ^ my_ylo
                 other = (owner & 1) ^ my_core
-                which = far * (1 + other)
-                at = ((owner >> 1) & 7) * 8 + (column & 7) + (1 - far) * other * 64
+                which = far * (1 + other) + (1 - far) * int(place >= EARLY)
+                at = ((owner >> 1) & 7) * 8 + (column & 7) + (1 - (which >> 1)) * (2 * far + other) * 64
 
                 @pl.when(slot < counts_ref[row])
                 def _(which=which, at=at, place=place):
@@ -78,14 +80,17 @@
 
                 place += 1
         out = []
-        for which in range(3):
+        for which in range(LISTS):
             n = pairs_ref[which]
             order_ref[which, n] = SKIP
             out.append((n + 1) & ~1)
         return tuple(out)
 
-    ends = lax.fori_loop(0, rows, one_row, (0, 0, 0))
-    for which in range(3):
+    ends = lax.fori_loop(0, rows // 2, one_row, (0,) * LISTS)
+    for which in range(LISTS):
+        pairs_ref[LISTS + which] = ends[which] >> 1
+    ends = lax.fori_loop(rows // 2, rows, one_row, ends)
+    for which in range(LISTS):
         for n in range(2 * STEP):
             order_ref[which, ends[which] + n] = SKIP
         for n in range(STEP):
@@ -100,15 +105,15 @@
         in_specs=[SMEM] * 3,
         out_specs=[SMEM] * 3,
         out_shape=[
-            jax.ShapeDtypeStruct((3, most + 2 * STEP), jnp.int32),
-            jax.ShapeDtypeStruct((3, most // 2 + STEP), jnp.int32),
-            jax.ShapeDtypeStruct((3,), jnp.int32),
+            jax.ShapeDtypeStruct((LISTS, most + 2 * STEP), jnp.int32),
+            jax.ShapeDtypeStruct((LISTS, most // 2 + STEP), jnp.int32),
+            jax.ShapeDtypeStruct((2 * LISTS,), jnp.int32),
         ],
         name="make_lists",
     )(place, cols, counts)
 
 
-def add_products(which, lists, blocks, panel, acc):
+def add_products(which, lists, blocks, panel, acc, first, end):
     order_ref, row_ref, pairs_ref = lists
 
     def one_step(step, carry):
@@ -133,47 +138,65 @@
             acc[row_ref[which, step * STEP + pair]] += term
         return carry
 
-    lax.fori_loop(0, (pairs_ref[which] + STEP - 1) // STEP, one_step, 0)
-
-
-def fetch(pairs, sems):
-    copies = [pltpu.make_async_copy(a, b, sems.at[n]) for n, (a, b) in enumerate(pairs)]
-    for copy in copies:
+    lax.fori_loop(first, end, one_step, 0)
+
+
+def all_steps(which, lists):
+    return (lists[2][which] + STEP - 1) // STEP
+
+
+def run(which, lists, panel_parts, pieces, panel, blocks, acc, before, sems):
+    half = blocks.shape[2] // 2
+    early, at = [], 0
+    for part in panel_parts:
+        early.append((part, panel.at[pl.ds(at, part.shape[0])]))
+        at += part.shape[0]
+    if before is not None:
+        early.append((before, acc))
+    rounds = [early + split_pieces(pieces, blocks, 0, half), split_pieces(pieces, blocks, half, half)]
+    copies, used = [], 0
+    for pairs in rounds:
+        copies.append([pltpu.make_async_copy(a, b, sems.at[used + n]) for n, (a, b) in enumerate(pairs)])
+        used += len(pairs)
+    for copy in copies[0] + copies[1]:
         copy.start()
-    for copy in copies:
+    if before is None:
+        acc[...] = jnp.zeros_like(acc)
+    for copy in copies[0]:
         copy.wait()
-
-
-def split_pieces(pieces, blocks):
+    middle = lists[2][LISTS + which] // STEP
+    add_products(which, lists, blocks, panel, acc, 0, middle)
+    for copy in copies[1]:
+        copy.wait()
+    add_products(which, lists, blocks, panel, acc, middle, all_steps(which, lists))
+
+
+def split_pieces(pieces, blocks, first, rows):
     pairs, at = [], 0
+    lines = pl.ds(first, rows)
     for piece in pieces:
         if isinstance(piece, tuple):
             size = piece[0].shape[0]
-            pairs += [(piece[n], blocks.at[n, pl.ds(at, size)]) for n in range(2)]
+            pairs += [(piece[n].at[:, lines], blocks.at[n, pl.ds(at, size), lines]) for n in range(2)]
         else:
             size = piece.shape[1]
-            pairs.append((piece, blocks.at[:, pl.ds(at, size)]))
+            pairs.append((piece.at[:, :, lines], blocks.at[:, pl.ds(at, size), lines]))
         at += size
     return pairs
 
 
-def group_pieces(refs):
-    return [*refs[:3], (refs[3], refs[4]), *refs[5:8], (refs[8], refs[9]), *refs[10:12]]
-
-
-def near_kernel(order_ref, row_ref, pairs_ref, near, near_other, *refs):
-    pieces, (acc, blocks, panel, sems) = refs[:12], refs[12:]
-    count = near.shape[0]
-    pairs = [(ref, panel.at[pl.ds(n * count, count)]) for n, ref in enumerate((near, near_other))]
-    fetch(pairs + split_pieces(group_pieces(pieces), blocks), sems)
-    acc[...] = jnp.zeros_like(acc)
-    add_products(0, (order_ref, row_ref, pairs_ref), blocks, panel, acc)
-
-
-def far_kernel(order_ref, row_ref, pairs_ref, far, before, *refs):
+def early_kernel(order_ref, row_ref, pairs_ref, near, near_other, *refs):
+    pieces, (acc, blocks, panel, sems) = refs[:8], refs[8:]
+    lists = (order_ref, row_ref, pairs_ref)
+    grouped = [*pieces[:3], (pieces[3], pieces[4]), *pieces[5:]]
+    run(0, lists, [near, near_other], grouped, panel, blocks, acc, None, sems)
+
+
+def main_kernel(order_ref, row_ref, pairs_ref, near, near_other, far, before, *refs):
     pieces, (blocks, acc, panel, sems) = refs[:12], refs[12:]
-    fetch([(far, panel), (before, acc)] + split_pieces(group_pieces(pieces), blocks), sems)
-    add_products(1, (order_ref, row_ref, pairs_ref), blocks, panel, acc)
+    lists = (order_ref, row_ref, pairs_ref)
+    grouped = [*pieces[:3], (pieces[3], pieces[4]), *pieces[5:8], (pieces[8], pieces[9]), *pieces[10:]]
+    run(1, lists, [near, near_other, far], grouped, panel, blocks, acc, before, sems)
 
 
 def last_kernel(
@@ -192,7 +215,8 @@
     acc,
 ):
     acc[...] = before[...]
-    add_products(2, (order_ref, row_ref, pairs_ref), blocks, panel, acc)
+    lists = (order_ref, row_ref, pairs_ref)
+    add_products(2, lists, blocks, panel, acc, 0, all_steps(2, lists))
 
     def one_row(row, carry):
         total = acc[row]
@@ -245,42 +269,42 @@
     return pl.CostEstimate(flops=0, bytes_accessed=int(micros * 3.0e6), transcendentals=0)
 
 
-def near_products(lists, rows, near, near_other, pieces):
-    count = near.shape[0]
-    return pl.pallas_call(
-        near_kernel,
+def early_products(lists, rows, panels, pieces):
+    return pl.pallas_call(
+        early_kernel,
         in_specs=[SMEM] * 3 + [ANY] * (2 + len(pieces)),
         out_specs=VMEM,
         out_shape=jax.ShapeDtypeStruct((rows, 2 * BLOCK, 2 * BLOCK), jnp.float32),
         scratch_shapes=[
-            pltpu.VMEM((2, 24, rows, BLOCK, BLOCK), jnp.bfloat16),
-            pltpu.VMEM((2 * count, BLOCK, 2 * BLOCK), jnp.bfloat16),
-            pltpu.SemaphoreType.DMA((2 + len(pieces),)),
+            pltpu.VMEM((2, EARLY, rows, BLOCK, BLOCK), jnp.bfloat16),
+            pltpu.VMEM((2 * panels[0].shape[0], BLOCK, 2 * BLOCK), jnp.bfloat16),
+            pltpu.SemaphoreType.DMA((2 + 2 * len(pieces),)),
         ],
-        compiler_params=pltpu.CompilerParams(vmem_limit_bytes=30 * 2**20),
+        compiler_params=pltpu.CompilerParams(vmem_limit_bytes=24 * 2**20),
         cost_estimate=cost(10),
-        name="products_near",
-    )(*lists, in_hbm(near), in_hbm(near_other), *map(in_hbm, pieces))
-
-
-def far_products(lists, far, before, pieces):
+        name="products_early",
+    )(*lists, *map(in_hbm, panels), *map(in_hbm, pieces))
+
+
+def main_products(lists, panels, before, pieces):
     rows = before.shape[0]
-    return pl.pallas_call(
-        far_kernel,
-        in_specs=[SMEM] * 3 + [ANY] * (2 + len(pieces)),
+    args = [*panels, before, *pieces]
+    return pl.pallas_call(
+        main_kernel,
+        in_specs=[SMEM] * 3 + [ANY] * len(args),
         out_specs=[VMEM, VMEM],
         out_shape=[
             pltpu.VMEM((2, 24, rows, BLOCK, BLOCK), jnp.bfloat16),
             pltpu.VMEM(before.shape, jnp.float32),
         ],
         scratch_shapes=[
-            pltpu.VMEM(far.shape, jnp.bfloat16),
-            pltpu.SemaphoreType.DMA((2 + len(pieces),)),
+            pltpu.VMEM((3 * panels[0].shape[0], BLOCK, 2 * BLOCK), jnp.bfloat16),
+            pltpu.SemaphoreType.DMA((4 + 2 * len(pieces),)),
         ],
-        compiler_params=pltpu.CompilerParams(vmem_limit_bytes=7 * 2**20),
-        cost_estimate=cost(8),
-        name="products_far",
-    )(*lists, in_hbm(far), in_hbm(before), *map(in_hbm, pieces))
+        compiler_params=pltpu.CompilerParams(vmem_limit_bytes=15 * 2**20),
+        cost_estimate=cost(10),
+        name="products_main",
+    )(*lists, *map(in_hbm, args))
 
 
 def last_products(lists, far_other, blocks, before, *flat):
@@ -313,46 +337,38 @@
     both = jnp.stack([ham_blocks.swapaxes(0, 1), margin_blocks.swapaxes(0, 1)], axis=0)
     panel = jnp.concatenate([pert_real, pert_imag], axis=1).reshape(rows, BLOCK, 2 * BLOCK)
 
+    near = lax.all_gather(panel, "z", axis=0, tiled=True)
     from_left = shift(both, "x", 1)
     from_right = shift(both, "x", -1)
     part = shift(both[:, :2], "yhi")
-    near = lax.all_gather(panel, "z", axis=0, tiled=True)
     lists = make_lists(place, block_cols, block_counts)
+
     neighbour = shift(panel, "ylo")
 
-    far = lax.all_gather(after(neighbour, from_left, from_right, part, *lists), "z", axis=0, tiled=True)
-    far_ham = shift(from_left[0], "x", 1)
-    far_margin = shift(from_right[1], "x", -1)
+    left_ham, right_margin = from_left[0], from_right[1]
+    far = lax.all_gather(
+        after(neighbour, left_ham, right_margin, part, lists[0]), "z", axis=0, tiled=True
+    )
     part_left = shift(part, "x", 1)
     part_right = shift(part, "x", -1)
+    far_ham = shift(left_ham, "x", 1)
+    far_margin = shift(right_margin, "x", -1)
     late = shift(
         jnp.concatenate([both[:, 2:], from_left[:, 2:], from_right[:, 2:]], axis=1), "yhi"
     )
 
-    near = after(near, far_ham, far_margin, part_left, part_right, late)
+    near = after(near, part_left, part_right, far_ham, far_margin, late)
     near_other = shift(near, "core")
-    late_far = shift(jnp.stack([far_ham[2:], far_margin[2:]], axis=0), "yhi")
     part_far_ham = shift(part_left[0], "x", 1)
     part_far_margin = shift(part_right[1], "x", -1)
-
-    pieces = (
-        both,
-        from_left,
-        from_right,
-        far_ham,
-        far_margin,
-        part,
-        part_left,
-        part_right,
-        part_far_ham,
-        part_far_margin,
-        late,
-        late_far,
-    )
-    acc = near_products(lists, rows, near, near_other, pieces)
-    far = after(far, acc)
+    late_far = shift(jnp.stack([far_ham[2:], far_margin[2:]], axis=0), "yhi")
+
+    early = (both, from_left, from_right, far_ham, far_margin, part, part_left, part_right)
+    pieces = early + (part_far_ham, part_far_margin, late, late_far)
+    acc = early_products(lists, rows, (near, near_other), early)
+    far = after(far, acc, part_far_ham, part_far_margin, late_far)
     far_other = shift(far, "core")
-    blocks, acc = far_products(lists, far, acc, pieces)
+    blocks, acc = main_products(lists, (near, near_other, far), acc, pieces)
     new_real, new_imag = last_products(
         lists, far_other, blocks, acc, pert_real, pert_imag, drive_real, drive_imag
     )

time: 165 us -> 148 us (0.90)
  waiting for transfers between devices: 79.1 us -> 65.6 us
  other arithmetic: 6.39 us -> 4.18 us
  starting transfers between devices: 22.6 us -> 20.7 us
    ppermute x14, waiting for transfers between devices: 79.1 us -> 64.3 us  [shift(): return lax.ppermute(array, AXES, moves(axis, by))]
    squeeze x2, local copies, waits for them, and re-layouts: 0.13 us -> 3.13 us  [per_device(): left_ham, right_margin = (from_left[0], from_right[1])]
    another operation x3, other arithmetic: 3.62 us -> 1.3 us  [per_device(): jnp.stack([ham_blocks.swapaxes(0, 1), margin_blocks.swapaxes(0, 1)], axis=0)]
    unnamed x46 -> x50, local copies, waits for them, and re-layouts: 6.74 us -> 4.76 us
    ppermute x14, starting transfers between devices: 22.5 us -> 20.6 us  [shift(): return lax.ppermute(array, AXES, moves(axis, by))]
  transfers between devices with their start and end apart: 16 -> 16, of which waited for: 8 -> 9; matrix products, arithmetic and copies ran while one was open for 5% -> 7% of each run, Pallas kernels for 16% -> 17%
where the time goes in v5:
time: 148 us
  waiting for transfers between devices  65.6 us (44%)
  Pallas kernels  29.6 us (20%)
  starting transfers between devices  20.7 us (14%)
  between operations  14.4 us (10%)
  local copies, waits for them, and re-layouts  13.3 us (9%)
  other arithmetic  4.18 us (3%)
    ppermute x14, waiting for transfers between devices, shift(): return lax.ppermute(array, AXES, moves(axis, by))  64.3 us
    ppermute x14, starting transfers between devices, shift(): return lax.ppermute(array, AXES, moves(axis, by))  20.6 us
    pallas_call x1, Pallas kernels, main_products(): pl.pallas_call(main_kernel, in_specs=[SMEM] * 3 + [ANY] * len(args), out_...  11.3 us
    pallas_call x1, Pallas kernels, early_products(): pl.pallas_call(early_kernel, in_specs=[SMEM] * 3 + [ANY] * (2 + len(piece...  9.53 us
    unnamed x50, local copies, waits for them, and re-layouts  4.76 us
    pallas_call x1, Pallas kernels, make_lists(): pl.pallas_call(list_kernel, in_specs=[SMEM] * 3, out_specs=[SMEM] * 3, ou...  4.59 us
    pallas_call x1, Pallas kernels, last_products(): pl.pallas_call(last_kernel, in_specs=[SMEM] * 3 + [VMEM] * 7, out_specs=[...  4.19 us
    squeeze x2, local copies, waits for them, and re-layouts, per_device(): left_ham, right_margin = (from_left[0], from_right[1])  3.13 us
  transfers between devices with their start and end apart: 16, of which 9 were waited for; matrix products, arithmetic and copies ran while one was open for 7% of the time, Pallas kernels for 17%

profile of v5, /device:TPU:1, one launch (start us, length us, event | category | flops | bytes accessed | tf_op | source)
XLA Modules:
  0.0 147.7 jit_solution(1278155534314251513)
XLA Ops:
  7.2 0.0 copy-start.23
  7.2 0.0 copy-start.24
  7.2 0.0 all-gather.5.cloned.1.call-start
  7.2 2.0 %pad_maximum_fusion.2 = bf16[1024,256]{1,0:T(8,128)(2,1)} fusion(bf16[1024,128]{1,0:T(8,128)(2,1)} %pert_imag.1, bf16[1024,128]{1,0:T(8,128)(2,1)} %pert_real.1), kind=kLoop, calls=%fused_computation.14 | loop fusion | flops 1048576 | bytes 1048576 | tf_op jit(solution)/shard_map/concatenate | solution.py:338
  9.2 0.0 all-gather.5.cloned.1.call-update
  9.2 0.0 all-gather.3.cloned.1.call-start
  9.3 0.2 copy_bitcast_fusion
  9.5 0.1 pad_maximum_fusion.refs_0_
  9.7 3.4 %collective-permute-start.2 = (bf16[2,3,8,128,128]{4,3,2,1,0:T(8,128)(2,1)S(1)}, bf16[2,3,8,128,128]{4,3,2,1,0:T(8,128)(2,1)S(1)}, u32[]{:S(2)}, u32[]{:S(2)}) collective-permute-start(bf16[2,3,8,128,128]{4,3,2,1,0:T(8,128)(2,1)S(1)} %pad_maximum_fusion.refs_0_), channel_id=1, source_target_pairs={{0,6},{1,7},{2,0},{3,1},{4,2},{5,3},{6,4},{7,5},{8,14},{9,15},{10,... | collective-permute-start | bytes 4718600 | tf_op jit(solution)/shard_map/ppermute | solution.py:33
  13.1 0.0 collective-permute-start.1
  13.1 1.1 fusion
  14.2 2.9 %collective-permute-start.3 = (bf16[2,2,8,128,128]{4,3,2,1,0:T(8,128)(2,1)}, bf16[2,2,8,128,128]{4,3,2,1,0:T(8,128)(2,1)}, u32[]{:S(2)}, u32[]{:S(2)}) collective-permute-start(bf16[2,2,8,128,128]{4,3,2,1,0:T(8,128)(2,1)} %fusion), channel_id=1, source_target_pairs={{0,1},{1,0},{2,3},{3,2},{4,5},{5,4},{6,7},{7,6},{8,9},{9,8},{10,11... | collective-permute-start | bytes 3145736 | tf_op jit(solution)/shard_map/ppermute | solution.py:33
  17.1 0.4 collective-permute-start
  17.5 0.7 pad_add_fusion.place_ref
  18.1 4.6 %make_lists.1 = (s32[3,200]{1,0:T(4,128)}, s32[3,100]{1,0:T(4,128)}, s32[6]{0:T(128)}) custom-call(s32[4]{0:T(128)} %pad_add_fusion.place_ref, s32[8,24]{1,0:T(8,128)} %cols_ref.1, s32[8]{0:T(128)} %counts_ref.1), custom_call_target="tpu_custom_call" | custom-call | tf_op jit(solution)/shard_map/make_lists/pallas_call | solution.py:103
  22.7 23.4 %collective-permute-done.2.refs_2_ = bf16[2,3,8,128,128]{4,3,2,1,0:T(8,128)(2,1)S(1)} collective-permute-done((bf16[2,3,8,128,128]{4,3,2,1,0:T(8,128)(2,1)S(1)}, bf16[2,3,8,128,128]{4,3,2,1,0:T(8,128)(2,1)S(1)}, u32[]{:S(2)}, u32[]{:S(2)}) %collective-permute-start.2) | collective-permute-done | bytes 1572896 | tf_op jit(solution)/shard_map/ppermute | solution.py:33
  46.1 1.0 slice_bitcast_fusion.refs_2_
  47.1 2.2 %collective-permute-done.1.refs_1_ = bf16[2,3,8,128,128]{4,3,2,1,0:T(8,128)(2,1)} collective-permute-done((bf16[2,3,8,128,128]{4,3,2,1,0:T(8,128)(2,1)S(1)}, bf16[2,3,8,128,128]{4,3,2,1,0:T(8,128)(2,1)}, u32[]{:S(2)}, u32[]{:S(2)}) %collective-permute-start.1) | collective-permute-done | bytes 1572896 | tf_op jit(solution)/shard_map/ppermute | solution.py:33
  49.3 2.1 %slice_bitcast_fusion.1.refs_1_ = bf16[3,8,128,128]{3,2,1,0:T(8,128)(2,1)} fusion(bf16[2,3,8,128,128]{4,3,2,1,0:T(8,128)(2,1)} %collective-permute-done.1.refs_1_), kind=kLoop, calls=%fused_computation.8 | loop fusion | bytes 1572864 | tf_op jit(solution)/shard_map/squeeze | solution.py:348
  51.4 0.0 collective-permute-done.refs_0_
  51.4 0.0 collective-permute-done.3.refs_3_.refs_5_
  51.5 0.0 all-gather.3.cloned.1.call-update
  51.5 1.1 copy-done.14
  52.6 0.2 copy-done.16
  52.8 0.1 fusion.1
  52.9 1.1 slice.46
  54.0 0.2 pad_maximum_fusion.1
  54.2 3.0 %collective-permute-start.8 = (bf16[2,3,8,128,128]{4,3,2,1,0:T(8,128)(2,1)S(1)}, bf16[2,3,8,128,128]{4,3,2,1,0:T(8,128)(2,1)}, u32[]{:S(2)}, u32[]{:S(2)}) collective-permute-start(bf16[2,3,8,128,128]{4,3,2,1,0:T(8,128)(2,1)S(1)} %pad_maximum_fusion.1), channel_id=1, source_target_pairs={{0,1},{1,0},{2,3},{3,2},{4,5},{5,4},{6,7},{7,6},{8,9},{9,8},{10,11... | collective-permute-start | bytes 4718600 | tf_op jit(solution)/shard_map/ppermute | solution.py:33
  57.2 1.4 collective-permute-start.5
  58.6 0.1 collective-permute-start.4
  58.7 2.6 %collective-permute-start.7 = (bf16[3,8,128,128]{3,2,1,0:T(8,128)(2,1)S(1)}, bf16[3,8,128,128]{3,2,1,0:T(8,128)(2,1)S(1)}, u32[]{:S(2)}, u32[]{:S(2)}) collective-permute-start(bf16[3,8,128,128]{3,2,1,0:T(8,128)(2,1)S(1)} %copy-done.18), channel_id=1, source_target_pairs={{0,6},{1,7},{2,0},{3,1},{4,2},{5,3},{6,4},{7,5},{8,14},{9,15},{10,... | collective-permute-start | bytes 2359304 | tf_op jit(solution)/shard_map/ppermute | solution.py:33
  61.3 0.0 collective-permute-start.6
  61.3 18.8 %collective-permute-done.5.refs_2_.refs_7_ = bf16[2,2,8,128,128]{4,3,2,1,0:T(8,128)(2,1)S(1)} collective-permute-done((bf16[2,2,8,128,128]{4,3,2,1,0:T(8,128)(2,1)}, bf16[2,2,8,128,128]{4,3,2,1,0:T(8,128)(2,1)S(1)}, u32[]{:S(2)}, u32[]{:S(2)}) %collective-permute-start.5) | collective-permute-done | bytes 1048608 | tf_op jit(solution)/shard_map/ppermute | solution.py:33
  80.0 2.5 %collective-permute-done.4.refs_1_.refs_6_ = bf16[2,2,8,128,128]{4,3,2,1,0:T(8,128)(2,1)S(1)} collective-permute-done((bf16[2,2,8,128,128]{4,3,2,1,0:T(8,128)(2,1)}, bf16[2,2,8,128,128]{4,3,2,1,0:T(8,128)(2,1)S(1)}, u32[]{:S(2)}, u32[]{:S(2)}) %collective-permute-start.4) | collective-permute-done | bytes 1048608 | tf_op jit(solution)/shard_map/ppermute | solution.py:33
  82.5 14.3 %collective-permute-done.7.refs_4_ = bf16[3,8,128,128]{3,2,1,0:T(8,128)(2,1)S(1)} collective-permute-done((bf16[3,8,128,128]{3,2,1,0:T(8,128)(2,1)S(1)}, bf16[3,8,128,128]{3,2,1,0:T(8,128)(2,1)S(1)}, u32[]{:S(2)}, u32[]{:S(2)}) %collective-permute-start.7) | collective-permute-done | bytes 786464 | tf_op jit(solution)/shard_map/ppermute | solution.py:33
  96.9 2.5 %collective-permute-done.6.refs_3_ = bf16[3,8,128,128]{3,2,1,0:T(8,128)(2,1)} collective-permute-done((bf16[3,8,128,128]{3,2,1,0:T(8,128)(2,1)S(1)}, bf16[3,8,128,128]{3,2,1,0:T(8,128)(2,1)}, u32[]{:S(2)}, u32[]{:S(2)}) %collective-permute-start.6) | collective-permute-done | bytes 786464 | tf_op jit(solution)/shard_map/ppermute | solution.py:33
  99.4 0.0 collective-permute-done.8.refs_5_.refs_10_
  99.4 3.2 %collective-permute-start.9 = (bf16[64,128,256]{2,1,0:T(8,128)(2,1)}, bf16[64,128,256]{2,1,0:T(8,128)(2,1)S(1)}, u32[]{:S(2)}, u32[]{:S(2)}) collective-permute-start(bf16[64,128,256]{2,1,0:T(8,128)(2,1)} %gate.4.near), channel_id=1, source_target_pairs={{0,8},{1,9},{2,10},{3,11},{4,12},{5,13},{6,14},{7,15},{8,0},{9,1},... | collective-permute-start | bytes 12582920 | tf_op jit(solution)/shard_map/ppermute | solution.py:33
  102.7 1.1 slice_bitcast_fusion.2
  103.8 0.0 copy-start.5
  103.8 0.8 collective-permute-start.11
  104.6 1.1 slice_bitcast_fusion.3
  105.7 0.8 collective-permute-start.10
  106.5 1.0 slice_bitcast_fusion.4
  107.5 1.0 slice_bitcast_fusion.5
  108.4 0.1 pad_maximum_fusion.3
  108.5 1.0 collective-permute-start.12
  109.5 0.2 collective-permute-done.9.near_other
  109.7 2.0 %copy-done.8 = bf16[64,128,256]{2,1,0:T(8,128)(2,1)} copy-done((bf16[64,128,256]{2,1,0:T(8,128)(2,1)}, bf16[64,128,256]{2,1,0:T(8,128)(2,1)S(1)}, u32[]{:S(2)}) %copy-start.8) | copy-done | bytes 4194328
  111.7 9.5 %products_early.1.refs_1_.before = f32[8,256,256]{2,1,0:T(8,128)S(1)} custom-call(s32[3,200]{1,0:T(4,128)S(1)} %copy-done.5, s32[3,100]{1,0:T(4,128)S(1)} %copy-done.6, s32[6]{0:T(128)S(1)} %copy-done.7, bf16[64,128,256]{2,1,0:T(8,128)(2,1)} %gate.4.near, bf16[64,128,256]{2,1,0:T(8,128)(2,1)} %copy-done.8, bf16[2,3,8,128,128]{4,3,2,1,0:T(8,128)(2,1)} %copy-done.9, ...), custom_call_target="tpu_custom_call" | custom-call | bytes 30000000 | tf_op jit(solution)/shard_map/products_early/pallas_call | solution.py:273
  121.3 1.3 copy-done
  122.5 0.0 collective-permute-done.11.refs_3_.refs_9_
  122.5 0.0 collective-permute-done.10.refs_2_.refs_8_
  122.6 0.0 copy-start.21
  122.6 0.4 collective-permute-done.12.refs_4_.refs_11_
  123.0 1.3 all-gather.3.cloned.1.call-done.refs_0_
  124.3 0.0 copy-start.1
  124.3 0.0 copy-start.2
  124.3 0.0 copy-start.3
  124.3 0.0 copy-start.4
  124.3 1.0 collective-permute-start.13
  125.3 11.3 %products_main.1 = (bf16[2,24,8,128,128]{4,3,2,1,0:T(8,128)(2,1)S(1)}, f32[8,256,256]{2,1,0:T(8,128)S(1)}) custom-call(s32[3,200]{1,0:T(4,128)S(1)} %copy-done.5, s32[3,100]{1,0:T(4,128)S(1)} %copy-done.6, s32[6]{0:T(128)S(1)} %copy-done.7, bf16[64,128,256]{2,1,0:T(8,128)(2,1)} %gate.4.near, bf16[64,128,256]{2,1,0:T(8,128)(2,1)} %copy-done.8, ...), custom_call_target="tpu_custom_call" | custom-call | bytes 30000000 | tf_op jit(solution)/shard_map/products_main/pallas_call | solution.py:292
  136.7 0.0 collective-permute-done.13.panel
  136.7 4.2 %products_last.1 = (f32[1024,128]{1,0:T(8,128)}, f32[1024,128]{1,0:T(8,128)}) custom-call(s32[3,200]{1,0:T(4,128)S(1)} %copy-done.5, s32[3,100]{1,0:T(4,128)S(1)} %copy-done.6, s32[6]{0:T(128)S(1)} %copy-done.7, bf16[64,128,256]{2,1,0:T(8,128)(2,1)S(1)} %collective-permute-done.13.panel, bf16[2,24,8,128,128]{4,3,2,1,0:T(8,128)(2,1)S(1)} %get-tuple-element.10.blocks, ...), custom_call_target="tpu_custom_call" | custom-call | bytes 12000000 | tf_op jit(solution)/shard_map/products_last/pallas_call | solution.py:312
  (43 shorter events, 0.1 us)
Async XLA Ops:
  7.2 2.1 %copy-start.23 = (bf16[8,3,128,128]{3,2,1,0:T(8,128)(2,1)S(1)}, bf16[8,3,128,128]{3,2,1,0:T(8,128)(2,1)}, u32[]{:S(2)}) copy-start(bf16[8,3,128,128]{3,2,1,0:T(8,128)(2,1)} %param.9) | copy-start | bytes 2359300
  7.2 2.1 %copy-start.24 = (bf16[8,3,128,128]{3,2,1,0:T(8,128)(2,1)S(1)}, bf16[8,3,128,128]{3,2,1,0:T(8,128)(2,1)}, u32[]{:S(2)}) copy-start(bf16[8,3,128,128]{3,2,1,0:T(8,128)(2,1)} %param.8) | copy-start | bytes 2359300
  7.2 92.2 %all-gather.5.cloned.1.call-start = ((), (), s32[]{:S(2)}) async-start(), calls=%async_computation.1 | async-start | bytes 4718592 | tf_op jit(solution)/shard_map/all_gather | solution.py:340
  9.2 115.0 %all-gather.3.cloned.1.call-start = ((), (), s32[]{:S(2)}) async-start(), calls=%async_computation | async-start | bytes 4718592 | tf_op jit(solution)/shard_map/all_gather | solution.py:349
  9.5 3.6 %copy-start.13 = (bf16[1,3,8,128,128]{4,3,2,1,0:T(8,128)(2,1)}, bf16[1,3,8,128,128]{4,3,2,1,0:T(8,128)(2,1)S(1)}, u32[]{:S(2)}) copy-start(bf16[1,3,8,128,128]{4,3,2,1,0:T(8,128)(2,1)S(1)} %get-tuple-element.12) | copy-start | bytes 2359300
  9.5 3.6 %copy-start.15 = (bf16[1,3,8,128,128]{4,3,2,1,0:T(8,128)(2,1)}, bf16[1,3,8,128,128]{4,3,2,1,0:T(8,128)(2,1)S(1)}, u32[]{:S(2)}) copy-start(bf16[1,3,8,128,128]{4,3,2,1,0:T(8,128)(2,1)S(1)} %get-tuple-element.13) | copy-start | bytes 2359300
  9.7 37.5 %copy-start.9 = (bf16[2,3,8,128,128]{4,3,2,1,0:T(8,128)(2,1)}, bf16[2,3,8,128,128]{4,3,2,1,0:T(8,128)(2,1)S(1)}, u32[]{:S(2)}) copy-start(bf16[2,3,8,128,128]{4,3,2,1,0:T(8,128)(2,1)S(1)} %pad_maximum_fusion.refs_0_) | copy-start | bytes 4718596
  9.7 36.4 %collective-permute-start.2 = (bf16[2,3,8,128,128]{4,3,2,1,0:T(8,128)(2,1)S(1)}, bf16[2,3,8,128,128]{4,3,2,1,0:T(8,128)(2,1)S(1)}, u32[]{:S(2)}, u32[]{:S(2)}) collective-permute-start(bf16[2,3,8,128,128]{4,3,2,1,0:T(8,128)(2,1)S(1)} %pad_maximum_fusion.refs_0_), channel_id=1, source_target_pairs={{0,6},{1,7},{2,0},{3,1},{4,2},{5,3},{6,4},{7,5},{8,14},{9,15},{10,... | collective-permute-start | bytes 4718600 | tf_op jit(solution)/shard_map/ppermute | solution.py:33
  13.1 36.3 %collective-permute-start.1 = (bf16[2,3,8,128,128]{4,3,2,1,0:T(8,128)(2,1)S(1)}, bf16[2,3,8,128,128]{4,3,2,1,0:T(8,128)(2,1)}, u32[]{:S(2)}, u32[]{:S(2)}) collective-permute-start(bf16[2,3,8,128,128]{4,3,2,1,0:T(8,128)(2,1)S(1)} %pad_maximum_fusion.refs_0_), channel_id=1, source_target_pairs={{0,2},{1,3},{2,4},{3,5},{4,6},{5,7},{6,0},{7,1},{8,10},{9,11},{10,... | collective-permute-start | bytes 4718600 | tf_op jit(solution)/shard_map/ppermute | solution.py:33
  14.2 37.3 %collective-permute-start.3 = (bf16[2,2,8,128,128]{4,3,2,1,0:T(8,128)(2,1)}, bf16[2,2,8,128,128]{4,3,2,1,0:T(8,128)(2,1)}, u32[]{:S(2)}, u32[]{:S(2)}) collective-permute-start(bf16[2,2,8,128,128]{4,3,2,1,0:T(8,128)(2,1)} %fusion), channel_id=1, source_target_pairs={{0,1},{1,0},{2,3},{3,2},{4,5},{5,4},{6,7},{7,6},{8,9},{9,8},{10,11... | collective-permute-start | bytes 3145736 | tf_op jit(solution)/shard_map/ppermute | solution.py:33
  17.1 34.4 %collective-permute-start = (bf16[8,128,256]{2,1,0:T(8,128)(2,1)}, bf16[8,128,256]{2,1,0:T(8,128)(2,1)}, u32[]{:S(2)}, u32[]{:S(2)}) collective-permute-start(bf16[8,128,256]{2,1,0:T(8,128)(2,1)} %bitcast.4), channel_id=1, source_target_pairs={{0,128},{1,129},{2,130},{3,131},{4,132},{5,133},{6,134},{7,135},{8... | collective-permute-start | bytes 1572872 | tf_op jit(solution)/shard_map/ppermute | solution.py:33
  46.1 6.7 %copy-start.12 = (bf16[2,3,8,128,128]{4,3,2,1,0:T(8,128)(2,1)}, bf16[2,3,8,128,128]{4,3,2,1,0:T(8,128)(2,1)S(1)}, u32[]{:S(2)}) copy-start(bf16[2,3,8,128,128]{4,3,2,1,0:T(8,128)(2,1)S(1)} %collective-permute-done.2.refs_2_) | copy-start | bytes 4718596
  51.4 1.1 copy-start.14
  51.4 1.4 copy-start.16
  54.0 4.7 %copy-start.18 = (bf16[3,8,128,128]{3,2,1,0:T(8,128)(2,1)S(1)}, bf16[3,8,128,128]{3,2,1,0:T(8,128)(2,1)}, u32[]{:S(2)}) copy-start(bf16[3,8,128,128]{3,2,1,0:T(8,128)(2,1)} %slice_bitcast_fusion.refs_2_) | copy-start | bytes 2359300
  54.0 7.2 %copy-start.19 = (bf16[3,8,128,128]{3,2,1,0:T(8,128)(2,1)S(1)}, bf16[3,8,128,128]{3,2,1,0:T(8,128)(2,1)}, u32[]{:S(2)}) copy-start(bf16[3,8,128,128]{3,2,1,0:T(8,128)(2,1)} %slice_bitcast_fusion.1.refs_1_) | copy-start | bytes 2359300
  54.2 45.2 %collective-permute-start.8 = (bf16[2,3,8,128,128]{4,3,2,1,0:T(8,128)(2,1)S(1)}, bf16[2,3,8,128,128]{4,3,2,1,0:T(8,128)(2,1)}, u32[]{:S(2)}, u32[]{:S(2)}) collective-permute-start(bf16[2,3,8,128,128]{4,3,2,1,0:T(8,128)(2,1)S(1)} %pad_maximum_fusion.1), channel_id=1, source_target_pairs={{0,1},{1,0},{2,3},{3,2},{4,5},{5,4},{6,7},{7,6},{8,9},{9,8},{10,11... | collective-permute-start | bytes 4718600 | tf_op jit(solution)/shard_map/ppermute | solution.py:33
  57.2 22.8 %collective-permute-start.5 = (bf16[2,2,8,128,128]{4,3,2,1,0:T(8,128)(2,1)}, bf16[2,2,8,128,128]{4,3,2,1,0:T(8,128)(2,1)S(1)}, u32[]{:S(2)}, u32[]{:S(2)}) collective-permute-start(bf16[2,2,8,128,128]{4,3,2,1,0:T(8,128)(2,1)} %collective-permute-done.3.refs_3_.refs_5_), channel_id=1, source_target_pairs={{0,6},{1,7},{2,0},{3,1},{4,2},{5,3},{6,4},{7,5},{8,14},{9,15},{10,... | collective-permute-start | bytes 3145736 | tf_op jit(solution)/shard_map/ppermute | solution.py:33
  58.6 24.0 %collective-permute-start.4 = (bf16[2,2,8,128,128]{4,3,2,1,0:T(8,128)(2,1)}, bf16[2,2,8,128,128]{4,3,2,1,0:T(8,128)(2,1)S(1)}, u32[]{:S(2)}, u32[]{:S(2)}) collective-permute-start(bf16[2,2,8,128,128]{4,3,2,1,0:T(8,128)(2,1)} %collective-permute-done.3.refs_3_.refs_5_), channel_id=1, source_target_pairs={{0,2},{1,3},{2,4},{3,5},{4,6},{5,7},{6,0},{7,1},{8,10},{9,11},{10,... | collective-permute-start | bytes 3145736 | tf_op jit(solution)/shard_map/ppermute | solution.py:33
  58.7 38.2 %collective-permute-start.7 = (bf16[3,8,128,128]{3,2,1,0:T(8,128)(2,1)S(1)}, bf16[3,8,128,128]{3,2,1,0:T(8,128)(2,1)S(1)}, u32[]{:S(2)}, u32[]{:S(2)}) collective-permute-start(bf16[3,8,128,128]{3,2,1,0:T(8,128)(2,1)S(1)} %copy-done.18), channel_id=1, source_target_pairs={{0,6},{1,7},{2,0},{3,1},{4,2},{5,3},{6,4},{7,5},{8,14},{9,15},{10,... | collective-permute-start | bytes 2359304 | tf_op jit(solution)/shard_map/ppermute | solution.py:33
  61.3 38.1 %collective-permute-start.6 = (bf16[3,8,128,128]{3,2,1,0:T(8,128)(2,1)S(1)}, bf16[3,8,128,128]{3,2,1,0:T(8,128)(2,1)}, u32[]{:S(2)}, u32[]{:S(2)}) collective-permute-start(bf16[3,8,128,128]{3,2,1,0:T(8,128)(2,1)S(1)} %copy-done.19), channel_id=1, source_target_pairs={{0,2},{1,3},{2,4},{3,5},{4,6},{5,7},{6,0},{7,1},{8,10},{9,11},{10,... | collective-permute-start | bytes 2359304 | tf_op jit(solution)/shard_map/ppermute | solution.py:33
  80.0 19.4 %copy-start.10 = (bf16[2,2,8,128,128]{4,3,2,1,0:T(8,128)(2,1)}, bf16[2,2,8,128,128]{4,3,2,1,0:T(8,128)(2,1)S(1)}, u32[]{:S(2)}) copy-start(bf16[2,2,8,128,128]{4,3,2,1,0:T(8,128)(2,1)S(1)} %collective-permute-done.5.refs_2_.refs_7_) | copy-start | bytes 3145732
  82.5 16.9 %copy-start.11 = (bf16[2,2,8,128,128]{4,3,2,1,0:T(8,128)(2,1)}, bf16[2,2,8,128,128]{4,3,2,1,0:T(8,128)(2,1)S(1)}, u32[]{:S(2)}) copy-start(bf16[2,2,8,128,128]{4,3,2,1,0:T(8,128)(2,1)S(1)} %collective-permute-done.4.refs_1_.refs_6_) | copy-start | bytes 3145732
  96.9 2.5 %copy-start.17 = (bf16[3,8,128,128]{3,2,1,0:T(8,128)(2,1)}, bf16[3,8,128,128]{3,2,1,0:T(8,128)(2,1)S(1)}, u32[]{:S(2)}) copy-start(bf16[3,8,128,128]{3,2,1,0:T(8,128)(2,1)S(1)} %collective-permute-done.7.refs_4_) | copy-start | bytes 2359300
  99.4 10.2 %collective-permute-start.9 = (bf16[64,128,256]{2,1,0:T(8,128)(2,1)}, bf16[64,128,256]{2,1,0:T(8,128)(2,1)S(1)}, u32[]{:S(2)}, u32[]{:S(2)}) collective-permute-start(bf16[64,128,256]{2,1,0:T(8,128)(2,1)} %gate.4.near), channel_id=1, source_target_pairs={{0,8},{1,9},{2,10},{3,11},{4,12},{5,13},{6,14},{7,15},{8,0},{9,1},... | collective-permute-start | bytes 12582920 | tf_op jit(solution)/shard_map/ppermute | solution.py:33
  103.8 7.9 %copy-start.5 = (s32[3,200]{1,0:T(4,128)S(1)}, s32[3,200]{1,0:T(4,128)}, u32[]{:S(2)}) copy-start(s32[3,200]{1,0:T(4,128)} %get-tuple-element.7.refs_4_.order_ref) | copy-start | bytes 7204
  103.8 7.9 %copy-start.6 = (s32[3,100]{1,0:T(4,128)S(1)}, s32[3,100]{1,0:T(4,128)}, u32[]{:S(2)}) copy-start(s32[3,100]{1,0:T(4,128)} %get-tuple-element.8.row_ref) | copy-start | bytes 3604
  103.8 7.9 %copy-start.7 = (s32[6]{0:T(128)S(1)}, s32[6]{0:T(128)}, u32[]{:S(2)}) copy-start(s32[6]{0:T(128)} %get-tuple-element.9.pairs_ref) | copy-start | bytes 76
  103.8 18.8 %collective-permute-start.11 = (bf16[2,8,128,128]{3,2,1,0:T(8,128)(2,1)S(1)}, bf16[2,8,128,128]{3,2,1,0:T(8,128)(2,1)S(1)}, u32[]{:S(2)}, u32[]{:S(2)}) collective-permute-start(bf16[2,8,128,128]{3,2,1,0:T(8,128)(2,1)S(1)} %slice_bitcast_fusion.2), channel_id=1, source_target_pairs={{0,6},{1,7},{2,0},{3,1},{4,2},{5,3},{6,4},{7,5},{8,14},{9,15},{10,... | collective-permute-start | bytes 1572872 | tf_op jit(solution)/shard_map/ppermute | solution.py:33
  105.7 16.9 %collective-permute-start.10 = (bf16[2,8,128,128]{3,2,1,0:T(8,128)(2,1)S(1)}, bf16[2,8,128,128]{3,2,1,0:T(8,128)(2,1)S(1)}, u32[]{:S(2)}, u32[]{:S(2)}) collective-permute-start(bf16[2,8,128,128]{3,2,1,0:T(8,128)(2,1)S(1)} %slice_bitcast_fusion.3), channel_id=1, source_target_pairs={{0,2},{1,3},{2,4},{3,5},{4,6},{5,7},{6,0},{7,1},{8,10},{9,11},{10,... | collective-permute-start | bytes 1572872 | tf_op jit(solution)/shard_map/ppermute | solution.py:33
  108.5 14.5 %collective-permute-start.12 = (bf16[2,1,8,128,128]{4,3,2,1,0:T(8,128)(2,1)S(1)}, bf16[2,1,8,128,128]{4,3,2,1,0:T(8,128)(2,1)S(1)}, u32[]{:S(2)}, u32[]{:S(2)}) collective-permute-start(bf16[2,1,8,128,128]{4,3,2,1,0:T(8,128)(2,1)S(1)} %pad_maximum_fusion.3), channel_id=1, source_target_pairs={{0,1},{1,0},{2,3},{3,2},{4,5},{5,4},{6,7},{7,6},{8,9},{9,8},{10,11... | collective-permute-start | bytes 1572872 | tf_op jit(solution)/shard_map/ppermute | solution.py:33
  109.7 2.0 %copy-start.8 = (bf16[64,128,256]{2,1,0:T(8,128)(2,1)}, bf16[64,128,256]{2,1,0:T(8,128)(2,1)S(1)}, u32[]{:S(2)}) copy-start(bf16[64,128,256]{2,1,0:T(8,128)(2,1)S(1)} %collective-permute-done.9.near_other) | copy-start | bytes 12582916
  121.2 1.3 copy-start
  122.5 1.7 %copy-start.20 = (bf16[2,8,128,128]{3,2,1,0:T(8,128)(2,1)}, bf16[2,8,128,128]{3,2,1,0:T(8,128)(2,1)S(1)}, u32[]{:S(2)}) copy-start(bf16[2,8,128,128]{3,2,1,0:T(8,128)(2,1)S(1)} %collective-permute-done.11.refs_3_.refs_9_) | copy-start | bytes 1572868
  122.6 1.7 %copy-start.21 = (bf16[2,8,128,128]{3,2,1,0:T(8,128)(2,1)}, bf16[2,8,128,128]{3,2,1,0:T(8,128)(2,1)S(1)}, u32[]{:S(2)}) copy-start(bf16[2,8,128,128]{3,2,1,0:T(8,128)(2,1)S(1)} %collective-permute-done.10.refs_2_.refs_8_) | copy-start | bytes 1572868
  123.0 1.3 copy-start.22
  124.3 12.4 %copy-start.1 = (bf16[1024,128]{1,0:T(8,128)(2,1)S(1)}, bf16[1024,128]{1,0:T(8,128)(2,1)}, u32[]{:S(2)}) copy-start(bf16[1024,128]{1,0:T(8,128)(2,1)} %pert_imag.1) | copy-start | bytes 786436
  124.3 12.4 %copy-start.2 = (bf16[1024,128]{1,0:T(8,128)(2,1)S(1)}, bf16[1024,128]{1,0:T(8,128)(2,1)}, u32[]{:S(2)}) copy-start(bf16[1024,128]{1,0:T(8,128)(2,1)} %pert_real.1) | copy-start | bytes 786436
  124.3 12.4 %copy-start.3 = (bf16[1024,128]{1,0:T(8,128)(2,1)S(1)}, bf16[1024,128]{1,0:T(8,128)(2,1)}, u32[]{:S(2)}) copy-start(bf16[1024,128]{1,0:T(8,128)(2,1)} %drive_real.1) | copy-start | bytes 786436
  124.3 12.4 %copy-start.4 = (bf16[1024,128]{1,0:T(8,128)(2,1)S(1)}, bf16[1024,128]{1,0:T(8,128)(2,1)}, u32[]{:S(2)}) copy-start(bf16[1024,128]{1,0:T(8,128)(2,1)} %drive_imag.1) | copy-start | bytes 786436
  124.3 12.3 %collective-permute-start.13 = (bf16[64,128,256]{2,1,0:T(8,128)(2,1)}, bf16[64,128,256]{2,1,0:T(8,128)(2,1)S(1)}, u32[]{:S(2)}, u32[]{:S(2)}) collective-permute-start(bf16[64,128,256]{2,1,0:T(8,128)(2,1)} %gate.5.far), channel_id=1, source_target_pairs={{0,8},{1,9},{2,10},{3,11},{4,12},{5,13},{6,14},{7,15},{8,0},{9,1},... | collective-permute-start | bytes 12582920 | tf_op jit(solution)/shard_map/ppermute | solution.py:33
Sparse Core Ops, SparseCore 0:
  10.4 58.6 all-gather.4
  70.8 53.4 all-gather.2

commit v6 on v4

--- a/solution.py
+++ b/solution.py
@@ -49,6 +49,7 @@
 )
 STEP = 4
 EARLY = 18
+LISTS = 3
 SKIP = 2**16
 
 
@@ -57,7 +58,7 @@
     my_ylo, my_z, my_core, my_x, my_yhi = (place_ref[n] for n in range(5))
 
     def one_row(row, ends):
-        for which in range(3):
+        for which in range(LISTS):
             pairs_ref[which] = ends[which]
         place = 0
         for dx, dy, local in PIECES:
@@ -69,15 +70,14 @@
                 other = (owner & 1) ^ my_core
                 ahead = ((owner >> 1) - my_z) & 7
                 turn = jnp.where(ahead < 4, 2 * ahead, 15 - 2 * ahead)
-                last = far & (turn + 2 * other >= 7).astype(jnp.int32)
-                which = 2 * last + (1 - last) * (far | int(place >= EARLY))
-                at = jnp.where(
-                    far == 0,
-                    (owner & 15) * 8,
-                    jnp.where(
-                        last == 1, other * (turn - 4) * 8, 128 + 56 * other + turn * 8
-                    ),
-                ) + (column & 7)
+                last = (turn + 2 * other >= 7).astype(jnp.int32)
+                which = jnp.where(last == 1, 2, int(place >= EARLY))
+                at = far * 8 + (column & 7)
+                at += jnp.where(
+                    last == 1,
+                    jnp.where(other == 1, 16 * (turn - 4), 0),
+                    16 * turn + jnp.where(turn >= 5, 80, 80 * (owner & 1)),
+                )
 
                 @pl.when(slot < counts_ref[row])
                 def _(which=which, at=at, place=place):
@@ -88,17 +88,17 @@
 
                 place += 1
         out = []
-        for which in range(3):
+        for which in range(LISTS):
             n = pairs_ref[which]
             order_ref[which, n] = SKIP
             out.append((n + 1) & ~1)
         return tuple(out)
 
-    ends = lax.fori_loop(0, rows // 2, one_row, (0, 0, 0))
-    for which in range(3):
-        pairs_ref[3 + which] = ends[which] >> 1
+    ends = lax.fori_loop(0, rows // 2, one_row, (0,) * LISTS)
+    for which in range(LISTS):
+        pairs_ref[LISTS + which] = ends[which] >> 1
     ends = lax.fori_loop(rows // 2, rows, one_row, ends)
-    for which in range(3):
+    for which in range(LISTS):
         for n in range(2 * STEP):
             order_ref[which, ends[which] + n] = SKIP
         for n in range(STEP):
@@ -113,9 +113,9 @@
         in_specs=[SMEM] * 3,
         out_specs=[SMEM] * 3,
         out_shape=[
-            jax.ShapeDtypeStruct((3, most + 2 * STEP), jnp.int32),
-            jax.ShapeDtypeStruct((3, most // 2 + STEP), jnp.int32),
-            jax.ShapeDtypeStruct((6,), jnp.int32),
+            jax.ShapeDtypeStruct((LISTS, most + 2 * STEP), jnp.int32),
+            jax.ShapeDtypeStruct((LISTS, most // 2 + STEP), jnp.int32),
+            jax.ShapeDtypeStruct((2 * LISTS,), jnp.int32),
         ],
         name="make_lists",
     )(place, cols, counts)
@@ -172,7 +172,7 @@
         acc[...] = jnp.zeros_like(acc)
     for copy in copies[0]:
         copy.wait()
-    middle = lists[2][3 + which] // STEP
+    middle = lists[2][LISTS + which] // STEP
     add_products(which, lists, blocks, panel, acc, 0, middle)
     for copy in copies[1]:
         copy.wait()
@@ -193,24 +193,19 @@
     return pairs
 
 
-def group_pieces(refs):
-    out = [*refs[:3], (refs[3], refs[4]), *refs[5:8]]
-    if len(refs) > 8:
-        out += [(refs[8], refs[9]), *refs[10:12]]
-    return out
-
-
-def early_kernel(order_ref, row_ref, pairs_ref, near, *refs):
-    pieces, (acc, blocks, panel, sems) = refs[:8], refs[8:]
+def early_kernel(order_ref, row_ref, pairs_ref, *refs):
+    parts, pieces, (acc, blocks, panel, sems) = refs[:3], refs[3:11], refs[11:]
     lists = (order_ref, row_ref, pairs_ref)
-    run(0, lists, [near], group_pieces(pieces), panel, blocks, acc, None, sems)
+    grouped = [*pieces[:3], (pieces[3], pieces[4]), *pieces[5:]]
+    run(0, lists, parts, grouped, panel, blocks, acc, None, sems)
 
 
 def main_kernel(order_ref, row_ref, pairs_ref, *refs):
-    parts, before, pieces = refs[:9], refs[9], refs[10:22]
-    blocks, acc, panel, sems = refs[22:]
+    parts, before, pieces = refs[:3], refs[3], refs[4:16]
+    blocks, acc, panel, sems = refs[16:]
     lists = (order_ref, row_ref, pairs_ref)
-    run(1, lists, parts, group_pieces(pieces), panel, blocks, acc, before, sems)
+    grouped = [*pieces[:3], (pieces[3], pieces[4]), *pieces[5:8], (pieces[8], pieces[9]), *pieces[10:]]
+    run(1, lists, parts, grouped, panel, blocks, acc, before, sems)
 
 
 def last_kernel(
@@ -219,7 +214,6 @@
     pairs_ref,
     end_up,
     end_down,
-    other_third,
     other_end,
     blocks,
     before,
@@ -234,7 +228,7 @@
     sems,
 ):
     copies, at = [], 0
-    for n, part in enumerate((end_up, end_down, other_third, other_end)):
+    for n, part in enumerate((end_up, end_down, other_end)):
         copies.append(pltpu.make_async_copy(part, panel.at[pl.ds(at, part.shape[0])], sems.at[n]))
         at += part.shape[0]
     for copy in copies:
@@ -288,6 +282,31 @@
     return pltpu.with_memory_space_constraint(array, pltpu.HBM)
 
 
+def pack_kernel(*refs):
+    parts, out, sems = refs[:-2], refs[-2], refs[-1]
+    copies, at = [], 0
+    for n, part in enumerate(parts):
+        copies.append(pltpu.make_async_copy(part, out.at[pl.ds(at, part.shape[0])], sems.at[n]))
+        at += part.shape[0]
+    for copy in copies:
+        copy.start()
+    for copy in copies:
+        copy.wait()
+
+
+def pack(parts):
+    return pl.pallas_call(
+        pack_kernel,
+        in_specs=[ANY] * len(parts),
+        out_specs=ANY,
+        out_shape=jax.ShapeDtypeStruct((blocks_of(parts), BLOCK, 2 * BLOCK), jnp.bfloat16),
+        scratch_shapes=[pltpu.SemaphoreType.DMA((len(parts),))],
+        compiler_params=pltpu.CompilerParams(vmem_limit_bytes=2**16),
+        cost_estimate=cost(3),
+        name="pack",
+    )(*map(in_hbm, parts))
+
+
 def held(array):
     return pltpu.with_memory_space_constraint(array, pltpu.VMEM)
 
@@ -296,56 +315,61 @@
     return pl.CostEstimate(flops=0, bytes_accessed=int(micros * 3.0e6), transcendentals=0)
 
 
-def early_products(lists, rows, near, pieces):
+def blocks_of(parts):
+    return sum(a.shape[0] for a in parts)
+
+
+def early_products(lists, rows, parts, pieces):
+    args = [*parts, *pieces]
     return pl.pallas_call(
         early_kernel,
-        in_specs=[SMEM] * 3 + [ANY] * (1 + len(pieces)),
+        in_specs=[SMEM] * 3 + [ANY] * len(args),
         out_specs=VMEM,
         out_shape=jax.ShapeDtypeStruct((rows, 2 * BLOCK, 2 * BLOCK), jnp.float32),
         scratch_shapes=[
             pltpu.VMEM((2, EARLY, rows, BLOCK, BLOCK), jnp.bfloat16),
-            pltpu.VMEM(near.shape, jnp.bfloat16),
-            pltpu.SemaphoreType.DMA((1 + 2 * len(pieces),)),
+            pltpu.VMEM((blocks_of(parts), BLOCK, 2 * BLOCK), jnp.bfloat16),
+            pltpu.SemaphoreType.DMA((len(parts) + 2 * len(pieces),)),
         ],
-        compiler_params=pltpu.CompilerParams(vmem_limit_bytes=24 * 2**20),
+        compiler_params=pltpu.CompilerParams(vmem_limit_bytes=26 * 2**20),
         cost_estimate=cost(10),
         name="products_early",
-    )(*lists, in_hbm(near), *map(in_hbm, pieces))
+    )(*lists, *map(in_hbm, args))
 
 
 def main_products(lists, parts, before, pieces):
-    rows = before.shape[0]
+    args = [*parts, before, *pieces]
     return pl.pallas_call(
         main_kernel,
-        in_specs=[SMEM] * 3 + [ANY] * (len(parts) + 1 + len(pieces)),
+        in_specs=[SMEM] * 3 + [ANY] * len(args),
         out_specs=[VMEM, VMEM],
         out_shape=[
-            pltpu.VMEM((2, 24, rows, BLOCK, BLOCK), jnp.bfloat16),
+            pltpu.VMEM((2, 24, before.shape[0], BLOCK, BLOCK), jnp.bfloat16),
             pltpu.VMEM(before.shape, jnp.float32),
         ],
         scratch_shapes=[
-            pltpu.VMEM((sum(a.shape[0] for a in parts), BLOCK, 2 * BLOCK), jnp.bfloat16),
+            pltpu.VMEM((blocks_of(parts), BLOCK, 2 * BLOCK), jnp.bfloat16),
             pltpu.SemaphoreType.DMA((len(parts) + 1 + 2 * len(pieces),)),
         ],
-        compiler_params=pltpu.CompilerParams(vmem_limit_bytes=17 * 2**20),
+        compiler_params=pltpu.CompilerParams(vmem_limit_bytes=15 * 2**20),
         cost_estimate=cost(10),
         name="products_main",
-    )(*lists, *map(in_hbm, parts), in_hbm(before), *map(in_hbm, pieces))
+    )(*lists, *map(in_hbm, args))
 
 
 def last_products(lists, parts, blocks, before, *flat):
     rows = before.shape[0]
     return pl.pallas_call(
         last_kernel,
-        in_specs=[SMEM] * 3 + [ANY] * 4 + [VMEM] * 6,
+        in_specs=[SMEM] * 3 + [ANY] * len(parts) + [VMEM] * 6,
         out_specs=[VMEM] * 2,
         out_shape=[jax.ShapeDtypeStruct((rows * BLOCK, BLOCK), jnp.float32)] * 2,
         scratch_shapes=[
             pltpu.VMEM(before.shape, jnp.float32),
-            pltpu.VMEM((sum(a.shape[0] for a in parts), BLOCK, 2 * BLOCK), jnp.bfloat16),
-            pltpu.SemaphoreType.DMA((4,)),
+            pltpu.VMEM((blocks_of(parts), BLOCK, 2 * BLOCK), jnp.bfloat16),
+            pltpu.SemaphoreType.DMA((len(parts),)),
         ],
-        compiler_params=pltpu.CompilerParams(vmem_limit_bytes=9 * 2**20),
+        compiler_params=pltpu.CompilerParams(vmem_limit_bytes=11 * 2**20),
         cost_estimate=cost(4),
         name="products_last",
     )(*lists, *parts, held(blocks), held(before), *flat)
@@ -367,40 +391,48 @@
     both = jnp.stack([ham_blocks.swapaxes(0, 1), margin_blocks.swapaxes(0, 1)], axis=0)
     panel = jnp.concatenate([pert_real, pert_imag], axis=1).reshape(rows, BLOCK, 2 * BLOCK)
 
-    near = lax.all_gather(panel, ("z", "core"), axis=0, tiled=True)
     from_left = shift(both, "x", 1)
     from_right = shift(both, "x", -1)
-    part = shift(both[:, :2], "yhi")
     neighbour = shift(panel, "ylo")
-    lists = make_lists(place, block_cols, block_counts)
-    up1, down1 = shift(neighbour, "z", 1), shift(neighbour, "z", -1)
+    own_up, own_down = shift(panel, "z", 1), shift(panel, "z", -1)
+
+    part = shift(after(both[:, :2], neighbour), "yhi")
+    up1 = jnp.concatenate([own_up, shift(neighbour, "z", 1)], axis=0)
+    down1 = jnp.concatenate([own_down, shift(neighbour, "z", -1)], axis=0)
 
     far_ham = shift(from_left[0], "x", 1)
     far_margin = shift(from_right[1], "x", -1)
+    up2, down2 = shift(up1, "z", 1), shift(down1, "z", -1)
     late = shift(
         after(jnp.concatenate([both[:, 2:], from_left[:, 2:], from_right[:, 2:]], axis=1), part),
         "yhi",
     )
-    up2, down2 = shift(up1, "z", 1), shift(down1, "z", -1)
-
-    part = after(part, far_ham, far_margin, lists[0])
-    part_left = shift(part, "x", 1)
-    part_right = shift(part, "x", -1)
+    lists = make_lists(after(place, far_ham, far_margin), block_cols, block_counts)
+
+    part_on = after(part, far_ham, far_margin)
+    part_left = shift(part_on, "x", 1)
+    part_right = shift(part_on, "x", -1)
     up3, down3 = shift(up2, "z", 1), shift(down2, "z", -1)
+    come = (panel, neighbour, up1, down1, up2, down2)
+    both_come = lax.all_to_all(pack(come + come), "core", 0, 0, tiled=True)
     late_far = shift(
-        after(jnp.stack([far_ham[2:], far_margin[2:]], axis=0), late, part_left, part_right), "yhi"
+        after(jnp.stack([far_ham[2:], far_margin[2:]], axis=0), late, part_left, part_right, lists[0], both_come),
+        "yhi",
     )
+
     part_far_ham = shift(part_left[0], "x", 1)
     part_far_margin = shift(part_right[1], "x", -1)
-    up4, down4 = shift(up3[: rows // 2], "z", 1), shift(down3[rows // 2 :], "z", -1)
-
-    early = (both, from_left, from_right, far_ham, far_margin, part, part_left, part_right)
-    acc = early_products(lists, rows, near, early)
-    other_first = shift(
+    up3 = after(up3, part_left, part_right, late, both_come)
+    down3 = after(down3, part_left, part_right, late, both_come)
+    up4, down4 = shift(up3[:rows], "z", 1), shift(down3[rows:], "z", -1)
+
+    early = (both, from_left, from_right, far_ham, far_margin, part_on, part_left, part_right)
+    pieces = early + (part_far_ham, part_far_margin, late, late_far)
+    panels = (both_come, up3, down3)
+    acc = early_products(lists, rows, panels, early)
+    other_end = shift(
         after(
-            jnp.concatenate([neighbour, up1, down1, up2, down2], axis=0),
-            up3,
-            down3,
+            jnp.concatenate([up3, down3, up4, down4], axis=0),
             late_far,
             part_far_ham,
             part_far_margin,
@@ -408,15 +440,10 @@
         ),
         "core",
     )
-    other_third = shift(jnp.concatenate([up3, down3], axis=0), "core")
-    other_end = shift(jnp.concatenate([up4, down4], axis=0), "core")
-
-    pieces = early + (part_far_ham, part_far_margin, late, late_far)
-    parts = (near, neighbour, up1, down1, up2, down2, up3, down3, other_first)
-    blocks, acc = main_products(lists, parts, acc, pieces)
+    blocks, acc = main_products(lists, panels, acc, pieces)
     new_real, new_imag = last_products(
         lists,
-        (up4, down4, other_third, other_end),
+        (up4, down4, other_end),
         blocks,
         acc,
         pert_real,

time: 183 us -> 145 us (0.79)
  waiting for transfers between devices: 67 us -> 21.2 us
  starting transfers between devices: 40.9 us -> 62.9 us
  between operations: 14.5 us -> 1.21 us
  local copies, waits for them, and re-layouts: 24 us -> 15.6 us
  Pallas kernels: 29.9 us -> 36.7 us
    ppermute x23, waiting for transfers between devices: 67 us -> 20.6 us  [shift(): return lax.ppermute(array, AXES, moves(axis, by))]
    ppermute x23, starting transfers between devices: 40.9 us -> 52.2 us  [shift(): return lax.ppermute(array, AXES, moves(axis, by))]
    all_to_all x0 -> x1, starting transfers between devices: none -> 10.8 us  [per_device(): both_come = lax.all_to_all(pack(come + come), 'core', 0, 0, tiled=True)]
    pallas_call x3 -> x4, Pallas kernels: 24.3 us -> 31.5 us  [the longest x1 11.6 us: early_products(): pl.pallas_call(early_kernel, in_specs=[SMEM] * 3 + [ANY] * len(args), out...]
    unnamed x68 -> x54, local copies, waits for them, and re-layouts: 13.5 us -> 9.04 us
    concatenate x2 -> x1, other arithmetic: 1.34 us -> 3.92 us  [per_device(): jnp.concatenate([up3, down3, up4, down4], axis=0)]
    slice x2, local copies, waits for them, and re-layouts: 0.04 us -> 2.24 us  [per_device(): up4, down4 = (shift(up3[:rows], 'z', 1), shift(down3[rows:], 'z', -1))]
    concatenate x1, other arithmetic: 1.99 us -> 0.06 us  [per_device(): jnp.concatenate([pert_real, pert_imag], axis=1)]
  transfers between devices with their start and end apart: 24 -> 24, of which waited for: 5 -> 8; matrix products, arithmetic and copies ran while one was open for 10% -> 9% of each run, Pallas kernels for 14% -> 22%
where the time goes in v6:
time: 145 us
  starting transfers between devices  62.9 us (43%)
  Pallas kernels  36.7 us (25%)
  waiting for transfers between devices  21.2 us (15%)
  local copies, waits for them, and re-layouts  15.6 us (11%)
  other arithmetic  7.44 us (5%)
    ppermute x23, starting transfers between devices, shift(): return lax.ppermute(array, AXES, moves(axis, by))  52.2 us
    ppermute x23, waiting for transfers between devices, shift(): return lax.ppermute(array, AXES, moves(axis, by))  20.6 us
    pallas_call x1, Pallas kernels, early_products(): pl.pallas_call(early_kernel, in_specs=[SMEM] * 3 + [ANY] * len(args), out...  11.6 us
    pallas_call x1, Pallas kernels, main_products(): pl.pallas_call(main_kernel, in_specs=[SMEM] * 3 + [ANY] * len(args), out_...  10.8 us
    all_to_all x1, starting transfers between devices, per_device(): both_come = lax.all_to_all(pack(come + come), 'core', 0, 0, tiled=True)  10.8 us
    unnamed x54, local copies, waits for them, and re-layouts  9.04 us
    pallas_call x1, Pallas kernels, make_lists(): pl.pallas_call(list_kernel, in_specs=[SMEM] * 3, out_specs=[SMEM] * 3, ou...  5.24 us
    pallas_call x1, Pallas kernels, last_products(): pl.pallas_call(last_kernel, in_specs=[SMEM] * 3 + [ANY] * len(parts) + [V...  4.94 us
  transfers between devices with their start and end apart: 24, of which 8 were waited for; matrix products, arithmetic and copies ran while one was open for 9% of the time, Pallas kernels for 22%

profile of v6, /device:TPU:1, one launch (start us, length us, event | category | flops | bytes accessed | tf_op | source)
XLA Modules:
  0.0 145.1 jit_solution(6296583866295827070)
XLA Ops:
  0.6 1.5 %copy_bitcast_fusion = (bf16[1,3,8,128,128]{4,3,2,1,0:T(8,128)(2,1)S(1)}, bf16[1,3,8,128,128]{4,3,2,1,0:T(8,128)(2,1)S(1)}) fusion(bf16[8,3,128,128]{3,2,1,0:T(8,128)(2,1)} %param.9, bf16[8,3,128,128]{3,2,1,0:T(8,128)(2,1)} %param.8), kind=kLoop, calls=%fused_computation.10 | loop fusion | bytes 3145728 | tf_op jit(solution)/shard_map/stack | solution.py:391
  2.1 0.0 copy-start.2
  2.1 0.0 copy-start.3
  2.1 0.1 pad_maximum_fusion.1.refs_3_.refs_4_
  2.3 2.1 %collective-permute-start = (bf16[2,3,8,128,128]{4,3,2,1,0:T(8,128)(2,1)S(1)}, bf16[2,3,8,128,128]{4,3,2,1,0:T(8,128)(2,1)S(1)}, u32[]{:S(2)}, u32[]{:S(2)}) collective-permute-start(bf16[2,3,8,128,128]{4,3,2,1,0:T(8,128)(2,1)S(1)} %pad_maximum_fusion.1.refs_3_.refs_4_), channel_id=1, source_target_pairs={{0,2},{1,3},{2,4},{3,5},{4,6},{5,7},{6,0},{7,1},{8,10},{9,11},{10,... | collective-permute-start | bytes 4718600 | tf_op jit(solution)/shard_map/ppermute | solution.py:33
  4.4 1.4 collective-permute-start.2
  5.8 0.1 pad_maximum_fusion.3
  5.8 0.0 copy-start.22
  5.9 1.5 %collective-permute-start.5 = (bf16[8,128,256]{2,1,0:T(8,128)(2,1)S(1)}, bf16[8,128,256]{2,1,0:T(8,128)(2,1)S(1)}, u32[]{:S(2)}, u32[]{:S(2)}) collective-permute-start(bf16[8,128,256]{2,1,0:T(8,128)(2,1)S(1)} %bitcast.26), channel_id=1, source_target_pairs={{0,128},{1,129},{2,130},{3,131},{4,132},{5,133},{6,134},{7,135},{8... | collective-permute-start | bytes 1572872 | tf_op jit(solution)/shard_map/ppermute | solution.py:33
  7.3 5.6 %collective-permute-start.13 = (bf16[8,128,256]{2,1,0:T(8,128)(2,1)S(1)}, bf16[8,128,256]{2,1,0:T(8,128)(2,1)S(1)}, u32[]{:S(2)}, u32[]{:S(2)}) collective-permute-start(bf16[8,128,256]{2,1,0:T(8,128)(2,1)S(1)} %bitcast.27), channel_id=1, source_target_pairs={{0,112},{1,113},{2,114},{3,115},{4,116},{5,117},{6,118},{7,119},{8... | collective-permute-start | bytes 1572872 | tf_op jit(solution)/shard_map/ppermute | solution.py:33
  12.9 0.0 collective-permute-start.4
  12.9 4.2 %collective-permute-done.5.refs_1_.refs_7_ = bf16[8,128,256]{2,1,0:T(8,128)(2,1)S(1)} collective-permute-done((bf16[8,128,256]{2,1,0:T(8,128)(2,1)S(1)}, bf16[8,128,256]{2,1,0:T(8,128)(2,1)S(1)}, u32[]{:S(2)}, u32[]{:S(2)}) %collective-permute-start.5) | collective-permute-done | bytes 524320 | tf_op jit(solution)/shard_map/ppermute | solution.py:33
  17.2 6.6 %collective-permute-start.14 = (bf16[8,128,256]{2,1,0:T(8,128)(2,1)S(1)}, bf16[8,128,256]{2,1,0:T(8,128)(2,1)S(1)}, u32[]{:S(2)}, u32[]{:S(2)}) collective-permute-start(bf16[8,128,256]{2,1,0:T(8,128)(2,1)S(1)} %collective-permute-done.5.refs_1_.refs_7_), channel_id=1, source_target_pairs={{0,112},{1,113},{2,114},{3,115},{4,116},{5,117},{6,118},{7,119},{8... | collective-permute-start | bytes 1572872 | tf_op jit(solution)/shard_map/ppermute | solution.py:33
  23.8 1.1 fusion.refs_0_
  24.9 0.8 collective-permute-done.4
  25.7 2.6 %collective-permute-start.9 = (bf16[2,2,8,128,128]{4,3,2,1,0:T(8,128)(2,1)}, bf16[2,2,8,128,128]{4,3,2,1,0:T(8,128)(2,1)S(1)}, u32[]{:S(2)}, u32[]{:S(2)}) collective-permute-start(bf16[2,2,8,128,128]{4,3,2,1,0:T(8,128)(2,1)} %gate.9), channel_id=1, source_target_pairs={{0,1},{1,0},{2,3},{3,2},{4,5},{5,4},{6,7},{7,6},{8,9},{9,8},{10,11... | collective-permute-start | bytes 3145736 | tf_op jit(solution)/shard_map/ppermute | solution.py:33
  28.4 5.2 %collective-permute-done.14 = bf16[8,128,256]{2,1,0:T(8,128)(2,1)S(1)} collective-permute-done((bf16[8,128,256]{2,1,0:T(8,128)(2,1)S(1)}, bf16[8,128,256]{2,1,0:T(8,128)(2,1)S(1)}, u32[]{:S(2)}, u32[]{:S(2)}) %collective-permute-start.14) | collective-permute-done | bytes 524320 | tf_op jit(solution)/shard_map/ppermute | solution.py:33
  33.6 3.5 %collective-permute-start.15 = (bf16[16,128,256]{2,1,0:T(8,128)(2,1)S(1)}, bf16[16,128,256]{2,1,0:T(8,128)(2,1)}, u32[]{:S(2)}, u32[]{:S(2)}) collective-permute-start(bf16[16,128,256]{2,1,0:T(8,128)(2,1)S(1)} %constant_dynamic-update-slice_fusion.2.refs_3_.refs_9_), channel_id=1, source_target_pairs={{0,112},{1,113},{2,114},{3,115},{4,116},{5,117},{6,118},{7,119},{8... | collective-permute-start | bytes 3145736 | tf_op jit(solution)/shard_map/ppermute | solution.py:33
  37.1 0.1 collective-permute-start.7
  37.2 0.3 collective-permute-done.refs_4_.refs_5_
  37.5 0.1 slice_bitcast_fusion.1
  37.6 2.0 %collective-permute-start.1 = (bf16[3,8,128,128]{3,2,1,0:T(8,128)(2,1)S(1)}, bf16[3,8,128,128]{3,2,1,0:T(8,128)(2,1)S(1)}, u32[]{:S(2)}, u32[]{:S(2)}) collective-permute-start(bf16[3,8,128,128]{3,2,1,0:T(8,128)(2,1)S(1)} %slice_bitcast_fusion.1), channel_id=1, source_target_pairs={{0,2},{1,3},{2,4},{3,5},{4,6},{5,7},{6,0},{7,1},{8,10},{9,11},{10,... | collective-permute-start | bytes 2359304 | tf_op jit(solution)/shard_map/ppermute | solution.py:33
  39.6 0.1 slice_bitcast_fusion
  39.6 1.8 %collective-permute-start.3 = (bf16[3,8,128,128]{3,2,1,0:T(8,128)(2,1)S(1)}, bf16[3,8,128,128]{3,2,1,0:T(8,128)(2,1)S(1)}, u32[]{:S(2)}, u32[]{:S(2)}) collective-permute-start(bf16[3,8,128,128]{3,2,1,0:T(8,128)(2,1)S(1)} %slice_bitcast_fusion), channel_id=1, source_target_pairs={{0,6},{1,7},{2,0},{3,1},{4,2},{5,3},{6,4},{7,5},{8,14},{9,15},{10,... | collective-permute-start | bytes 2359304 | tf_op jit(solution)/shard_map/ppermute | solution.py:33
  41.4 0.1 fusion.1
  41.6 1.3 pad_maximum_fusion.2.refs_0_
  42.9 6.2 %collective-permute-done.9.refs_0_.refs_1_ = bf16[2,2,8,128,128]{4,3,2,1,0:T(8,128)(2,1)S(1)} collective-permute-done((bf16[2,2,8,128,128]{4,3,2,1,0:T(8,128)(2,1)}, bf16[2,2,8,128,128]{4,3,2,1,0:T(8,128)(2,1)S(1)}, u32[]{:S(2)}, u32[]{:S(2)}) %collective-permute-start.9) | collective-permute-done | bytes 1048608 | tf_op jit(solution)/shard_map/ppermute | solution.py:33
  49.1 1.0 copy-done.13
  50.1 3.0 %collective-permute-start.12 = (bf16[2,3,8,128,128]{4,3,2,1,0:T(8,128)(2,1)}, bf16[2,3,8,128,128]{4,3,2,1,0:T(8,128)(2,1)}, u32[]{:S(2)}, u32[]{:S(2)}) collective-permute-start(bf16[2,3,8,128,128]{4,3,2,1,0:T(8,128)(2,1)} %gate.11), channel_id=1, source_target_pairs={{0,1},{1,0},{2,3},{3,2},{4,5},{5,4},{6,7},{7,6},{8,9},{9,8},{10,11... | collective-permute-start | bytes 4718600 | tf_op jit(solution)/shard_map/ppermute | solution.py:33
  53.1 3.1 %collective-permute-done.1.refs_1_.refs_6_.refs_7_ = bf16[3,8,128,128]{3,2,1,0:T(8,128)(2,1)S(1)} collective-permute-done((bf16[3,8,128,128]{3,2,1,0:T(8,128)(2,1)S(1)}, bf16[3,8,128,128]{3,2,1,0:T(8,128)(2,1)S(1)}, u32[]{:S(2)}, u32[]{:S(2)}) %collective-permute-start.1) | collective-permute-done | bytes 786464 | tf_op jit(solution)/shard_map/ppermute | solution.py:33
  56.2 0.8 collective-permute-done.3.refs_2_.refs_7_.refs_8_
  57.0 0.1 copy-done.14
  57.2 0.9 copy-done.15
  58.0 1.6 %collective-permute-start.10 = (bf16[2,2,8,128,128]{4,3,2,1,0:T(8,128)(2,1)}, bf16[2,2,8,128,128]{4,3,2,1,0:T(8,128)(2,1)S(1)}, u32[]{:S(2)}, u32[]{:S(2)}) collective-permute-start(bf16[2,2,8,128,128]{4,3,2,1,0:T(8,128)(2,1)} %gate.10.refs_8_.refs_9_), channel_id=1, source_target_pairs={{0,2},{1,3},{2,4},{3,5},{4,6},{5,7},{6,0},{7,1},{8,10},{9,11},{10,... | collective-permute-start | bytes 3145736 | tf_op jit(solution)/shard_map/ppermute | solution.py:33
  59.6 1.1 collective-permute-start.11
  60.7 8.2 %collective-permute-start.17 = (bf16[16,128,256]{2,1,0:T(8,128)(2,1)}, bf16[16,128,256]{2,1,0:T(8,128)(2,1)}, u32[]{:S(2)}, u32[]{:S(2)}) collective-permute-start(bf16[16,128,256]{2,1,0:T(8,128)(2,1)} %collective-permute-done.15.refs_5_.refs_11_), channel_id=1, source_target_pairs={{0,112},{1,113},{2,114},{3,115},{4,116},{5,117},{6,118},{7,119},{8... | collective-permute-start | bytes 3145736 | tf_op jit(solution)/shard_map/ppermute | solution.py:33
  68.9 0.6 stack.41.refs_0_
  69.5 4.2 %pack.1 = bf16[160,128,256]{2,1,0:T(8,128)(2,1)S(1)} custom-call(bf16[8,128,256]{2,1,0:T(8,128)(2,1)} %bitcast.29, bf16[8,128,256]{2,1,0:T(8,128)(2,1)} %copy-done.21, bf16[16,128,256]{2,1,0:T(8,128)(2,1)} %copy-done.19, bf16[16,128,256]{2,1,0:T(8,128)(2,1)} %copy-done.20, bf16[16,128,256]{2,1,0:T(8,128)(2,1)} %collective-permute-done.7.refs_4_.refs_10_, ...), custom_call_target="tpu_custom_call" | custom-call | bytes 9000000 | tf_op jit(solution)/shard_map/pack/pallas_call | solution.py:298
  73.7 3.8 %copy-done = bf16[160,128,256]{2,1,0:T(8,128)(2,1)} copy-done((bf16[160,128,256]{2,1,0:T(8,128)(2,1)}, bf16[160,128,256]{2,1,0:T(8,128)(2,1)S(1)}, u32[]{:S(2)}) %copy-start) | copy-done | bytes 10485784
  77.5 10.8 %all-to-all-start = ((bf16[160,128,256]{2,1,0:T(8,128)(2,1)}), bf16[160,128,256]{2,1,0:T(8,128)(2,1)}, u32[]{:S(2)}, u32[]{:S(2)}) async-start(bf16[160,128,256]{2,1,0:T(8,128)(2,1)} %copy-done), calls=%async_computation | async-start | bytes 20971520 | tf_op jit(solution)/shard_map/all_to_all | solution.py:417
  88.3 5.2 %make_lists.1 = (s32[3,200]{1,0:T(4,128)}, s32[3,100]{1,0:T(4,128)}, s32[6]{0:T(128)}) custom-call(s32[5]{0:T(128)} %gate.8.place_ref, s32[8,24]{1,0:T(8,128)} %cols_ref.1, s32[8]{0:T(128)} %counts_ref.1), custom_call_target="tpu_custom_call" | custom-call | tf_op jit(solution)/shard_map/make_lists/pallas_call | solution.py:111
  93.5 1.0 slice_bitcast_fusion.4
  94.5 1.0 slice_bitcast_fusion.5
  95.5 0.8 pad_maximum_fusion.4.refs_0_
  96.3 0.6 all-to-all-done.refs_4_.refs_5_.refs_0_
  96.9 0.9 copy-done.9
  97.9 0.4 copy-done.11
  98.3 2.9 %collective-permute-start.19 = (bf16[2,1,8,128,128]{4,3,2,1,0:T(8,128)(2,1)}, bf16[2,1,8,128,128]{4,3,2,1,0:T(8,128)(2,1)S(1)}, u32[]{:S(2)}, u32[]{:S(2)}) collective-permute-start(bf16[2,1,8,128,128]{4,3,2,1,0:T(8,128)(2,1)} %gate.14), channel_id=1, source_target_pairs={{0,1},{1,0},{2,3},{3,2},{4,5},{5,4},{6,7},{7,6},{8,9},{9,8},{10,11... | collective-permute-start | bytes 1572872 | tf_op jit(solution)/shard_map/ppermute | solution.py:33
  101.2 1.1 slice.57
  102.3 3.0 %collective-permute-start.18 = (bf16[8,128,256]{2,1,0:T(8,128)(2,1)S(1)}, bf16[8,128,256]{2,1,0:T(8,128)(2,1)S(1)}, u32[]{:S(2)}, u32[]{:S(2)}) collective-permute-start(bf16[8,128,256]{2,1,0:T(8,128)(2,1)S(1)} %slice.57), channel_id=1, source_target_pairs={{0,112},{1,113},{2,114},{3,115},{4,116},{5,117},{6,118},{7,119},{8... | collective-permute-start | bytes 1572872 | tf_op jit(solution)/shard_map/ppermute | solution.py:33
  105.3 1.2 slice.56
  106.5 0.1 collective-permute-start.16
  106.6 0.1 collective-permute-start.20
  106.8 2.7 %collective-permute-start.21 = (bf16[2,8,128,128]{3,2,1,0:T(8,128)(2,1)S(1)}, bf16[2,8,128,128]{3,2,1,0:T(8,128)(2,1)S(1)}, u32[]{:S(2)}, u32[]{:S(2)}) collective-permute-start(bf16[2,8,128,128]{3,2,1,0:T(8,128)(2,1)S(1)} %slice_bitcast_fusion.2), channel_id=1, source_target_pairs={{0,6},{1,7},{2,0},{3,1},{4,2},{5,3},{6,4},{7,5},{8,14},{9,15},{10,... | collective-permute-start | bytes 1572872 | tf_op jit(solution)/shard_map/ppermute | solution.py:33
  109.5 11.6 %products_early.1.refs_4_.refs_3_ = f32[8,256,256]{2,1,0:T(8,128)S(1)} custom-call(s32[3,200]{1,0:T(4,128)S(1)} %copy-done.6, s32[3,100]{1,0:T(4,128)S(1)} %copy-done.7, s32[6]{0:T(128)S(1)} %copy-done.8, bf16[160,128,256]{2,1,0:T(8,128)(2,1)} %all-to-all-done.refs_4_.refs_5_.refs_0_, bf16[16,128,256]{2,1,0:T(8,128)(2,1)} %gate.12.refs_1_, ...), custom_call_target="tpu_custom_call" | custom-call | bytes 30000000 | tf_op jit(solution)/shard_map/products_early/pallas_call | solution.py:324
  121.1 3.9 %pad_maximum_fusion.refs_0_ = bf16[48,128,256]{2,1,0:T(8,128)(2,1)} fusion(bf16[8,128,256]{2,1,0:T(8,128)(2,1)S(1)} %collective-permute-done.18.end_down, bf16[8,128,256]{2,1,0:T(8,128)(2,1)S(1)} %collective-permute-done.16.end_up, bf16[16,128,256]{2,1,0:T(8,128)(2,1)} %gate.13.refs_2_, bf16[16,128,256]{2,1,0:T(8,128)(2,1)} %gate.12.refs_1_), kind=kLoop, calls=%fused_computation | loop fusion | flops 4718592 | bytes 6291456 | tf_op jit(solution)/shard_map/concatenate | solution.py:435
  125.0 0.0 copy-start.23
  125.1 0.0 copy-start.24
  125.1 0.8 copy-done.23
  125.8 0.2 copy-done.24
  126.0 0.8 copy-done.25
  126.8 2.3 %collective-permute-start.22 = (bf16[48,128,256]{2,1,0:T(8,128)(2,1)}, bf16[48,128,256]{2,1,0:T(8,128)(2,1)S(1)}, u32[]{:S(2)}, u32[]{:S(2)}) collective-permute-start(bf16[48,128,256]{2,1,0:T(8,128)(2,1)} %gate.15), channel_id=1, source_target_pairs={{0,8},{1,9},{2,10},{3,11},{4,12},{5,13},{6,14},{7,15},{8,0},{9,1},... | collective-permute-start | bytes 9437192 | tf_op jit(solution)/shard_map/ppermute | solution.py:33
  129.1 10.8 %products_main.1 = (bf16[2,24,8,128,128]{4,3,2,1,0:T(8,128)(2,1)S(1)}, f32[8,256,256]{2,1,0:T(8,128)S(1)}) custom-call(s32[3,200]{1,0:T(4,128)S(1)} %copy-done.6, s32[3,100]{1,0:T(4,128)S(1)} %copy-done.7, s32[6]{0:T(128)S(1)} %copy-done.8, bf16[160,128,256]{2,1,0:T(8,128)(2,1)} %all-to-all-done.refs_4_.refs_5_.refs_0_, bf16[16,128,256]{2,1,0:T(8,128)(2,1)} %gate.12.refs_1_, ...), custom_call_target="tpu_custom_call" | custom-call | bytes 30000000 | tf_op jit(solution)/shard_map/products_main/pallas_call | solution.py:342
  140.0 4.9 %products_last.1 = (f32[1024,128]{1,0:T(8,128)}, f32[1024,128]{1,0:T(8,128)}) custom-call(s32[3,200]{1,0:T(4,128)S(1)} %copy-done.6, s32[3,100]{1,0:T(4,128)S(1)} %copy-done.7, s32[6]{0:T(128)S(1)} %copy-done.8, bf16[8,128,256]{2,1,0:T(8,128)(2,1)S(1)} %collective-permute-done.16.end_up, bf16[8,128,256]{2,1,0:T(8,128)(2,1)S(1)} %collective-permute-done.18.end_down, ...), custom_call_target="tpu_custom_call" | custom-call | bytes 12000000 | tf_op jit(solution)/shard_map/products_last/pallas_call | solution.py:362
  (72 shorter events, 0.4 us)
Async XLA Ops:
  2.1 3.7 %copy-start.2 = (bf16[1024,128]{1,0:T(8,128)(2,1)S(1)}, bf16[1024,128]{1,0:T(8,128)(2,1)}, u32[]{:S(2)}) copy-start(bf16[1024,128]{1,0:T(8,128)(2,1)} %pert_imag.1) | copy-start | bytes 786436
  2.1 3.7 %copy-start.3 = (bf16[1024,128]{1,0:T(8,128)(2,1)S(1)}, bf16[1024,128]{1,0:T(8,128)(2,1)}, u32[]{:S(2)}) copy-start(bf16[1024,128]{1,0:T(8,128)(2,1)} %pert_real.1) | copy-start | bytes 786436
  2.3 22.6 %copy-start.16 = (bf16[2,3,8,128,128]{4,3,2,1,0:T(8,128)(2,1)}, bf16[2,3,8,128,128]{4,3,2,1,0:T(8,128)(2,1)S(1)}, u32[]{:S(2)}) copy-start(bf16[2,3,8,128,128]{4,3,2,1,0:T(8,128)(2,1)S(1)} %pad_maximum_fusion.1.refs_3_.refs_4_) | copy-start | bytes 4718596
  2.3 35.2 %collective-permute-start = (bf16[2,3,8,128,128]{4,3,2,1,0:T(8,128)(2,1)S(1)}, bf16[2,3,8,128,128]{4,3,2,1,0:T(8,128)(2,1)S(1)}, u32[]{:S(2)}, u32[]{:S(2)}) collective-permute-start(bf16[2,3,8,128,128]{4,3,2,1,0:T(8,128)(2,1)S(1)} %pad_maximum_fusion.1.refs_3_.refs_4_), channel_id=1, source_target_pairs={{0,2},{1,3},{2,4},{3,5},{4,6},{5,7},{6,0},{7,1},{8,10},{9,11},{10,... | collective-permute-start | bytes 4718600 | tf_op jit(solution)/shard_map/ppermute | solution.py:33
  4.4 35.1 %collective-permute-start.2 = (bf16[2,3,8,128,128]{4,3,2,1,0:T(8,128)(2,1)S(1)}, bf16[2,3,8,128,128]{4,3,2,1,0:T(8,128)(2,1)S(1)}, u32[]{:S(2)}, u32[]{:S(2)}) collective-permute-start(bf16[2,3,8,128,128]{4,3,2,1,0:T(8,128)(2,1)S(1)} %pad_maximum_fusion.1.refs_3_.refs_4_), channel_id=1, source_target_pairs={{0,6},{1,7},{2,0},{3,1},{4,2},{5,3},{6,4},{7,5},{8,14},{9,15},{10,... | collective-permute-start | bytes 4718600 | tf_op jit(solution)/shard_map/ppermute | solution.py:33
  5.8 19.1 %copy-start.22 = (bf16[1024,256]{1,0:T(8,128)(2,1)}, bf16[1024,256]{1,0:T(8,128)(2,1)S(1)}, u32[]{:S(2)}) copy-start(bf16[1024,256]{1,0:T(8,128)(2,1)S(1)} %pad_maximum_fusion.3) | copy-start | bytes 1572868
  5.9 11.3 %collective-permute-start.5 = (bf16[8,128,256]{2,1,0:T(8,128)(2,1)S(1)}, bf16[8,128,256]{2,1,0:T(8,128)(2,1)S(1)}, u32[]{:S(2)}, u32[]{:S(2)}) collective-permute-start(bf16[8,128,256]{2,1,0:T(8,128)(2,1)S(1)} %bitcast.26), channel_id=1, source_target_pairs={{0,128},{1,129},{2,130},{3,131},{4,132},{5,133},{6,134},{7,135},{8... | collective-permute-start | bytes 1572872 | tf_op jit(solution)/shard_map/ppermute | solution.py:33
  7.3 16.5 %collective-permute-start.13 = (bf16[8,128,256]{2,1,0:T(8,128)(2,1)S(1)}, bf16[8,128,256]{2,1,0:T(8,128)(2,1)S(1)}, u32[]{:S(2)}, u32[]{:S(2)}) collective-permute-start(bf16[8,128,256]{2,1,0:T(8,128)(2,1)S(1)} %bitcast.27), channel_id=1, source_target_pairs={{0,112},{1,113},{2,114},{3,115},{4,116},{5,117},{6,118},{7,119},{8... | collective-permute-start | bytes 1572872 | tf_op jit(solution)/shard_map/ppermute | solution.py:33
  12.9 12.8 %collective-permute-start.4 = (bf16[8,128,256]{2,1,0:T(8,128)(2,1)S(1)}, bf16[8,128,256]{2,1,0:T(8,128)(2,1)S(1)}, u32[]{:S(2)}, u32[]{:S(2)}) collective-permute-start(bf16[8,128,256]{2,1,0:T(8,128)(2,1)S(1)} %bitcast.28), channel_id=1, source_target_pairs={{0,16},{1,17},{2,18},{3,19},{4,20},{5,21},{6,22},{7,23},{8,24},{9,... | collective-permute-start | bytes 1572872 | tf_op jit(solution)/shard_map/ppermute | solution.py:33
  17.2 7.7 %copy-start.21 = (bf16[8,128,256]{2,1,0:T(8,128)(2,1)}, bf16[8,128,256]{2,1,0:T(8,128)(2,1)S(1)}, u32[]{:S(2)}) copy-start(bf16[8,128,256]{2,1,0:T(8,128)(2,1)S(1)} %collective-permute-done.5.refs_1_.refs_7_) | copy-start | bytes 1572868
  17.2 16.4 %collective-permute-start.14 = (bf16[8,128,256]{2,1,0:T(8,128)(2,1)S(1)}, bf16[8,128,256]{2,1,0:T(8,128)(2,1)S(1)}, u32[]{:S(2)}, u32[]{:S(2)}) collective-permute-start(bf16[8,128,256]{2,1,0:T(8,128)(2,1)S(1)} %collective-permute-done.5.refs_1_.refs_7_), channel_id=1, source_target_pairs={{0,112},{1,113},{2,114},{3,115},{4,116},{5,117},{6,118},{7,119},{8... | collective-permute-start | bytes 1572872 | tf_op jit(solution)/shard_map/ppermute | solution.py:33
  23.8 13.3 %collective-permute-start.6 = (bf16[8,128,256]{2,1,0:T(8,128)(2,1)S(1)}, bf16[8,128,256]{2,1,0:T(8,128)(2,1)S(1)}, u32[]{:S(2)}, u32[]{:S(2)}) collective-permute-start(bf16[8,128,256]{2,1,0:T(8,128)(2,1)S(1)} %collective-permute-done.5.refs_1_.refs_7_), channel_id=1, source_target_pairs={{0,16},{1,17},{2,18},{3,19},{4,20},{5,21},{6,22},{7,23},{8,24},{9,... | collective-permute-start | bytes 1572872 | tf_op jit(solution)/shard_map/ppermute | solution.py:33
  25.7 23.4 %collective-permute-start.9 = (bf16[2,2,8,128,128]{4,3,2,1,0:T(8,128)(2,1)}, bf16[2,2,8,128,128]{4,3,2,1,0:T(8,128)(2,1)S(1)}, u32[]{:S(2)}, u32[]{:S(2)}) collective-permute-start(bf16[2,2,8,128,128]{4,3,2,1,0:T(8,128)(2,1)} %gate.9), channel_id=1, source_target_pairs={{0,1},{1,0},{2,3},{3,2},{4,5},{5,4},{6,7},{7,6},{8,9},{9,8},{10,11... | collective-permute-start | bytes 3145736 | tf_op jit(solution)/shard_map/ppermute | solution.py:33
  33.6 6.0 %copy-start.20 = (bf16[16,128,256]{2,1,0:T(8,128)(2,1)}, bf16[16,128,256]{2,1,0:T(8,128)(2,1)S(1)}, u32[]{:S(2)}) copy-start(bf16[16,128,256]{2,1,0:T(8,128)(2,1)S(1)} %constant_dynamic-update-slice_fusion.2.refs_3_.refs_9_) | copy-start | bytes 3145732
  33.6 27.1 %collective-permute-start.15 = (bf16[16,128,256]{2,1,0:T(8,128)(2,1)S(1)}, bf16[16,128,256]{2,1,0:T(8,128)(2,1)}, u32[]{:S(2)}, u32[]{:S(2)}) collective-permute-start(bf16[16,128,256]{2,1,0:T(8,128)(2,1)S(1)} %constant_dynamic-update-slice_fusion.2.refs_3_.refs_9_), channel_id=1, source_target_pairs={{0,112},{1,113},{2,114},{3,115},{4,116},{5,117},{6,118},{7,119},{8... | collective-permute-start | bytes 3145736 | tf_op jit(solution)/shard_map/ppermute | solution.py:33
  37.1 2.5 %copy-start.19 = (bf16[16,128,256]{2,1,0:T(8,128)(2,1)}, bf16[16,128,256]{2,1,0:T(8,128)(2,1)S(1)}, u32[]{:S(2)}) copy-start(bf16[16,128,256]{2,1,0:T(8,128)(2,1)S(1)} %constant_dynamic-update-slice_fusion.refs_2_.refs_8_) | copy-start | bytes 3145732
  37.1 31.8 %collective-permute-start.7 = (bf16[16,128,256]{2,1,0:T(8,128)(2,1)S(1)}, bf16[16,128,256]{2,1,0:T(8,128)(2,1)}, u32[]{:S(2)}, u32[]{:S(2)}) collective-permute-start(bf16[16,128,256]{2,1,0:T(8,128)(2,1)S(1)} %constant_dynamic-update-slice_fusion.refs_2_.refs_8_), channel_id=1, source_target_pairs={{0,16},{1,17},{2,18},{3,19},{4,20},{5,21},{6,22},{7,23},{8,24},{9,... | collective-permute-start | bytes 3145736 | tf_op jit(solution)/shard_map/ppermute | solution.py:33
  37.5 4.0 %copy-start.17 = (bf16[2,3,8,128,128]{4,3,2,1,0:T(8,128)(2,1)}, bf16[2,3,8,128,128]{4,3,2,1,0:T(8,128)(2,1)S(1)}, u32[]{:S(2)}) copy-start(bf16[2,3,8,128,128]{4,3,2,1,0:T(8,128)(2,1)S(1)} %collective-permute-done.refs_4_.refs_5_) | copy-start | bytes 4718596
  37.6 18.6 %collective-permute-start.1 = (bf16[3,8,128,128]{3,2,1,0:T(8,128)(2,1)S(1)}, bf16[3,8,128,128]{3,2,1,0:T(8,128)(2,1)S(1)}, u32[]{:S(2)}, u32[]{:S(2)}) collective-permute-start(bf16[3,8,128,128]{3,2,1,0:T(8,128)(2,1)S(1)} %slice_bitcast_fusion.1), channel_id=1, source_target_pairs={{0,2},{1,3},{2,4},{3,5},{4,6},{5,7},{6,0},{7,1},{8,10},{9,11},{10,... | collective-permute-start | bytes 2359304 | tf_op jit(solution)/shard_map/ppermute | solution.py:33
  39.6 2.0 %copy-start.18 = (bf16[2,3,8,128,128]{4,3,2,1,0:T(8,128)(2,1)}, bf16[2,3,8,128,128]{4,3,2,1,0:T(8,128)(2,1)S(1)}, u32[]{:S(2)}) copy-start(bf16[2,3,8,128,128]{4,3,2,1,0:T(8,128)(2,1)S(1)} %collective-permute-done.2.refs_5_.refs_6_) | copy-start | bytes 4718596
  39.6 17.4 %collective-permute-start.3 = (bf16[3,8,128,128]{3,2,1,0:T(8,128)(2,1)S(1)}, bf16[3,8,128,128]{3,2,1,0:T(8,128)(2,1)S(1)}, u32[]{:S(2)}, u32[]{:S(2)}) collective-permute-start(bf16[3,8,128,128]{3,2,1,0:T(8,128)(2,1)S(1)} %slice_bitcast_fusion), channel_id=1, source_target_pairs={{0,6},{1,7},{2,0},{3,1},{4,2},{5,3},{6,4},{7,5},{8,14},{9,15},{10,... | collective-permute-start | bytes 2359304 | tf_op jit(solution)/shard_map/ppermute | solution.py:33
  49.1 1.0 copy-start.13
  50.1 46.8 %collective-permute-start.12 = (bf16[2,3,8,128,128]{4,3,2,1,0:T(8,128)(2,1)}, bf16[2,3,8,128,128]{4,3,2,1,0:T(8,128)(2,1)}, u32[]{:S(2)}, u32[]{:S(2)}) collective-permute-start(bf16[2,3,8,128,128]{4,3,2,1,0:T(8,128)(2,1)} %gate.11), channel_id=1, source_target_pairs={{0,1},{1,0},{2,3},{3,2},{4,5},{5,4},{6,7},{7,6},{8,9},{9,8},{10,11... | collective-permute-start | bytes 4718600 | tf_op jit(solution)/shard_map/ppermute | solution.py:33
  56.2 0.9 copy-start.14
  57.1 0.9 copy-start.15
  58.0 38.9 %collective-permute-start.10 = (bf16[2,2,8,128,128]{4,3,2,1,0:T(8,128)(2,1)}, bf16[2,2,8,128,128]{4,3,2,1,0:T(8,128)(2,1)S(1)}, u32[]{:S(2)}, u32[]{:S(2)}) collective-permute-start(bf16[2,2,8,128,128]{4,3,2,1,0:T(8,128)(2,1)} %gate.10.refs_8_.refs_9_), channel_id=1, source_target_pairs={{0,2},{1,3},{2,4},{3,5},{4,6},{5,7},{6,0},{7,1},{8,10},{9,11},{10,... | collective-permute-start | bytes 3145736 | tf_op jit(solution)/shard_map/ppermute | solution.py:33
  59.6 37.3 %collective-permute-start.11 = (bf16[2,2,8,128,128]{4,3,2,1,0:T(8,128)(2,1)}, bf16[2,2,8,128,128]{4,3,2,1,0:T(8,128)(2,1)S(1)}, u32[]{:S(2)}, u32[]{:S(2)}) collective-permute-start(bf16[2,2,8,128,128]{4,3,2,1,0:T(8,128)(2,1)} %gate.10.refs_8_.refs_9_), channel_id=1, source_target_pairs={{0,6},{1,7},{2,0},{3,1},{4,2},{5,3},{6,4},{7,5},{8,14},{9,15},{10,... | collective-permute-start | bytes 3145736 | tf_op jit(solution)/shard_map/ppermute | solution.py:33
  60.7 40.5 %collective-permute-start.17 = (bf16[16,128,256]{2,1,0:T(8,128)(2,1)}, bf16[16,128,256]{2,1,0:T(8,128)(2,1)}, u32[]{:S(2)}, u32[]{:S(2)}) collective-permute-start(bf16[16,128,256]{2,1,0:T(8,128)(2,1)} %collective-permute-done.15.refs_5_.refs_11_), channel_id=1, source_target_pairs={{0,112},{1,113},{2,114},{3,115},{4,116},{5,117},{6,118},{7,119},{8... | collective-permute-start | bytes 3145736 | tf_op jit(solution)/shard_map/ppermute | solution.py:33
  68.9 36.4 %collective-permute-start.8 = (bf16[16,128,256]{2,1,0:T(8,128)(2,1)}, bf16[16,128,256]{2,1,0:T(8,128)(2,1)}, u32[]{:S(2)}, u32[]{:S(2)}) collective-permute-start(bf16[16,128,256]{2,1,0:T(8,128)(2,1)} %collective-permute-done.7.refs_4_.refs_10_), channel_id=1, source_target_pairs={{0,16},{1,17},{2,18},{3,19},{4,20},{5,21},{6,22},{7,23},{8,24},{9,... | collective-permute-start | bytes 3145736 | tf_op jit(solution)/shard_map/ppermute | solution.py:33
  73.6 3.9 %copy-start = (bf16[160,128,256]{2,1,0:T(8,128)(2,1)}, bf16[160,128,256]{2,1,0:T(8,128)(2,1)S(1)}, u32[]{:S(2)}) copy-start(bf16[160,128,256]{2,1,0:T(8,128)(2,1)S(1)} %pack.1) | copy-start | bytes 31457284
  77.5 19.4 %all-to-all-start = ((bf16[160,128,256]{2,1,0:T(8,128)(2,1)}), bf16[160,128,256]{2,1,0:T(8,128)(2,1)}, u32[]{:S(2)}, u32[]{:S(2)}) async-start(bf16[160,128,256]{2,1,0:T(8,128)(2,1)} %copy-done), calls=%async_computation | async-start | bytes 20971520 | tf_op jit(solution)/shard_map/all_to_all | solution.py:417
  96.9 1.0 copy-start.9
  96.9 1.3 copy-start.11
  98.3 26.8 %collective-permute-start.19 = (bf16[2,1,8,128,128]{4,3,2,1,0:T(8,128)(2,1)}, bf16[2,1,8,128,128]{4,3,2,1,0:T(8,128)(2,1)S(1)}, u32[]{:S(2)}, u32[]{:S(2)}) collective-permute-start(bf16[2,1,8,128,128]{4,3,2,1,0:T(8,128)(2,1)} %gate.14), channel_id=1, source_target_pairs={{0,1},{1,0},{2,3},{3,2},{4,5},{5,4},{6,7},{7,6},{8,9},{9,8},{10,11... | collective-permute-start | bytes 1572872 | tf_op jit(solution)/shard_map/ppermute | solution.py:33
  102.2 4.3 %copy-start.10 = (bf16[2,2,8,128,128]{4,3,2,1,0:T(8,128)(2,1)S(1)}, bf16[2,2,8,128,128]{4,3,2,1,0:T(8,128)(2,1)}, u32[]{:S(2)}) copy-start(bf16[2,2,8,128,128]{4,3,2,1,0:T(8,128)(2,1)} %copy-done.9) | copy-start | bytes 3145732
  102.3 18.8 %collective-permute-start.18 = (bf16[8,128,256]{2,1,0:T(8,128)(2,1)S(1)}, bf16[8,128,256]{2,1,0:T(8,128)(2,1)S(1)}, u32[]{:S(2)}, u32[]{:S(2)}) collective-permute-start(bf16[8,128,256]{2,1,0:T(8,128)(2,1)S(1)} %slice.57), channel_id=1, source_target_pairs={{0,112},{1,113},{2,114},{3,115},{4,116},{5,117},{6,118},{7,119},{8... | collective-permute-start | bytes 1572872 | tf_op jit(solution)/shard_map/ppermute | solution.py:33
  105.3 1.4 copy-start.12
  105.3 4.2 %copy-start.6 = (s32[3,200]{1,0:T(4,128)S(1)}, s32[3,200]{1,0:T(4,128)}, u32[]{:S(2)}) copy-start(s32[3,200]{1,0:T(4,128)} %get-tuple-element.7.refs_4_.order_ref) | copy-start | bytes 7204
  105.3 4.2 %copy-start.7 = (s32[3,100]{1,0:T(4,128)S(1)}, s32[3,100]{1,0:T(4,128)}, u32[]{:S(2)}) copy-start(s32[3,100]{1,0:T(4,128)} %get-tuple-element.8.row_ref) | copy-start | bytes 3604
  105.3 4.2 %copy-start.8 = (s32[6]{0:T(128)S(1)}, s32[6]{0:T(128)}, u32[]{:S(2)}) copy-start(s32[6]{0:T(128)} %get-tuple-element.9.pairs_ref) | copy-start | bytes 76
  106.5 14.6 %collective-permute-start.16 = (bf16[8,128,256]{2,1,0:T(8,128)(2,1)S(1)}, bf16[8,128,256]{2,1,0:T(8,128)(2,1)S(1)}, u32[]{:S(2)}, u32[]{:S(2)}) collective-permute-start(bf16[8,128,256]{2,1,0:T(8,128)(2,1)S(1)} %slice.56), channel_id=1, source_target_pairs={{0,16},{1,17},{2,18},{3,19},{4,20},{5,21},{6,22},{7,23},{8,24},{9,... | collective-permute-start | bytes 1572872 | tf_op jit(solution)/shard_map/ppermute | solution.py:33
  106.6 18.4 %collective-permute-start.20 = (bf16[2,8,128,128]{3,2,1,0:T(8,128)(2,1)S(1)}, bf16[2,8,128,128]{3,2,1,0:T(8,128)(2,1)S(1)}, u32[]{:S(2)}, u32[]{:S(2)}) collective-permute-start(bf16[2,8,128,128]{3,2,1,0:T(8,128)(2,1)S(1)} %slice_bitcast_fusion.3), channel_id=1, source_target_pairs={{0,2},{1,3},{2,4},{3,5},{4,6},{5,7},{6,0},{7,1},{8,10},{9,11},{10,... | collective-permute-start | bytes 1572872 | tf_op jit(solution)/shard_map/ppermute | solution.py:33
  106.8 18.3 %collective-permute-start.21 = (bf16[2,8,128,128]{3,2,1,0:T(8,128)(2,1)S(1)}, bf16[2,8,128,128]{3,2,1,0:T(8,128)(2,1)S(1)}, u32[]{:S(2)}, u32[]{:S(2)}) collective-permute-start(bf16[2,8,128,128]{3,2,1,0:T(8,128)(2,1)S(1)} %slice_bitcast_fusion.2), channel_id=1, source_target_pairs={{0,6},{1,7},{2,0},{3,1},{4,2},{5,3},{6,4},{7,5},{8,14},{9,15},{10,... | collective-permute-start | bytes 1572872 | tf_op jit(solution)/shard_map/ppermute | solution.py:33
  121.1 4.0 %copy-start.1 = (f32[8,256,256]{2,1,0:T(8,128)}, f32[8,256,256]{2,1,0:T(8,128)S(1)}, u32[]{:S(2)}) copy-start(f32[8,256,256]{2,1,0:T(8,128)S(1)} %products_early.1.refs_4_.refs_3_) | copy-start | bytes 6291460
  125.0 0.8 copy-start.23
  125.1 0.9 copy-start.24
  126.0 0.8 copy-start.25
  126.8 13.2 %copy-start.4 = (bf16[1024,128]{1,0:T(8,128)(2,1)S(1)}, bf16[1024,128]{1,0:T(8,128)(2,1)}, u32[]{:S(2)}) copy-start(bf16[1024,128]{1,0:T(8,128)(2,1)} %drive_real.1) | copy-start | bytes 786436
  126.8 13.2 %copy-start.5 = (bf16[1024,128]{1,0:T(8,128)(2,1)S(1)}, bf16[1024,128]{1,0:T(8,128)(2,1)}, u32[]{:S(2)}) copy-start(bf16[1024,128]{1,0:T(8,128)(2,1)} %drive_imag.1) | copy-start | bytes 786436
  126.8 13.2 %collective-permute-start.22 = (bf16[48,128,256]{2,1,0:T(8,128)(2,1)}, bf16[48,128,256]{2,1,0:T(8,128)(2,1)S(1)}, u32[]{:S(2)}, u32[]{:S(2)}) collective-permute-start(bf16[48,128,256]{2,1,0:T(8,128)(2,1)} %gate.15), channel_id=1, source_target_pairs={{0,8},{1,9},{2,10},{3,11},{4,12},{5,13},{6,14},{7,15},{8,0},{9,1},... | collective-permute-start | bytes 9437192 | tf_op jit(solution)/shard_map/ppermute | solution.py:33

commit v7 on v6

--- a/solution.py
+++ b/solution.py
@@ -153,22 +153,19 @@
     return (lists[2][which] + STEP - 1) // STEP
 
 
-def run(which, lists, panel_parts, pieces, panel, blocks, acc, before, sems):
+def run(which, lists, early, pieces, offset, panel, blocks, acc, sems, fresh):
     half = blocks.shape[2] // 2
-    early, at = [], 0
-    for part in panel_parts:
-        early.append((part, panel.at[pl.ds(at, part.shape[0])]))
-        at += part.shape[0]
-    if before is not None:
-        early.append((before, acc))
-    rounds = [early + split_pieces(pieces, blocks, 0, half), split_pieces(pieces, blocks, half, half)]
+    rounds = [
+        early + split_pieces(pieces, blocks, offset, 0, half),
+        split_pieces(pieces, blocks, offset, half, half),
+    ]
     copies, used = [], 0
     for pairs in rounds:
         copies.append([pltpu.make_async_copy(a, b, sems.at[used + n]) for n, (a, b) in enumerate(pairs)])
         used += len(pairs)
     for copy in copies[0] + copies[1]:
         copy.start()
-    if before is None:
+    if fresh:
         acc[...] = jnp.zeros_like(acc)
     for copy in copies[0]:
         copy.wait()
@@ -179,8 +176,8 @@
     add_products(which, lists, blocks, panel, acc, middle, all_steps(which, lists))
 
 
-def split_pieces(pieces, blocks, first, rows):
-    pairs, at = [], 0
+def split_pieces(pieces, blocks, offset, first, rows):
+    pairs, at = [], offset
     lines = pl.ds(first, rows)
     for piece in pieces:
         if isinstance(piece, tuple):
@@ -194,18 +191,22 @@
 
 
 def early_kernel(order_ref, row_ref, pairs_ref, *refs):
-    parts, pieces, (acc, blocks, panel, sems) = refs[:3], refs[3:11], refs[11:]
+    parts, pieces, (panel, blocks, acc, token, sems) = refs[:3], refs[3:11], refs[11:]
     lists = (order_ref, row_ref, pairs_ref)
+    early, at = [], 0
+    for part in parts:
+        early.append((part, panel.at[pl.ds(at, part.shape[0])]))
+        at += part.shape[0]
     grouped = [*pieces[:3], (pieces[3], pieces[4]), *pieces[5:]]
-    run(0, lists, parts, grouped, panel, blocks, acc, None, sems)
-
-
-def main_kernel(order_ref, row_ref, pairs_ref, *refs):
-    parts, before, pieces = refs[:3], refs[3], refs[4:16]
-    blocks, acc, panel, sems = refs[16:]
+    run(0, lists, early, grouped, 0, panel, blocks, acc, sems, True)
+    token[...] = jnp.zeros_like(token)
+
+
+def main_kernel(order_ref, row_ref, pairs_ref, panel, *refs):
+    pieces, (blocks, acc, sems) = refs[2:6], refs[6:]
     lists = (order_ref, row_ref, pairs_ref)
-    grouped = [*pieces[:3], (pieces[3], pieces[4]), *pieces[5:8], (pieces[8], pieces[9]), *pieces[10:]]
-    run(1, lists, parts, grouped, panel, blocks, acc, before, sems)
+    grouped = [(pieces[0], pieces[1]), *pieces[2:]]
+    run(1, lists, [], grouped, EARLY, panel, blocks, acc, sems, False)
 
 
 def last_kernel(
@@ -214,6 +215,8 @@
     pairs_ref,
     end_up,
     end_down,
+    other_up,
+    other_down,
     other_end,
     blocks,
     before,
@@ -228,7 +231,7 @@
     sems,
 ):
     copies, at = [], 0
-    for n, part in enumerate((end_up, end_down, other_end)):
+    for n, part in enumerate((end_up, end_down, other_up, other_down, other_end)):
         copies.append(pltpu.make_async_copy(part, panel.at[pl.ds(at, part.shape[0])], sems.at[n]))
         at += part.shape[0]
     for copy in copies:
@@ -324,37 +327,32 @@
     return pl.pallas_call(
         early_kernel,
         in_specs=[SMEM] * 3 + [ANY] * len(args),
-        out_specs=VMEM,
-        out_shape=jax.ShapeDtypeStruct((rows, 2 * BLOCK, 2 * BLOCK), jnp.float32),
-        scratch_shapes=[
-            pltpu.VMEM((2, EARLY, rows, BLOCK, BLOCK), jnp.bfloat16),
+        out_specs=[VMEM] * 4,
+        out_shape=[
             pltpu.VMEM((blocks_of(parts), BLOCK, 2 * BLOCK), jnp.bfloat16),
-            pltpu.SemaphoreType.DMA((len(parts) + 2 * len(pieces),)),
+            pltpu.VMEM((2, 24, rows, BLOCK, BLOCK), jnp.bfloat16),
+            pltpu.VMEM((rows, 2 * BLOCK, 2 * BLOCK), jnp.float32),
+            jax.ShapeDtypeStruct((8, BLOCK), jnp.float32),
         ],
-        compiler_params=pltpu.CompilerParams(vmem_limit_bytes=26 * 2**20),
+        scratch_shapes=[pltpu.SemaphoreType.DMA((len(parts) + 2 * len(pieces),))],
+        compiler_params=pltpu.CompilerParams(vmem_limit_bytes=2 * 2**20),
         cost_estimate=cost(10),
         name="products_early",
     )(*lists, *map(in_hbm, args))
 
 
-def main_products(lists, parts, before, pieces):
-    args = [*parts, before, *pieces]
+def main_products(lists, panel, blocks, before, pieces):
     return pl.pallas_call(
         main_kernel,
-        in_specs=[SMEM] * 3 + [ANY] * len(args),
+        in_specs=[SMEM] * 3 + [VMEM] * 3 + [ANY] * len(pieces),
         out_specs=[VMEM, VMEM],
-        out_shape=[
-            pltpu.VMEM((2, 24, before.shape[0], BLOCK, BLOCK), jnp.bfloat16),
-            pltpu.VMEM(before.shape, jnp.float32),
-        ],
-        scratch_shapes=[
-            pltpu.VMEM((blocks_of(parts), BLOCK, 2 * BLOCK), jnp.bfloat16),
-            pltpu.SemaphoreType.DMA((len(parts) + 1 + 2 * len(pieces),)),
-        ],
-        compiler_params=pltpu.CompilerParams(vmem_limit_bytes=15 * 2**20),
-        cost_estimate=cost(10),
+        out_shape=[pltpu.VMEM(blocks.shape, blocks.dtype), pltpu.VMEM(before.shape, before.dtype)],
+        scratch_shapes=[pltpu.SemaphoreType.DMA((2 * len(pieces),))],
+        input_output_aliases={4: 0, 5: 1},
+        compiler_params=pltpu.CompilerParams(vmem_limit_bytes=2 * 2**20),
+        cost_estimate=cost(4),
         name="products_main",
-    )(*lists, *map(in_hbm, args))
+    )(*lists, held(panel), held(blocks), held(before), *map(in_hbm, pieces))
 
 
 def last_products(lists, parts, blocks, before, *flat):
@@ -427,23 +425,15 @@
     up4, down4 = shift(up3[:rows], "z", 1), shift(down3[rows:], "z", -1)
 
     early = (both, from_left, from_right, far_ham, far_margin, part_on, part_left, part_right)
-    pieces = early + (part_far_ham, part_far_margin, late, late_far)
-    panels = (both_come, up3, down3)
-    acc = early_products(lists, rows, panels, early)
-    other_end = shift(
-        after(
-            jnp.concatenate([up3, down3, up4, down4], axis=0),
-            late_far,
-            part_far_ham,
-            part_far_margin,
-            acc,
-        ),
-        "core",
-    )
-    blocks, acc = main_products(lists, panels, acc, pieces)
+    kept, blocks, acc, token = early_products(lists, rows, (both_come, up3, down3), early)
+    other_up = shift(after(up3, late_far, part_far_ham, part_far_margin, token), "core")
+    other_down = shift(after(down3, late_far, part_far_ham, part_far_margin, token), "core")
+    other_end = shift(jnp.concatenate([up4, down4], axis=0), "core")
+    late_ones = (part_far_ham, part_far_margin, late, late_far)
+    blocks, acc = main_products(lists, kept, blocks, acc, late_ones)
     new_real, new_imag = last_products(
         lists,
-        (up4, down4, other_end),
+        (up4, down4, other_up, other_down, other_end),
         blocks,
         acc,
         pert_real,

time: 145 us -> 136 us (0.938)
  Pallas kernels: 36.7 us -> 27.9 us
  other arithmetic: 7.44 us -> 3.64 us
  local copies, waits for them, and re-layouts: 15.6 us -> 17.7 us
    pallas_call x1, Pallas kernels: 10.8 us -> 3.36 us  [main_products(): pl.pallas_call(main_kernel, in_specs=[SMEM] * 3 + [VMEM] * 3 + [ANY] * le...]
    concatenate x1, other arithmetic: 3.92 us -> 0.09 us  [per_device(): other_end = shift(jnp.concatenate([up4, down4], axis=0), 'core')]
    ppermute x23 -> x25, waiting for transfers between devices: 20.6 us -> 21 us  [shift(): return lax.ppermute(array, AXES, moves(axis, by))]
    ppermute x23 -> x25, starting transfers between devices: 52.2 us -> 51.8 us  [shift(): return lax.ppermute(array, AXES, moves(axis, by))]
    unnamed x54 -> x50, local copies, waits for them, and re-layouts: 9.04 us -> 9.11 us
  transfers between devices with their start and end apart: 24 -> 26, of which waited for: 8 -> 9; matrix products, arithmetic and copies ran while one was open for 9% -> 8% of each run, Pallas kernels for 22% -> 18%
where the time goes in v7:
time: 136 us; the launch traced here: 135 us
  starting transfers between devices  62.7 us (46%)
  Pallas kernels  27.9 us (21%)
  waiting for transfers between devices  21.6 us (16%)
  local copies, waits for them, and re-layouts  17.7 us (13%)
  other arithmetic  3.64 us (3%)
    ppermute x25, starting transfers between devices, shift(): return lax.ppermute(array, AXES, moves(axis, by))  51.8 us
    ppermute x25, waiting for transfers between devices, shift(): return lax.ppermute(array, AXES, moves(axis, by))  21 us
    pallas_call x1, Pallas kernels, early_products(): pl.pallas_call(early_kernel, in_specs=[SMEM] * 3 + [ANY] * len(args), out...  11.3 us
    all_to_all x1, starting transfers between devices, per_device(): both_come = lax.all_to_all(pack(come + come), 'core', 0, 0, tiled=True)  10.9 us
    unnamed x50, local copies, waits for them, and re-layouts  9.11 us
    pallas_call x1, Pallas kernels, make_lists(): pl.pallas_call(list_kernel, in_specs=[SMEM] * 3, out_specs=[SMEM] * 3, ou...  5.24 us
    pallas_call x1, Pallas kernels, pack(): pl.pallas_call(pack_kernel, in_specs=[ANY] * len(parts), out_specs=ANY, o...  4.27 us
    pallas_call x1, Pallas kernels, last_products(): pl.pallas_call(last_kernel, in_specs=[SMEM] * 3 + [ANY] * len(parts) + [V...  3.69 us
  transfers between devices with their start and end apart: 26, of which 9 were waited for; matrix products, arithmetic and copies ran while one was open for 8% of the time, Pallas kernels for 18%

profile of v7, /device:TPU:1, one launch (start us, length us, event | category | flops | bytes accessed | tf_op | source)
XLA Modules:
  0.0 134.8 jit_solution(2320670365190917339)
XLA Ops:
  0.6 1.5 %copy_bitcast_fusion = (bf16[1,3,8,128,128]{4,3,2,1,0:T(8,128)(2,1)S(1)}, bf16[1,3,8,128,128]{4,3,2,1,0:T(8,128)(2,1)S(1)}) fusion(bf16[8,3,128,128]{3,2,1,0:T(8,128)(2,1)} %param.9, bf16[8,3,128,128]{3,2,1,0:T(8,128)(2,1)} %param.8), kind=kLoop, calls=%fused_computation.10 | loop fusion | bytes 3145728 | tf_op jit(solution)/shard_map/stack | solution.py:389
  2.1 0.1 pad_maximum_fusion.refs_3_
  2.3 2.1 %collective-permute-start = (bf16[2,3,8,128,128]{4,3,2,1,0:T(8,128)(2,1)S(1)}, bf16[2,3,8,128,128]{4,3,2,1,0:T(8,128)(2,1)S(1)}, u32[]{:S(2)}, u32[]{:S(2)}) collective-permute-start(bf16[2,3,8,128,128]{4,3,2,1,0:T(8,128)(2,1)S(1)} %pad_maximum_fusion.refs_3_), channel_id=1, source_target_pairs={{0,2},{1,3},{2,4},{3,5},{4,6},{5,7},{6,0},{7,1},{8,10},{9,11},{10,... | collective-permute-start | bytes 4718600 | tf_op jit(solution)/shard_map/ppermute | solution.py:33
  4.4 1.4 %collective-permute-start.2 = (bf16[2,3,8,128,128]{4,3,2,1,0:T(8,128)(2,1)S(1)}, bf16[2,3,8,128,128]{4,3,2,1,0:T(8,128)(2,1)S(1)}, u32[]{:S(2)}, u32[]{:S(2)}) collective-permute-start(bf16[2,3,8,128,128]{4,3,2,1,0:T(8,128)(2,1)S(1)} %pad_maximum_fusion.refs_3_), channel_id=1, source_target_pairs={{0,6},{1,7},{2,0},{3,1},{4,2},{5,3},{6,4},{7,5},{8,14},{9,15},{10,... | collective-permute-start | bytes 4718600 | tf_op jit(solution)/shard_map/ppermute | solution.py:33
  5.8 0.1 pad_maximum_fusion.3
  5.9 1.5 %collective-permute-start.5 = (bf16[8,128,256]{2,1,0:T(8,128)(2,1)S(1)}, bf16[8,128,256]{2,1,0:T(8,128)(2,1)S(1)}, u32[]{:S(2)}, u32[]{:S(2)}) collective-permute-start(bf16[8,128,256]{2,1,0:T(8,128)(2,1)S(1)} %bitcast.26), channel_id=1, source_target_pairs={{0,128},{1,129},{2,130},{3,131},{4,132},{5,133},{6,134},{7,135},{8... | collective-permute-start | bytes 1572872 | tf_op jit(solution)/shard_map/ppermute | solution.py:33
  7.3 5.6 %collective-permute-start.13 = (bf16[8,128,256]{2,1,0:T(8,128)(2,1)S(1)}, bf16[8,128,256]{2,1,0:T(8,128)(2,1)S(1)}, u32[]{:S(2)}, u32[]{:S(2)}) collective-permute-start(bf16[8,128,256]{2,1,0:T(8,128)(2,1)S(1)} %bitcast.27), channel_id=1, source_target_pairs={{0,112},{1,113},{2,114},{3,115},{4,116},{5,117},{6,118},{7,119},{8... | collective-permute-start | bytes 1572872 | tf_op jit(solution)/shard_map/ppermute | solution.py:33
  12.9 4.2 %collective-permute-done.5.refs_1_.refs_7_ = bf16[8,128,256]{2,1,0:T(8,128)(2,1)S(1)} collective-permute-done((bf16[8,128,256]{2,1,0:T(8,128)(2,1)S(1)}, bf16[8,128,256]{2,1,0:T(8,128)(2,1)S(1)}, u32[]{:S(2)}, u32[]{:S(2)}) %collective-permute-start.5) | collective-permute-done | bytes 524320 | tf_op jit(solution)/shard_map/ppermute | solution.py:33
  17.2 6.6 %collective-permute-start.14 = (bf16[8,128,256]{2,1,0:T(8,128)(2,1)S(1)}, bf16[8,128,256]{2,1,0:T(8,128)(2,1)S(1)}, u32[]{:S(2)}, u32[]{:S(2)}) collective-permute-start(bf16[8,128,256]{2,1,0:T(8,128)(2,1)S(1)} %collective-permute-done.5.refs_1_.refs_7_), channel_id=1, source_target_pairs={{0,112},{1,113},{2,114},{3,115},{4,116},{5,117},{6,118},{7,119},{8... | collective-permute-start | bytes 1572872 | tf_op jit(solution)/shard_map/ppermute | solution.py:33
  23.8 1.1 fusion.refs_0_
  25.0 0.7 collective-permute-done.4
  25.7 2.6 %collective-permute-start.9 = (bf16[2,2,8,128,128]{4,3,2,1,0:T(8,128)(2,1)}, bf16[2,2,8,128,128]{4,3,2,1,0:T(8,128)(2,1)S(1)}, u32[]{:S(2)}, u32[]{:S(2)}) collective-permute-start(bf16[2,2,8,128,128]{4,3,2,1,0:T(8,128)(2,1)} %gate.10), channel_id=1, source_target_pairs={{0,1},{1,0},{2,3},{3,2},{4,5},{5,4},{6,7},{7,6},{8,9},{9,8},{10,11... | collective-permute-start | bytes 3145736 | tf_op jit(solution)/shard_map/ppermute | solution.py:33
  28.4 5.2 %collective-permute-done.14 = bf16[8,128,256]{2,1,0:T(8,128)(2,1)S(1)} collective-permute-done((bf16[8,128,256]{2,1,0:T(8,128)(2,1)S(1)}, bf16[8,128,256]{2,1,0:T(8,128)(2,1)S(1)}, u32[]{:S(2)}, u32[]{:S(2)}) %collective-permute-start.14) | collective-permute-done | bytes 524320 | tf_op jit(solution)/shard_map/ppermute | solution.py:33
  33.6 3.5 %collective-permute-start.15 = (bf16[16,128,256]{2,1,0:T(8,128)(2,1)S(1)}, bf16[16,128,256]{2,1,0:T(8,128)(2,1)}, u32[]{:S(2)}, u32[]{:S(2)}) collective-permute-start(bf16[16,128,256]{2,1,0:T(8,128)(2,1)S(1)} %constant_dynamic-update-slice_fusion.2.refs_3_.refs_9_), channel_id=1, source_target_pairs={{0,112},{1,113},{2,114},{3,115},{4,116},{5,117},{6,118},{7,119},{8... | collective-permute-start | bytes 3145736 | tf_op jit(solution)/shard_map/ppermute | solution.py:33
  37.1 0.1 collective-permute-start.7
  37.2 0.3 collective-permute-done.refs_4_
  37.5 0.1 slice_bitcast_fusion.1
  37.6 2.0 %collective-permute-start.1 = (bf16[3,8,128,128]{3,2,1,0:T(8,128)(2,1)S(1)}, bf16[3,8,128,128]{3,2,1,0:T(8,128)(2,1)S(1)}, u32[]{:S(2)}, u32[]{:S(2)}) collective-permute-start(bf16[3,8,128,128]{3,2,1,0:T(8,128)(2,1)S(1)} %slice_bitcast_fusion.1), channel_id=1, source_target_pairs={{0,2},{1,3},{2,4},{3,5},{4,6},{5,7},{6,0},{7,1},{8,10},{9,11},{10,... | collective-permute-start | bytes 2359304 | tf_op jit(solution)/shard_map/ppermute | solution.py:33
  39.6 0.1 slice_bitcast_fusion
  39.6 1.8 %collective-permute-start.3 = (bf16[3,8,128,128]{3,2,1,0:T(8,128)(2,1)S(1)}, bf16[3,8,128,128]{3,2,1,0:T(8,128)(2,1)S(1)}, u32[]{:S(2)}, u32[]{:S(2)}) collective-permute-start(bf16[3,8,128,128]{3,2,1,0:T(8,128)(2,1)S(1)} %slice_bitcast_fusion), channel_id=1, source_target_pairs={{0,6},{1,7},{2,0},{3,1},{4,2},{5,3},{6,4},{7,5},{8,14},{9,15},{10,... | collective-permute-start | bytes 2359304 | tf_op jit(solution)/shard_map/ppermute | solution.py:33
  41.4 0.1 fusion.1
  41.6 1.3 pad_maximum_fusion.1.refs_0_
  42.9 6.2 %collective-permute-done.9.refs_0_.refs_1_ = bf16[2,2,8,128,128]{4,3,2,1,0:T(8,128)(2,1)S(1)} collective-permute-done((bf16[2,2,8,128,128]{4,3,2,1,0:T(8,128)(2,1)}, bf16[2,2,8,128,128]{4,3,2,1,0:T(8,128)(2,1)S(1)}, u32[]{:S(2)}, u32[]{:S(2)}) %collective-permute-start.9) | collective-permute-done | bytes 1048608 | tf_op jit(solution)/shard_map/ppermute | solution.py:33
  49.1 1.0 copy-done.11
  50.1 3.0 %collective-permute-start.12 = (bf16[2,3,8,128,128]{4,3,2,1,0:T(8,128)(2,1)}, bf16[2,3,8,128,128]{4,3,2,1,0:T(8,128)(2,1)S(1)}, u32[]{:S(2)}, u32[]{:S(2)}) collective-permute-start(bf16[2,3,8,128,128]{4,3,2,1,0:T(8,128)(2,1)} %gate.12), channel_id=1, source_target_pairs={{0,1},{1,0},{2,3},{3,2},{4,5},{5,4},{6,7},{7,6},{8,9},{9,8},{10,11... | collective-permute-start | bytes 4718600 | tf_op jit(solution)/shard_map/ppermute | solution.py:33
  53.1 3.1 %collective-permute-done.1.refs_1_.refs_6_ = bf16[3,8,128,128]{3,2,1,0:T(8,128)(2,1)S(1)} collective-permute-done((bf16[3,8,128,128]{3,2,1,0:T(8,128)(2,1)S(1)}, bf16[3,8,128,128]{3,2,1,0:T(8,128)(2,1)S(1)}, u32[]{:S(2)}, u32[]{:S(2)}) %collective-permute-start.1) | collective-permute-done | bytes 786464 | tf_op jit(solution)/shard_map/ppermute | solution.py:33
  56.2 0.8 collective-permute-done.3.refs_2_.refs_7_
  57.0 0.1 copy-done.12
  57.1 0.9 copy-done.13
  58.0 1.6 %collective-permute-start.10 = (bf16[2,2,8,128,128]{4,3,2,1,0:T(8,128)(2,1)}, bf16[2,2,8,128,128]{4,3,2,1,0:T(8,128)(2,1)S(1)}, u32[]{:S(2)}, u32[]{:S(2)}) collective-permute-start(bf16[2,2,8,128,128]{4,3,2,1,0:T(8,128)(2,1)} %gate.11.refs_8_), channel_id=1, source_target_pairs={{0,2},{1,3},{2,4},{3,5},{4,6},{5,7},{6,0},{7,1},{8,10},{9,11},{10,... | collective-permute-start | bytes 3145736 | tf_op jit(solution)/shard_map/ppermute | solution.py:33
  59.6 1.1 collective-permute-start.11
  60.7 8.1 %collective-permute-start.17 = (bf16[16,128,256]{2,1,0:T(8,128)(2,1)}, bf16[16,128,256]{2,1,0:T(8,128)(2,1)}, u32[]{:S(2)}, u32[]{:S(2)}) collective-permute-start(bf16[16,128,256]{2,1,0:T(8,128)(2,1)} %collective-permute-done.15.refs_5_.refs_11_), channel_id=1, source_target_pairs={{0,112},{1,113},{2,114},{3,115},{4,116},{5,117},{6,118},{7,119},{8... | collective-permute-start | bytes 3145736 | tf_op jit(solution)/shard_map/ppermute | solution.py:33
  68.8 0.6 stack.41.refs_0_
  69.4 4.3 %pack.1 = bf16[160,128,256]{2,1,0:T(8,128)(2,1)S(1)} custom-call(bf16[8,128,256]{2,1,0:T(8,128)(2,1)} %bitcast.29, bf16[8,128,256]{2,1,0:T(8,128)(2,1)} %copy-done.22, bf16[16,128,256]{2,1,0:T(8,128)(2,1)} %copy-done.14, bf16[16,128,256]{2,1,0:T(8,128)(2,1)} %copy-done.15, bf16[16,128,256]{2,1,0:T(8,128)(2,1)} %collective-permute-done.7.refs_4_.refs_10_, ...), custom_call_target="tpu_custom_call" | custom-call | bytes 9000000 | tf_op jit(solution)/shard_map/pack/pallas_call | solution.py:301
  73.7 3.9 %copy-done = bf16[160,128,256]{2,1,0:T(8,128)(2,1)} copy-done((bf16[160,128,256]{2,1,0:T(8,128)(2,1)}, bf16[160,128,256]{2,1,0:T(8,128)(2,1)S(1)}, u32[]{:S(2)}) %copy-start) | copy-done | bytes 10485784
  77.6 10.9 %all-to-all-start = ((bf16[160,128,256]{2,1,0:T(8,128)(2,1)}), bf16[160,128,256]{2,1,0:T(8,128)(2,1)}, u32[]{:S(2)}, u32[]{:S(2)}) async-start(bf16[160,128,256]{2,1,0:T(8,128)(2,1)} %copy-done), calls=%async_computation | async-start | bytes 20971520 | tf_op jit(solution)/shard_map/all_to_all | solution.py:415
  88.5 5.2 %make_lists.1 = (s32[3,200]{1,0:T(4,128)}, s32[3,100]{1,0:T(4,128)}, s32[6]{0:T(128)}) custom-call(s32[5]{0:T(128)} %gate.9.place_ref, s32[8,24]{1,0:T(8,128)} %cols_ref.1, s32[8]{0:T(128)} %counts_ref.1), custom_call_target="tpu_custom_call" | custom-call | tf_op jit(solution)/shard_map/make_lists/pallas_call | solution.py:111
  93.7 1.0 slice_bitcast_fusion.4
  94.7 1.0 slice_bitcast_fusion.5
  95.7 0.8 pad_maximum_fusion.4.refs_0_
  96.5 0.6 all-to-all-done.refs_4_.refs_5_.refs_0_
  97.1 1.1 copy-done.9
  98.3 0.3 copy-done.10
  98.6 2.9 %collective-permute-start.19 = (bf16[2,1,8,128,128]{4,3,2,1,0:T(8,128)(2,1)}, bf16[2,1,8,128,128]{4,3,2,1,0:T(8,128)(2,1)S(1)}, u32[]{:S(2)}, u32[]{:S(2)}) collective-permute-start(bf16[2,1,8,128,128]{4,3,2,1,0:T(8,128)(2,1)} %gate.15), channel_id=1, source_target_pairs={{0,1},{1,0},{2,3},{3,2},{4,5},{5,4},{6,7},{7,6},{8,9},{9,8},{10,11... | collective-permute-start | bytes 1572872 | tf_op jit(solution)/shard_map/ppermute | solution.py:33
  101.5 1.1 slice_bitcast_fusion.3
  102.6 0.1 collective-permute-start.20
  102.7 1.1 slice.57
  103.8 3.0 %collective-permute-start.18 = (bf16[8,128,256]{2,1,0:T(8,128)(2,1)S(1)}, bf16[8,128,256]{2,1,0:T(8,128)(2,1)S(1)}, u32[]{:S(2)}, u32[]{:S(2)}) collective-permute-start(bf16[8,128,256]{2,1,0:T(8,128)(2,1)S(1)} %slice.57), channel_id=1, source_target_pairs={{0,112},{1,113},{2,114},{3,115},{4,116},{5,117},{6,118},{7,119},{8... | collective-permute-start | bytes 1572872 | tf_op jit(solution)/shard_map/ppermute | solution.py:33
  106.8 1.1 slice.56
  107.9 0.1 collective-permute-start.16
  108.0 1.1 slice_bitcast_fusion.2
  109.1 2.7 %collective-permute-start.21 = (bf16[2,8,128,128]{3,2,1,0:T(8,128)(2,1)S(1)}, bf16[2,8,128,128]{3,2,1,0:T(8,128)(2,1)S(1)}, u32[]{:S(2)}, u32[]{:S(2)}) collective-permute-start(bf16[2,8,128,128]{3,2,1,0:T(8,128)(2,1)S(1)} %slice_bitcast_fusion.2), channel_id=1, source_target_pairs={{0,6},{1,7},{2,0},{3,1},{4,2},{5,3},{6,4},{7,5},{8,14},{9,15},{10,... | collective-permute-start | bytes 1572872 | tf_op jit(solution)/shard_map/ppermute | solution.py:33
  111.8 11.3 %products_early.1 = (bf16[192,128,256]{2,1,0:T(8,128)(2,1)S(1)}, bf16[2,24,8,128,128]{4,3,2,1,0:T(8,128)(2,1)S(1)}, f32[8,256,256]{2,1,0:T(8,128)S(1)}, f32[8,128]{1,0:T(8,128)S(1)}) custom-call(s32[3,200]{1,0:T(4,128)S(1)} %copy-done.5, s32[3,100]{1,0:T(4,128)S(1)} %copy-done.6, s32[6]{0:T(128)S(1)} %copy-done.8, ...), custom_call_target="tpu_custom_call" | custom-call | bytes 30000000 | tf_op jit(solution)/shard_map/products_early/pallas_call | solution.py:327
  123.2 0.6 copy-done.7
  123.7 0.1 pad_maximum_fusion.2
  123.8 1.6 %collective-permute-start.24 = (bf16[16,128,256]{2,1,0:T(8,128)(2,1)S(1)}, bf16[16,128,256]{2,1,0:T(8,128)(2,1)S(1)}, u32[]{:S(2)}, u32[]{:S(2)}) collective-permute-start(bf16[16,128,256]{2,1,0:T(8,128)(2,1)S(1)} %pad_maximum_fusion.2), channel_id=1, source_target_pairs={{0,8},{1,9},{2,10},{3,11},{4,12},{5,13},{6,14},{7,15},{8,0},{9,1},... | collective-permute-start | bytes 3145736 | tf_op jit(solution)/shard_map/ppermute | solution.py:33
  125.5 0.8 copy-done.19
  126.2 0.2 copy-done.20
  126.4 0.2 copy-done.21
  126.6 0.0 collective-permute-start.23
  126.6 0.5 collective-permute-start.22
  127.1 3.4 %products_main.1 = (bf16[2,24,8,128,128]{4,3,2,1,0:T(8,128)(2,1)S(1)}, f32[8,256,256]{2,1,0:T(8,128)S(1)}) custom-call(s32[3,200]{1,0:T(4,128)S(1)} %copy-done.5, s32[3,100]{1,0:T(4,128)S(1)} %copy-done.6, s32[6]{0:T(128)S(1)} %copy-done.8, bf16[192,128,256]{2,1,0:T(8,128)(2,1)S(1)} %get-tuple-element.15.panel, ...), custom_call_target="tpu_custom_call", output_to_operand_aliasing={{0}: (4, {}), {1}: (5, {})} | custom-call | bytes 12000000 | tf_op jit(solution)/shard_map/products_main/pallas_call | solution.py:345
  130.5 0.5 collective-permute-done.22.other_up
  130.9 3.7 %products_last.1 = (f32[1024,128]{1,0:T(8,128)}, f32[1024,128]{1,0:T(8,128)}) custom-call(s32[3,200]{1,0:T(4,128)S(1)} %copy-done.5, s32[3,100]{1,0:T(4,128)S(1)} %copy-done.6, s32[6]{0:T(128)S(1)} %copy-done.8, bf16[8,128,256]{2,1,0:T(8,128)(2,1)S(1)} %collective-permute-done.16.end_up, bf16[8,128,256]{2,1,0:T(8,128)(2,1)S(1)} %collective-permute-done.18.end_down, ...), custom_call_target="tpu_custom_call" | custom-call | bytes 12000000 | tf_op jit(solution)/shard_map/products_last/pallas_call | solution.py:360
  (73 shorter events, 0.4 us)
Async XLA Ops:
  2.1 3.7 %copy-start.1 = (bf16[1024,128]{1,0:T(8,128)(2,1)S(1)}, bf16[1024,128]{1,0:T(8,128)(2,1)}, u32[]{:S(2)}) copy-start(bf16[1024,128]{1,0:T(8,128)(2,1)} %pert_imag.1) | copy-start | bytes 786436
  2.1 3.7 %copy-start.2 = (bf16[1024,128]{1,0:T(8,128)(2,1)S(1)}, bf16[1024,128]{1,0:T(8,128)(2,1)}, u32[]{:S(2)}) copy-start(bf16[1024,128]{1,0:T(8,128)(2,1)} %pert_real.1) | copy-start | bytes 786436
  2.3 22.7 %copy-start.16 = (bf16[2,3,8,128,128]{4,3,2,1,0:T(8,128)(2,1)}, bf16[2,3,8,128,128]{4,3,2,1,0:T(8,128)(2,1)S(1)}, u32[]{:S(2)}) copy-start(bf16[2,3,8,128,128]{4,3,2,1,0:T(8,128)(2,1)S(1)} %pad_maximum_fusion.refs_3_) | copy-start | bytes 4718596
  2.3 35.2 %collective-permute-start = (bf16[2,3,8,128,128]{4,3,2,1,0:T(8,128)(2,1)S(1)}, bf16[2,3,8,128,128]{4,3,2,1,0:T(8,128)(2,1)S(1)}, u32[]{:S(2)}, u32[]{:S(2)}) collective-permute-start(bf16[2,3,8,128,128]{4,3,2,1,0:T(8,128)(2,1)S(1)} %pad_maximum_fusion.refs_3_), channel_id=1, source_target_pairs={{0,2},{1,3},{2,4},{3,5},{4,6},{5,7},{6,0},{7,1},{8,10},{9,11},{10,... | collective-permute-start | bytes 4718600 | tf_op jit(solution)/shard_map/ppermute | solution.py:33
  4.4 35.1 %collective-permute-start.2 = (bf16[2,3,8,128,128]{4,3,2,1,0:T(8,128)(2,1)S(1)}, bf16[2,3,8,128,128]{4,3,2,1,0:T(8,128)(2,1)S(1)}, u32[]{:S(2)}, u32[]{:S(2)}) collective-permute-start(bf16[2,3,8,128,128]{4,3,2,1,0:T(8,128)(2,1)S(1)} %pad_maximum_fusion.refs_3_), channel_id=1, source_target_pairs={{0,6},{1,7},{2,0},{3,1},{4,2},{5,3},{6,4},{7,5},{8,14},{9,15},{10,... | collective-permute-start | bytes 4718600 | tf_op jit(solution)/shard_map/ppermute | solution.py:33
  5.8 19.1 %copy-start.23 = (bf16[1024,256]{1,0:T(8,128)(2,1)}, bf16[1024,256]{1,0:T(8,128)(2,1)S(1)}, u32[]{:S(2)}) copy-start(bf16[1024,256]{1,0:T(8,128)(2,1)S(1)} %pad_maximum_fusion.3) | copy-start | bytes 1572868
  5.9 11.3 %collective-permute-start.5 = (bf16[8,128,256]{2,1,0:T(8,128)(2,1)S(1)}, bf16[8,128,256]{2,1,0:T(8,128)(2,1)S(1)}, u32[]{:S(2)}, u32[]{:S(2)}) collective-permute-start(bf16[8,128,256]{2,1,0:T(8,128)(2,1)S(1)} %bitcast.26), channel_id=1, source_target_pairs={{0,128},{1,129},{2,130},{3,131},{4,132},{5,133},{6,134},{7,135},{8... | collective-permute-start | bytes 1572872 | tf_op jit(solution)/shard_map/ppermute | solution.py:33
  7.3 16.5 %collective-permute-start.13 = (bf16[8,128,256]{2,1,0:T(8,128)(2,1)S(1)}, bf16[8,128,256]{2,1,0:T(8,128)(2,1)S(1)}, u32[]{:S(2)}, u32[]{:S(2)}) collective-permute-start(bf16[8,128,256]{2,1,0:T(8,128)(2,1)S(1)} %bitcast.27), channel_id=1, source_target_pairs={{0,112},{1,113},{2,114},{3,115},{4,116},{5,117},{6,118},{7,119},{8... | collective-permute-start | bytes 1572872 | tf_op jit(solution)/shard_map/ppermute | solution.py:33
  12.9 12.8 %collective-permute-start.4 = (bf16[8,128,256]{2,1,0:T(8,128)(2,1)S(1)}, bf16[8,128,256]{2,1,0:T(8,128)(2,1)S(1)}, u32[]{:S(2)}, u32[]{:S(2)}) collective-permute-start(bf16[8,128,256]{2,1,0:T(8,128)(2,1)S(1)} %bitcast.28), channel_id=1, source_target_pairs={{0,16},{1,17},{2,18},{3,19},{4,20},{5,21},{6,22},{7,23},{8,24},{9,... | collective-permute-start | bytes 1572872 | tf_op jit(solution)/shard_map/ppermute | solution.py:33
  17.2 7.8 %copy-start.22 = (bf16[8,128,256]{2,1,0:T(8,128)(2,1)}, bf16[8,128,256]{2,1,0:T(8,128)(2,1)S(1)}, u32[]{:S(2)}) copy-start(bf16[8,128,256]{2,1,0:T(8,128)(2,1)S(1)} %collective-permute-done.5.refs_1_.refs_7_) | copy-start | bytes 1572868
  17.2 16.4 %collective-permute-start.14 = (bf16[8,128,256]{2,1,0:T(8,128)(2,1)S(1)}, bf16[8,128,256]{2,1,0:T(8,128)(2,1)S(1)}, u32[]{:S(2)}, u32[]{:S(2)}) collective-permute-start(bf16[8,128,256]{2,1,0:T(8,128)(2,1)S(1)} %collective-permute-done.5.refs_1_.refs_7_), channel_id=1, source_target_pairs={{0,112},{1,113},{2,114},{3,115},{4,116},{5,117},{6,118},{7,119},{8... | collective-permute-start | bytes 1572872 | tf_op jit(solution)/shard_map/ppermute | solution.py:33
  23.8 13.3 %collective-permute-start.6 = (bf16[8,128,256]{2,1,0:T(8,128)(2,1)S(1)}, bf16[8,128,256]{2,1,0:T(8,128)(2,1)S(1)}, u32[]{:S(2)}, u32[]{:S(2)}) collective-permute-start(bf16[8,128,256]{2,1,0:T(8,128)(2,1)S(1)} %collective-permute-done.5.refs_1_.refs_7_), channel_id=1, source_target_pairs={{0,16},{1,17},{2,18},{3,19},{4,20},{5,21},{6,22},{7,23},{8,24},{9,... | collective-permute-start | bytes 1572872 | tf_op jit(solution)/shard_map/ppermute | solution.py:33
  25.7 23.4 %collective-permute-start.9 = (bf16[2,2,8,128,128]{4,3,2,1,0:T(8,128)(2,1)}, bf16[2,2,8,128,128]{4,3,2,1,0:T(8,128)(2,1)S(1)}, u32[]{:S(2)}, u32[]{:S(2)}) collective-permute-start(bf16[2,2,8,128,128]{4,3,2,1,0:T(8,128)(2,1)} %gate.10), channel_id=1, source_target_pairs={{0,1},{1,0},{2,3},{3,2},{4,5},{5,4},{6,7},{7,6},{8,9},{9,8},{10,11... | collective-permute-start | bytes 3145736 | tf_op jit(solution)/shard_map/ppermute | solution.py:33
  33.6 6.0 %copy-start.15 = (bf16[16,128,256]{2,1,0:T(8,128)(2,1)}, bf16[16,128,256]{2,1,0:T(8,128)(2,1)S(1)}, u32[]{:S(2)}) copy-start(bf16[16,128,256]{2,1,0:T(8,128)(2,1)S(1)} %constant_dynamic-update-slice_fusion.2.refs_3_.refs_9_) | copy-start | bytes 3145732
  33.6 27.1 %collective-permute-start.15 = (bf16[16,128,256]{2,1,0:T(8,128)(2,1)S(1)}, bf16[16,128,256]{2,1,0:T(8,128)(2,1)}, u32[]{:S(2)}, u32[]{:S(2)}) collective-permute-start(bf16[16,128,256]{2,1,0:T(8,128)(2,1)S(1)} %constant_dynamic-update-slice_fusion.2.refs_3_.refs_9_), channel_id=1, source_target_pairs={{0,112},{1,113},{2,114},{3,115},{4,116},{5,117},{6,118},{7,119},{8... | collective-permute-start | bytes 3145736 | tf_op jit(solution)/shard_map/ppermute | solution.py:33
  37.1 2.5 %copy-start.14 = (bf16[16,128,256]{2,1,0:T(8,128)(2,1)}, bf16[16,128,256]{2,1,0:T(8,128)(2,1)S(1)}, u32[]{:S(2)}) copy-start(bf16[16,128,256]{2,1,0:T(8,128)(2,1)S(1)} %constant_dynamic-update-slice_fusion.refs_2_.refs_8_) | copy-start | bytes 3145732
  37.1 31.6 %collective-permute-start.7 = (bf16[16,128,256]{2,1,0:T(8,128)(2,1)S(1)}, bf16[16,128,256]{2,1,0:T(8,128)(2,1)}, u32[]{:S(2)}, u32[]{:S(2)}) collective-permute-start(bf16[16,128,256]{2,1,0:T(8,128)(2,1)S(1)} %constant_dynamic-update-slice_fusion.refs_2_.refs_8_), channel_id=1, source_target_pairs={{0,16},{1,17},{2,18},{3,19},{4,20},{5,21},{6,22},{7,23},{8,24},{9,... | collective-permute-start | bytes 3145736 | tf_op jit(solution)/shard_map/ppermute | solution.py:33
  37.5 4.0 %copy-start.17 = (bf16[2,3,8,128,128]{4,3,2,1,0:T(8,128)(2,1)}, bf16[2,3,8,128,128]{4,3,2,1,0:T(8,128)(2,1)S(1)}, u32[]{:S(2)}) copy-start(bf16[2,3,8,128,128]{4,3,2,1,0:T(8,128)(2,1)S(1)} %collective-permute-done.refs_4_) | copy-start | bytes 4718596
  37.6 18.6 %collective-permute-start.1 = (bf16[3,8,128,128]{3,2,1,0:T(8,128)(2,1)S(1)}, bf16[3,8,128,128]{3,2,1,0:T(8,128)(2,1)S(1)}, u32[]{:S(2)}, u32[]{:S(2)}) collective-permute-start(bf16[3,8,128,128]{3,2,1,0:T(8,128)(2,1)S(1)} %slice_bitcast_fusion.1), channel_id=1, source_target_pairs={{0,2},{1,3},{2,4},{3,5},{4,6},{5,7},{6,0},{7,1},{8,10},{9,11},{10,... | collective-permute-start | bytes 2359304 | tf_op jit(solution)/shard_map/ppermute | solution.py:33
  39.6 2.0 %copy-start.18 = (bf16[2,3,8,128,128]{4,3,2,1,0:T(8,128)(2,1)}, bf16[2,3,8,128,128]{4,3,2,1,0:T(8,128)(2,1)S(1)}, u32[]{:S(2)}) copy-start(bf16[2,3,8,128,128]{4,3,2,1,0:T(8,128)(2,1)S(1)} %collective-permute-done.2.refs_5_) | copy-start | bytes 4718596
  39.6 17.4 %collective-permute-start.3 = (bf16[3,8,128,128]{3,2,1,0:T(8,128)(2,1)S(1)}, bf16[3,8,128,128]{3,2,1,0:T(8,128)(2,1)S(1)}, u32[]{:S(2)}, u32[]{:S(2)}) collective-permute-start(bf16[3,8,128,128]{3,2,1,0:T(8,128)(2,1)S(1)} %slice_bitcast_fusion), channel_id=1, source_target_pairs={{0,6},{1,7},{2,0},{3,1},{4,2},{5,3},{6,4},{7,5},{8,14},{9,15},{10,... | collective-permute-start | bytes 2359304 | tf_op jit(solution)/shard_map/ppermute | solution.py:33
  49.1 1.0 copy-start.11
  50.1 47.0 %collective-permute-start.12 = (bf16[2,3,8,128,128]{4,3,2,1,0:T(8,128)(2,1)}, bf16[2,3,8,128,128]{4,3,2,1,0:T(8,128)(2,1)S(1)}, u32[]{:S(2)}, u32[]{:S(2)}) collective-permute-start(bf16[2,3,8,128,128]{4,3,2,1,0:T(8,128)(2,1)} %gate.12), channel_id=1, source_target_pairs={{0,1},{1,0},{2,3},{3,2},{4,5},{5,4},{6,7},{7,6},{8,9},{9,8},{10,11... | collective-permute-start | bytes 4718600 | tf_op jit(solution)/shard_map/ppermute | solution.py:33
  56.2 0.9 copy-start.12
  57.1 0.9 copy-start.13
  58.0 39.1 %collective-permute-start.10 = (bf16[2,2,8,128,128]{4,3,2,1,0:T(8,128)(2,1)}, bf16[2,2,8,128,128]{4,3,2,1,0:T(8,128)(2,1)S(1)}, u32[]{:S(2)}, u32[]{:S(2)}) collective-permute-start(bf16[2,2,8,128,128]{4,3,2,1,0:T(8,128)(2,1)} %gate.11.refs_8_), channel_id=1, source_target_pairs={{0,2},{1,3},{2,4},{3,5},{4,6},{5,7},{6,0},{7,1},{8,10},{9,11},{10,... | collective-permute-start | bytes 3145736 | tf_op jit(solution)/shard_map/ppermute | solution.py:33
  59.6 37.5 %collective-permute-start.11 = (bf16[2,2,8,128,128]{4,3,2,1,0:T(8,128)(2,1)}, bf16[2,2,8,128,128]{4,3,2,1,0:T(8,128)(2,1)}, u32[]{:S(2)}, u32[]{:S(2)}) collective-permute-start(bf16[2,2,8,128,128]{4,3,2,1,0:T(8,128)(2,1)} %gate.11.refs_8_), channel_id=1, source_target_pairs={{0,6},{1,7},{2,0},{3,1},{4,2},{5,3},{6,4},{7,5},{8,14},{9,15},{10,... | collective-permute-start | bytes 3145736 | tf_op jit(solution)/shard_map/ppermute | solution.py:33
  60.7 42.0 %collective-permute-start.17 = (bf16[16,128,256]{2,1,0:T(8,128)(2,1)}, bf16[16,128,256]{2,1,0:T(8,128)(2,1)}, u32[]{:S(2)}, u32[]{:S(2)}) collective-permute-start(bf16[16,128,256]{2,1,0:T(8,128)(2,1)} %collective-permute-done.15.refs_5_.refs_11_), channel_id=1, source_target_pairs={{0,112},{1,113},{2,114},{3,115},{4,116},{5,117},{6,118},{7,119},{8... | collective-permute-start | bytes 3145736 | tf_op jit(solution)/shard_map/ppermute | solution.py:33
  68.8 38.0 %collective-permute-start.8 = (bf16[16,128,256]{2,1,0:T(8,128)(2,1)}, bf16[16,128,256]{2,1,0:T(8,128)(2,1)}, u32[]{:S(2)}, u32[]{:S(2)}) collective-permute-start(bf16[16,128,256]{2,1,0:T(8,128)(2,1)} %collective-permute-done.7.refs_4_.refs_10_), channel_id=1, source_target_pairs={{0,16},{1,17},{2,18},{3,19},{4,20},{5,21},{6,22},{7,23},{8,24},{9,... | collective-permute-start | bytes 3145736 | tf_op jit(solution)/shard_map/ppermute | solution.py:33
  73.7 3.9 %copy-start = (bf16[160,128,256]{2,1,0:T(8,128)(2,1)}, bf16[160,128,256]{2,1,0:T(8,128)(2,1)S(1)}, u32[]{:S(2)}) copy-start(bf16[160,128,256]{2,1,0:T(8,128)(2,1)S(1)} %pack.1) | copy-start | bytes 31457284
  77.6 19.5 %all-to-all-start = ((bf16[160,128,256]{2,1,0:T(8,128)(2,1)}), bf16[160,128,256]{2,1,0:T(8,128)(2,1)}, u32[]{:S(2)}, u32[]{:S(2)}) async-start(bf16[160,128,256]{2,1,0:T(8,128)(2,1)} %copy-done), calls=%async_computation | async-start | bytes 20971520 | tf_op jit(solution)/shard_map/all_to_all | solution.py:415
  97.1 1.2 copy-start.9
  97.1 1.5 %copy-start.10 = (bf16[2,2,8,128,128]{4,3,2,1,0:T(8,128)(2,1)}, bf16[2,2,8,128,128]{4,3,2,1,0:T(8,128)(2,1)S(1)}, u32[]{:S(2)}) copy-start(bf16[2,2,8,128,128]{4,3,2,1,0:T(8,128)(2,1)S(1)} %collective-permute-done.10.refs_1_.refs_2_.refs_9_) | copy-start | bytes 3145732
  98.6 26.8 %collective-permute-start.19 = (bf16[2,1,8,128,128]{4,3,2,1,0:T(8,128)(2,1)}, bf16[2,1,8,128,128]{4,3,2,1,0:T(8,128)(2,1)S(1)}, u32[]{:S(2)}, u32[]{:S(2)}) collective-permute-start(bf16[2,1,8,128,128]{4,3,2,1,0:T(8,128)(2,1)} %gate.15), channel_id=1, source_target_pairs={{0,1},{1,0},{2,3},{3,2},{4,5},{5,4},{6,7},{7,6},{8,9},{9,8},{10,11... | collective-permute-start | bytes 1572872 | tf_op jit(solution)/shard_map/ppermute | solution.py:33
  102.6 22.9 %collective-permute-start.20 = (bf16[2,8,128,128]{3,2,1,0:T(8,128)(2,1)S(1)}, bf16[2,8,128,128]{3,2,1,0:T(8,128)(2,1)S(1)}, u32[]{:S(2)}, u32[]{:S(2)}) collective-permute-start(bf16[2,8,128,128]{3,2,1,0:T(8,128)(2,1)S(1)} %slice_bitcast_fusion.3), channel_id=1, source_target_pairs={{0,2},{1,3},{2,4},{3,5},{4,6},{5,7},{6,0},{7,1},{8,10},{9,11},{10,... | collective-permute-start | bytes 1572872 | tf_op jit(solution)/shard_map/ppermute | solution.py:33
  103.8 20.0 %collective-permute-start.18 = (bf16[8,128,256]{2,1,0:T(8,128)(2,1)S(1)}, bf16[8,128,256]{2,1,0:T(8,128)(2,1)S(1)}, u32[]{:S(2)}, u32[]{:S(2)}) collective-permute-start(bf16[8,128,256]{2,1,0:T(8,128)(2,1)S(1)} %slice.57), channel_id=1, source_target_pairs={{0,112},{1,113},{2,114},{3,115},{4,116},{5,117},{6,118},{7,119},{8... | collective-permute-start | bytes 1572872 | tf_op jit(solution)/shard_map/ppermute | solution.py:33
  106.8 5.0 %copy-start.5 = (s32[3,200]{1,0:T(4,128)S(1)}, s32[3,200]{1,0:T(4,128)}, u32[]{:S(2)}) copy-start(s32[3,200]{1,0:T(4,128)} %get-tuple-element.11.refs_4_.order_ref) | copy-start | bytes 7204
  106.8 5.0 %copy-start.6 = (s32[3,100]{1,0:T(4,128)S(1)}, s32[3,100]{1,0:T(4,128)}, u32[]{:S(2)}) copy-start(s32[3,100]{1,0:T(4,128)} %get-tuple-element.12.row_ref) | copy-start | bytes 3604
  106.8 5.0 %copy-start.8 = (s32[6]{0:T(128)S(1)}, s32[6]{0:T(128)}, u32[]{:S(2)}) copy-start(s32[6]{0:T(128)} %get-tuple-element.13.pairs_ref) | copy-start | bytes 76
  107.9 15.8 %collective-permute-start.16 = (bf16[8,128,256]{2,1,0:T(8,128)(2,1)S(1)}, bf16[8,128,256]{2,1,0:T(8,128)(2,1)S(1)}, u32[]{:S(2)}, u32[]{:S(2)}) collective-permute-start(bf16[8,128,256]{2,1,0:T(8,128)(2,1)S(1)} %slice.56), channel_id=1, source_target_pairs={{0,16},{1,17},{2,18},{3,19},{4,20},{5,21},{6,22},{7,23},{8,24},{9,... | collective-permute-start | bytes 1572872 | tf_op jit(solution)/shard_map/ppermute | solution.py:33
  109.1 16.4 %collective-permute-start.21 = (bf16[2,8,128,128]{3,2,1,0:T(8,128)(2,1)S(1)}, bf16[2,8,128,128]{3,2,1,0:T(8,128)(2,1)S(1)}, u32[]{:S(2)}, u32[]{:S(2)}) collective-permute-start(bf16[2,8,128,128]{3,2,1,0:T(8,128)(2,1)S(1)} %slice_bitcast_fusion.2), channel_id=1, source_target_pairs={{0,6},{1,7},{2,0},{3,1},{4,2},{5,3},{6,4},{7,5},{8,14},{9,15},{10,... | collective-permute-start | bytes 1572872 | tf_op jit(solution)/shard_map/ppermute | solution.py:33
  123.1 0.6 copy-start.7
  123.8 6.6 %collective-permute-start.24 = (bf16[16,128,256]{2,1,0:T(8,128)(2,1)S(1)}, bf16[16,128,256]{2,1,0:T(8,128)(2,1)S(1)}, u32[]{:S(2)}, u32[]{:S(2)}) collective-permute-start(bf16[16,128,256]{2,1,0:T(8,128)(2,1)S(1)} %pad_maximum_fusion.2), channel_id=1, source_target_pairs={{0,8},{1,9},{2,10},{3,11},{4,12},{5,13},{6,14},{7,15},{8,0},{9,1},... | collective-permute-start | bytes 3145736 | tf_op jit(solution)/shard_map/ppermute | solution.py:33
  125.4 0.8 copy-start.19
  125.4 1.0 copy-start.20
  125.5 1.1 copy-start.21
  126.6 3.9 %collective-permute-start.23 = (bf16[16,128,256]{2,1,0:T(8,128)(2,1)}, bf16[16,128,256]{2,1,0:T(8,128)(2,1)S(1)}, u32[]{:S(2)}, u32[]{:S(2)}) collective-permute-start(bf16[16,128,256]{2,1,0:T(8,128)(2,1)} %gate.17), channel_id=1, source_target_pairs={{0,8},{1,9},{2,10},{3,11},{4,12},{5,13},{6,14},{7,15},{8,0},{9,1},... | collective-permute-start | bytes 3145736 | tf_op jit(solution)/shard_map/ppermute | solution.py:33
  126.6 4.3 %collective-permute-start.22 = (bf16[16,128,256]{2,1,0:T(8,128)(2,1)}, bf16[16,128,256]{2,1,0:T(8,128)(2,1)S(1)}, u32[]{:S(2)}, u32[]{:S(2)}) collective-permute-start(bf16[16,128,256]{2,1,0:T(8,128)(2,1)} %gate.16), channel_id=1, source_target_pairs={{0,8},{1,9},{2,10},{3,11},{4,12},{5,13},{6,14},{7,15},{8,0},{9,1},... | collective-permute-start | bytes 3145736 | tf_op jit(solution)/shard_map/ppermute | solution.py:33
  127.1 3.9 %copy-start.3 = (bf16[1024,128]{1,0:T(8,128)(2,1)S(1)}, bf16[1024,128]{1,0:T(8,128)(2,1)}, u32[]{:S(2)}) copy-start(bf16[1024,128]{1,0:T(8,128)(2,1)} %drive_real.1) | copy-start | bytes 786436
  127.1 3.9 %copy-start.4 = (bf16[1024,128]{1,0:T(8,128)(2,1)S(1)}, bf16[1024,128]{1,0:T(8,128)(2,1)}, u32[]{:S(2)}) copy-start(bf16[1024,128]{1,0:T(8,128)(2,1)} %drive_imag.1) | copy-start | bytes 786436

commit v8 on v7

--- a/solution.py
+++ b/solution.py
@@ -302,7 +302,7 @@
         pack_kernel,
         in_specs=[ANY] * len(parts),
         out_specs=ANY,
-        out_shape=jax.ShapeDtypeStruct((blocks_of(parts), BLOCK, 2 * BLOCK), jnp.bfloat16),
+        out_shape=pltpu.HBM((blocks_of(parts), BLOCK, 2 * BLOCK), jnp.bfloat16),
         scratch_shapes=[pltpu.SemaphoreType.DMA((len(parts),))],
         compiler_params=pltpu.CompilerParams(vmem_limit_bytes=2**16),
         cost_estimate=cost(3),
@@ -394,7 +394,7 @@
     neighbour = shift(panel, "ylo")
     own_up, own_down = shift(panel, "z", 1), shift(panel, "z", -1)
 
-    part = shift(after(both[:, :2], neighbour), "yhi")
+    part = shift(after(both[:, :2], neighbour, own_up, own_down), "yhi")
     up1 = jnp.concatenate([own_up, shift(neighbour, "z", 1)], axis=0)
     down1 = jnp.concatenate([own_down, shift(neighbour, "z", -1)], axis=0)
 
@@ -405,7 +405,7 @@
         after(jnp.concatenate([both[:, 2:], from_left[:, 2:], from_right[:, 2:]], axis=1), part),
         "yhi",
     )
-    lists = make_lists(after(place, far_ham, far_margin), block_cols, block_counts)
+    lists = make_lists(after(place, neighbour), block_cols, block_counts)
 
     part_on = after(part, far_ham, far_margin)
     part_left = shift(part_on, "x", 1)
@@ -413,13 +413,13 @@
     up3, down3 = shift(up2, "z", 1), shift(down2, "z", -1)
     come = (panel, neighbour, up1, down1, up2, down2)
     both_come = lax.all_to_all(pack(come + come), "core", 0, 0, tiled=True)
+    part_far_ham = shift(part_left[0], "x", 1)
+    part_far_margin = shift(part_right[1], "x", -1)
     late_far = shift(
-        after(jnp.stack([far_ham[2:], far_margin[2:]], axis=0), late, part_left, part_right, lists[0], both_come),
+        after(jnp.stack([far_ham[2:], far_margin[2:]], axis=0), late, part_far_ham, part_far_margin, lists[0], both_come),
         "yhi",
     )
 
-    part_far_ham = shift(part_left[0], "x", 1)
-    part_far_margin = shift(part_right[1], "x", -1)
     up3 = after(up3, part_left, part_right, late, both_come)
     down3 = after(down3, part_left, part_right, late, both_come)
     up4, down4 = shift(up3[:rows], "z", 1), shift(down3[rows:], "z", -1)

time: 136 us -> 453 us (3.33)
  Pallas kernels: 27.9 us -> 344 us
  waiting for transfers between devices: 21.6 us -> 33.4 us
  starting transfers between devices: 62.7 us -> 54.7 us
    pallas_call x1, Pallas kernels: 4.27 us -> 319 us  [pack(): pl.pallas_call(pack_kernel, in_specs=[ANY] * len(parts), out_specs=ANY, o...]
    ppermute x25, waiting for transfers between devices: 21 us -> 31.2 us  [shift(): return lax.ppermute(array, AXES, moves(axis, by))]
    ppermute x25, starting transfers between devices: 51.8 us -> 43.2 us  [shift(): return lax.ppermute(array, AXES, moves(axis, by))]
    unnamed x50 -> x52, local copies, waits for them, and re-layouts: 9.11 us -> 6.09 us
  transfers between devices with their start and end apart: 26 -> 26, of which waited for: 9 -> 9; matrix products, arithmetic and copies ran while one was open for 8% -> 2% of each run, Pallas kernels for 18% -> 75%
where the time goes in v8:
time: 453 us; the launch traced here: 452 us
  Pallas kernels  344 us (76%)
  starting transfers between devices  54.7 us (12%)
  waiting for transfers between devices  33.4 us (7%)
  local copies, waits for them, and re-layouts  15.3 us (3%)
    pallas_call x1, Pallas kernels, pack(): pl.pallas_call(pack_kernel, in_specs=[ANY] * len(parts), out_specs=ANY, o...  319 us
    ppermute x25, starting transfers between devices, shift(): return lax.ppermute(array, AXES, moves(axis, by))  43.2 us
    ppermute x25, waiting for transfers between devices, shift(): return lax.ppermute(array, AXES, moves(axis, by))  31.2 us
    pallas_call x1, Pallas kernels, early_products(): pl.pallas_call(early_kernel, in_specs=[SMEM] * 3 + [ANY] * len(args), out...  11.5 us
    all_to_all x1, starting transfers between devices, per_device(): both_come = lax.all_to_all(pack(come + come), 'core', 0, 0, tiled=True)  11.5 us
  transfers between devices with their start and end apart: 26, of which 9 were waited for; matrix products, arithmetic and copies ran while one was open for 2% of the time, Pallas kernels for 75%

profile of v8, /device:TPU:1, one launch (start us, length us, event | category | flops | bytes accessed | tf_op | source)
XLA Modules:
  0.0 452.4 jit_solution(2118963530015151191)
XLA Ops:
  0.6 1.5 copy_bitcast_fusion
  2.1 0.0 copy-start
  2.1 0.0 copy-start.1
  2.1 0.1 pad_maximum_fusion.refs_3_
  2.3 3.4 collective-permute-start.9
  5.7 0.1 pad_maximum_fusion.3
  5.8 1.4 collective-permute-start
  7.2 5.6 %collective-permute-start.5 = (bf16[8,128,256]{2,1,0:T(8,128)(2,1)S(1)}, bf16[8,128,256]{2,1,0:T(8,128)(2,1)S(1)}, u32[]{:S(2)}, u32[]{:S(2)}) collective-permute-start(bf16[8,128,256]{2,1,0:T(8,128)(2,1)S(1)} %bitcast.27), channel_id=1, source_target_pairs={{0,112},{1,113},{2,114},{3,115},{4,116},{5,117},{6,118},{7,119},{8... | collective-permute-start | bytes 1572872 | tf_op jit(solution)/shard_map/ppermute | solution.py:33
  12.7 0.0 collective-permute-start.1
  12.7 1.0 fusion.refs_0_
  13.8 3.6 collective-permute-done.refs_1_.refs_7_
  17.4 5.3 %collective-permute-done.5.refs_3_ = bf16[8,128,256]{2,1,0:T(8,128)(2,1)S(1)} collective-permute-done((bf16[8,128,256]{2,1,0:T(8,128)(2,1)S(1)}, bf16[8,128,256]{2,1,0:T(8,128)(2,1)S(1)}, u32[]{:S(2)}, u32[]{:S(2)}) %collective-permute-start.5) | collective-permute-done | bytes 524320 | tf_op jit(solution)/shard_map/ppermute | solution.py:33
  22.7 3.1 collective-permute-done.1.refs_2_
  25.8 0.8 copy-done.23
  26.6 2.6 collective-permute-start.6
  29.3 1.1 collective-permute-start.14
  30.3 0.4 collective-permute-start.2
  30.7 8.0 %collective-permute-done.9.refs_5_ = bf16[2,3,8,128,128]{4,3,2,1,0:T(8,128)(2,1)S(1)} collective-permute-done((bf16[2,3,8,128,128]{4,3,2,1,0:T(8,128)(2,1)S(1)}, bf16[2,3,8,128,128]{4,3,2,1,0:T(8,128)(2,1)S(1)}, u32[]{:S(2)}, u32[]{:S(2)}) %collective-permute-start.9) | collective-permute-done | bytes 1572896 | tf_op jit(solution)/shard_map/ppermute | solution.py:33
  38.7 0.1 slice_bitcast_fusion
  38.8 0.0 copy-start.24
  38.8 3.5 collective-permute-start.10
  42.3 0.0 collective-permute-done.7.refs_4_
  42.3 0.1 slice_bitcast_fusion.1
  42.4 0.1 collective-permute-start.8
  42.7 5.7 %collective-permute-start.15 = (bf16[16,128,256]{2,1,0:T(8,128)(2,1)S(1)}, bf16[16,128,256]{2,1,0:T(8,128)(2,1)}, u32[]{:S(2)}, u32[]{:S(2)}) collective-permute-start(bf16[16,128,256]{2,1,0:T(8,128)(2,1)S(1)} %constant_dynamic-update-slice_fusion.2.refs_3_.refs_9_), channel_id=1, source_target_pairs={{0,112},{1,113},{2,114},{3,115},{4,116},{5,117},{6,118},{7,119},{8... | collective-permute-start | bytes 3145736 | tf_op jit(solution)/shard_map/ppermute | solution.py:33
  48.4 0.1 collective-permute-start.3
  48.5 0.1 fusion.1
  48.6 0.7 copy-done.12
  49.4 1.3 pad_maximum_fusion.1.refs_0_
  50.7 1.0 copy-done.10
  51.7 6.0 %collective-permute-done.10.refs_2_.refs_7_ = bf16[3,8,128,128]{3,2,1,0:T(8,128)(2,1)S(1)} collective-permute-done((bf16[3,8,128,128]{3,2,1,0:T(8,128)(2,1)S(1)}, bf16[3,8,128,128]{3,2,1,0:T(8,128)(2,1)S(1)}, u32[]{:S(2)}, u32[]{:S(2)}) %collective-permute-start.10) | collective-permute-done | bytes 786464 | tf_op jit(solution)/shard_map/ppermute | solution.py:33
  57.6 3.4 collective-permute-done.8.refs_1_.refs_6_
  61.0 0.9 copy-done.20
  61.9 2.9 collective-permute-start.13
  64.8 2.7 collective-permute-start.12
  67.5 1.5 collective-permute-done.15.refs_5_.refs_11_
  68.9 4.1 collective-permute-start.17
  73.1 0.6 stack.41.refs_0_
  73.7 5.2 %make_lists.1 = (s32[3,200]{1,0:T(4,128)}, s32[3,100]{1,0:T(4,128)}, s32[6]{0:T(128)}) custom-call(s32[5]{0:T(128)} %gate.9.place_ref, s32[8,24]{1,0:T(8,128)} %cols_ref.1, s32[8]{0:T(128)} %counts_ref.1), custom_call_target="tpu_custom_call" | custom-call | tf_op jit(solution)/shard_map/make_lists/pallas_call | solution.py:111
  79.0 318.9 %pack.1 = bf16[160,128,256]{2,1,0:T(8,128)(2,1)} custom-call(bf16[8,128,256]{2,1,0:T(8,128)(2,1)} %bitcast.29, bf16[8,128,256]{2,1,0:T(8,128)(2,1)} %copy-done.11, bf16[16,128,256]{2,1,0:T(8,128)(2,1)} %copy-done.12, bf16[16,128,256]{2,1,0:T(8,128)(2,1)} %copy-done.13, bf16[16,128,256]{2,1,0:T(8,128)(2,1)} %collective-permute-done.3.refs_4_.refs_10_, ...), custom_call_target="tpu_custom_call" | custom-call | bytes 9000000 | tf_op jit(solution)/shard_map/pack/pallas_call | solution.py:301
  397.8 11.5 %all-to-all-start = ((bf16[160,128,256]{2,1,0:T(8,128)(2,1)}), bf16[160,128,256]{2,1,0:T(8,128)(2,1)}, u32[]{:S(2)}, u32[]{:S(2)}) async-start(bf16[160,128,256]{2,1,0:T(8,128)(2,1)} %pack.1), calls=%async_computation | async-start | bytes 20971520 | tf_op jit(solution)/shard_map/all_to_all | solution.py:415
  409.3 0.9 slice_bitcast_fusion.3
  410.2 1.9 slice_bitcast_fusion.2
  412.0 2.7 collective-permute-start.20
  414.7 1.0 slice_bitcast_fusion.4
  415.7 2.2 all-to-all-done.refs_4_.refs_5_.refs_0_
  417.9 1.2 copy-done.8
  419.1 1.1 slice.57
  420.2 3.0 collective-permute-start.18
  423.2 1.1 slice.56
  424.3 0.1 collective-permute-start.16
  424.4 1.0 slice_bitcast_fusion.5
  425.4 0.8 pad_maximum_fusion.4.refs_0_
  426.2 1.7 collective-permute-start.21
  427.9 11.5 %products_early.1 = (bf16[192,128,256]{2,1,0:T(8,128)(2,1)S(1)}, bf16[2,24,8,128,128]{4,3,2,1,0:T(8,128)(2,1)S(1)}, f32[8,256,256]{2,1,0:T(8,128)S(1)}, f32[8,128]{1,0:T(8,128)S(1)}) custom-call(s32[3,200]{1,0:T(4,128)S(1)} %copy-done.4, s32[3,100]{1,0:T(4,128)S(1)} %copy-done.5, s32[6]{0:T(128)S(1)} %copy-done.7, ...), custom_call_target="tpu_custom_call" | custom-call | bytes 30000000 | tf_op jit(solution)/shard_map/products_early/pallas_call | solution.py:327
  439.4 0.0 copy-start.6
  439.4 0.6 copy-done.6
  440.0 0.1 pad_maximum_fusion.2
  440.1 1.7 collective-permute-start.24
  441.8 0.8 copy-done.17
  442.6 0.6 collective-permute-start.23
  443.2 3.8 products_main.1
  447.0 0.2 collective-permute-done.22.other_up
  447.3 4.9 %products_last.1 = (f32[1024,128]{1,0:T(8,128)}, f32[1024,128]{1,0:T(8,128)}) custom-call(s32[3,200]{1,0:T(4,128)S(1)} %copy-done.4, s32[3,100]{1,0:T(4,128)S(1)} %copy-done.5, s32[6]{0:T(128)S(1)} %copy-done.7, bf16[8,128,256]{2,1,0:T(8,128)(2,1)S(1)} %collective-permute-done.16.end_up, bf16[8,128,256]{2,1,0:T(8,128)(2,1)S(1)} %collective-permute-done.18.end_down, ...), custom_call_target="tpu_custom_call" | custom-call | bytes 12000000 | tf_op jit(solution)/shard_map/products_last/pallas_call | solution.py:360
  (75 shorter events, 0.4 us)
Async XLA Ops:
  2.1 3.6 copy-start
  2.1 3.6 copy-start.1
  2.3 11.5 %copy-start.14 = (bf16[2,3,8,128,128]{4,3,2,1,0:T(8,128)(2,1)}, bf16[2,3,8,128,128]{4,3,2,1,0:T(8,128)(2,1)S(1)}, u32[]{:S(2)}) copy-start(bf16[2,3,8,128,128]{4,3,2,1,0:T(8,128)(2,1)S(1)} %pad_maximum_fusion.refs_3_) | copy-start | bytes 4718596
  2.3 36.4 %collective-permute-start.9 = (bf16[2,3,8,128,128]{4,3,2,1,0:T(8,128)(2,1)S(1)}, bf16[2,3,8,128,128]{4,3,2,1,0:T(8,128)(2,1)S(1)}, u32[]{:S(2)}, u32[]{:S(2)}) collective-permute-start(bf16[2,3,8,128,128]{4,3,2,1,0:T(8,128)(2,1)S(1)} %pad_maximum_fusion.refs_3_), channel_id=1, source_target_pairs={{0,6},{1,7},{2,0},{3,1},{4,2},{5,3},{6,4},{7,5},{8,14},{9,15},{10,... | collective-permute-start | bytes 4718600 | tf_op jit(solution)/shard_map/ppermute | solution.py:33
  5.7 36.6 %collective-permute-start.7 = (bf16[2,3,8,128,128]{4,3,2,1,0:T(8,128)(2,1)S(1)}, bf16[2,3,8,128,128]{4,3,2,1,0:T(8,128)(2,1)S(1)}, u32[]{:S(2)}, u32[]{:S(2)}) collective-permute-start(bf16[2,3,8,128,128]{4,3,2,1,0:T(8,128)(2,1)S(1)} %pad_maximum_fusion.refs_3_), channel_id=1, source_target_pairs={{0,2},{1,3},{2,4},{3,5},{4,6},{5,7},{6,0},{7,1},{8,10},{9,11},{10,... | collective-permute-start | bytes 4718600 | tf_op jit(solution)/shard_map/ppermute | solution.py:33
  5.8 20.9 %copy-start.18 = (bf16[1024,256]{1,0:T(8,128)(2,1)}, bf16[1024,256]{1,0:T(8,128)(2,1)S(1)}, u32[]{:S(2)}) copy-start(bf16[1024,256]{1,0:T(8,128)(2,1)S(1)} %pad_maximum_fusion.3) | copy-start | bytes 1572868
  5.8 11.7 %collective-permute-start = (bf16[8,128,256]{2,1,0:T(8,128)(2,1)S(1)}, bf16[8,128,256]{2,1,0:T(8,128)(2,1)S(1)}, u32[]{:S(2)}, u32[]{:S(2)}) collective-permute-start(bf16[8,128,256]{2,1,0:T(8,128)(2,1)S(1)} %bitcast.26), channel_id=1, source_target_pairs={{0,128},{1,129},{2,130},{3,131},{4,132},{5,133},{6,134},{7,135},{8... | collective-permute-start | bytes 1572872 | tf_op jit(solution)/shard_map/ppermute | solution.py:33
  7.2 15.6 %collective-permute-start.5 = (bf16[8,128,256]{2,1,0:T(8,128)(2,1)S(1)}, bf16[8,128,256]{2,1,0:T(8,128)(2,1)S(1)}, u32[]{:S(2)}, u32[]{:S(2)}) collective-permute-start(bf16[8,128,256]{2,1,0:T(8,128)(2,1)S(1)} %bitcast.27), channel_id=1, source_target_pairs={{0,112},{1,113},{2,114},{3,115},{4,116},{5,117},{6,118},{7,119},{8... | collective-permute-start | bytes 1572872 | tf_op jit(solution)/shard_map/ppermute | solution.py:33
  12.7 13.1 %collective-permute-start.1 = (bf16[8,128,256]{2,1,0:T(8,128)(2,1)S(1)}, bf16[8,128,256]{2,1,0:T(8,128)(2,1)S(1)}, u32[]{:S(2)}, u32[]{:S(2)}) collective-permute-start(bf16[8,128,256]{2,1,0:T(8,128)(2,1)S(1)} %bitcast.28), channel_id=1, source_target_pairs={{0,16},{1,17},{2,18},{3,19},{4,20},{5,21},{6,22},{7,23},{8,24},{9,... | collective-permute-start | bytes 1572872 | tf_op jit(solution)/shard_map/ppermute | solution.py:33
  17.4 8.4 %copy-start.11 = (bf16[8,128,256]{2,1,0:T(8,128)(2,1)}, bf16[8,128,256]{2,1,0:T(8,128)(2,1)S(1)}, u32[]{:S(2)}) copy-start(bf16[8,128,256]{2,1,0:T(8,128)(2,1)S(1)} %collective-permute-done.refs_1_.refs_7_) | copy-start | bytes 1572868
  22.7 3.1 copy-start.21
  25.8 0.8 copy-start.23
  26.6 15.9 %copy-start.22 = (bf16[8,128,256]{2,1,0:T(8,128)(2,1)S(1)}, bf16[8,128,256]{2,1,0:T(8,128)(2,1)}, u32[]{:S(2)}) copy-start(bf16[8,128,256]{2,1,0:T(8,128)(2,1)} %copy-done.21) | copy-start | bytes 1572868
  26.6 24.0 %collective-permute-start.6 = (bf16[2,2,8,128,128]{4,3,2,1,0:T(8,128)(2,1)}, bf16[2,2,8,128,128]{4,3,2,1,0:T(8,128)(2,1)S(1)}, u32[]{:S(2)}, u32[]{:S(2)}) collective-permute-start(bf16[2,2,8,128,128]{4,3,2,1,0:T(8,128)(2,1)} %gate.10), channel_id=1, source_target_pairs={{0,1},{1,0},{2,3},{3,2},{4,5},{5,4},{6,7},{7,6},{8,9},{9,8},{10,11... | collective-permute-start | bytes 3145736 | tf_op jit(solution)/shard_map/ppermute | solution.py:33
  29.3 13.3 %collective-permute-start.14 = (bf16[8,128,256]{2,1,0:T(8,128)(2,1)}, bf16[8,128,256]{2,1,0:T(8,128)(2,1)S(1)}, u32[]{:S(2)}, u32[]{:S(2)}) collective-permute-start(bf16[8,128,256]{2,1,0:T(8,128)(2,1)} %copy-done.11), channel_id=1, source_target_pairs={{0,112},{1,113},{2,114},{3,115},{4,116},{5,117},{6,118},{7,119},{8... | collective-permute-start | bytes 1572872 | tf_op jit(solution)/shard_map/ppermute | solution.py:33
  30.3 18.0 %collective-permute-start.2 = (bf16[8,128,256]{2,1,0:T(8,128)(2,1)}, bf16[8,128,256]{2,1,0:T(8,128)(2,1)S(1)}, u32[]{:S(2)}, u32[]{:S(2)}) collective-permute-start(bf16[8,128,256]{2,1,0:T(8,128)(2,1)} %copy-done.11), channel_id=1, source_target_pairs={{0,16},{1,17},{2,18},{3,19},{4,20},{5,21},{6,22},{7,23},{8,24},{9,... | collective-permute-start | bytes 1572872 | tf_op jit(solution)/shard_map/ppermute | solution.py:33
  38.7 9.8 %copy-start.15 = (bf16[2,3,8,128,128]{4,3,2,1,0:T(8,128)(2,1)}, bf16[2,3,8,128,128]{4,3,2,1,0:T(8,128)(2,1)S(1)}, u32[]{:S(2)}) copy-start(bf16[2,3,8,128,128]{4,3,2,1,0:T(8,128)(2,1)S(1)} %collective-permute-done.9.refs_5_) | copy-start | bytes 4718596
  38.8 3.7 copy-start.24
  38.8 18.8 %collective-permute-start.10 = (bf16[3,8,128,128]{3,2,1,0:T(8,128)(2,1)S(1)}, bf16[3,8,128,128]{3,2,1,0:T(8,128)(2,1)S(1)}, u32[]{:S(2)}, u32[]{:S(2)}) collective-permute-start(bf16[3,8,128,128]{3,2,1,0:T(8,128)(2,1)S(1)} %slice_bitcast_fusion), channel_id=1, source_target_pairs={{0,6},{1,7},{2,0},{3,1},{4,2},{5,3},{6,4},{7,5},{8,14},{9,15},{10,... | collective-permute-start | bytes 2359304 | tf_op jit(solution)/shard_map/ppermute | solution.py:33
  42.3 6.2 %copy-start.16 = (bf16[2,3,8,128,128]{4,3,2,1,0:T(8,128)(2,1)}, bf16[2,3,8,128,128]{4,3,2,1,0:T(8,128)(2,1)S(1)}, u32[]{:S(2)}) copy-start(bf16[2,3,8,128,128]{4,3,2,1,0:T(8,128)(2,1)S(1)} %collective-permute-done.7.refs_4_) | copy-start | bytes 4718596
  42.4 18.6 %collective-permute-start.8 = (bf16[3,8,128,128]{3,2,1,0:T(8,128)(2,1)S(1)}, bf16[3,8,128,128]{3,2,1,0:T(8,128)(2,1)S(1)}, u32[]{:S(2)}, u32[]{:S(2)}) collective-permute-start(bf16[3,8,128,128]{3,2,1,0:T(8,128)(2,1)S(1)} %slice_bitcast_fusion.1), channel_id=1, source_target_pairs={{0,2},{1,3},{2,4},{3,5},{4,6},{5,7},{6,0},{7,1},{8,10},{9,11},{10,... | collective-permute-start | bytes 2359304 | tf_op jit(solution)/shard_map/ppermute | solution.py:33
  42.7 5.9 %copy-start.13 = (bf16[16,128,256]{2,1,0:T(8,128)(2,1)}, bf16[16,128,256]{2,1,0:T(8,128)(2,1)S(1)}, u32[]{:S(2)}) copy-start(bf16[16,128,256]{2,1,0:T(8,128)(2,1)S(1)} %constant_dynamic-update-slice_fusion.2.refs_3_.refs_9_) | copy-start | bytes 3145732
  42.7 26.3 %collective-permute-start.15 = (bf16[16,128,256]{2,1,0:T(8,128)(2,1)S(1)}, bf16[16,128,256]{2,1,0:T(8,128)(2,1)}, u32[]{:S(2)}, u32[]{:S(2)}) collective-permute-start(bf16[16,128,256]{2,1,0:T(8,128)(2,1)S(1)} %constant_dynamic-update-slice_fusion.2.refs_3_.refs_9_), channel_id=1, source_target_pairs={{0,112},{1,113},{2,114},{3,115},{4,116},{5,117},{6,118},{7,119},{8... | collective-permute-start | bytes 3145736 | tf_op jit(solution)/shard_map/ppermute | solution.py:33
  48.4 1.0 copy-start.12
  48.4 24.7 %collective-permute-start.3 = (bf16[16,128,256]{2,1,0:T(8,128)(2,1)S(1)}, bf16[16,128,256]{2,1,0:T(8,128)(2,1)}, u32[]{:S(2)}, u32[]{:S(2)}) collective-permute-start(bf16[16,128,256]{2,1,0:T(8,128)(2,1)S(1)} %constant_dynamic-update-slice_fusion.refs_2_.refs_8_), channel_id=1, source_target_pairs={{0,16},{1,17},{2,18},{3,19},{4,20},{5,21},{6,22},{7,23},{8,24},{9,... | collective-permute-start | bytes 3145736 | tf_op jit(solution)/shard_map/ppermute | solution.py:33
  50.7 1.0 copy-start.10
  57.6 3.4 copy-start.19
  61.0 0.9 copy-start.20
  61.9 347.4 %collective-permute-start.11 = (bf16[2,2,8,128,128]{4,3,2,1,0:T(8,128)(2,1)}, bf16[2,2,8,128,128]{4,3,2,1,0:T(8,128)(2,1)S(1)}, u32[]{:S(2)}, u32[]{:S(2)}) collective-permute-start(bf16[2,2,8,128,128]{4,3,2,1,0:T(8,128)(2,1)} %gate.11.refs_8_), channel_id=1, source_target_pairs={{0,2},{1,3},{2,4},{3,5},{4,6},{5,7},{6,0},{7,1},{8,10},{9,11},{10,... | collective-permute-start | bytes 3145736 | tf_op jit(solution)/shard_map/ppermute | solution.py:33
  61.9 356.0 %collective-permute-start.13 = (bf16[2,3,8,128,128]{4,3,2,1,0:T(8,128)(2,1)}, bf16[2,3,8,128,128]{4,3,2,1,0:T(8,128)(2,1)S(1)}, u32[]{:S(2)}, u32[]{:S(2)}) collective-permute-start(bf16[2,3,8,128,128]{4,3,2,1,0:T(8,128)(2,1)} %gate.12), channel_id=1, source_target_pairs={{0,1},{1,0},{2,3},{3,2},{4,5},{5,4},{6,7},{7,6},{8,9},{9,8},{10,11... | collective-permute-start | bytes 4718600 | tf_op jit(solution)/shard_map/ppermute | solution.py:33
  64.8 345.3 %collective-permute-start.12 = (bf16[2,2,8,128,128]{4,3,2,1,0:T(8,128)(2,1)}, bf16[2,2,8,128,128]{4,3,2,1,0:T(8,128)(2,1)}, u32[]{:S(2)}, u32[]{:S(2)}) collective-permute-start(bf16[2,2,8,128,128]{4,3,2,1,0:T(8,128)(2,1)} %gate.11.refs_8_), channel_id=1, source_target_pairs={{0,6},{1,7},{2,0},{3,1},{4,2},{5,3},{6,4},{7,5},{8,14},{9,15},{10,... | collective-permute-start | bytes 3145736 | tf_op jit(solution)/shard_map/ppermute | solution.py:33
  68.9 349.0 %collective-permute-start.17 = (bf16[16,128,256]{2,1,0:T(8,128)(2,1)}, bf16[16,128,256]{2,1,0:T(8,128)(2,1)}, u32[]{:S(2)}, u32[]{:S(2)}) collective-permute-start(bf16[16,128,256]{2,1,0:T(8,128)(2,1)} %collective-permute-done.15.refs_5_.refs_11_), channel_id=1, source_target_pairs={{0,112},{1,113},{2,114},{3,115},{4,116},{5,117},{6,118},{7,119},{8... | collective-permute-start | bytes 3145736 | tf_op jit(solution)/shard_map/ppermute | solution.py:33
  73.1 350.1 %collective-permute-start.4 = (bf16[16,128,256]{2,1,0:T(8,128)(2,1)}, bf16[16,128,256]{2,1,0:T(8,128)(2,1)}, u32[]{:S(2)}, u32[]{:S(2)}) collective-permute-start(bf16[16,128,256]{2,1,0:T(8,128)(2,1)} %collective-permute-done.3.refs_4_.refs_10_), channel_id=1, source_target_pairs={{0,16},{1,17},{2,18},{3,19},{4,20},{5,21},{6,22},{7,23},{8,24},{9,... | collective-permute-start | bytes 3145736 | tf_op jit(solution)/shard_map/ppermute | solution.py:33
  397.8 20.1 %all-to-all-start = ((bf16[160,128,256]{2,1,0:T(8,128)(2,1)}), bf16[160,128,256]{2,1,0:T(8,128)(2,1)}, u32[]{:S(2)}, u32[]{:S(2)}) async-start(bf16[160,128,256]{2,1,0:T(8,128)(2,1)} %pack.1), calls=%async_computation | async-start | bytes 20971520 | tf_op jit(solution)/shard_map/all_to_all | solution.py:415
  409.3 8.6 %copy-start.9 = (bf16[2,2,8,128,128]{4,3,2,1,0:T(8,128)(2,1)}, bf16[2,2,8,128,128]{4,3,2,1,0:T(8,128)(2,1)S(1)}, u32[]{:S(2)}) copy-start(bf16[2,2,8,128,128]{4,3,2,1,0:T(8,128)(2,1)S(1)} %collective-permute-done.11.refs_1_.refs_9_) | copy-start | bytes 3145732
  410.2 16.0 %collective-permute-start.19 = (bf16[2,8,128,128]{3,2,1,0:T(8,128)(2,1)}, bf16[2,8,128,128]{3,2,1,0:T(8,128)(2,1)}, u32[]{:S(2)}, u32[]{:S(2)}) collective-permute-start(bf16[2,8,128,128]{3,2,1,0:T(8,128)(2,1)} %slice_bitcast_fusion.3), channel_id=1, source_target_pairs={{0,2},{1,3},{2,4},{3,5},{4,6},{5,7},{6,0},{7,1},{8,10},{9,11},{10,... | collective-permute-start | bytes 1572872 | tf_op jit(solution)/shard_map/ppermute | solution.py:33
  412.0 14.1 %collective-permute-start.20 = (bf16[2,8,128,128]{3,2,1,0:T(8,128)(2,1)}, bf16[2,8,128,128]{3,2,1,0:T(8,128)(2,1)}, u32[]{:S(2)}, u32[]{:S(2)}) collective-permute-start(bf16[2,8,128,128]{3,2,1,0:T(8,128)(2,1)} %slice_bitcast_fusion.2), channel_id=1, source_target_pairs={{0,6},{1,7},{2,0},{3,1},{4,2},{5,3},{6,4},{7,5},{8,14},{9,15},{10,... | collective-permute-start | bytes 1572872 | tf_op jit(solution)/shard_map/ppermute | solution.py:33
  417.9 1.2 copy-start.8
  420.2 19.8 %collective-permute-start.18 = (bf16[8,128,256]{2,1,0:T(8,128)(2,1)S(1)}, bf16[8,128,256]{2,1,0:T(8,128)(2,1)S(1)}, u32[]{:S(2)}, u32[]{:S(2)}) collective-permute-start(bf16[8,128,256]{2,1,0:T(8,128)(2,1)S(1)} %slice.57), channel_id=1, source_target_pairs={{0,112},{1,113},{2,114},{3,115},{4,116},{5,117},{6,118},{7,119},{8... | collective-permute-start | bytes 1572872 | tf_op jit(solution)/shard_map/ppermute | solution.py:33
  424.3 15.7 %collective-permute-start.16 = (bf16[8,128,256]{2,1,0:T(8,128)(2,1)S(1)}, bf16[8,128,256]{2,1,0:T(8,128)(2,1)S(1)}, u32[]{:S(2)}, u32[]{:S(2)}) collective-permute-start(bf16[8,128,256]{2,1,0:T(8,128)(2,1)S(1)} %slice.56), channel_id=1, source_target_pairs={{0,16},{1,17},{2,18},{3,19},{4,20},{5,21},{6,22},{7,23},{8,24},{9,... | collective-permute-start | bytes 1572872 | tf_op jit(solution)/shard_map/ppermute | solution.py:33
  426.2 1.7 copy-start.4
  426.2 1.7 copy-start.5
  426.2 1.7 copy-start.7
  426.2 15.5 %collective-permute-start.21 = (bf16[2,1,8,128,128]{4,3,2,1,0:T(8,128)(2,1)}, bf16[2,1,8,128,128]{4,3,2,1,0:T(8,128)(2,1)S(1)}, u32[]{:S(2)}, u32[]{:S(2)}) collective-permute-start(bf16[2,1,8,128,128]{4,3,2,1,0:T(8,128)(2,1)} %gate.15), channel_id=1, source_target_pairs={{0,1},{1,0},{2,3},{3,2},{4,5},{5,4},{6,7},{7,6},{8,9},{9,8},{10,11... | collective-permute-start | bytes 1572872 | tf_op jit(solution)/shard_map/ppermute | solution.py:33
  439.4 0.6 copy-start.6
  440.1 6.9 %collective-permute-start.24 = (bf16[16,128,256]{2,1,0:T(8,128)(2,1)S(1)}, bf16[16,128,256]{2,1,0:T(8,128)(2,1)S(1)}, u32[]{:S(2)}, u32[]{:S(2)}) collective-permute-start(bf16[16,128,256]{2,1,0:T(8,128)(2,1)S(1)} %pad_maximum_fusion.2), channel_id=1, source_target_pairs={{0,8},{1,9},{2,10},{3,11},{4,12},{5,13},{6,14},{7,15},{8,0},{9,1},... | collective-permute-start | bytes 3145736 | tf_op jit(solution)/shard_map/ppermute | solution.py:33
  441.8 0.8 copy-start.17
  442.6 4.4 collective-permute-start.23
  443.2 4.1 collective-permute-start.22
  443.2 4.1 copy-start.2
  443.2 4.1 copy-start.3

commit v9 on v8

--- a/solution.py
+++ b/solution.py
@@ -286,26 +286,39 @@
 
 
 def pack_kernel(*refs):
-    parts, out, sems = refs[:-2], refs[-2], refs[-1]
+    parts, (out, whole, sems) = refs[:-3], refs[-3:]
+    count = whole.shape[0]
     copies, at = [], 0
     for n, part in enumerate(parts):
-        copies.append(pltpu.make_async_copy(part, out.at[pl.ds(at, part.shape[0])], sems.at[n]))
+        copies.append(pltpu.make_async_copy(part, whole.at[pl.ds(at, part.shape[0])], sems.at[n]))
         at += part.shape[0]
     for copy in copies:
         copy.start()
     for copy in copies:
         copy.wait()
-
-
-def pack(parts):
+    halves = [
+        pltpu.make_async_copy(whole, out.at[pl.ds(n * count, count)], sems.at[len(parts) + n])
+        for n in range(2)
+    ]
+    for copy in halves:
+        copy.start()
+    for copy in halves:
+        copy.wait()
+
+
+def pack_twice(parts):
+    count = blocks_of(parts)
     return pl.pallas_call(
         pack_kernel,
         in_specs=[ANY] * len(parts),
         out_specs=ANY,
-        out_shape=pltpu.HBM((blocks_of(parts), BLOCK, 2 * BLOCK), jnp.bfloat16),
-        scratch_shapes=[pltpu.SemaphoreType.DMA((len(parts),))],
-        compiler_params=pltpu.CompilerParams(vmem_limit_bytes=2**16),
-        cost_estimate=cost(3),
+        out_shape=pltpu.HBM((2 * count, BLOCK, 2 * BLOCK), jnp.bfloat16),
+        scratch_shapes=[
+            pltpu.VMEM((count, BLOCK, 2 * BLOCK), jnp.bfloat16),
+            pltpu.SemaphoreType.DMA((len(parts) + 2,)),
+        ],
+        compiler_params=pltpu.CompilerParams(vmem_limit_bytes=6 * 2**20),
+        cost_estimate=cost(4),
         name="pack",
     )(*map(in_hbm, parts))
 
@@ -394,7 +407,8 @@
     neighbour = shift(panel, "ylo")
     own_up, own_down = shift(panel, "z", 1), shift(panel, "z", -1)
 
-    part = shift(after(both[:, :2], neighbour, own_up, own_down), "yhi")
+    lists = make_lists(place, block_cols, block_counts)
+    part = shift(after(both[:, :2], neighbour, own_up, own_down, lists[0]), "yhi")
     up1 = jnp.concatenate([own_up, shift(neighbour, "z", 1)], axis=0)
     down1 = jnp.concatenate([own_down, shift(neighbour, "z", -1)], axis=0)
 
@@ -405,14 +419,13 @@
         after(jnp.concatenate([both[:, 2:], from_left[:, 2:], from_right[:, 2:]], axis=1), part),
         "yhi",
     )
-    lists = make_lists(after(place, neighbour), block_cols, block_counts)
 
     part_on = after(part, far_ham, far_margin)
     part_left = shift(part_on, "x", 1)
     part_right = shift(part_on, "x", -1)
     up3, down3 = shift(up2, "z", 1), shift(down2, "z", -1)
     come = (panel, neighbour, up1, down1, up2, down2)
-    both_come = lax.all_to_all(pack(come + come), "core", 0, 0, tiled=True)
+    both_come = lax.all_to_all(pack_twice(come), "core", 0, 0, tiled=True)
     part_far_ham = shift(part_left[0], "x", 1)
     part_far_margin = shift(part_right[1], "x", -1)
     late_far = shift(

time: 453 us -> 142 us (0.31)
  Pallas kernels: 344 us -> 31.2 us
  waiting for transfers between devices: 33.4 us -> 26.6 us
  local copies, waits for them, and re-layouts: 15.3 us -> 20.4 us
    pallas_call x1, Pallas kernels: 319 us -> 6.41 us  [pack_twice(): pl.pallas_call(pack_kernel, in_specs=[ANY] * len(parts), out_specs=ANY, o...]
    ppermute x25, waiting for transfers between devices: 31.2 us -> 24.4 us  [shift(): return lax.ppermute(array, AXES, moves(axis, by))]
  transfers between devices with their start and end apart: 26 -> 26, of which waited for: 9 -> 7; matrix products, arithmetic and copies ran while one was open for 2% -> 13% of each run, Pallas kernels for 75% -> 19%
where the time goes in v9:
time: 142 us; the launch traced here: 141 us
  starting transfers between devices  56.7 us (40%)
  Pallas kernels  31.2 us (22%)
  waiting for transfers between devices  26.6 us (19%)
  local copies, waits for them, and re-layouts  20.4 us (14%)
  other arithmetic  4.76 us (3%)
    ppermute x25, starting transfers between devices, shift(): return lax.ppermute(array, AXES, moves(axis, by))  46 us
    ppermute x25, waiting for transfers between devices, shift(): return lax.ppermute(array, AXES, moves(axis, by))  24.4 us
    pallas_call x1, Pallas kernels, early_products(): pl.pallas_call(early_kernel, in_specs=[SMEM] * 3 + [ANY] * len(args), out...  11.7 us
    all_to_all x1, starting transfers between devices, per_device(): both_come = lax.all_to_all(pack_twice(come), 'core', 0, 0, tiled=True)  10.7 us
    unnamed x38, local copies, waits for them, and re-layouts  6.64 us
    pallas_call x1, Pallas kernels, pack_twice(): pl.pallas_call(pack_kernel, in_specs=[ANY] * len(parts), out_specs=ANY, o...  6.41 us
    pallas_call x1, Pallas kernels, make_lists(): pl.pallas_call(list_kernel, in_specs=[SMEM] * 3, out_specs=[SMEM] * 3, ou...  5.24 us
    pallas_call x1, Pallas kernels, last_products(): pl.pallas_call(last_kernel, in_specs=[SMEM] * 3 + [ANY] * len(parts) + [V...  4.53 us
  transfers between devices with their start and end apart: 26, of which 7 were waited for; matrix products, arithmetic and copies ran while one was open for 13% of the time, Pallas kernels for 19%

profile of v9, /device:TPU:1, one launch (start us, length us, event | category | flops | bytes accessed | tf_op | source)
XLA Modules:
  0.0 140.8 jit_solution(7585620630171480103)
XLA Ops:
  0.6 1.5 %copy_bitcast_fusion = (bf16[1,3,8,128,128]{4,3,2,1,0:T(8,128)(2,1)S(1)}, bf16[1,3,8,128,128]{4,3,2,1,0:T(8,128)(2,1)S(1)}) fusion(bf16[8,3,128,128]{3,2,1,0:T(8,128)(2,1)} %param.9, bf16[8,3,128,128]{3,2,1,0:T(8,128)(2,1)} %param.8), kind=kLoop, calls=%fused_computation.10 | loop fusion | bytes 3145728 | tf_op jit(solution)/shard_map/stack | solution.py:402
  2.1 0.0 copy-start
  2.1 0.0 copy-start.1
  2.1 1.3 pad_maximum_fusion.refs_3_
  3.5 3.3 %collective-permute-start.9 = (bf16[2,3,8,128,128]{4,3,2,1,0:T(8,128)(2,1)}, bf16[2,3,8,128,128]{4,3,2,1,0:T(8,128)(2,1)}, u32[]{:S(2)}, u32[]{:S(2)}) collective-permute-start(bf16[2,3,8,128,128]{4,3,2,1,0:T(8,128)(2,1)} %pad_maximum_fusion.refs_3_), channel_id=1, source_target_pairs={{0,6},{1,7},{2,0},{3,1},{4,2},{5,3},{6,4},{7,5},{8,14},{9,15},{10,... | collective-permute-start | bytes 4718600 | tf_op jit(solution)/shard_map/ppermute | solution.py:33
  6.8 0.1 pad_maximum_fusion.3
  6.9 0.0 copy-start.16
  6.9 1.4 collective-permute-start.1
  8.2 1.6 %collective-permute-start = (bf16[8,128,256]{2,1,0:T(8,128)(2,1)S(1)}, bf16[8,128,256]{2,1,0:T(8,128)(2,1)}, u32[]{:S(2)}, u32[]{:S(2)}) collective-permute-start(bf16[8,128,256]{2,1,0:T(8,128)(2,1)S(1)} %bitcast.27), channel_id=1, source_target_pairs={{0,16},{1,17},{2,18},{3,19},{4,20},{5,21},{6,22},{7,23},{8,24},{9,... | collective-permute-start | bytes 1572872 | tf_op jit(solution)/shard_map/ppermute | solution.py:33
  9.9 3.9 %collective-permute-start.5 = (bf16[8,128,256]{2,1,0:T(8,128)(2,1)S(1)}, bf16[8,128,256]{2,1,0:T(8,128)(2,1)}, u32[]{:S(2)}, u32[]{:S(2)}) collective-permute-start(bf16[8,128,256]{2,1,0:T(8,128)(2,1)S(1)} %bitcast.28), channel_id=1, source_target_pairs={{0,112},{1,113},{2,114},{3,115},{4,116},{5,117},{6,118},{7,119},{8... | collective-permute-start | bytes 1572872 | tf_op jit(solution)/shard_map/ppermute | solution.py:33
  13.8 0.7 stack.41.place_ref
  14.5 5.2 %make_lists.1 = (s32[3,200]{1,0:T(4,128)}, s32[3,100]{1,0:T(4,128)}, s32[6]{0:T(128)}) custom-call(s32[5]{0:T(128)} %stack.41.place_ref, s32[8,24]{1,0:T(8,128)} %cols_ref.1, s32[8]{0:T(128)} %counts_ref.1), custom_call_target="tpu_custom_call" | custom-call | tf_op jit(solution)/shard_map/make_lists/pallas_call | solution.py:111
  19.7 1.1 fusion.refs_0_
  20.8 0.0 collective-permute-done.1.refs_1_
  20.8 4.1 %collective-permute-done.refs_2_ = bf16[8,128,256]{2,1,0:T(8,128)(2,1)} collective-permute-done((bf16[8,128,256]{2,1,0:T(8,128)(2,1)S(1)}, bf16[8,128,256]{2,1,0:T(8,128)(2,1)}, u32[]{:S(2)}, u32[]{:S(2)}) %collective-permute-start) | collective-permute-done | bytes 524320 | tf_op jit(solution)/shard_map/ppermute | solution.py:33
  25.0 2.7 %collective-permute-start.6 = (bf16[2,2,8,128,128]{4,3,2,1,0:T(8,128)(2,1)}, bf16[2,2,8,128,128]{4,3,2,1,0:T(8,128)(2,1)S(1)}, u32[]{:S(2)}, u32[]{:S(2)}) collective-permute-start(bf16[2,2,8,128,128]{4,3,2,1,0:T(8,128)(2,1)} %gate.8), channel_id=1, source_target_pairs={{0,1},{1,0},{2,3},{3,2},{4,5},{5,4},{6,7},{7,6},{8,9},{9,8},{10,11... | collective-permute-start | bytes 3145736 | tf_op jit(solution)/shard_map/ppermute | solution.py:33
  27.7 2.3 %collective-permute-start.14 = (bf16[8,128,256]{2,1,0:T(8,128)(2,1)}, bf16[8,128,256]{2,1,0:T(8,128)(2,1)S(1)}, u32[]{:S(2)}, u32[]{:S(2)}) collective-permute-start(bf16[8,128,256]{2,1,0:T(8,128)(2,1)} %copy-done.17), channel_id=1, source_target_pairs={{0,112},{1,113},{2,114},{3,115},{4,116},{5,117},{6,118},{7,119},{8... | collective-permute-start | bytes 1572872 | tf_op jit(solution)/shard_map/ppermute | solution.py:33
  30.0 10.2 %collective-permute-done.9.refs_5_ = bf16[2,3,8,128,128]{4,3,2,1,0:T(8,128)(2,1)} collective-permute-done((bf16[2,3,8,128,128]{4,3,2,1,0:T(8,128)(2,1)}, bf16[2,3,8,128,128]{4,3,2,1,0:T(8,128)(2,1)}, u32[]{:S(2)}, u32[]{:S(2)}) %collective-permute-start.9) | collective-permute-done | bytes 1572896 | tf_op jit(solution)/shard_map/ppermute | solution.py:33
  40.2 1.2 slice_bitcast_fusion
  41.3 3.5 %collective-permute-start.10 = (bf16[3,8,128,128]{3,2,1,0:T(8,128)(2,1)S(1)}, bf16[3,8,128,128]{3,2,1,0:T(8,128)(2,1)S(1)}, u32[]{:S(2)}, u32[]{:S(2)}) collective-permute-start(bf16[3,8,128,128]{3,2,1,0:T(8,128)(2,1)S(1)} %slice_bitcast_fusion), channel_id=1, source_target_pairs={{0,6},{1,7},{2,0},{3,1},{4,2},{5,3},{6,4},{7,5},{8,14},{9,15},{10,... | collective-permute-start | bytes 2359304 | tf_op jit(solution)/shard_map/ppermute | solution.py:33
  44.8 1.2 slice_bitcast_fusion.1
  46.0 0.1 collective-permute-start.8
  46.1 1.1 constant_dynamic-update-slice_fusion.3
  47.2 1.1 constant_dynamic-update-slice_fusion.1
  48.3 5.7 %collective-permute-start.15 = (bf16[16,128,256]{2,1,0:T(8,128)(2,1)S(1)}, bf16[16,128,256]{2,1,0:T(8,128)(2,1)}, u32[]{:S(2)}, u32[]{:S(2)}) collective-permute-start(bf16[16,128,256]{2,1,0:T(8,128)(2,1)S(1)} %constant_dynamic-update-slice_fusion.2.refs_3_), channel_id=1, source_target_pairs={{0,112},{1,113},{2,114},{3,115},{4,116},{5,117},{6,118},{7,119},{8... | collective-permute-start | bytes 3145736 | tf_op jit(solution)/shard_map/ppermute | solution.py:33
  54.0 0.1 collective-permute-start.3
  54.1 0.1 fusion.1
  54.2 1.3 slice.54
  55.5 1.1 slice.55
  56.6 1.3 pad_maximum_fusion.1.refs_0_
  57.9 1.0 copy-done.10
  58.9 1.2 collective-permute-done.10.refs_2_.refs_7_
  60.1 4.5 %collective-permute-done.8.refs_1_.refs_6_ = bf16[3,8,128,128]{3,2,1,0:T(8,128)(2,1)S(1)} collective-permute-done((bf16[3,8,128,128]{3,2,1,0:T(8,128)(2,1)S(1)}, bf16[3,8,128,128]{3,2,1,0:T(8,128)(2,1)S(1)}, u32[]{:S(2)}, u32[]{:S(2)}) %collective-permute-start.8) | collective-permute-done | bytes 786464 | tf_op jit(solution)/shard_map/ppermute | solution.py:33
  64.6 0.9 copy-done.13
  65.5 2.9 %collective-permute-start.13 = (bf16[2,3,8,128,128]{4,3,2,1,0:T(8,128)(2,1)}, bf16[2,3,8,128,128]{4,3,2,1,0:T(8,128)(2,1)S(1)}, u32[]{:S(2)}, u32[]{:S(2)}) collective-permute-start(bf16[2,3,8,128,128]{4,3,2,1,0:T(8,128)(2,1)} %gate.10), channel_id=1, source_target_pairs={{0,1},{1,0},{2,3},{3,2},{4,5},{5,4},{6,7},{7,6},{8,9},{9,8},{10,11... | collective-permute-start | bytes 4718600 | tf_op jit(solution)/shard_map/ppermute | solution.py:33
  68.5 2.7 %collective-permute-start.12 = (bf16[2,2,8,128,128]{4,3,2,1,0:T(8,128)(2,1)}, bf16[2,2,8,128,128]{4,3,2,1,0:T(8,128)(2,1)}, u32[]{:S(2)}, u32[]{:S(2)}) collective-permute-start(bf16[2,2,8,128,128]{4,3,2,1,0:T(8,128)(2,1)} %gate.9.refs_8_), channel_id=1, source_target_pairs={{0,6},{1,7},{2,0},{3,1},{4,2},{5,3},{6,4},{7,5},{8,14},{9,15},{10,... | collective-permute-start | bytes 3145736 | tf_op jit(solution)/shard_map/ppermute | solution.py:33
  71.1 3.5 %collective-permute-done.15.refs_5_ = bf16[16,128,256]{2,1,0:T(8,128)(2,1)} collective-permute-done((bf16[16,128,256]{2,1,0:T(8,128)(2,1)S(1)}, bf16[16,128,256]{2,1,0:T(8,128)(2,1)}, u32[]{:S(2)}, u32[]{:S(2)}) %collective-permute-start.15) | collective-permute-done | bytes 1048608 | tf_op jit(solution)/shard_map/ppermute | solution.py:33
  74.6 3.5 %collective-permute-start.17 = (bf16[16,128,256]{2,1,0:T(8,128)(2,1)}, bf16[16,128,256]{2,1,0:T(8,128)(2,1)}, u32[]{:S(2)}, u32[]{:S(2)}) collective-permute-start(bf16[16,128,256]{2,1,0:T(8,128)(2,1)} %collective-permute-done.15.refs_5_), channel_id=1, source_target_pairs={{0,112},{1,113},{2,114},{3,115},{4,116},{5,117},{6,118},{7,119},{8... | collective-permute-start | bytes 3145736 | tf_op jit(solution)/shard_map/ppermute | solution.py:33
  78.1 6.4 %pack.1 = bf16[160,128,256]{2,1,0:T(8,128)(2,1)} custom-call(bf16[8,128,256]{2,1,0:T(8,128)(2,1)} %bitcast.29, bf16[8,128,256]{2,1,0:T(8,128)(2,1)} %copy-done.17, bf16[16,128,256]{2,1,0:T(8,128)(2,1)} %copy-done.14, bf16[16,128,256]{2,1,0:T(8,128)(2,1)} %copy-done.15, bf16[16,128,256]{2,1,0:T(8,128)(2,1)} %collective-permute-done.3.refs_4_, ...), custom_call_target="tpu_custom_call" | custom-call | bytes 12000000 | tf_op jit(solution)/shard_map/pack/pallas_call | solution.py:311
  84.6 10.7 %all-to-all-start = ((bf16[160,128,256]{2,1,0:T(8,128)(2,1)}), bf16[160,128,256]{2,1,0:T(8,128)(2,1)}, u32[]{:S(2)}, u32[]{:S(2)}) async-start(bf16[160,128,256]{2,1,0:T(8,128)(2,1)} %pack.1), calls=%async_computation | async-start | bytes 20971520 | tf_op jit(solution)/shard_map/all_to_all | solution.py:428
  95.3 0.9 slice_bitcast_fusion.3
  96.2 1.9 %slice_bitcast_fusion.2 = bf16[2,8,128,128]{3,2,1,0:T(8,128)(2,1)} fusion(bf16[2,2,8,128,128]{4,3,2,1,0:T(8,128)(2,1)} %collective-permute-done.12.refs_2_.refs_10_), kind=kLoop, calls=%fused_computation.13 | loop fusion | bytes 1048576 | tf_op jit(solution)/shard_map/squeeze | solution.py:430
  98.1 2.7 %collective-permute-start.20 = (bf16[2,8,128,128]{3,2,1,0:T(8,128)(2,1)}, bf16[2,8,128,128]{3,2,1,0:T(8,128)(2,1)}, u32[]{:S(2)}, u32[]{:S(2)}) collective-permute-start(bf16[2,8,128,128]{3,2,1,0:T(8,128)(2,1)} %slice_bitcast_fusion.2), channel_id=1, source_target_pairs={{0,6},{1,7},{2,0},{3,1},{4,2},{5,3},{6,4},{7,5},{8,14},{9,15},{10,... | collective-permute-start | bytes 1572872 | tf_op jit(solution)/shard_map/ppermute | solution.py:33
  100.7 1.0 slice_bitcast_fusion.4
  101.7 2.2 %all-to-all-done.refs_4_.refs_5_.refs_0_ = bf16[160,128,256]{2,1,0:T(8,128)(2,1)} async-done(((bf16[160,128,256]{2,1,0:T(8,128)(2,1)}), bf16[160,128,256]{2,1,0:T(8,128)(2,1)}, u32[]{:S(2)}, u32[]{:S(2)}) %all-to-all-start) | async-done | bytes 10485792 | tf_op jit(solution)/shard_map/all_to_all | solution.py:428
  103.9 1.2 copy-done.8
  105.1 1.1 slice.57
  106.2 3.0 %collective-permute-start.18 = (bf16[8,128,256]{2,1,0:T(8,128)(2,1)S(1)}, bf16[8,128,256]{2,1,0:T(8,128)(2,1)S(1)}, u32[]{:S(2)}, u32[]{:S(2)}) collective-permute-start(bf16[8,128,256]{2,1,0:T(8,128)(2,1)S(1)} %slice.57), channel_id=1, source_target_pairs={{0,112},{1,113},{2,114},{3,115},{4,116},{5,117},{6,118},{7,119},{8... | collective-permute-start | bytes 1572872 | tf_op jit(solution)/shard_map/ppermute | solution.py:33
  109.2 1.1 slice.56
  110.3 0.1 collective-permute-start.16
  110.4 1.0 slice_bitcast_fusion.5
  111.4 0.8 pad_maximum_fusion.4.refs_0_
  112.2 3.0 %collective-permute-start.21 = (bf16[2,1,8,128,128]{4,3,2,1,0:T(8,128)(2,1)}, bf16[2,1,8,128,128]{4,3,2,1,0:T(8,128)(2,1)S(1)}, u32[]{:S(2)}, u32[]{:S(2)}) collective-permute-start(bf16[2,1,8,128,128]{4,3,2,1,0:T(8,128)(2,1)} %gate.13), channel_id=1, source_target_pairs={{0,1},{1,0},{2,3},{3,2},{4,5},{5,4},{6,7},{7,6},{8,9},{9,8},{10,11... | collective-permute-start | bytes 1572872 | tf_op jit(solution)/shard_map/ppermute | solution.py:33
  115.2 11.7 %products_early.1 = (bf16[192,128,256]{2,1,0:T(8,128)(2,1)S(1)}, bf16[2,24,8,128,128]{4,3,2,1,0:T(8,128)(2,1)S(1)}, f32[8,256,256]{2,1,0:T(8,128)S(1)}, f32[8,128]{1,0:T(8,128)S(1)}) custom-call(s32[3,200]{1,0:T(4,128)S(1)} %copy-done.4, s32[3,100]{1,0:T(4,128)S(1)} %copy-done.5, s32[6]{0:T(128)S(1)} %copy-done.7, ...), custom_call_target="tpu_custom_call" | custom-call | bytes 30000000 | tf_op jit(solution)/shard_map/products_early/pallas_call | solution.py:340
  126.9 0.0 copy-start.6
  126.9 0.6 copy-done.6
  127.5 0.1 pad_maximum_fusion.2
  127.6 3.0 %collective-permute-start.24 = (bf16[16,128,256]{2,1,0:T(8,128)(2,1)S(1)}, bf16[16,128,256]{2,1,0:T(8,128)(2,1)S(1)}, u32[]{:S(2)}, u32[]{:S(2)}) collective-permute-start(bf16[16,128,256]{2,1,0:T(8,128)(2,1)S(1)} %pad_maximum_fusion.2), channel_id=1, source_target_pairs={{0,8},{1,9},{2,10},{3,11},{4,12},{5,13},{6,14},{7,15},{8,0},{9,1},... | collective-permute-start | bytes 3145736 | tf_op jit(solution)/shard_map/ppermute | solution.py:33
  130.7 0.8 copy-done.11
  131.4 0.0 collective-permute-start.23
  131.5 0.5 collective-permute-start.22
  132.0 3.4 %products_main.1 = (bf16[2,24,8,128,128]{4,3,2,1,0:T(8,128)(2,1)S(1)}, f32[8,256,256]{2,1,0:T(8,128)S(1)}) custom-call(s32[3,200]{1,0:T(4,128)S(1)} %copy-done.4, s32[3,100]{1,0:T(4,128)S(1)} %copy-done.5, s32[6]{0:T(128)S(1)} %copy-done.7, bf16[192,128,256]{2,1,0:T(8,128)(2,1)S(1)} %get-tuple-element.15.panel, ...), custom_call_target="tpu_custom_call", output_to_operand_aliasing={{0}: (4, {}), {1}: (5, {})} | custom-call | bytes 12000000 | tf_op jit(solution)/shard_map/products_main/pallas_call | solution.py:358
  135.4 0.8 collective-permute-done.22.other_up
  136.1 4.5 %products_last.1 = (f32[1024,128]{1,0:T(8,128)}, f32[1024,128]{1,0:T(8,128)}) custom-call(s32[3,200]{1,0:T(4,128)S(1)} %copy-done.4, s32[3,100]{1,0:T(4,128)S(1)} %copy-done.5, s32[6]{0:T(128)S(1)} %copy-done.7, bf16[8,128,256]{2,1,0:T(8,128)(2,1)S(1)} %collective-permute-done.16.end_up, bf16[8,128,256]{2,1,0:T(8,128)(2,1)S(1)} %collective-permute-done.18.end_down, ...), custom_call_target="tpu_custom_call" | custom-call | bytes 12000000 | tf_op jit(solution)/shard_map/products_last/pallas_call | solution.py:373
  (60 shorter events, 0.2 us)
Async XLA Ops:
  2.1 4.7 %copy-start = (bf16[1024,128]{1,0:T(8,128)(2,1)S(1)}, bf16[1024,128]{1,0:T(8,128)(2,1)}, u32[]{:S(2)}) copy-start(bf16[1024,128]{1,0:T(8,128)(2,1)} %pert_imag.1) | copy-start | bytes 786436
  2.1 4.7 %copy-start.1 = (bf16[1024,128]{1,0:T(8,128)(2,1)S(1)}, bf16[1024,128]{1,0:T(8,128)(2,1)}, u32[]{:S(2)}) copy-start(bf16[1024,128]{1,0:T(8,128)(2,1)} %pert_real.1) | copy-start | bytes 786436
  3.5 36.7 %collective-permute-start.9 = (bf16[2,3,8,128,128]{4,3,2,1,0:T(8,128)(2,1)}, bf16[2,3,8,128,128]{4,3,2,1,0:T(8,128)(2,1)}, u32[]{:S(2)}, u32[]{:S(2)}) collective-permute-start(bf16[2,3,8,128,128]{4,3,2,1,0:T(8,128)(2,1)} %pad_maximum_fusion.refs_3_), channel_id=1, source_target_pairs={{0,6},{1,7},{2,0},{3,1},{4,2},{5,3},{6,4},{7,5},{8,14},{9,15},{10,... | collective-permute-start | bytes 4718600 | tf_op jit(solution)/shard_map/ppermute | solution.py:33
  6.8 38.1 %collective-permute-start.7 = (bf16[2,3,8,128,128]{4,3,2,1,0:T(8,128)(2,1)}, bf16[2,3,8,128,128]{4,3,2,1,0:T(8,128)(2,1)}, u32[]{:S(2)}, u32[]{:S(2)}) collective-permute-start(bf16[2,3,8,128,128]{4,3,2,1,0:T(8,128)(2,1)} %pad_maximum_fusion.refs_3_), channel_id=1, source_target_pairs={{0,2},{1,3},{2,4},{3,5},{4,6},{5,7},{6,0},{7,1},{8,10},{9,11},{10,... | collective-permute-start | bytes 4718600 | tf_op jit(solution)/shard_map/ppermute | solution.py:33
  6.9 18.1 %copy-start.16 = (bf16[1024,256]{1,0:T(8,128)(2,1)}, bf16[1024,256]{1,0:T(8,128)(2,1)S(1)}, u32[]{:S(2)}) copy-start(bf16[1024,256]{1,0:T(8,128)(2,1)S(1)} %pad_maximum_fusion.3) | copy-start | bytes 1572868
  6.9 13.9 %collective-permute-start.1 = (bf16[8,128,256]{2,1,0:T(8,128)(2,1)S(1)}, bf16[8,128,256]{2,1,0:T(8,128)(2,1)S(1)}, u32[]{:S(2)}, u32[]{:S(2)}) collective-permute-start(bf16[8,128,256]{2,1,0:T(8,128)(2,1)S(1)} %bitcast.26), channel_id=1, source_target_pairs={{0,128},{1,129},{2,130},{3,131},{4,132},{5,133},{6,134},{7,135},{8... | collective-permute-start | bytes 1572872 | tf_op jit(solution)/shard_map/ppermute | solution.py:33
  8.2 16.7 %collective-permute-start = (bf16[8,128,256]{2,1,0:T(8,128)(2,1)S(1)}, bf16[8,128,256]{2,1,0:T(8,128)(2,1)}, u32[]{:S(2)}, u32[]{:S(2)}) collective-permute-start(bf16[8,128,256]{2,1,0:T(8,128)(2,1)S(1)} %bitcast.27), channel_id=1, source_target_pairs={{0,16},{1,17},{2,18},{3,19},{4,20},{5,21},{6,22},{7,23},{8,24},{9,... | collective-permute-start | bytes 1572872 | tf_op jit(solution)/shard_map/ppermute | solution.py:33
  9.9 15.1 %collective-permute-start.5 = (bf16[8,128,256]{2,1,0:T(8,128)(2,1)S(1)}, bf16[8,128,256]{2,1,0:T(8,128)(2,1)}, u32[]{:S(2)}, u32[]{:S(2)}) collective-permute-start(bf16[8,128,256]{2,1,0:T(8,128)(2,1)S(1)} %bitcast.28), channel_id=1, source_target_pairs={{0,112},{1,113},{2,114},{3,115},{4,116},{5,117},{6,118},{7,119},{8... | collective-permute-start | bytes 1572872 | tf_op jit(solution)/shard_map/ppermute | solution.py:33
  20.8 4.1 %copy-start.17 = (bf16[8,128,256]{2,1,0:T(8,128)(2,1)}, bf16[8,128,256]{2,1,0:T(8,128)(2,1)S(1)}, u32[]{:S(2)}) copy-start(bf16[8,128,256]{2,1,0:T(8,128)(2,1)S(1)} %collective-permute-done.1.refs_1_) | copy-start | bytes 1572868
  25.0 33.0 %collective-permute-start.6 = (bf16[2,2,8,128,128]{4,3,2,1,0:T(8,128)(2,1)}, bf16[2,2,8,128,128]{4,3,2,1,0:T(8,128)(2,1)S(1)}, u32[]{:S(2)}, u32[]{:S(2)}) collective-permute-start(bf16[2,2,8,128,128]{4,3,2,1,0:T(8,128)(2,1)} %gate.8), channel_id=1, source_target_pairs={{0,1},{1,0},{2,3},{3,2},{4,5},{5,4},{6,7},{7,6},{8,9},{9,8},{10,11... | collective-permute-start | bytes 3145736 | tf_op jit(solution)/shard_map/ppermute | solution.py:33
  27.7 20.6 %collective-permute-start.14 = (bf16[8,128,256]{2,1,0:T(8,128)(2,1)}, bf16[8,128,256]{2,1,0:T(8,128)(2,1)S(1)}, u32[]{:S(2)}, u32[]{:S(2)}) collective-permute-start(bf16[8,128,256]{2,1,0:T(8,128)(2,1)} %copy-done.17), channel_id=1, source_target_pairs={{0,112},{1,113},{2,114},{3,115},{4,116},{5,117},{6,118},{7,119},{8... | collective-permute-start | bytes 1572872 | tf_op jit(solution)/shard_map/ppermute | solution.py:33
  29.9 24.0 %collective-permute-start.2 = (bf16[8,128,256]{2,1,0:T(8,128)(2,1)}, bf16[8,128,256]{2,1,0:T(8,128)(2,1)S(1)}, u32[]{:S(2)}, u32[]{:S(2)}) collective-permute-start(bf16[8,128,256]{2,1,0:T(8,128)(2,1)} %copy-done.17), channel_id=1, source_target_pairs={{0,16},{1,17},{2,18},{3,19},{4,20},{5,21},{6,22},{7,23},{8,24},{9,... | collective-permute-start | bytes 1572872 | tf_op jit(solution)/shard_map/ppermute | solution.py:33
  41.3 18.8 %collective-permute-start.10 = (bf16[3,8,128,128]{3,2,1,0:T(8,128)(2,1)S(1)}, bf16[3,8,128,128]{3,2,1,0:T(8,128)(2,1)S(1)}, u32[]{:S(2)}, u32[]{:S(2)}) collective-permute-start(bf16[3,8,128,128]{3,2,1,0:T(8,128)(2,1)S(1)} %slice_bitcast_fusion), channel_id=1, source_target_pairs={{0,6},{1,7},{2,0},{3,1},{4,2},{5,3},{6,4},{7,5},{8,14},{9,15},{10,... | collective-permute-start | bytes 2359304 | tf_op jit(solution)/shard_map/ppermute | solution.py:33
  46.0 18.6 %collective-permute-start.8 = (bf16[3,8,128,128]{3,2,1,0:T(8,128)(2,1)S(1)}, bf16[3,8,128,128]{3,2,1,0:T(8,128)(2,1)S(1)}, u32[]{:S(2)}, u32[]{:S(2)}) collective-permute-start(bf16[3,8,128,128]{3,2,1,0:T(8,128)(2,1)S(1)} %slice_bitcast_fusion.1), channel_id=1, source_target_pairs={{0,2},{1,3},{2,4},{3,5},{4,6},{5,7},{6,0},{7,1},{8,10},{9,11},{10,... | collective-permute-start | bytes 2359304 | tf_op jit(solution)/shard_map/ppermute | solution.py:33
  48.3 5.9 %copy-start.15 = (bf16[16,128,256]{2,1,0:T(8,128)(2,1)}, bf16[16,128,256]{2,1,0:T(8,128)(2,1)S(1)}, u32[]{:S(2)}) copy-start(bf16[16,128,256]{2,1,0:T(8,128)(2,1)S(1)} %constant_dynamic-update-slice_fusion.2.refs_3_) | copy-start | bytes 3145732
  48.3 26.3 %collective-permute-start.15 = (bf16[16,128,256]{2,1,0:T(8,128)(2,1)S(1)}, bf16[16,128,256]{2,1,0:T(8,128)(2,1)}, u32[]{:S(2)}, u32[]{:S(2)}) collective-permute-start(bf16[16,128,256]{2,1,0:T(8,128)(2,1)S(1)} %constant_dynamic-update-slice_fusion.2.refs_3_), channel_id=1, source_target_pairs={{0,112},{1,113},{2,114},{3,115},{4,116},{5,117},{6,118},{7,119},{8... | collective-permute-start | bytes 3145736 | tf_op jit(solution)/shard_map/ppermute | solution.py:33
  54.0 1.5 %copy-start.14 = (bf16[16,128,256]{2,1,0:T(8,128)(2,1)}, bf16[16,128,256]{2,1,0:T(8,128)(2,1)S(1)}, u32[]{:S(2)}) copy-start(bf16[16,128,256]{2,1,0:T(8,128)(2,1)S(1)} %constant_dynamic-update-slice_fusion.refs_2_) | copy-start | bytes 3145732
  54.0 24.1 %collective-permute-start.3 = (bf16[16,128,256]{2,1,0:T(8,128)(2,1)S(1)}, bf16[16,128,256]{2,1,0:T(8,128)(2,1)}, u32[]{:S(2)}, u32[]{:S(2)}) collective-permute-start(bf16[16,128,256]{2,1,0:T(8,128)(2,1)S(1)} %constant_dynamic-update-slice_fusion.refs_2_), channel_id=1, source_target_pairs={{0,16},{1,17},{2,18},{3,19},{4,20},{5,21},{6,22},{7,23},{8,24},{9,... | collective-permute-start | bytes 3145736 | tf_op jit(solution)/shard_map/ppermute | solution.py:33
  57.9 1.0 copy-start.10
  60.1 4.5 %copy-start.12 = (bf16[3,8,128,128]{3,2,1,0:T(8,128)(2,1)}, bf16[3,8,128,128]{3,2,1,0:T(8,128)(2,1)S(1)}, u32[]{:S(2)}) copy-start(bf16[3,8,128,128]{3,2,1,0:T(8,128)(2,1)S(1)} %collective-permute-done.10.refs_2_.refs_7_) | copy-start | bytes 2359300
  64.6 0.9 copy-start.13
  65.5 29.8 %collective-permute-start.11 = (bf16[2,2,8,128,128]{4,3,2,1,0:T(8,128)(2,1)}, bf16[2,2,8,128,128]{4,3,2,1,0:T(8,128)(2,1)S(1)}, u32[]{:S(2)}, u32[]{:S(2)}) collective-permute-start(bf16[2,2,8,128,128]{4,3,2,1,0:T(8,128)(2,1)} %gate.9.refs_8_), channel_id=1, source_target_pairs={{0,2},{1,3},{2,4},{3,5},{4,6},{5,7},{6,0},{7,1},{8,10},{9,11},{10,... | collective-permute-start | bytes 3145736 | tf_op jit(solution)/shard_map/ppermute | solution.py:33
  65.5 38.4 %collective-permute-start.13 = (bf16[2,3,8,128,128]{4,3,2,1,0:T(8,128)(2,1)}, bf16[2,3,8,128,128]{4,3,2,1,0:T(8,128)(2,1)S(1)}, u32[]{:S(2)}, u32[]{:S(2)}) collective-permute-start(bf16[2,3,8,128,128]{4,3,2,1,0:T(8,128)(2,1)} %gate.10), channel_id=1, source_target_pairs={{0,1},{1,0},{2,3},{3,2},{4,5},{5,4},{6,7},{7,6},{8,9},{9,8},{10,11... | collective-permute-start | bytes 4718600 | tf_op jit(solution)/shard_map/ppermute | solution.py:33
  68.5 27.7 %collective-permute-start.12 = (bf16[2,2,8,128,128]{4,3,2,1,0:T(8,128)(2,1)}, bf16[2,2,8,128,128]{4,3,2,1,0:T(8,128)(2,1)}, u32[]{:S(2)}, u32[]{:S(2)}) collective-permute-start(bf16[2,2,8,128,128]{4,3,2,1,0:T(8,128)(2,1)} %gate.9.refs_8_), channel_id=1, source_target_pairs={{0,6},{1,7},{2,0},{3,1},{4,2},{5,3},{6,4},{7,5},{8,14},{9,15},{10,... | collective-permute-start | bytes 3145736 | tf_op jit(solution)/shard_map/ppermute | solution.py:33
  74.6 29.3 %collective-permute-start.17 = (bf16[16,128,256]{2,1,0:T(8,128)(2,1)}, bf16[16,128,256]{2,1,0:T(8,128)(2,1)}, u32[]{:S(2)}, u32[]{:S(2)}) collective-permute-start(bf16[16,128,256]{2,1,0:T(8,128)(2,1)} %collective-permute-done.15.refs_5_), channel_id=1, source_target_pairs={{0,112},{1,113},{2,114},{3,115},{4,116},{5,117},{6,118},{7,119},{8... | collective-permute-start | bytes 3145736 | tf_op jit(solution)/shard_map/ppermute | solution.py:33
  78.1 31.1 %collective-permute-start.4 = (bf16[16,128,256]{2,1,0:T(8,128)(2,1)}, bf16[16,128,256]{2,1,0:T(8,128)(2,1)}, u32[]{:S(2)}, u32[]{:S(2)}) collective-permute-start(bf16[16,128,256]{2,1,0:T(8,128)(2,1)} %collective-permute-done.3.refs_4_), channel_id=1, source_target_pairs={{0,16},{1,17},{2,18},{3,19},{4,20},{5,21},{6,22},{7,23},{8,24},{9,... | collective-permute-start | bytes 3145736 | tf_op jit(solution)/shard_map/ppermute | solution.py:33
  84.6 19.3 %all-to-all-start = ((bf16[160,128,256]{2,1,0:T(8,128)(2,1)}), bf16[160,128,256]{2,1,0:T(8,128)(2,1)}, u32[]{:S(2)}, u32[]{:S(2)}) async-start(bf16[160,128,256]{2,1,0:T(8,128)(2,1)} %pack.1), calls=%async_computation | async-start | bytes 20971520 | tf_op jit(solution)/shard_map/all_to_all | solution.py:428
  95.3 8.6 %copy-start.9 = (bf16[2,2,8,128,128]{4,3,2,1,0:T(8,128)(2,1)}, bf16[2,2,8,128,128]{4,3,2,1,0:T(8,128)(2,1)S(1)}, u32[]{:S(2)}) copy-start(bf16[2,2,8,128,128]{4,3,2,1,0:T(8,128)(2,1)S(1)} %collective-permute-done.11.refs_1_.refs_9_) | copy-start | bytes 3145732
  96.2 16.0 %collective-permute-start.19 = (bf16[2,8,128,128]{3,2,1,0:T(8,128)(2,1)}, bf16[2,8,128,128]{3,2,1,0:T(8,128)(2,1)}, u32[]{:S(2)}, u32[]{:S(2)}) collective-permute-start(bf16[2,8,128,128]{3,2,1,0:T(8,128)(2,1)} %slice_bitcast_fusion.3), channel_id=1, source_target_pairs={{0,2},{1,3},{2,4},{3,5},{4,6},{5,7},{6,0},{7,1},{8,10},{9,11},{10,... | collective-permute-start | bytes 1572872 | tf_op jit(solution)/shard_map/ppermute | solution.py:33
  98.1 14.2 %collective-permute-start.20 = (bf16[2,8,128,128]{3,2,1,0:T(8,128)(2,1)}, bf16[2,8,128,128]{3,2,1,0:T(8,128)(2,1)}, u32[]{:S(2)}, u32[]{:S(2)}) collective-permute-start(bf16[2,8,128,128]{3,2,1,0:T(8,128)(2,1)} %slice_bitcast_fusion.2), channel_id=1, source_target_pairs={{0,6},{1,7},{2,0},{3,1},{4,2},{5,3},{6,4},{7,5},{8,14},{9,15},{10,... | collective-permute-start | bytes 1572872 | tf_op jit(solution)/shard_map/ppermute | solution.py:33
  103.9 1.2 copy-start.8
  106.2 21.4 %collective-permute-start.18 = (bf16[8,128,256]{2,1,0:T(8,128)(2,1)S(1)}, bf16[8,128,256]{2,1,0:T(8,128)(2,1)S(1)}, u32[]{:S(2)}, u32[]{:S(2)}) collective-permute-start(bf16[8,128,256]{2,1,0:T(8,128)(2,1)S(1)} %slice.57), channel_id=1, source_target_pairs={{0,112},{1,113},{2,114},{3,115},{4,116},{5,117},{6,118},{7,119},{8... | collective-permute-start | bytes 1572872 | tf_op jit(solution)/shard_map/ppermute | solution.py:33
  110.3 17.2 %collective-permute-start.16 = (bf16[8,128,256]{2,1,0:T(8,128)(2,1)S(1)}, bf16[8,128,256]{2,1,0:T(8,128)(2,1)S(1)}, u32[]{:S(2)}, u32[]{:S(2)}) collective-permute-start(bf16[8,128,256]{2,1,0:T(8,128)(2,1)S(1)} %slice.56), channel_id=1, source_target_pairs={{0,16},{1,17},{2,18},{3,19},{4,20},{5,21},{6,22},{7,23},{8,24},{9,... | collective-permute-start | bytes 1572872 | tf_op jit(solution)/shard_map/ppermute | solution.py:33
  112.2 3.0 %copy-start.4 = (s32[3,200]{1,0:T(4,128)S(1)}, s32[3,200]{1,0:T(4,128)}, u32[]{:S(2)}) copy-start(s32[3,200]{1,0:T(4,128)} %get-tuple-element.11.refs_4_.order_ref) | copy-start | bytes 7204
  112.2 3.0 %copy-start.5 = (s32[3,100]{1,0:T(4,128)S(1)}, s32[3,100]{1,0:T(4,128)}, u32[]{:S(2)}) copy-start(s32[3,100]{1,0:T(4,128)} %get-tuple-element.12.row_ref) | copy-start | bytes 3604
  112.2 3.0 %copy-start.7 = (s32[6]{0:T(128)S(1)}, s32[6]{0:T(128)}, u32[]{:S(2)}) copy-start(s32[6]{0:T(128)} %get-tuple-element.13.pairs_ref) | copy-start | bytes 76
  112.2 18.4 %collective-permute-start.21 = (bf16[2,1,8,128,128]{4,3,2,1,0:T(8,128)(2,1)}, bf16[2,1,8,128,128]{4,3,2,1,0:T(8,128)(2,1)S(1)}, u32[]{:S(2)}, u32[]{:S(2)}) collective-permute-start(bf16[2,1,8,128,128]{4,3,2,1,0:T(8,128)(2,1)} %gate.13), channel_id=1, source_target_pairs={{0,1},{1,0},{2,3},{3,2},{4,5},{5,4},{6,7},{7,6},{8,9},{9,8},{10,11... | collective-permute-start | bytes 1572872 | tf_op jit(solution)/shard_map/ppermute | solution.py:33
  126.9 0.6 copy-start.6
  127.6 7.7 %collective-permute-start.24 = (bf16[16,128,256]{2,1,0:T(8,128)(2,1)S(1)}, bf16[16,128,256]{2,1,0:T(8,128)(2,1)S(1)}, u32[]{:S(2)}, u32[]{:S(2)}) collective-permute-start(bf16[16,128,256]{2,1,0:T(8,128)(2,1)S(1)} %pad_maximum_fusion.2), channel_id=1, source_target_pairs={{0,8},{1,9},{2,10},{3,11},{4,12},{5,13},{6,14},{7,15},{8,0},{9,1},... | collective-permute-start | bytes 3145736 | tf_op jit(solution)/shard_map/ppermute | solution.py:33
  130.6 0.8 copy-start.11
  131.4 3.9 %collective-permute-start.23 = (bf16[16,128,256]{2,1,0:T(8,128)(2,1)}, bf16[16,128,256]{2,1,0:T(8,128)(2,1)S(1)}, u32[]{:S(2)}, u32[]{:S(2)}) collective-permute-start(bf16[16,128,256]{2,1,0:T(8,128)(2,1)} %gate.15), channel_id=1, source_target_pairs={{0,8},{1,9},{2,10},{3,11},{4,12},{5,13},{6,14},{7,15},{8,0},{9,1},... | collective-permute-start | bytes 3145736 | tf_op jit(solution)/shard_map/ppermute | solution.py:33
  131.5 4.7 %collective-permute-start.22 = (bf16[16,128,256]{2,1,0:T(8,128)(2,1)}, bf16[16,128,256]{2,1,0:T(8,128)(2,1)S(1)}, u32[]{:S(2)}, u32[]{:S(2)}) collective-permute-start(bf16[16,128,256]{2,1,0:T(8,128)(2,1)} %gate.14), channel_id=1, source_target_pairs={{0,8},{1,9},{2,10},{3,11},{4,12},{5,13},{6,14},{7,15},{8,0},{9,1},... | collective-permute-start | bytes 3145736 | tf_op jit(solution)/shard_map/ppermute | solution.py:33
  132.0 4.2 %copy-start.2 = (bf16[1024,128]{1,0:T(8,128)(2,1)S(1)}, bf16[1024,128]{1,0:T(8,128)(2,1)}, u32[]{:S(2)}) copy-start(bf16[1024,128]{1,0:T(8,128)(2,1)} %drive_real.1) | copy-start | bytes 786436
  132.0 4.2 %copy-start.3 = (bf16[1024,128]{1,0:T(8,128)(2,1)S(1)}, bf16[1024,128]{1,0:T(8,128)(2,1)}, u32[]{:S(2)}) copy-start(bf16[1024,128]{1,0:T(8,128)(2,1)} %drive_imag.1) | copy-start | bytes 786436

commit v10 on v9

--- a/solution.py
+++ b/solution.py
@@ -408,15 +408,19 @@
     own_up, own_down = shift(panel, "z", 1), shift(panel, "z", -1)
 
     lists = make_lists(place, block_cols, block_counts)
-    part = shift(after(both[:, :2], neighbour, own_up, own_down, lists[0]), "yhi")
+    part = shift(after(both[:, :2], neighbour), "yhi")
     up1 = jnp.concatenate([own_up, shift(neighbour, "z", 1)], axis=0)
     down1 = jnp.concatenate([own_down, shift(neighbour, "z", -1)], axis=0)
 
-    far_ham = shift(from_left[0], "x", 1)
-    far_margin = shift(from_right[1], "x", -1)
+    far_ham = shift(after(from_left[0], up1), "x", 1)
+    far_margin = shift(after(from_right[1], down1), "x", -1)
     up2, down2 = shift(up1, "z", 1), shift(down1, "z", -1)
     late = shift(
-        after(jnp.concatenate([both[:, 2:], from_left[:, 2:], from_right[:, 2:]], axis=1), part),
+        after(
+            jnp.concatenate([both[:, 2:], from_left[:, 2:], from_right[:, 2:]], axis=1),
+            part,
+            lists[0],
+        ),
         "yhi",
     )
 
@@ -433,8 +437,8 @@
         "yhi",
     )
 
-    up3 = after(up3, part_left, part_right, late, both_come)
-    down3 = after(down3, part_left, part_right, late, both_come)
+    up3 = after(up3, part_left, part_right, both_come)
+    down3 = after(down3, part_left, part_right, both_come)
     up4, down4 = shift(up3[:rows], "z", 1), shift(down3[rows:], "z", -1)
 
     early = (both, from_left, from_right, far_ham, far_margin, part_on, part_left, part_right)

time: 142 us -> 137 us (0.965)
  local copies, waits for them, and re-layouts: 20.4 us -> 17 us
  starting transfers between devices: 56.7 us -> 59.7 us
  waiting for transfers between devices: 26.6 us -> 23.8 us
    ppermute x25, waiting for transfers between devices: 24.4 us -> 20.6 us  [shift(): return lax.ppermute(array, AXES, moves(axis, by))]
    ppermute x25, starting transfers between devices: 46 us -> 48.2 us  [shift(): return lax.ppermute(array, AXES, moves(axis, by))]
    unnamed x38 -> x40, local copies, waits for them, and re-layouts: 6.64 us -> 4.99 us
  transfers between devices with their start and end apart: 26 -> 26, of which waited for: 7 -> 8; matrix products, arithmetic and copies ran while one was open for 13% -> 10% of each run, Pallas kernels for 19% -> 19%
where the time goes in v10:
time: 137 us; the launch traced here: 136 us
  starting transfers between devices  59.7 us (44%)
  Pallas kernels  30.8 us (22%)
  waiting for transfers between devices  23.8 us (17%)
  local copies, waits for them, and re-layouts  17 us (12%)
  other arithmetic  3.61 us (3%)
    ppermute x25, starting transfers between devices, shift(): return lax.ppermute(array, AXES, moves(axis, by))  48.2 us
    ppermute x25, waiting for transfers between devices, shift(): return lax.ppermute(array, AXES, moves(axis, by))  20.6 us
    all_to_all x1, starting transfers between devices, per_device(): both_come = lax.all_to_all(pack_twice(come), 'core', 0, 0, tiled=True)  11.5 us
    pallas_call x1, Pallas kernels, early_products(): pl.pallas_call(early_kernel, in_specs=[SMEM] * 3 + [ANY] * len(args), out...  10.9 us
    pallas_call x1, Pallas kernels, pack_twice(): pl.pallas_call(pack_kernel, in_specs=[ANY] * len(parts), out_specs=ANY, o...  6.41 us
    pallas_call x1, Pallas kernels, make_lists(): pl.pallas_call(list_kernel, in_specs=[SMEM] * 3, out_specs=[SMEM] * 3, ou...  5.24 us
    unnamed x40, local copies, waits for them, and re-layouts  4.99 us
    pallas_call x1, Pallas kernels, last_products(): pl.pallas_call(last_kernel, in_specs=[SMEM] * 3 + [ANY] * len(parts) + [V...  4.95 us
  transfers between devices with their start and end apart: 26, of which 8 were waited for; matrix products, arithmetic and copies ran while one was open for 10% of the time, Pallas kernels for 19%

profile of v10, /device:TPU:1, one launch (start us, length us, event | category | flops | bytes accessed | tf_op | source)
XLA Modules:
  0.0 135.9 jit_solution(13741918175406941410)
XLA Ops:
  0.6 1.5 %copy_bitcast_fusion = (bf16[1,3,8,128,128]{4,3,2,1,0:T(8,128)(2,1)S(1)}, bf16[1,3,8,128,128]{4,3,2,1,0:T(8,128)(2,1)S(1)}) fusion(bf16[8,3,128,128]{3,2,1,0:T(8,128)(2,1)} %param.9, bf16[8,3,128,128]{3,2,1,0:T(8,128)(2,1)} %param.8), kind=kLoop, calls=%fused_computation.10 | loop fusion | bytes 3145728 | tf_op jit(solution)/shard_map/stack | solution.py:402
  2.1 0.0 copy-start
  2.1 0.0 copy-start.1
  2.1 0.1 pad_maximum_fusion.refs_3_
  2.3 3.4 %collective-permute-start.8 = (bf16[2,3,8,128,128]{4,3,2,1,0:T(8,128)(2,1)S(1)}, bf16[2,3,8,128,128]{4,3,2,1,0:T(8,128)(2,1)S(1)}, u32[]{:S(2)}, u32[]{:S(2)}) collective-permute-start(bf16[2,3,8,128,128]{4,3,2,1,0:T(8,128)(2,1)S(1)} %pad_maximum_fusion.refs_3_), channel_id=1, source_target_pairs={{0,6},{1,7},{2,0},{3,1},{4,2},{5,3},{6,4},{7,5},{8,14},{9,15},{10,... | collective-permute-start | bytes 4718600 | tf_op jit(solution)/shard_map/ppermute | solution.py:33
  5.7 0.1 pad_maximum_fusion.3
  5.8 0.0 copy-start.18
  5.8 1.4 %collective-permute-start.1 = (bf16[8,128,256]{2,1,0:T(8,128)(2,1)S(1)}, bf16[8,128,256]{2,1,0:T(8,128)(2,1)S(1)}, u32[]{:S(2)}, u32[]{:S(2)}) collective-permute-start(bf16[8,128,256]{2,1,0:T(8,128)(2,1)S(1)} %bitcast.26), channel_id=1, source_target_pairs={{0,128},{1,129},{2,130},{3,131},{4,132},{5,133},{6,134},{7,135},{8... | collective-permute-start | bytes 1572872 | tf_op jit(solution)/shard_map/ppermute | solution.py:33
  7.2 5.6 %collective-permute-start.9 = (bf16[8,128,256]{2,1,0:T(8,128)(2,1)S(1)}, bf16[8,128,256]{2,1,0:T(8,128)(2,1)S(1)}, u32[]{:S(2)}, u32[]{:S(2)}) collective-permute-start(bf16[8,128,256]{2,1,0:T(8,128)(2,1)S(1)} %bitcast.27), channel_id=1, source_target_pairs={{0,112},{1,113},{2,114},{3,115},{4,116},{5,117},{6,118},{7,119},{8... | collective-permute-start | bytes 1572872 | tf_op jit(solution)/shard_map/ppermute | solution.py:33
  12.7 4.7 %collective-permute-done.1.refs_1_ = bf16[8,128,256]{2,1,0:T(8,128)(2,1)S(1)} collective-permute-done((bf16[8,128,256]{2,1,0:T(8,128)(2,1)S(1)}, bf16[8,128,256]{2,1,0:T(8,128)(2,1)S(1)}, u32[]{:S(2)}, u32[]{:S(2)}) %collective-permute-start.1) | collective-permute-done | bytes 524320 | tf_op jit(solution)/shard_map/ppermute | solution.py:33
  17.4 6.5 %collective-permute-start.10 = (bf16[8,128,256]{2,1,0:T(8,128)(2,1)S(1)}, bf16[8,128,256]{2,1,0:T(8,128)(2,1)S(1)}, u32[]{:S(2)}, u32[]{:S(2)}) collective-permute-start(bf16[8,128,256]{2,1,0:T(8,128)(2,1)S(1)} %collective-permute-done.1.refs_1_), channel_id=1, source_target_pairs={{0,112},{1,113},{2,114},{3,115},{4,116},{5,117},{6,118},{7,119},{8... | collective-permute-start | bytes 1572872 | tf_op jit(solution)/shard_map/ppermute | solution.py:33
  23.9 0.0 collective-permute-done.9
  23.9 0.0 collective-permute-start.2
  23.9 1.1 fusion.refs_0_
  25.0 0.8 constant_dynamic-update-slice_fusion.3
  25.8 2.9 %collective-permute-start.5 = (bf16[2,2,8,128,128]{4,3,2,1,0:T(8,128)(2,1)}, bf16[2,2,8,128,128]{4,3,2,1,0:T(8,128)(2,1)S(1)}, u32[]{:S(2)}, u32[]{:S(2)}) collective-permute-start(bf16[2,2,8,128,128]{4,3,2,1,0:T(8,128)(2,1)} %gate.10), channel_id=1, source_target_pairs={{0,1},{1,0},{2,3},{3,2},{4,5},{5,4},{6,7},{7,6},{8,9},{9,8},{10,11... | collective-permute-start | bytes 3145736 | tf_op jit(solution)/shard_map/ppermute | solution.py:33
  28.8 4.6 %collective-permute-done.10 = bf16[8,128,256]{2,1,0:T(8,128)(2,1)S(1)} collective-permute-done((bf16[8,128,256]{2,1,0:T(8,128)(2,1)S(1)}, bf16[8,128,256]{2,1,0:T(8,128)(2,1)S(1)}, u32[]{:S(2)}, u32[]{:S(2)}) %collective-permute-start.10) | collective-permute-done | bytes 524320 | tf_op jit(solution)/shard_map/ppermute | solution.py:33
  33.4 0.8 constant_dynamic-update-slice_fusion.2.refs_1_.refs_3_
  34.2 2.3 %collective-permute-done.2 = bf16[8,128,256]{2,1,0:T(8,128)(2,1)S(1)} collective-permute-done((bf16[8,128,256]{2,1,0:T(8,128)(2,1)S(1)}, bf16[8,128,256]{2,1,0:T(8,128)(2,1)S(1)}, u32[]{:S(2)}, u32[]{:S(2)}) %collective-permute-start.2) | collective-permute-done | bytes 524320 | tf_op jit(solution)/shard_map/ppermute | solution.py:33
  36.5 2.2 %collective-permute-done.8.refs_5_ = bf16[2,3,8,128,128]{4,3,2,1,0:T(8,128)(2,1)S(1)} collective-permute-done((bf16[2,3,8,128,128]{4,3,2,1,0:T(8,128)(2,1)S(1)}, bf16[2,3,8,128,128]{4,3,2,1,0:T(8,128)(2,1)S(1)}, u32[]{:S(2)}, u32[]{:S(2)}) %collective-permute-start.8) | collective-permute-done | bytes 1572896 | tf_op jit(solution)/shard_map/ppermute | solution.py:33
  38.7 1.0 slice_bitcast_fusion.refs_0_
  39.7 0.4 copy-done.14
  40.2 3.4 %collective-permute-start.11 = (bf16[3,8,128,128]{3,2,1,0:T(8,128)(2,1)}, bf16[3,8,128,128]{3,2,1,0:T(8,128)(2,1)}, u32[]{:S(2)}, u32[]{:S(2)}) collective-permute-start(bf16[3,8,128,128]{3,2,1,0:T(8,128)(2,1)} %gate.12), channel_id=1, source_target_pairs={{0,6},{1,7},{2,0},{3,1},{4,2},{5,3},{6,4},{7,5},{8,14},{9,15},{10,... | collective-permute-start | bytes 2359304 | tf_op jit(solution)/shard_map/ppermute | solution.py:33
  43.6 1.0 slice_bitcast_fusion.1.refs_0_
  44.6 0.5 copy-done.15
  45.1 5.6 %collective-permute-start.14 = (bf16[16,128,256]{2,1,0:T(8,128)(2,1)}, bf16[16,128,256]{2,1,0:T(8,128)(2,1)}, u32[]{:S(2)}, u32[]{:S(2)}) collective-permute-start(bf16[16,128,256]{2,1,0:T(8,128)(2,1)} %constant_dynamic-update-slice_fusion.2.refs_1_.refs_3_), channel_id=1, source_target_pairs={{0,112},{1,113},{2,114},{3,115},{4,116},{5,117},{6,118},{7,119},{8... | collective-permute-start | bytes 3145736 | tf_op jit(solution)/shard_map/ppermute | solution.py:33
  50.7 0.6 stack.41.place_ref
  51.3 5.2 %make_lists.1 = (s32[3,200]{1,0:T(4,128)}, s32[3,100]{1,0:T(4,128)}, s32[6]{0:T(128)}) custom-call(s32[5]{0:T(128)} %stack.41.place_ref, s32[8,24]{1,0:T(8,128)} %cols_ref.1, s32[8]{0:T(128)} %counts_ref.1), custom_call_target="tpu_custom_call" | custom-call | tf_op jit(solution)/shard_map/make_lists/pallas_call | solution.py:111
  56.6 0.1 fusion.1
  56.7 1.0 slice-done
  57.6 0.2 slice-done.1
  57.8 1.3 pad_maximum_fusion.1.refs_0_
  59.1 1.0 copy-done.10
  60.1 3.7 %collective-permute-done.7.refs_1_.refs_6_ = bf16[3,8,128,128]{3,2,1,0:T(8,128)(2,1)} collective-permute-done((bf16[3,8,128,128]{3,2,1,0:T(8,128)(2,1)}, bf16[3,8,128,128]{3,2,1,0:T(8,128)(2,1)}, u32[]{:S(2)}, u32[]{:S(2)}) %collective-permute-start.7) | collective-permute-done | bytes 786464 | tf_op jit(solution)/shard_map/ppermute | solution.py:33
  63.9 2.7 %collective-permute-start.13 = (bf16[2,2,8,128,128]{4,3,2,1,0:T(8,128)(2,1)}, bf16[2,2,8,128,128]{4,3,2,1,0:T(8,128)(2,1)S(1)}, u32[]{:S(2)}, u32[]{:S(2)}) collective-permute-start(bf16[2,2,8,128,128]{4,3,2,1,0:T(8,128)(2,1)} %gate.13.refs_8_), channel_id=1, source_target_pairs={{0,6},{1,7},{2,0},{3,1},{4,2},{5,3},{6,4},{7,5},{8,14},{9,15},{10,... | collective-permute-start | bytes 3145736 | tf_op jit(solution)/shard_map/ppermute | solution.py:33
  66.5 2.9 %collective-permute-start.18 = (bf16[2,3,8,128,128]{4,3,2,1,0:T(8,128)(2,1)}, bf16[2,3,8,128,128]{4,3,2,1,0:T(8,128)(2,1)}, u32[]{:S(2)}, u32[]{:S(2)}) collective-permute-start(bf16[2,3,8,128,128]{4,3,2,1,0:T(8,128)(2,1)} %gate.16), channel_id=1, source_target_pairs={{0,1},{1,0},{2,3},{3,2},{4,5},{5,4},{6,7},{7,6},{8,9},{9,8},{10,11... | collective-permute-start | bytes 4718600 | tf_op jit(solution)/shard_map/ppermute | solution.py:33
  69.5 2.2 %collective-permute-done.14.refs_5_ = bf16[16,128,256]{2,1,0:T(8,128)(2,1)} collective-permute-done((bf16[16,128,256]{2,1,0:T(8,128)(2,1)}, bf16[16,128,256]{2,1,0:T(8,128)(2,1)}, u32[]{:S(2)}, u32[]{:S(2)}) %collective-permute-start.14) | collective-permute-done | bytes 1048608 | tf_op jit(solution)/shard_map/ppermute | solution.py:33
  71.7 3.4 %collective-permute-start.16 = (bf16[16,128,256]{2,1,0:T(8,128)(2,1)}, bf16[16,128,256]{2,1,0:T(8,128)(2,1)}, u32[]{:S(2)}, u32[]{:S(2)}) collective-permute-start(bf16[16,128,256]{2,1,0:T(8,128)(2,1)} %collective-permute-done.14.refs_5_), channel_id=1, source_target_pairs={{0,112},{1,113},{2,114},{3,115},{4,116},{5,117},{6,118},{7,119},{8... | collective-permute-start | bytes 3145736 | tf_op jit(solution)/shard_map/ppermute | solution.py:33
  75.1 6.4 %pack.1 = bf16[160,128,256]{2,1,0:T(8,128)(2,1)} custom-call(bf16[8,128,256]{2,1,0:T(8,128)(2,1)} %bitcast.29, bf16[8,128,256]{2,1,0:T(8,128)(2,1)} %copy-done.17, bf16[16,128,256]{2,1,0:T(8,128)(2,1)} %copy-done.12, bf16[16,128,256]{2,1,0:T(8,128)(2,1)} %constant_dynamic-update-slice_fusion.2.refs_1_.refs_3_, ...), custom_call_target="tpu_custom_call" | custom-call | bytes 12000000 | tf_op jit(solution)/shard_map/pack/pallas_call | solution.py:311
  81.5 11.5 %all-to-all-start = ((bf16[160,128,256]{2,1,0:T(8,128)(2,1)}), bf16[160,128,256]{2,1,0:T(8,128)(2,1)}, u32[]{:S(2)}, u32[]{:S(2)}) async-start(bf16[160,128,256]{2,1,0:T(8,128)(2,1)} %pack.1), calls=%async_computation | async-start | bytes 20971520 | tf_op jit(solution)/shard_map/all_to_all | solution.py:432
  93.0 0.9 slice_bitcast_fusion.3
  93.9 0.9 slice_bitcast_fusion.2
  94.8 2.7 %collective-permute-start.20 = (bf16[2,8,128,128]{3,2,1,0:T(8,128)(2,1)}, bf16[2,8,128,128]{3,2,1,0:T(8,128)(2,1)}, u32[]{:S(2)}, u32[]{:S(2)}) collective-permute-start(bf16[2,8,128,128]{3,2,1,0:T(8,128)(2,1)} %slice_bitcast_fusion.2), channel_id=1, source_target_pairs={{0,6},{1,7},{2,0},{3,1},{4,2},{5,3},{6,4},{7,5},{8,14},{9,15},{10,... | collective-permute-start | bytes 1572872 | tf_op jit(solution)/shard_map/ppermute | solution.py:33
  97.5 1.0 slice_bitcast_fusion.4
  98.4 3.2 %all-to-all-done.refs_3_.refs_5_.refs_0_ = bf16[160,128,256]{2,1,0:T(8,128)(2,1)} async-done(((bf16[160,128,256]{2,1,0:T(8,128)(2,1)}), bf16[160,128,256]{2,1,0:T(8,128)(2,1)}, u32[]{:S(2)}, u32[]{:S(2)}) %all-to-all-start) | async-done | bytes 10485792 | tf_op jit(solution)/shard_map/all_to_all | solution.py:432
  101.7 1.1 slice.53
  102.8 3.0 %collective-permute-start.17 = (bf16[8,128,256]{2,1,0:T(8,128)(2,1)S(1)}, bf16[8,128,256]{2,1,0:T(8,128)(2,1)S(1)}, u32[]{:S(2)}, u32[]{:S(2)}) collective-permute-start(bf16[8,128,256]{2,1,0:T(8,128)(2,1)S(1)} %slice.53), channel_id=1, source_target_pairs={{0,112},{1,113},{2,114},{3,115},{4,116},{5,117},{6,118},{7,119},{8... | collective-permute-start | bytes 1572872 | tf_op jit(solution)/shard_map/ppermute | solution.py:33
  105.8 1.1 slice.52
  106.9 0.1 collective-permute-start.15
  107.0 1.0 slice_bitcast_fusion.5
  107.9 0.8 pad_maximum_fusion.4.refs_0_
  108.8 0.0 collective-permute-done.19.refs_2_
  108.9 0.8 copy-done.11
  109.6 2.1 %collective-permute-start.21 = (bf16[2,1,8,128,128]{4,3,2,1,0:T(8,128)(2,1)}, bf16[2,1,8,128,128]{4,3,2,1,0:T(8,128)(2,1)S(1)}, u32[]{:S(2)}, u32[]{:S(2)}) collective-permute-start(bf16[2,1,8,128,128]{4,3,2,1,0:T(8,128)(2,1)} %gate.17), channel_id=1, source_target_pairs={{0,1},{1,0},{2,3},{3,2},{4,5},{5,4},{6,7},{7,6},{8,9},{9,8},{10,11... | collective-permute-start | bytes 1572872 | tf_op jit(solution)/shard_map/ppermute | solution.py:33
  111.8 10.9 %products_early.1 = (bf16[192,128,256]{2,1,0:T(8,128)(2,1)S(1)}, bf16[2,24,8,128,128]{4,3,2,1,0:T(8,128)(2,1)S(1)}, f32[8,256,256]{2,1,0:T(8,128)S(1)}, f32[8,128]{1,0:T(8,128)S(1)}) custom-call(s32[3,200]{1,0:T(4,128)S(1)} %copy-done.4, s32[3,100]{1,0:T(4,128)S(1)} %copy-done.5, s32[6]{0:T(128)S(1)} %copy-done.7, ...), custom_call_target="tpu_custom_call" | custom-call | bytes 30000000 | tf_op jit(solution)/shard_map/products_early/pallas_call | solution.py:340
  122.6 0.6 copy-done.6
  123.2 0.1 pad_maximum_fusion.2
  123.3 2.0 %collective-permute-start.24 = (bf16[16,128,256]{2,1,0:T(8,128)(2,1)S(1)}, bf16[16,128,256]{2,1,0:T(8,128)(2,1)S(1)}, u32[]{:S(2)}, u32[]{:S(2)}) collective-permute-start(bf16[16,128,256]{2,1,0:T(8,128)(2,1)S(1)} %pad_maximum_fusion.2), channel_id=1, source_target_pairs={{0,8},{1,9},{2,10},{3,11},{4,12},{5,13},{6,14},{7,15},{8,0},{9,1},... | collective-permute-start | bytes 3145736 | tf_op jit(solution)/shard_map/ppermute | solution.py:33
  125.3 0.8 copy-done.16
  126.1 0.4 collective-permute-start.23
  126.5 0.1 collective-permute-start.22
  126.6 3.4 %products_main.1 = (bf16[2,24,8,128,128]{4,3,2,1,0:T(8,128)(2,1)S(1)}, f32[8,256,256]{2,1,0:T(8,128)S(1)}) custom-call(s32[3,200]{1,0:T(4,128)S(1)} %copy-done.4, s32[3,100]{1,0:T(4,128)S(1)} %copy-done.5, s32[6]{0:T(128)S(1)} %copy-done.7, bf16[192,128,256]{2,1,0:T(8,128)(2,1)S(1)} %get-tuple-element.15.panel, ...), custom_call_target="tpu_custom_call", output_to_operand_aliasing={{0}: (4, {}), {1}: (5, {})} | custom-call | bytes 12000000 | tf_op jit(solution)/shard_map/products_main/pallas_call | solution.py:358
  130.0 0.8 collective-permute-done.22.other_up
  130.8 5.0 %products_last.1 = (f32[1024,128]{1,0:T(8,128)}, f32[1024,128]{1,0:T(8,128)}) custom-call(s32[3,200]{1,0:T(4,128)S(1)} %copy-done.4, s32[3,100]{1,0:T(4,128)S(1)} %copy-done.5, s32[6]{0:T(128)S(1)} %copy-done.7, bf16[8,128,256]{2,1,0:T(8,128)(2,1)S(1)} %collective-permute-done.15.end_up, bf16[8,128,256]{2,1,0:T(8,128)(2,1)S(1)} %collective-permute-done.17.end_down, ...), custom_call_target="tpu_custom_call" | custom-call | bytes 12000000 | tf_op jit(solution)/shard_map/products_last/pallas_call | solution.py:373
  (66 shorter events, 0.2 us)
Async XLA Ops:
  2.1 3.6 %copy-start = (bf16[1024,128]{1,0:T(8,128)(2,1)S(1)}, bf16[1024,128]{1,0:T(8,128)(2,1)}, u32[]{:S(2)}) copy-start(bf16[1024,128]{1,0:T(8,128)(2,1)} %pert_imag.1) | copy-start | bytes 786436
  2.1 3.6 %copy-start.1 = (bf16[1024,128]{1,0:T(8,128)(2,1)S(1)}, bf16[1024,128]{1,0:T(8,128)(2,1)}, u32[]{:S(2)}) copy-start(bf16[1024,128]{1,0:T(8,128)(2,1)} %pert_real.1) | copy-start | bytes 786436
  2.3 22.7 %copy-start.13 = (bf16[2,3,8,128,128]{4,3,2,1,0:T(8,128)(2,1)}, bf16[2,3,8,128,128]{4,3,2,1,0:T(8,128)(2,1)S(1)}, u32[]{:S(2)}) copy-start(bf16[2,3,8,128,128]{4,3,2,1,0:T(8,128)(2,1)S(1)} %pad_maximum_fusion.refs_3_) | copy-start | bytes 4718596
  2.3 36.4 %collective-permute-start.8 = (bf16[2,3,8,128,128]{4,3,2,1,0:T(8,128)(2,1)S(1)}, bf16[2,3,8,128,128]{4,3,2,1,0:T(8,128)(2,1)S(1)}, u32[]{:S(2)}, u32[]{:S(2)}) collective-permute-start(bf16[2,3,8,128,128]{4,3,2,1,0:T(8,128)(2,1)S(1)} %pad_maximum_fusion.refs_3_), channel_id=1, source_target_pairs={{0,6},{1,7},{2,0},{3,1},{4,2},{5,3},{6,4},{7,5},{8,14},{9,15},{10,... | collective-permute-start | bytes 4718600 | tf_op jit(solution)/shard_map/ppermute | solution.py:33
  5.7 37.9 %collective-permute-start.6 = (bf16[2,3,8,128,128]{4,3,2,1,0:T(8,128)(2,1)S(1)}, bf16[2,3,8,128,128]{4,3,2,1,0:T(8,128)(2,1)S(1)}, u32[]{:S(2)}, u32[]{:S(2)}) collective-permute-start(bf16[2,3,8,128,128]{4,3,2,1,0:T(8,128)(2,1)S(1)} %pad_maximum_fusion.refs_3_), channel_id=1, source_target_pairs={{0,2},{1,3},{2,4},{3,5},{4,6},{5,7},{6,0},{7,1},{8,10},{9,11},{10,... | collective-permute-start | bytes 4718600 | tf_op jit(solution)/shard_map/ppermute | solution.py:33
  5.8 19.2 %copy-start.18 = (bf16[1024,256]{1,0:T(8,128)(2,1)}, bf16[1024,256]{1,0:T(8,128)(2,1)S(1)}, u32[]{:S(2)}) copy-start(bf16[1024,256]{1,0:T(8,128)(2,1)S(1)} %pad_maximum_fusion.3) | copy-start | bytes 1572868
  5.8 11.7 %collective-permute-start.1 = (bf16[8,128,256]{2,1,0:T(8,128)(2,1)S(1)}, bf16[8,128,256]{2,1,0:T(8,128)(2,1)S(1)}, u32[]{:S(2)}, u32[]{:S(2)}) collective-permute-start(bf16[8,128,256]{2,1,0:T(8,128)(2,1)S(1)} %bitcast.26), channel_id=1, source_target_pairs={{0,128},{1,129},{2,130},{3,131},{4,132},{5,133},{6,134},{7,135},{8... | collective-permute-start | bytes 1572872 | tf_op jit(solution)/shard_map/ppermute | solution.py:33
  7.2 16.8 %collective-permute-start.9 = (bf16[8,128,256]{2,1,0:T(8,128)(2,1)S(1)}, bf16[8,128,256]{2,1,0:T(8,128)(2,1)S(1)}, u32[]{:S(2)}, u32[]{:S(2)}) collective-permute-start(bf16[8,128,256]{2,1,0:T(8,128)(2,1)S(1)} %bitcast.27), channel_id=1, source_target_pairs={{0,112},{1,113},{2,114},{3,115},{4,116},{5,117},{6,118},{7,119},{8... | collective-permute-start | bytes 1572872 | tf_op jit(solution)/shard_map/ppermute | solution.py:33
  12.7 13.1 %collective-permute-start = (bf16[8,128,256]{2,1,0:T(8,128)(2,1)S(1)}, bf16[8,128,256]{2,1,0:T(8,128)(2,1)S(1)}, u32[]{:S(2)}, u32[]{:S(2)}) collective-permute-start(bf16[8,128,256]{2,1,0:T(8,128)(2,1)S(1)} %bitcast.28), channel_id=1, source_target_pairs={{0,16},{1,17},{2,18},{3,19},{4,20},{5,21},{6,22},{7,23},{8,24},{9,... | collective-permute-start | bytes 1572872 | tf_op jit(solution)/shard_map/ppermute | solution.py:33
  17.4 7.6 %copy-start.17 = (bf16[8,128,256]{2,1,0:T(8,128)(2,1)}, bf16[8,128,256]{2,1,0:T(8,128)(2,1)S(1)}, u32[]{:S(2)}) copy-start(bf16[8,128,256]{2,1,0:T(8,128)(2,1)S(1)} %collective-permute-done.1.refs_1_) | copy-start | bytes 1572868
  17.4 15.9 %collective-permute-start.10 = (bf16[8,128,256]{2,1,0:T(8,128)(2,1)S(1)}, bf16[8,128,256]{2,1,0:T(8,128)(2,1)S(1)}, u32[]{:S(2)}, u32[]{:S(2)}) collective-permute-start(bf16[8,128,256]{2,1,0:T(8,128)(2,1)S(1)} %collective-permute-done.1.refs_1_), channel_id=1, source_target_pairs={{0,112},{1,113},{2,114},{3,115},{4,116},{5,117},{6,118},{7,119},{8... | collective-permute-start | bytes 1572872 | tf_op jit(solution)/shard_map/ppermute | solution.py:33
  23.9 12.6 %collective-permute-start.2 = (bf16[8,128,256]{2,1,0:T(8,128)(2,1)S(1)}, bf16[8,128,256]{2,1,0:T(8,128)(2,1)S(1)}, u32[]{:S(2)}, u32[]{:S(2)}) collective-permute-start(bf16[8,128,256]{2,1,0:T(8,128)(2,1)S(1)} %collective-permute-done.1.refs_1_), channel_id=1, source_target_pairs={{0,16},{1,17},{2,18},{3,19},{4,20},{5,21},{6,22},{7,23},{8,24},{9,... | collective-permute-start | bytes 1572872 | tf_op jit(solution)/shard_map/ppermute | solution.py:33
  25.8 33.3 %collective-permute-start.5 = (bf16[2,2,8,128,128]{4,3,2,1,0:T(8,128)(2,1)}, bf16[2,2,8,128,128]{4,3,2,1,0:T(8,128)(2,1)S(1)}, u32[]{:S(2)}, u32[]{:S(2)}) collective-permute-start(bf16[2,2,8,128,128]{4,3,2,1,0:T(8,128)(2,1)} %gate.10), channel_id=1, source_target_pairs={{0,1},{1,0},{2,3},{3,2},{4,5},{5,4},{6,7},{7,6},{8,9},{9,8},{10,11... | collective-permute-start | bytes 3145736 | tf_op jit(solution)/shard_map/ppermute | solution.py:33
  36.5 8.1 %copy-start.12 = (bf16[16,128,256]{2,1,0:T(8,128)(2,1)}, bf16[16,128,256]{2,1,0:T(8,128)(2,1)S(1)}, u32[]{:S(2)}) copy-start(bf16[16,128,256]{2,1,0:T(8,128)(2,1)S(1)} %constant_dynamic-update-slice_fusion.refs_1_.refs_2_) | copy-start | bytes 3145732
  38.7 1.4 %copy-start.14 = (bf16[2,3,8,128,128]{4,3,2,1,0:T(8,128)(2,1)}, bf16[2,3,8,128,128]{4,3,2,1,0:T(8,128)(2,1)S(1)}, u32[]{:S(2)}) copy-start(bf16[2,3,8,128,128]{4,3,2,1,0:T(8,128)(2,1)S(1)} %collective-permute-done.8.refs_5_) | copy-start | bytes 4718596
  40.2 20.0 %collective-permute-start.11 = (bf16[3,8,128,128]{3,2,1,0:T(8,128)(2,1)}, bf16[3,8,128,128]{3,2,1,0:T(8,128)(2,1)}, u32[]{:S(2)}, u32[]{:S(2)}) collective-permute-start(bf16[3,8,128,128]{3,2,1,0:T(8,128)(2,1)} %gate.12), channel_id=1, source_target_pairs={{0,6},{1,7},{2,0},{3,1},{4,2},{5,3},{6,4},{7,5},{8,14},{9,15},{10,... | collective-permute-start | bytes 2359304 | tf_op jit(solution)/shard_map/ppermute | solution.py:33
  43.6 1.6 %copy-start.15 = (bf16[2,3,8,128,128]{4,3,2,1,0:T(8,128)(2,1)}, bf16[2,3,8,128,128]{4,3,2,1,0:T(8,128)(2,1)S(1)}, u32[]{:S(2)}) copy-start(bf16[2,3,8,128,128]{4,3,2,1,0:T(8,128)(2,1)S(1)} %collective-permute-done.6.refs_4_) | copy-start | bytes 4718596
  45.1 18.7 %collective-permute-start.7 = (bf16[3,8,128,128]{3,2,1,0:T(8,128)(2,1)}, bf16[3,8,128,128]{3,2,1,0:T(8,128)(2,1)}, u32[]{:S(2)}, u32[]{:S(2)}) collective-permute-start(bf16[3,8,128,128]{3,2,1,0:T(8,128)(2,1)} %gate.11), channel_id=1, source_target_pairs={{0,2},{1,3},{2,4},{3,5},{4,6},{5,7},{6,0},{7,1},{8,10},{9,11},{10,... | collective-permute-start | bytes 2359304 | tf_op jit(solution)/shard_map/ppermute | solution.py:33
  45.1 26.5 %collective-permute-start.14 = (bf16[16,128,256]{2,1,0:T(8,128)(2,1)}, bf16[16,128,256]{2,1,0:T(8,128)(2,1)}, u32[]{:S(2)}, u32[]{:S(2)}) collective-permute-start(bf16[16,128,256]{2,1,0:T(8,128)(2,1)} %constant_dynamic-update-slice_fusion.2.refs_1_.refs_3_), channel_id=1, source_target_pairs={{0,112},{1,113},{2,114},{3,115},{4,116},{5,117},{6,118},{7,119},{8... | collective-permute-start | bytes 3145736 | tf_op jit(solution)/shard_map/ppermute | solution.py:33
  50.7 24.4 %collective-permute-start.3 = (bf16[16,128,256]{2,1,0:T(8,128)(2,1)}, bf16[16,128,256]{2,1,0:T(8,128)(2,1)}, u32[]{:S(2)}, u32[]{:S(2)}) collective-permute-start(bf16[16,128,256]{2,1,0:T(8,128)(2,1)} %copy-done.12), channel_id=1, source_target_pairs={{0,16},{1,17},{2,18},{3,19},{4,20},{5,21},{6,22},{7,23},{8,24},{9,... | collective-permute-start | bytes 3145736 | tf_op jit(solution)/shard_map/ppermute | solution.py:33
  56.6 1.0 slice-start
  56.6 1.2 slice-start.1
  59.1 1.0 copy-start.10
  63.9 29.2 %collective-permute-start.12 = (bf16[2,2,8,128,128]{4,3,2,1,0:T(8,128)(2,1)}, bf16[2,2,8,128,128]{4,3,2,1,0:T(8,128)(2,1)S(1)}, u32[]{:S(2)}, u32[]{:S(2)}) collective-permute-start(bf16[2,2,8,128,128]{4,3,2,1,0:T(8,128)(2,1)} %gate.13.refs_8_), channel_id=1, source_target_pairs={{0,2},{1,3},{2,4},{3,5},{4,6},{5,7},{6,0},{7,1},{8,10},{9,11},{10,... | collective-permute-start | bytes 3145736 | tf_op jit(solution)/shard_map/ppermute | solution.py:33
  63.9 30.1 %collective-permute-start.13 = (bf16[2,2,8,128,128]{4,3,2,1,0:T(8,128)(2,1)}, bf16[2,2,8,128,128]{4,3,2,1,0:T(8,128)(2,1)S(1)}, u32[]{:S(2)}, u32[]{:S(2)}) collective-permute-start(bf16[2,2,8,128,128]{4,3,2,1,0:T(8,128)(2,1)} %gate.13.refs_8_), channel_id=1, source_target_pairs={{0,6},{1,7},{2,0},{3,1},{4,2},{5,3},{6,4},{7,5},{8,14},{9,15},{10,... | collective-permute-start | bytes 3145736 | tf_op jit(solution)/shard_map/ppermute | solution.py:33
  66.5 42.2 %collective-permute-start.18 = (bf16[2,3,8,128,128]{4,3,2,1,0:T(8,128)(2,1)}, bf16[2,3,8,128,128]{4,3,2,1,0:T(8,128)(2,1)}, u32[]{:S(2)}, u32[]{:S(2)}) collective-permute-start(bf16[2,3,8,128,128]{4,3,2,1,0:T(8,128)(2,1)} %gate.16), channel_id=1, source_target_pairs={{0,1},{1,0},{2,3},{3,2},{4,5},{5,4},{6,7},{7,6},{8,9},{9,8},{10,11... | collective-permute-start | bytes 4718600 | tf_op jit(solution)/shard_map/ppermute | solution.py:33
  71.7 30.0 %collective-permute-start.16 = (bf16[16,128,256]{2,1,0:T(8,128)(2,1)}, bf16[16,128,256]{2,1,0:T(8,128)(2,1)}, u32[]{:S(2)}, u32[]{:S(2)}) collective-permute-start(bf16[16,128,256]{2,1,0:T(8,128)(2,1)} %collective-permute-done.14.refs_5_), channel_id=1, source_target_pairs={{0,112},{1,113},{2,114},{3,115},{4,116},{5,117},{6,118},{7,119},{8... | collective-permute-start | bytes 3145736 | tf_op jit(solution)/shard_map/ppermute | solution.py:33
  75.1 30.7 %collective-permute-start.4 = (bf16[16,128,256]{2,1,0:T(8,128)(2,1)}, bf16[16,128,256]{2,1,0:T(8,128)(2,1)}, u32[]{:S(2)}, u32[]{:S(2)}) collective-permute-start(bf16[16,128,256]{2,1,0:T(8,128)(2,1)} %collective-permute-done.3.refs_4_), channel_id=1, source_target_pairs={{0,16},{1,17},{2,18},{3,19},{4,20},{5,21},{6,22},{7,23},{8,24},{9,... | collective-permute-start | bytes 3145736 | tf_op jit(solution)/shard_map/ppermute | solution.py:33
  81.5 20.2 %all-to-all-start = ((bf16[160,128,256]{2,1,0:T(8,128)(2,1)}), bf16[160,128,256]{2,1,0:T(8,128)(2,1)}, u32[]{:S(2)}, u32[]{:S(2)}) async-start(bf16[160,128,256]{2,1,0:T(8,128)(2,1)} %pack.1), calls=%async_computation | async-start | bytes 20971520 | tf_op jit(solution)/shard_map/all_to_all | solution.py:432
  93.0 8.6 %copy-start.8 = (bf16[2,2,8,128,128]{4,3,2,1,0:T(8,128)(2,1)}, bf16[2,2,8,128,128]{4,3,2,1,0:T(8,128)(2,1)S(1)}, u32[]{:S(2)}) copy-start(bf16[2,2,8,128,128]{4,3,2,1,0:T(8,128)(2,1)S(1)} %collective-permute-done.12.refs_1_.refs_9_) | copy-start | bytes 3145732
  93.9 14.9 %collective-permute-start.19 = (bf16[2,8,128,128]{3,2,1,0:T(8,128)(2,1)}, bf16[2,8,128,128]{3,2,1,0:T(8,128)(2,1)S(1)}, u32[]{:S(2)}, u32[]{:S(2)}) collective-permute-start(bf16[2,8,128,128]{3,2,1,0:T(8,128)(2,1)} %slice_bitcast_fusion.3), channel_id=1, source_target_pairs={{0,2},{1,3},{2,4},{3,5},{4,6},{5,7},{6,0},{7,1},{8,10},{9,11},{10,... | collective-permute-start | bytes 1572872 | tf_op jit(solution)/shard_map/ppermute | solution.py:33
  93.9 7.8 %copy-start.9 = (bf16[2,2,8,128,128]{4,3,2,1,0:T(8,128)(2,1)}, bf16[2,2,8,128,128]{4,3,2,1,0:T(8,128)(2,1)S(1)}, u32[]{:S(2)}) copy-start(bf16[2,2,8,128,128]{4,3,2,1,0:T(8,128)(2,1)S(1)} %collective-permute-done.13.refs_2_.refs_10_) | copy-start | bytes 3145732
  94.8 14.1 %collective-permute-start.20 = (bf16[2,8,128,128]{3,2,1,0:T(8,128)(2,1)}, bf16[2,8,128,128]{3,2,1,0:T(8,128)(2,1)}, u32[]{:S(2)}, u32[]{:S(2)}) collective-permute-start(bf16[2,8,128,128]{3,2,1,0:T(8,128)(2,1)} %slice_bitcast_fusion.2), channel_id=1, source_target_pairs={{0,6},{1,7},{2,0},{3,1},{4,2},{5,3},{6,4},{7,5},{8,14},{9,15},{10,... | collective-permute-start | bytes 1572872 | tf_op jit(solution)/shard_map/ppermute | solution.py:33
  102.8 20.4 %collective-permute-start.17 = (bf16[8,128,256]{2,1,0:T(8,128)(2,1)S(1)}, bf16[8,128,256]{2,1,0:T(8,128)(2,1)S(1)}, u32[]{:S(2)}, u32[]{:S(2)}) collective-permute-start(bf16[8,128,256]{2,1,0:T(8,128)(2,1)S(1)} %slice.53), channel_id=1, source_target_pairs={{0,112},{1,113},{2,114},{3,115},{4,116},{5,117},{6,118},{7,119},{8... | collective-permute-start | bytes 1572872 | tf_op jit(solution)/shard_map/ppermute | solution.py:33
  106.9 16.3 %collective-permute-start.15 = (bf16[8,128,256]{2,1,0:T(8,128)(2,1)S(1)}, bf16[8,128,256]{2,1,0:T(8,128)(2,1)S(1)}, u32[]{:S(2)}, u32[]{:S(2)}) collective-permute-start(bf16[8,128,256]{2,1,0:T(8,128)(2,1)S(1)} %slice.52), channel_id=1, source_target_pairs={{0,16},{1,17},{2,18},{3,19},{4,20},{5,21},{6,22},{7,23},{8,24},{9,... | collective-permute-start | bytes 1572872 | tf_op jit(solution)/shard_map/ppermute | solution.py:33
  108.8 3.0 %copy-start.4 = (s32[3,200]{1,0:T(4,128)S(1)}, s32[3,200]{1,0:T(4,128)}, u32[]{:S(2)}) copy-start(s32[3,200]{1,0:T(4,128)} %get-tuple-element.11.refs_2_.refs_4_.order_ref) | copy-start | bytes 7204
  108.8 3.0 %copy-start.5 = (s32[3,100]{1,0:T(4,128)S(1)}, s32[3,100]{1,0:T(4,128)}, u32[]{:S(2)}) copy-start(s32[3,100]{1,0:T(4,128)} %get-tuple-element.12.row_ref) | copy-start | bytes 3604
  108.8 3.0 %copy-start.7 = (s32[6]{0:T(128)S(1)}, s32[6]{0:T(128)}, u32[]{:S(2)}) copy-start(s32[6]{0:T(128)} %get-tuple-element.13.pairs_ref) | copy-start | bytes 76
  108.8 0.8 copy-start.11
  109.6 15.7 %collective-permute-start.21 = (bf16[2,1,8,128,128]{4,3,2,1,0:T(8,128)(2,1)}, bf16[2,1,8,128,128]{4,3,2,1,0:T(8,128)(2,1)S(1)}, u32[]{:S(2)}, u32[]{:S(2)}) collective-permute-start(bf16[2,1,8,128,128]{4,3,2,1,0:T(8,128)(2,1)} %gate.17), channel_id=1, source_target_pairs={{0,1},{1,0},{2,3},{3,2},{4,5},{5,4},{6,7},{7,6},{8,9},{9,8},{10,11... | collective-permute-start | bytes 1572872 | tf_op jit(solution)/shard_map/ppermute | solution.py:33
  122.6 0.6 copy-start.6
  123.3 6.7 %collective-permute-start.24 = (bf16[16,128,256]{2,1,0:T(8,128)(2,1)S(1)}, bf16[16,128,256]{2,1,0:T(8,128)(2,1)S(1)}, u32[]{:S(2)}, u32[]{:S(2)}) collective-permute-start(bf16[16,128,256]{2,1,0:T(8,128)(2,1)S(1)} %pad_maximum_fusion.2), channel_id=1, source_target_pairs={{0,8},{1,9},{2,10},{3,11},{4,12},{5,13},{6,14},{7,15},{8,0},{9,1},... | collective-permute-start | bytes 3145736 | tf_op jit(solution)/shard_map/ppermute | solution.py:33
  125.3 0.8 copy-start.16
  126.1 3.9 %collective-permute-start.23 = (bf16[16,128,256]{2,1,0:T(8,128)(2,1)}, bf16[16,128,256]{2,1,0:T(8,128)(2,1)S(1)}, u32[]{:S(2)}, u32[]{:S(2)}) collective-permute-start(bf16[16,128,256]{2,1,0:T(8,128)(2,1)} %gate.19), channel_id=1, source_target_pairs={{0,8},{1,9},{2,10},{3,11},{4,12},{5,13},{6,14},{7,15},{8,0},{9,1},... | collective-permute-start | bytes 3145736 | tf_op jit(solution)/shard_map/ppermute | solution.py:33
  126.5 4.3 %collective-permute-start.22 = (bf16[16,128,256]{2,1,0:T(8,128)(2,1)}, bf16[16,128,256]{2,1,0:T(8,128)(2,1)S(1)}, u32[]{:S(2)}, u32[]{:S(2)}) collective-permute-start(bf16[16,128,256]{2,1,0:T(8,128)(2,1)} %gate.18), channel_id=1, source_target_pairs={{0,8},{1,9},{2,10},{3,11},{4,12},{5,13},{6,14},{7,15},{8,0},{9,1},... | collective-permute-start | bytes 3145736 | tf_op jit(solution)/shard_map/ppermute | solution.py:33
  126.6 4.2 %copy-start.2 = (bf16[1024,128]{1,0:T(8,128)(2,1)S(1)}, bf16[1024,128]{1,0:T(8,128)(2,1)}, u32[]{:S(2)}) copy-start(bf16[1024,128]{1,0:T(8,128)(2,1)} %drive_real.1) | copy-start | bytes 786436
  126.6 4.2 %copy-start.3 = (bf16[1024,128]{1,0:T(8,128)(2,1)S(1)}, bf16[1024,128]{1,0:T(8,128)(2,1)}, u32[]{:S(2)}) copy-start(bf16[1024,128]{1,0:T(8,128)(2,1)} %drive_imag.1) | copy-start | bytes 786436
